TPU v7x, 32 devices: a whole 2x2x4 slice. The times are simulated.
32 devices in a mesh: dp: 8 (over z, x), tensor: 4 (over y, core).
Axes of the slice: x: 2, y: 2, z: 4, core: 2. Of those that a mesh axis runs over, the one named last changes fastest.
Arguments:
- tokens: bfloat16 [24, 1024, 512], P(None, 'dp'), may hold values from -6 to 6
- cotangent: bfloat16 [24, 1024, 512], P(None, 'dp'), may hold values from -6 to 6
- ln_gain: float32 [512], replicated, may hold values from 0.5 to 1.5
- ln_bias: float32 [512], replicated, may hold values from -3 to 3
- skip_gain: float32 [512], replicated, may hold values from -3 to 3
- in_real: bfloat16 [512, 256], P(None, 'tensor'), may hold values from -0.25 to 0.25
- in_imag: bfloat16 [512, 256], P(None, 'tensor'), may hold values from -0.25 to 0.25
- out_real: bfloat16 [256, 512], P('tensor'), may hold values from -0.25 to 0.25
- out_imag: bfloat16 [256, 512], P('tensor'), may hold values from -0.25 to 0.25
- nu_log: float32 [256], P('tensor'), may hold values from -6.9 to -3
- theta_log: float32 [256], P('tensor'), may hold values from -4 to 0
- gamma_log: float32 [256], P('tensor'), may hold values from -4 to -2
- up_weight: bfloat16 [512, 1024], P(None, 'tensor'), may hold values from -0.25 to 0.25
- gate_weight: bfloat16 [512, 1024], P(None, 'tensor'), may hold values from -0.25 to 0.25
- down_weight: bfloat16 [1024, 512], P('tensor'), may hold values from -0.375 to 0.375
- lengths: int32 [24], replicated, may hold values from 128 to 1024, as said below
Outputs:
- block_out: bfloat16 [24, 1024, 512], P(None, 'dp')
- input_grad: float32 [24, 1024, 512], P(None, 'dp')
- ln_gain_grad: float32 [512], replicated
- ln_bias_grad: float32 [512], replicated
- skip_gain_grad: float32 [512], replicated
- in_real_grad: float32 [512, 256], P(None, 'tensor')
- in_imag_grad: float32 [512, 256], P(None, 'tensor')
- out_real_grad: float32 [256, 512], P('tensor')
- out_imag_grad: float32 [256, 512], P('tensor')
- nu_log_grad: float32 [256], P('tensor')
- theta_log_grad: float32 [256], P('tensor')
- gamma_log_grad: float32 [256], P('tensor')
- up_weight_grad: float32 [512, 1024], P(None, 'tensor')
- gate_weight_grad: float32 [512, 1024], P(None, 'tensor')
- down_weight_grad: float32 [1024, 512], P('tensor')
Inputs may be any that keep to these rules, and one draw needn't show every extreme that they name: `lengths`: live positions of each sequence; its other positions up to 1024 are padding.
All inputs are finite; a program needn't handle non-finite values.
Results may differ from a plain program's by a relative error of at most 0.0095.
Values may be sent and summed in bfloat16 or wider, within the bound.
No kernel may reach another device: no remote copies, remote signals or barrier semaphores. Data moves between devices by JAX's collectives and lax.ppermute only.
A program may use at most 192 MiB of HBM per device.

v0:
```python
import jax
import jax.numpy as jnp
from jax import lax
from jax.sharding import PartitionSpec as P

EPSILON = 1e-05


def layer_norm(token_rows, ln_gain, ln_bias):
    centre = jnp.mean(token_rows, axis=-1, keepdims=True)
    shifted = token_rows - centre
    variance = jnp.mean(shifted * shifted, axis=-1, keepdims=True)
    inv_scale = lax.rsqrt(variance + EPSILON)
    normed = shifted * inv_scale
    return (normed, inv_scale, normed * ln_gain + ln_bias)


def decay_terms(nu_log, theta_log, gamma_log):
    modulus = jnp.exp(-jnp.exp(nu_log))
    angle = jnp.exp(theta_log)
    return (modulus * jnp.cos(angle), modulus * jnp.sin(angle), jnp.exp(gamma_log))


def complex_step(earlier, latter):
    return (
        latter[0] * earlier[0] - latter[1] * earlier[1],
        latter[0] * earlier[1] + latter[1] * earlier[0],
        latter[0] * earlier[2] - latter[1] * earlier[3] + latter[2],
        latter[0] * earlier[3] + latter[1] * earlier[2] + latter[3],
    )


def linear_scan(decay_real, decay_imag, drive_real, drive_imag, backwards):
    full_shape = drive_real.shape
    elements = (
        jnp.broadcast_to(decay_real, full_shape),
        jnp.broadcast_to(decay_imag, full_shape),
        drive_real,
        drive_imag,
    )
    scanned = lax.associative_scan(complex_step, elements, reverse=backwards, axis=1)
    return (scanned[2], scanned[3])


def over_rows(left, right):
    return lax.dot_general(
        left, right, (((0,), (0,)), ((), ())), preferred_element_type=jnp.float32
    )


def against(left, right):
    return lax.dot_general(
        left, right, (((1,), (1,)), ((), ())), preferred_element_type=jnp.float32
    )


def deal_order(lengths, groups):
    seq_count = lengths.shape[0]
    per_device = seq_count // groups
    series = lax.iota(jnp.int32, seq_count)
    ranked = jnp.argsort(-(lengths * seq_count + series), stable=True)
    rounds = series // groups
    within = series % groups
    device_rank = jnp.where(rounds % 2 == 0, within, groups - 1 - within)
    slot_index = device_rank * per_device + rounds
    return jnp.zeros((seq_count,), jnp.int32).at[slot_index].set(ranked)


def forward_local(dealt_tokens, params):
    (
        ln_gain,
        ln_bias,
        skip_gain,
        in_real,
        in_imag,
        out_real,
        out_imag,
        decay_real,
        decay_imag,
        input_gain,
        up_weight,
        gate_weight,
    ) = params
    per_device, positions, model_width = dealt_tokens.shape
    token_rows = dealt_tokens.reshape(per_device * positions, model_width).astype(jnp.float32)
    normed, inv_scale, normed_out = layer_norm(token_rows, ln_gain, ln_bias)
    normed_low = normed_out.astype(jnp.bfloat16)
    states = in_real.shape[1]
    scan_shape = (per_device, positions, states)
    drive_real = jnp.dot(normed_low, in_real, preferred_element_type=jnp.float32).reshape(
        scan_shape
    )
    drive_imag = jnp.dot(normed_low, in_imag, preferred_element_type=jnp.float32).reshape(
        scan_shape
    )
    state_real, state_imag = linear_scan(
        decay_real, decay_imag, input_gain * drive_real, input_gain * drive_imag, False
    )
    state_low_real = state_real.reshape(per_device * positions, states).astype(jnp.bfloat16)
    state_low_imag = state_imag.reshape(per_device * positions, states).astype(jnp.bfloat16)
    mixed_part = jnp.dot(state_low_real, out_real, preferred_element_type=jnp.float32) - jnp.dot(
        state_low_imag, out_imag, preferred_element_type=jnp.float32
    )
    mixed = lax.psum(mixed_part, "tensor") + skip_gain * normed_out
    act_low = jax.nn.gelu(mixed).astype(jnp.bfloat16)
    up_proj = jnp.dot(act_low, up_weight, preferred_element_type=jnp.float32)
    gate_sig = jax.nn.sigmoid(jnp.dot(act_low, gate_weight, preferred_element_type=jnp.float32))
    hidden_low = (up_proj * gate_sig).astype(jnp.bfloat16)
    return {
        "token_rows": token_rows,
        "normed": normed,
        "inv_scale": inv_scale,
        "normed_out": normed_out,
        "normed_low": normed_low,
        "drive_real": drive_real,
        "drive_imag": drive_imag,
        "state_real": state_real,
        "state_imag": state_imag,
        "state_low_real": state_low_real,
        "state_low_imag": state_low_imag,
        "mixed": mixed,
        "act_low": act_low,
        "up_proj": up_proj,
        "gate_sig": gate_sig,
        "hidden_low": hidden_low,
    }


def shards(
    tokens,
    cotangent,
    ln_gain,
    ln_bias,
    skip_gain,
    in_real,
    in_imag,
    out_real,
    out_imag,
    nu_log,
    theta_log,
    gamma_log,
    up_weight,
    gate_weight,
    down_weight,
    lengths,
):
    groups = lax.axis_size("dp")
    dealing = deal_order(lengths, groups)
    per_device = dealing.shape[0] // groups
    model_width = tokens.shape[2]
    positions = tokens.shape[1] * groups
    total_rows = per_device * positions
    own_slots = lax.dynamic_slice_in_dim(dealing, lax.axis_index("dp") * per_device, per_device)
    own_lengths = jnp.take(lengths, own_slots)
    live_mask = (
        lax.broadcasted_iota(jnp.int32, (per_device, positions), 1) < own_lengths[:, None]
    ).astype(jnp.float32)
    live_rows = live_mask.reshape(total_rows, 1)
    inverse = jnp.zeros_like(dealing).at[dealing].set(lax.iota(jnp.int32, dealing.shape[0]))
    decay_real, decay_imag, input_gain = decay_terms(nu_log, theta_log, gamma_log)
    params = (
        ln_gain,
        ln_bias,
        skip_gain,
        in_real,
        in_imag,
        out_real,
        out_imag,
        decay_real,
        decay_imag,
        input_gain,
        up_weight,
        gate_weight,
    )
    dealt_tokens = lax.all_to_all(
        jnp.take(tokens, dealing, axis=0), "dp", split_axis=0, concat_axis=1, tiled=True
    )
    first_pass = forward_local(dealt_tokens, params)
    hidden_low = first_pass["hidden_low"]
    token_rows = first_pass["token_rows"]
    branch_sum = lax.psum(
        jnp.dot(hidden_low, down_weight, preferred_element_type=jnp.float32), "tensor"
    )
    result = (live_rows * (token_rows + branch_sum)).astype(jnp.bfloat16)
    returned = lax.all_to_all(
        result.reshape(per_device, positions, model_width),
        "dp",
        split_axis=1,
        concat_axis=0,
        tiled=True,
    )
    block_out = jnp.take(returned, inverse, axis=0)
    dealt_again, cot_dealt = (
        lax.all_to_all(
            jnp.take(tokens, dealing, axis=0), "dp", split_axis=0, concat_axis=1, tiled=True
        ),
        lax.all_to_all(
            jnp.take(cotangent, dealing, axis=0), "dp", split_axis=0, concat_axis=1, tiled=True
        ),
    )
    kept = forward_local(dealt_again, params)
    cot_rows = cot_dealt.reshape(total_rows, model_width).astype(jnp.float32) * live_rows
    cot_low = cot_rows.astype(jnp.bfloat16)
    down_grad = over_rows(kept["hidden_low"], cot_low)
    hidden_grad = against(cot_low, down_weight)
    gate_sig = kept["gate_sig"]
    up_grad_low = (hidden_grad * gate_sig).astype(jnp.bfloat16)
    gate_grad_low = (hidden_grad * kept["up_proj"] * gate_sig * (1.0 - gate_sig)).astype(
        jnp.bfloat16
    )
    up_grad = over_rows(kept["act_low"], up_grad_low)
    gate_grad = over_rows(kept["act_low"], gate_grad_low)
    act_grad = lax.psum(
        against(up_grad_low, up_weight) + against(gate_grad_low, gate_weight), "tensor"
    )
    mixed_grad = jax.vjp(jax.nn.gelu, kept["mixed"])[1](act_grad)[0]
    skip_grad = jnp.sum(mixed_grad * kept["normed_out"], axis=0)
    mixed_low = mixed_grad.astype(jnp.bfloat16)
    out_real_grad = over_rows(kept["state_low_real"], mixed_low)
    out_imag_grad = -over_rows(kept["state_low_imag"], mixed_low)
    states = out_real.shape[0]
    scan_shape = (per_device, positions, states)
    back_real, back_imag = linear_scan(
        decay_real,
        -decay_imag,
        against(mixed_low, out_real).reshape(scan_shape),
        (-against(mixed_low, out_imag)).reshape(scan_shape),
        True,
    )
    state_real = kept["state_real"]
    state_imag = kept["state_imag"]
    before_real = jnp.concatenate([jnp.zeros_like(state_real[:, :1]), state_real[:, :-1]], axis=1)
    before_imag = jnp.concatenate([jnp.zeros_like(state_imag[:, :1]), state_imag[:, :-1]], axis=1)
    decay_grad_real = jnp.sum(back_real * before_real + back_imag * before_imag, axis=(0, 1))
    decay_grad_imag = jnp.sum(back_imag * before_real - back_real * before_imag, axis=(0, 1))
    modulus = jnp.exp(-jnp.exp(nu_log))
    angle = jnp.exp(theta_log)
    nu_grad = (
        -jnp.exp(nu_log)
        * modulus
        * (decay_grad_real * jnp.cos(angle) + decay_grad_imag * jnp.sin(angle))
    )
    theta_grad = (
        angle * modulus * (decay_grad_imag * jnp.cos(angle) - decay_grad_real * jnp.sin(angle))
    )
    gamma_grad = input_gain * jnp.sum(
        back_real * kept["drive_real"] + back_imag * kept["drive_imag"], axis=(0, 1)
    )
    drive_low_real = (input_gain * back_real).reshape(total_rows, states).astype(jnp.bfloat16)
    drive_low_imag = (input_gain * back_imag).reshape(total_rows, states).astype(jnp.bfloat16)
    in_real_grad = over_rows(kept["normed_low"], drive_low_real)
    in_imag_grad = over_rows(kept["normed_low"], drive_low_imag)
    norm_grad = (
        lax.psum(
            (against(drive_low_real, in_real) + against(drive_low_imag, in_imag)).astype(
                jnp.bfloat16
            ),
            "tensor",
        ).astype(jnp.float32)
        + mixed_grad * skip_gain
    )
    normed = kept["normed"]
    gain_grad = jnp.sum(norm_grad * normed, axis=0)
    bias_grad = jnp.sum(norm_grad, axis=0)
    scaled = norm_grad * ln_gain
    input_rows = (
        kept["inv_scale"]
        * (
            scaled
            - jnp.mean(scaled, axis=-1, keepdims=True)
            - normed * jnp.mean(scaled * normed, axis=-1, keepdims=True)
        )
        + cot_rows
    )
    summed = lax.psum(
        (
            gain_grad,
            bias_grad,
            skip_grad,
            in_real_grad,
            in_imag_grad,
            out_real_grad,
            out_imag_grad,
            nu_grad,
            theta_grad,
            gamma_grad,
            up_grad,
            gate_grad,
            down_grad,
        ),
        "dp",
    )
    sent_back = lax.all_to_all(
        input_rows.reshape(per_device, positions, model_width),
        "dp",
        split_axis=1,
        concat_axis=0,
        tiled=True,
    )
    input_grad = jnp.take(sent_back, inverse, axis=0)
    return (block_out, input_grad) + tuple(summed)


def solution(mesh):
    in_specs = (
        P(None, "dp", None),
        P(None, "dp", None),
        P(),
        P(),
        P(),
        P(None, "tensor"),
        P(None, "tensor"),
        P("tensor", None),
        P("tensor", None),
        P("tensor"),
        P("tensor"),
        P("tensor"),
        P(None, "tensor"),
        P(None, "tensor"),
        P("tensor", None),
        P(),
    )
    out_specs = (
        P(None, "dp", None),
        P(None, "dp", None),
        P(),
        P(),
        P(),
        P(None, "tensor"),
        P(None, "tensor"),
        P("tensor", None),
        P("tensor", None),
        P("tensor"),
        P("tensor"),
        P("tensor"),
        P(None, "tensor"),
        P(None, "tensor"),
        P("tensor", None),
    )
    return jax.shard_map(shards, mesh=mesh, in_specs=in_specs, out_specs=out_specs, check_vma=False)
```

profile of v0, /device:TPU:0, one launch (start us, length us, event | category | flops | bytes accessed | tf_op | source)
XLA Modules:
  0.0 1517.3 jit_solution(6878926659934725661)
XLA Ops:
  13.9 4.6 gather_fusion.2
  18.4 5.2 broadcast_select_fusion.2
  23.6 7.4 all-to-all-start
  33.4 68.3 %all-to-all-done = bf16[24,128,512]{2,1,0:T(8,128)(2,1)S(1)} async-done(((bf16[24,128,512]{2,1,0:T(8,128)(2,1)}), bf16[24,128,512]{2,1,0:T(8,128)(2,1)S(1)}, u32[]{:S(2)}, u32[]{:S(2)}) %all-to-all-start) | async-done | bytes 3145760 | tf_op jit(solution)/shard_map/all_to_all | solution.py:175
  101.7 4.5 all-to-all-start.2
  116.1 5.8 slice.1084
  122.0 5.7 slice.1077
  329.7 4.2 pad.325
  350.7 111.2 %all-reduce.90.cloned.1.call-done = f32[3072,512]{1,0:T(8,128)} async-done(((f32[3072,512]{1,0:T(8,128)}), f32[3072,512]{1,0:T(8,128)}) %all-reduce.90.cloned.1.call-update) | async-done | bytes 6291472 | tf_op jit(solution)/shard_map/psum | solution.py:104
  461.9 6.8 multiply_convert_fusion
  482.6 4.3 slice.1206
  486.9 4.1 slice.1205
  496.2 7.0 slice.1210
  507.8 196.1 %all-reduce.96.cloned.1.call-done = (f32[3072,512]{1,0:T(8,128)}, f32[3072,512]{1,0:T(8,128)}) async-done(((f32[3072,512]{1,0:T(8,128)}, f32[3072,512]{1,0:T(8,128)}), (f32[3072,512]{1,0:T(8,128)}, f32[3072,512]{1,0:T(8,128)})) %all-reduce.96.cloned.1.call-update) | async-done | bytes 12582928 | tf_op jit(solution)/shard_map/psum | solution.py:181
  703.8 12.3 fusion.39
  720.8 5.7 slice.1355
  726.5 5.7 slice.1213
  732.2 5.7 slice.1207
  741.9 5.7 slice.1358
  747.6 5.7 slice.1220
  753.3 5.7 slice.1211
  759.0 6.8 slice.1208
  765.8 6.8 slice.1214
  772.5 6.8 slice.1212
  779.3 6.8 slice.1221
  786.1 4.2 add_add_fusion.1
  891.0 7.0 slice.1356
  898.0 7.0 slice.1359
  976.7 4.1 pad.362
  987.1 4.2 pad.363
  994.4 12.7 rev.4
  1007.1 4.3 pad.365
  1014.6 12.7 rev.5
  1027.3 5.0 add_reduce_fusion.1
  1036.2 68.8 %all-reduce.92.cloned.1.call-done = bf16[3072,512]{1,0:T(8,128)(2,1)} async-done(((bf16[3072,512]{1,0:T(8,128)(2,1)}), bf16[3072,512]{1,0:T(8,128)(2,1)}) %all-reduce.92.cloned.1.call-update) | async-done | bytes 3145744 | tf_op jit(solution)/shard_map/psum | solution.py:254
  1105.0 10.7 multiply_reduce_fusion.1
  1115.8 8.5 multiply_add_fusion
  1124.3 4.8 copy.156
  1129.1 5.8 all-to-all-start.1
  1134.9 10.5 copy.170
  1145.4 82.6 %all-to-all-done.1 = bf16[3,1024,512]{2,0,1:T(4,128)(2,1)} async-done(((bf16[3,1024,512]{2,0,1:T(4,128)(2,1)}), bf16[3,1024,512]{2,0,1:T(4,128)(2,1)}, u32[]{:S(2)}, u32[]{:S(2)}) %all-to-all-start.1) | async-done | bytes 3145760 | tf_op jit(solution)/shard_map/all_to_all | solution.py:185
  1228.0 5.0 all-to-all-start.3
  1248.8 158.5 %all-reduce.82 = (f32[512]{0:T(512)}, f32[512]{0:T(512)}, f32[512]{0:T(512)}, f32[64]{0:T(128)}, f32[64]{0:T(128)}, /*index=5*/f32[64]{0:T(128)}) all-reduce(f32[512]{0:T(512)S(1)} %get-tuple-element.18, f32[512]{0:T(512)S(1)} %get-tuple-element.24, f32[512]{0:T(512)S(1)} %get-tuple-element.20, ...), channel_id=1, replica_groups=mesh['dp'=8,'tensor'=4] {'dp'}, use_global_device_ids=true, to_apply=%region_12.14 | all-reduce | flops 1728 | bytes 13824 | tf_op jit(solution)/shard_map/psum | solution.py:275
  1416.9 26.9 %all-to-all-done.3 = f32[3,1024,512]{2,0,1:T(4,128)} async-done(((f32[3,1024,512]{2,0,1:T(4,128)}), f32[3,1024,512]{2,0,1:T(4,128)}, u32[]{:S(2)}, u32[]{:S(2)}) %all-to-all-start.3) | async-done | bytes 6291488 | tf_op jit(solution)/shard_map/all_to_all | solution.py:293
  1443.9 5.4 copy.171
  1453.1 6.4 gather_fusion.1
  1459.5 6.9 broadcast_select_fusion
  1466.4 33.3 %all-reduce.94.cloned.1.call-done = (f32[512,64]{0,1:T(8,128)}, f32[512,64]{0,1:T(8,128)}, f32[64,512]{1,0:T(8,128)}, f32[64,512]{1,0:T(8,128)}, f32[512,256]{1,...) async-done(((f32[512,64]{0,1:T(8,128)}, f32[512,64]{0,1:T(8,128)}, f32[64,512]{1,0:T(8,128)}, f32[64,512]{1,0:T(8,128)}, f32[512,256]{1,0:T(8,128)}, ...) | async-done | bytes 2097168 | tf_op jit(solution)/shard_map/psum | solution.py:275
  (702 shorter events, 497.2 us)
Async XLA Ops:
  23.6 78.1 %all-to-all-start = ((bf16[24,128,512]{2,1,0:T(8,128)(2,1)}), bf16[24,128,512]{2,1,0:T(8,128)(2,1)S(1)}, u32[]{:S(2)}, u32[]{:S(2)}) async-start(bf16[24,128,512]{2,1,0:T(8,128)(2,1)} %get-tuple-element.196), calls=%async_computation | async-start | bytes 6291456 | tf_op jit(solution)/shard_map/all_to_all | solution.py:175
  31.1 81.8 %copy-start.117 = (f32[64]{0:T(128)}, f32[64]{0:T(128)S(1)}, u32[]{:S(2)}) copy-start(f32[64]{0:T(128)S(1)} %exp.20) | copy-start | bytes 772
  31.6 102.8 %copy-start.96 = (f32[64]{0:T(128)}, f32[64]{0:T(128)S(1)}, u32[]{:S(2)}) copy-start(f32[64]{0:T(128)S(1)} %get-tuple-element.46) | copy-start | bytes 772
  32.3 102.1 %copy-start.94 = (f32[64]{0:T(128)}, f32[64]{0:T(128)S(1)}, u32[]{:S(2)}) copy-start(f32[64]{0:T(128)S(1)} %get-tuple-element.66) | copy-start | bytes 772
  101.7 240.7 %all-to-all-start.2 = ((bf16[24,128,512]{2,1,0:T(8,128)(2,1)}), bf16[24,128,512]{2,1,0:T(8,128)(2,1)}, u32[]{:S(2)}, u32[]{:S(2)}) async-start(bf16[24,128,512]{2,1,0:T(8,128)(2,1)} %get-tuple-element.195), calls=%async_computation.2 | async-start | bytes 6291456 | tf_op jit(solution)/shard_map/all_to_all | solution.py:197
  106.2 355.7 %all-reduce.90.cloned.1.call-start = ((), (), s32[]{:S(2)}) async-start(), calls=%async_computation.4 | async-start | bytes 12582912 | tf_op jit(solution)/shard_map/psum | solution.py:104
  116.1 11.5 copy-start.21
  136.5 11.5 copy-start.36
  136.5 11.5 copy-start.37
  153.3 144.0 %copy-start.22 = (f32[3,1024,64]{2,1,0:T(8,128)S(1)}, f32[3,1024,64]{2,1,0:T(8,128)}, u32[]{:S(2)}) copy-start(f32[3,1024,64]{2,1,0:T(8,128)} %get-tuple-element.197) | copy-start | bytes 2359300
  301.9 13.5 copy-start.53
  301.9 13.5 copy-start.54
  301.9 13.6 copy-start.51
  302.0 13.6 copy-start.52
  305.4 11.1 copy-start.57
  323.8 12.1 copy-start.12
  340.9 363.0 %all-reduce.96.cloned.1.call-start = ((), (), s32[]{:S(2)}) async-start(), calls=%async_computation.7 | async-start | bytes 25165824 | tf_op jit(solution)/shard_map/psum | solution.py:181
  348.0 113.9 %copy-start.59 = (f32[3072]{0:T(1024)S(1)}, f32[3072]{0:T(1024)}, u32[]{:S(2)}) copy-start(f32[3072]{0:T(1024)} %get-tuple-element.170) | copy-start | bytes 36868
  348.0 113.9 %copy-start.83 = (f32[512]{0:T(512)S(1)}, f32[512]{0:T(512)}, u32[]{:S(2)}) copy-start(f32[512]{0:T(512)} %param.21) | copy-start | bytes 6148
  348.0 113.9 %copy-start.92 = (f32[512]{0:T(512)S(1)}, f32[512]{0:T(512)}, u32[]{:S(2)}) copy-start(f32[512]{0:T(512)} %param.22) | copy-start | bytes 6148
  482.5 622.5 %all-reduce.92.cloned.1.call-start = ((), (), s32[]{:S(2)}) async-start(), calls=%async_computation.5 | async-start | bytes 6291456 | tf_op jit(solution)/shard_map/psum | solution.py:254
  882.2 27.1 %copy-start.69 = (f32[3,31,64]{2,1,0:T(8,128)S(1)}, f32[3,31,64]{2,1,0:T(8,128)}, u32[]{:S(2)}) copy-start(f32[3,31,64]{2,1,0:T(8,128)} %slice.1326) | copy-start | bytes 71428
  882.2 27.1 %copy-start.70 = (f32[3,31,64]{2,1,0:T(8,128)S(1)}, f32[3,31,64]{2,1,0:T(8,128)}, u32[]{:S(2)}) copy-start(f32[3,31,64]{2,1,0:T(8,128)} %slice.1247) | copy-start | bytes 71428
  882.2 27.1 %copy-start.71 = (f32[3,31,64]{2,1,0:T(8,128)S(1)}, f32[3,31,64]{2,1,0:T(8,128)}, u32[]{:S(2)}) copy-start(f32[3,31,64]{2,1,0:T(8,128)} %slice.1334) | copy-start | bytes 71428
  884.3 21.5 %copy-start.77 = (f32[3,15,64]{2,1,0:T(8,128)S(1)}, f32[3,15,64]{2,1,0:T(8,128)}, u32[]{:S(2)}) copy-start(f32[3,15,64]{2,1,0:T(8,128)} %slice.1257) | copy-start | bytes 34564
  884.3 21.5 %copy-start.78 = (f32[3,15,64]{2,1,0:T(8,128)S(1)}, f32[3,15,64]{2,1,0:T(8,128)}, u32[]{:S(2)}) copy-start(f32[3,15,64]{2,1,0:T(8,128)} %slice.1320) | copy-start | bytes 34564
  884.3 21.5 %copy-start.79 = (f32[3,15,64]{2,1,0:T(8,128)S(1)}, f32[3,15,64]{2,1,0:T(8,128)}, u32[]{:S(2)}) copy-start(f32[3,15,64]{2,1,0:T(8,128)} %slice.1324) | copy-start | bytes 34564
  888.0 17.5 %copy-start.85 = (f32[3,7,64]{2,1,0:T(8,128)S(1)}, f32[3,7,64]{2,1,0:T(8,128)}, u32[]{:S(2)}) copy-start(f32[3,7,64]{2,1,0:T(8,128)} %slice.1314) | copy-start | bytes 16132
  888.0 17.5 %copy-start.86 = (f32[3,7,64]{2,1,0:T(8,128)S(1)}, f32[3,7,64]{2,1,0:T(8,128)}, u32[]{:S(2)}) copy-start(f32[3,7,64]{2,1,0:T(8,128)} %slice.1267) | copy-start | bytes 16132
  888.1 17.5 %copy-start.87 = (f32[3,7,64]{2,1,0:T(8,128)S(1)}, f32[3,7,64]{2,1,0:T(8,128)}, u32[]{:S(2)}) copy-start(f32[3,7,64]{2,1,0:T(8,128)} %slice.1322) | copy-start | bytes 16132
  888.1 17.5 %copy-start.88 = (f32[3,7,64]{2,1,0:T(8,128)S(1)}, f32[3,7,64]{2,1,0:T(8,128)}, u32[]{:S(2)}) copy-start(f32[3,7,64]{2,1,0:T(8,128)} %slice.1318) | copy-start | bytes 16132
  890.6 14.6 copy-start.90
  890.6 14.6 copy-start.91
  890.9 14.7 copy-start.104
  890.9 14.4 copy-start.106
  891.0 14.4 copy-start.107
  891.0 14.6 copy-start.105
  952.4 13.5 copy-start.46
  1011.4 15.9 %copy-start.118 = (f32[64]{0:T(128)S(1)}, f32[64]{0:T(128)}, u32[]{:S(2)}) copy-start(f32[64]{0:T(128)} %copy-done.117) | copy-start | bytes 772
  1036.2 68.8 %copy-start.60 = (f32[3072]{0:T(1024)S(1)}, f32[3072]{0:T(1024)}, u32[]{:S(2)}) copy-start(f32[3072]{0:T(1024)} %get-tuple-element.170) | copy-start | bytes 36868
  1036.2 68.8 %copy-start.84 = (f32[512]{0:T(512)S(1)}, f32[512]{0:T(512)}, u32[]{:S(2)}) copy-start(f32[512]{0:T(512)} %param.21) | copy-start | bytes 6148
  1036.2 68.8 %copy-start.93 = (f32[512]{0:T(512)S(1)}, f32[512]{0:T(512)}, u32[]{:S(2)}) copy-start(f32[512]{0:T(512)} %param.22) | copy-start | bytes 6148
  1129.1 98.9 %all-to-all-start.1 = ((bf16[3,1024,512]{2,0,1:T(4,128)(2,1)}), bf16[3,1024,512]{2,0,1:T(4,128)(2,1)}, u32[]{:S(2)}, u32[]{:S(2)}) async-start(bf16[3,1024,512]{2,0,1:T(4,128)(2,1)} %copy.156), calls=%async_computation.1 | async-start | bytes 8388608 | tf_op jit(solution)/shard_map/all_to_all | solution.py:185
  1145.4 87.6 %copy-start.76 = (f32[3,8,128]{2,1,0:T(8,128)S(1)}, f32[3,8,128]{2,1,0:T(8,128)}, u32[]{:S(2)}) copy-start(f32[3,8,128]{2,1,0:T(8,128)} %copy-done.75) | copy-start | bytes 36868
  1145.4 87.6 %copy-start.89 = (f32[3,8,128]{2,1,0:T(8,128)S(1)}, f32[3,8,128]{2,1,0:T(8,128)}, u32[]{:S(2)}) copy-start(f32[3,8,128]{2,1,0:T(8,128)} %get-tuple-element.168) | copy-start | bytes 36868
  1228.0 215.9 %all-to-all-start.3 = ((f32[3,1024,512]{2,0,1:T(4,128)}), f32[3,1024,512]{2,0,1:T(4,128)}, u32[]{:S(2)}, u32[]{:S(2)}) async-start(f32[3,1024,512]{2,0,1:T(4,128)} %copy.170), calls=%async_computation.3 | async-start | bytes 16777216 | tf_op jit(solution)/shard_map/all_to_all | solution.py:293
  1233.0 266.7 %all-reduce.94.cloned.1.call-start = ((), (), s32[]{:S(2)}) async-start(), calls=%async_computation.6 | async-start | bytes 4194304 | tf_op jit(solution)/shard_map/psum | solution.py:275
  1459.5 51.0 %copy-start.1 = (bf16[24,128,512]{2,1,0:T(8,128)(2,1)S(1)}, bf16[24,128,512]{2,1,0:T(8,128)(2,1)}, u32[]{:S(2)}) copy-start(bf16[24,128,512]{2,1,0:T(8,128)(2,1)} %param.19) | copy-start | bytes 9437188
  (88 other events, 317.9 us)
Sparse Core Ops, SparseCore 0:
  341.0 120.8 all-reduce.89
  482.6 221.2 all-reduce.95
  1036.3 68.6 all-reduce.91
  1248.0 251.6 all-reduce.93
where the time goes:
time: 1540 us; the launch traced here: 1520 us
  waiting for transfers between devices  587 us (38%)
  local copies, waits for them, and re-layouts  502 us (33%)
  other arithmetic  191 us (12%)
  blocking collectives  158 us (10%)
  matrix products  39.7 us (3%)
  starting transfers between devices  23 us (1%)
  between operations  16.1 us (1%)
    slice x196, local copies, waits for them, and re-layouts, linear_scan(): lax.associative_scan(complex_step, elements, reverse=backwards, axis=1)  287 us
    psum x1, waiting for transfers between devices, shards(): lax.psum(jnp.dot(hidden_low, down_weight, preferred_element_type=jnp.floa...  196 us
    psum x1, blocking collectives, shards(): lax.psum((gain_grad, bias_grad, skip_grad, in_real_grad, in_imag_grad, ou...  158 us
    pad x72, local copies, waits for them, and re-layouts, linear_scan(): lax.associative_scan(complex_step, elements, reverse=backwards, axis=1)  113 us
    psum x1, waiting for transfers between devices, forward_local(): mixed = lax.psum(mixed_part, 'tensor') + skip_gain * normed_out  111 us
    all_to_all x1, waiting for transfers between devices, shards(): lax.all_to_all(result.reshape(per_device, positions, model_width), 'dp',...  82.6 us
    psum x1, waiting for transfers between devices, shards(): lax.psum((against(drive_low_real, in_real) + against(drive_low_imag, in_i...  68.8 us
    all_to_all x1, waiting for transfers between devices, shards(): lax.all_to_all(jnp.take(tokens, dealing, axis=0), 'dp', split_axis=0, con...  68.3 us
  transfers between devices with their start and end apart: 8, of which 7 were waited for; matrix products, arithmetic and copies ran while one was open for 21% of the time, Pallas kernels for 0%

commit v1 on v0

v1 whole, which is shorter than its diff:
```python
import functools
import math

import jax
import jax.numpy as jnp
from jax import lax
from jax.experimental import pallas as pl
from jax.experimental.pallas import tpu as pltpu
from jax.sharding import PartitionSpec as P

EPSILON = 1e-05
TENSOR = 4
TILE = 8
BLOCK = 256
PARAM_ROWS = 16
F32 = jnp.float32
BF16 = jnp.bfloat16
GELU_K = math.sqrt(2.0 / math.pi)
VMEM_BYTES = 56 * 1024 * 1024


def dot(left, right):
    return jnp.dot(left, right, preferred_element_type=F32)


def dot_nt(left, right):
    return lax.dot_general(left, right, (((1,), (1,)), ((), ())), preferred_element_type=F32)


def dot_tn(left, right):
    return lax.dot_general(left, right, (((0,), (0,)), ((), ())), preferred_element_type=F32)


def layer_norm(rows):
    centre = jnp.mean(rows, axis=-1, keepdims=True)
    shifted = rows - centre
    variance = jnp.mean(shifted * shifted, axis=-1, keepdims=True)
    inv_scale = lax.rsqrt(variance + EPSILON)
    return shifted * inv_scale, inv_scale


def cmul(ar, ai, br, bi):
    return ar * br - ai * bi, ar * bi + ai * br


def read_params(packs, row):
    total = None
    for pack in packs:
        rows = pack[row : row + PARAM_ROWS, :].astype(F32)
        total = rows if total is None else total + rows
    states = total.shape[1] // 2
    at = lambda k: total[k : k + 1, :states] + total[k + 3 : k + 4, :states] + total[k + 6 : k + 7, :states]
    return at(0), at(1), at(2)


def powers_of(decay_real, decay_imag, exponent):
    out_r = jnp.ones(exponent.shape, F32)
    out_i = jnp.zeros(exponent.shape, F32)
    br, bi = decay_real, decay_imag
    for bit in range(4):
        mr, mi = cmul(out_r, out_i, br, bi)
        on = ((exponent >> bit) & 1) == 1
        out_r = jnp.where(on, mr, out_r)
        out_i = jnp.where(on, mi, out_i)
        br, bi = cmul(br, bi, br, bi)
    return out_r, out_i


def fill_tables(decay_real, decay_imag, length, backwards, step_ref, full_ref):
    states = decay_real.shape[1]
    row = lax.broadcasted_iota(jnp.int32, (TILE, states), 0)
    if backwards:
        row = TILE - 1 - row
    zero = jnp.zeros((TILE, states), F32)
    for k, shift in enumerate((1, 2, 4)):
        pr, pi = powers_of(decay_real, decay_imag, jnp.full((TILE, states), shift, jnp.int32))
        step_ref[k, 0] = jnp.where(row >= shift, pr, zero)
        step_ref[k, 1] = jnp.where(row >= shift, pi, zero)
    pr, pi = powers_of(decay_real, decay_imag, row + 1)
    step_ref[3, 0] = pr
    step_ref[3, 1] = pi
    if full_ref is not None:
        er, ei = powers_of(decay_real, decay_imag, jnp.full((TILE, states), TILE, jnp.int32))
        tiles = length // TILE
        for n in range(tiles):
            at = (tiles - 1 - n if backwards else n) * TILE
            full_ref[0, at : at + TILE, :] = pr
            full_ref[1, at : at + TILE, :] = pi
            pr, pi = cmul(pr, pi, er, ei)


def scan_block(drive_ref, out_ref, step_ref, length, backwards, finish):
    rows, lanes = drive_ref.shape
    states = lanes // 2
    tiles = length // TILE
    table = [(step_ref[k, 0], step_ref[k, 1]) for k in range(4)]
    edge = 0 if backwards else TILE - 1
    for s in range(rows // length):
        cr = ci = None
        for n in range(tiles):
            at = s * length + (tiles - 1 - n if backwards else n) * TILE
            hr = drive_ref[at : at + TILE, :states]
            hi = drive_ref[at : at + TILE, states:]
            for k, shift in enumerate((1, 2, 4)):
                turn = TILE - shift if backwards else shift
                sr = pltpu.roll(hr, turn, 0)
                si = pltpu.roll(hi, turn, 0)
                mr, mi = cmul(table[k][0], table[k][1], sr, si)
                hr, hi = hr + mr, hi + mi
            if cr is not None:
                mr, mi = cmul(table[3][0], table[3][1], cr, ci)
                hr, hi = hr + mr, hi + mi
            out_ref[at : at + TILE, :states] = hr
            out_ref[at : at + TILE, states:] = hi
            cr, ci = hr[edge : edge + 1], hi[edge : edge + 1]
        finish(s, cr, ci)


def incoming(ends_ref, place, decay_r, decay_i, backwards, out_ref):
    groups, seqs, lanes = ends_ref.shape
    states = lanes // 2
    sr = jnp.zeros((seqs, states), F32)
    si = jnp.zeros((seqs, states), F32)
    for j in reversed(range(groups)) if backwards else range(groups):
        mr, mi = cmul(decay_r, decay_i, sr, si)
        use = j > place if backwards else j < place
        sr = jnp.where(use, mr + ends_ref[j, :, :states], sr)
        si = jnp.where(use, mi + ends_ref[j, :, states:], si)
    out_ref[:, :states] = sr
    out_ref[:, states:] = si


def assemble_input(packs, shard, out_ref):
    per = packs[0].shape[0] - PARAM_ROWS
    half = per // 2
    states = out_ref.shape[0] // 2
    for k, pack in enumerate(packs):
        at = pl.multiple_of((shard ^ k) * half, half)
        out_ref[pl.ds(at, half), :] = pack[:half, :]
        out_ref[pl.ds(states + at, half), :] = pack[half:per, :]


def drive_kernel(where_ref, tok_ref, a0, a1, a2, a3, gain_ref, bias_ref, local_ref, ends_ref, in_t, step, drive, gam, *, length):
    block = pl.program_id(0)
    packs = (a0, a1, a2, a3)
    states = in_t.shape[0] // 2

    @pl.when(block == 0)
    def _():
        assemble_input(packs, where_ref[2], in_t)
        dr, di, gain = read_params(packs, a0.shape[0] - PARAM_ROWS)
        fill_tables(dr, di, length, False, step, None)
        gam[...] = jnp.concatenate([gain, gain], axis=1)

    normed, _ = layer_norm(tok_ref[...].astype(F32))
    low = (normed * gain_ref[...] + bias_ref[...]).astype(BF16)
    drive[...] = dot_nt(low, in_t[...]) * gam[...]
    per_block = drive.shape[0] // length

    def finish(s, r, i):
        ends_ref[pl.ds(block * per_block + s, 1), :states] = r
        ends_ref[pl.ds(block * per_block + s, 1), states:] = i

    scan_block(drive, local_ref, step, length, False, finish)


def middle_kernel(
    where_ref,
    lens_ref,
    tok_ref,
    cot_ref,
    local_ref,
    ends_ref,
    a0,
    a1,
    a2,
    a3,
    gain_ref,
    bias_ref,
    skip_ref,
    b0,
    b1,
    b2,
    b3,
    out_ref,
    state_ref,
    back_ref,
    backends_ref,
    ylow_ref,
    hid_half_ref,
    cotm_ref,
    act_ref,
    ul_half_ref,
    skip_grad_ref,
    c_all,
    down_all,
    ug_all,
    step,
    full,
    carry,
    hid,
    ul,
    slope,
    eback,
    sems,
    *,
    length,
):
    block = pl.program_id(0)
    place, core, shard = where_ref[0], where_ref[1], where_ref[2]
    states = c_all.shape[0] // 2
    rows, width = tok_ref.shape
    per_block = rows // length
    per_s = states // TENSOR
    per_f = down_all.shape[0] // TENSOR

    @pl.when(block == 0)
    def _():
        copies = []
        for k, pack in enumerate((b0, b1, b2, b3)):
            t = shard ^ k
            moves = (
                (pack.at[pl.ds(0, per_s), :], c_all.at[pl.ds(pl.multiple_of(t * per_s, per_s), per_s), :]),
                (pack.at[pl.ds(per_s, per_s), :], c_all.at[pl.ds(pl.multiple_of(states + t * per_s, per_s), per_s), :]),
                (pack.at[pl.ds(2 * per_s, per_f), :], down_all.at[pl.ds(pl.multiple_of(t * per_f, per_f), per_f), :]),
                (
                    pack.at[pl.ds(2 * per_s + per_f, width), :],
                    ug_all.at[:, pl.ds(pl.multiple_of(t * 2 * per_f, 2 * per_f), 2 * per_f)],
                ),
            )
            for n, (src, dst) in enumerate(moves):
                copies.append(pltpu.make_async_copy(src, dst, sems.at[k, n]))
        for copy in copies:
            copy.start()
        dr, di, _ = read_params((a0, a1, a2, a3), a0.shape[0] - PARAM_ROWS)
        fill_tables(dr, di, length, False, step, full)
        incoming(ends_ref, place, full[0, length - 1 :, :], full[1, length - 1 :, :], False, carry)
        fill_tables(dr, di, length, True, step, None)
        skip_grad_ref[...] = jnp.zeros(skip_grad_ref.shape, F32)
        for copy in copies:
            copy.wait()

    x = tok_ref[...].astype(F32)
    normed, _ = layer_norm(x)
    u = normed * gain_ref[...] + bias_ref[...]
    for s in range(per_block):
        seq = block * per_block + s
        span = slice(s * length, (s + 1) * length)
        sr = carry[pl.ds(seq, 1), :states]
        si = carry[pl.ds(seq, 1), states:]
        mr, mi = cmul(full[0], full[1], sr, si)
        state_ref[span, :states] = (local_ref[span, :states] + mr).astype(BF16)
        state_ref[span, states:] = (-(local_ref[span, states:] + mi)).astype(BF16)
        live = lax.broadcasted_iota(jnp.int32, (length, width), 0) < (lens_ref[core * ends_ref.shape[1] + seq] - place * length)
        cotm_ref[span, :] = jnp.where(live, cot_ref[span, :].astype(F32), 0.0).astype(BF16)
    y = dot(state_ref[...], c_all[...]) + skip_ref[...] * u
    square = y * y
    th = jnp.tanh(GELU_K * y * (1.0 + 0.044715 * square))
    act_ref[...] = (0.5 * y * (1.0 + th)).astype(BF16)
    slope[...] = 0.5 * (1.0 + th) + (0.5 * GELU_K) * y * (1.0 - th * th) * (1.0 + (3 * 0.044715) * square)
    act = act_ref[...]
    cotm = cotm_ref[...]
    for t in range(TENSOR):
        both = dot(act, ug_all[:, 2 * per_f * t : 2 * per_f * (t + 1)])
        up = both[:, :per_f]
        sig = jax.nn.sigmoid(both[:, per_f:])
        hid[:, per_f * t : per_f * (t + 1)] = (up * sig).astype(BF16)
        hid_grad = dot_nt(cotm, down_all[per_f * t : per_f * (t + 1), :])
        up_grad = hid_grad * sig
        ul[:, 2 * per_f * t : 2 * per_f * t + per_f] = up_grad.astype(BF16)
        ul[:, 2 * per_f * t + per_f : 2 * per_f * (t + 1)] = (up_grad * up * (1.0 - sig)).astype(BF16)
    added = dot(hid[...], down_all[...])
    act_grad = dot_nt(ul[...], ug_all[...])
    for s in range(per_block):
        seq = block * per_block + s
        span = slice(s * length, (s + 1) * length)
        live = lax.broadcasted_iota(jnp.int32, (length, width), 0) < (lens_ref[core * ends_ref.shape[1] + seq] - place * length)
        out_ref[span, :] = jnp.where(live, tok_ref[span, :].astype(F32) + added[span, :], 0.0).astype(BF16)
    y_grad = act_grad * slope[...]
    skip_grad_ref[...] += jnp.sum(y_grad * u, axis=0, keepdims=True)
    ylow_ref[...] = y_grad.astype(BF16)
    eback[...] = dot_nt(ylow_ref[...], c_all[...])

    def finish(s, r, i):
        backends_ref[pl.ds(block * per_block + s, 1), :states] = r
        backends_ref[pl.ds(block * per_block + s, 1), states:] = i

    scan_block(eback, back_ref, step, length, True, finish)
    side = shard // 2
    hid_half_ref[...] = hid[:, pl.ds(pl.multiple_of(side * 2 * per_f, 2 * per_f), 2 * per_f)]
    ul_half_ref[...] = ul[:, pl.ds(pl.multiple_of(side * 4 * per_f, 4 * per_f), 4 * per_f)]


def weight_kernel(where_ref, hid_ref, cotm_ref, act_ref, ul_ref, state_ref, ylow_ref, own_ref, sent_ref):
    core, shard = where_ref[1], where_ref[2]
    states = state_ref.shape[1] // 2
    per_s = states // TENSOR
    per_f = hid_ref.shape[1] // 2
    side = shard // 2
    cols = [
        state_ref[:, pl.ds(pl.multiple_of(k * states + side * 2 * per_s, 2 * per_s), 2 * per_s)] for k in range(2)
    ]
    ylow = ylow_ref[...]
    out_grad = [dot_tn(c, ylow) for c in cols]
    for n, ref in ((core, own_ref), (1 - core, sent_ref)):
        for k in range(2):
            part = jnp.where(n == 0, out_grad[k][:per_s], out_grad[k][per_s:])
            ref[k * per_s : (k + 1) * per_s, :] = part.astype(ref.dtype)
        hid = hid_ref[:, pl.ds(pl.multiple_of(n * per_f, per_f), per_f)]
        ref[2 * per_s : 2 * per_s + per_f, :] = dot_tn(hid, cotm_ref[...]).astype(ref.dtype)
        ul = ul_ref[:, pl.ds(pl.multiple_of(n * 2 * per_f, 2 * per_f), 2 * per_f)]
        ref[2 * per_s + per_f :, :] = dot_tn(act_ref[...], ul).astype(ref.dtype)


def last_kernel(
    where_ref,
    tok_ref,
    cotm_ref,
    back_ref,
    state_ref,
    ylow_ref,
    ends_ref,
    skip_grad_ref,
    a0,
    a1,
    a2,
    a3,
    gain_ref,
    bias_ref,
    skip_ref,
    grad_ref,
    own_ref,
    sent_ref,
    in_t,
    step,
    full,
    carry,
    gam,
    dlow,
    in_grad,
    lam_grad,
    gain_grad,
    bias_grad,
    *,
    length,
):
    block = pl.program_id(0)
    place, core, shard = where_ref[0], where_ref[1], where_ref[2]
    states = in_t.shape[0] // 2
    rows, width = tok_ref.shape
    per_block = rows // length
    per_s = states // TENSOR
    packs = (a0, a1, a2, a3)

    @pl.when(block == 0)
    def _():
        assemble_input(packs, shard, in_t)
        dr, di, gain = read_params(packs, a0.shape[0] - PARAM_ROWS)
        fill_tables(dr, di, length, True, step, full)
        incoming(ends_ref, place, full[0, :1, :], full[1, :1, :], True, carry)
        gam[...] = jnp.concatenate([gain, -gain], axis=1)
        in_grad[...] = jnp.zeros(in_grad.shape, F32)
        lam_grad[...] = jnp.zeros(lam_grad.shape, F32)
        gain_grad[...] = jnp.zeros(gain_grad.shape, F32)
        bias_grad[...] = jnp.zeros(bias_grad.shape, F32)

    normed, inv_scale = layer_norm(tok_ref[...].astype(F32))
    low = (normed * gain_ref[...] + bias_ref[...]).astype(BF16)
    for s in range(per_block):
        seq = block * per_block + s
        span = slice(s * length, (s + 1) * length)
        sr = carry[pl.ds(seq, 1), :states]
        si = carry[pl.ds(seq, 1), states:]
        mr, mi = cmul(full[0], full[1], sr, si)
        gr = back_ref[span, :states] + mr
        gi = back_ref[span, states:] + mi
        dlow[span, :states] = (gr * gam[:, :states]).astype(BF16)
        dlow[span, states:] = (gi * gam[:, states:]).astype(BF16)
        nr = jnp.concatenate([gr[1:], sr], axis=0)
        ni = jnp.concatenate([gi[1:], si], axis=0)
        hr = state_ref[span, :states].astype(F32)
        hi = state_ref[span, states:].astype(F32)
        lam_grad[:, :states] += jnp.sum(nr * hr + ni * hi, axis=0, keepdims=True)
        lam_grad[:, states:] += jnp.sum(nr * hi - ni * hr, axis=0, keepdims=True)
    u_grad = dot(dlow[...], in_t[...]) + ylow_ref[...].astype(F32) * skip_ref[...]
    bias_grad[...] += jnp.sum(u_grad, axis=0, keepdims=True)
    gain_grad[...] += jnp.sum(u_grad * normed, axis=0, keepdims=True)
    scaled = u_grad * gain_ref[...]
    grad = (
        scaled
        - jnp.mean(scaled, axis=-1, keepdims=True)
        - normed * jnp.mean(scaled * normed, axis=-1, keepdims=True)
    )
    grad_ref[...] = (cotm_ref[...].astype(F32) + inv_scale * grad).astype(BF16)
    at = pl.multiple_of((shard // 2) * 2 * per_s, 2 * per_s)
    for k in range(2):
        cols = dlow[:, pl.ds(k * states + at, 2 * per_s)]
        in_grad[2 * per_s * k : 2 * per_s * (k + 1), :] += dot_tn(cols, low)

    @pl.when(block == pl.num_programs(0) - 1)
    def _():
        for n, ref in ((core, own_ref), (1 - core, sent_ref)):
            for k in range(2):
                part = in_grad[pl.ds(pl.multiple_of(2 * per_s * k + n * per_s, per_s), per_s), :]
                ref[k * per_s : (k + 1) * per_s, :] = part.astype(BF16)
            small = jnp.concatenate(
                [
                    gain_grad[...],
                    bias_grad[...],
                    skip_grad_ref[...],
                    lam_grad[...],
                    jnp.zeros((PARAM_ROWS - 4, width), F32),
                ],
                axis=0,
            )
            ref[2 * per_s :, :] = small.astype(BF16)


def whole(shape):
    return pl.BlockSpec(shape, lambda *_: (0,) * len(shape))


def call(kernel, grid, prefetch, in_specs, out_specs, out_shape, scratch, cost):
    return pl.pallas_call(
        kernel,
        grid_spec=pltpu.PrefetchScalarGridSpec(
            num_scalar_prefetch=prefetch,
            grid=grid,
            in_specs=in_specs,
            out_specs=out_specs,
            scratch_shapes=scratch,
        ),
        out_shape=out_shape,
        compiler_params=pltpu.CompilerParams(vmem_limit_bytes=VMEM_BYTES),
        cost_estimate=pl.CostEstimate(flops=cost[0], bytes_accessed=cost[1], transcendentals=0),
    )


def split_low(value):
    high = lax.reduce_precision(value, 8, 7)
    middle = lax.reduce_precision(value - high, 8, 7)
    return high, middle, value - high - middle


def core_swap(value):
    return lax.ppermute(value, "tensor", [(t, t ^ 1) for t in range(TENSOR)])


def side_swap(value):
    return lax.ppermute(value, "tensor", [(t, t ^ 2) for t in range(TENSOR)])


def gather_tensor(own):
    across = side_swap(own)
    return own, core_swap(own), across, core_swap(across)


def share_over_dp(value, groups):
    return lax.all_to_all(
        jnp.broadcast_to(value[None], (groups,) + value.shape), "dp", split_axis=0, concat_axis=0, tiled=True
    )


def sum_over_dp(value, groups):
    rows, width = value.shape
    parts = value.reshape(groups, rows // groups, width)
    mine = lax.all_to_all(parts, "dp", split_axis=0, concat_axis=0, tiled=True)
    total = jnp.sum(mine.astype(F32), axis=0).astype(BF16)
    return share_over_dp(total, groups).reshape(rows, width).astype(F32)


def sum_over_dp_small(value, groups):
    bit = 1
    while bit < groups:
        other = lax.ppermute(value, "dp", [(i, i ^ bit) for i in range(groups)])
        value = (value.astype(F32) + other.astype(F32)).astype(BF16)
        bit *= 2
    return value.astype(F32)


def shards(
    tokens,
    cotangent,
    ln_gain,
    ln_bias,
    skip_gain,
    in_real,
    in_imag,
    out_real,
    out_imag,
    nu_log,
    theta_log,
    gamma_log,
    up_weight,
    gate_weight,
    down_weight,
    lengths,
    *,
    groups,
):
    seqs, length, width = tokens.shape
    per_s = in_real.shape[1]
    per_f = up_weight.shape[1]
    states = per_s * TENSOR
    own_seqs = seqs // 2
    rows = own_seqs * length
    blocks = rows // BLOCK
    place = lax.axis_index("dp").astype(jnp.int32)
    shard = lax.axis_index("tensor").astype(jnp.int32)
    core = shard % 2
    where = jnp.stack([place, core, shard])

    modulus = jnp.exp(-jnp.exp(nu_log))
    angle = jnp.exp(theta_log)
    gain = jnp.exp(gamma_log)
    parts = [split_low(v) for v in (modulus * jnp.cos(angle), modulus * jnp.sin(angle), gain)]
    table = jnp.stack([parts[v][k] for k in range(3) for v in range(3)])
    placed = jnp.where(
        lax.broadcasted_iota(jnp.int32, (9, width), 1) // per_s == shard, jnp.tile(table, (1, width // per_s)), 0.0
    )
    pack_a = jnp.concatenate(
        [in_real.T, in_imag.T, placed.astype(BF16), jnp.zeros((PARAM_ROWS - 9, width), BF16)], axis=0
    )
    pack_b = jnp.concatenate(
        [out_real, out_imag, down_weight, jnp.concatenate([up_weight, gate_weight], axis=1)], axis=0
    )
    packs_a = gather_tensor(pack_a)
    packs_b = gather_tensor(pack_b)

    tok_rows = tokens.reshape(seqs * length, width)
    cot_rows = cotangent.reshape(seqs * length, width)
    row = lambda v: v.reshape(1, width)
    half_spec = pl.BlockSpec((BLOCK, width), lambda b, w, *_: (w[1] * blocks + b, 0))
    row_spec = lambda lanes: pl.BlockSpec((BLOCK, lanes), lambda b, *_: (b, 0))
    pack_spec = [whole(pack_a.shape)] * TENSOR
    vec_spec = whole((1, width))
    shape = jax.ShapeDtypeStruct
    lanes = 2 * states

    local, ends = call(
        functools.partial(drive_kernel, length=length),
        (blocks,),
        1,
        [half_spec] + pack_spec + [vec_spec] * 2,
        [row_spec(lanes), whole((own_seqs, lanes))],
        [shape((rows, lanes), F32), shape((own_seqs, lanes), F32)],
        [
            pltpu.VMEM((lanes, width), BF16),
            pltpu.VMEM((4, 2, TILE, states), F32),
            pltpu.VMEM((BLOCK, lanes), F32),
            pltpu.VMEM((1, lanes), F32),
        ],
        (2 * rows * width * lanes, rows * width * 8),
    )(where, tok_rows, *packs_a, row(ln_gain), row(ln_bias))

    all_ends = share_over_dp(ends, groups)

    out_own, state, back, back_ends, y_low, hid_half, cot_m, act, ul_half, skip_grad = call(
        functools.partial(middle_kernel, length=length),
        (blocks,),
        2,
        [half_spec, half_spec, row_spec(lanes), whole((groups, own_seqs, lanes))]
        + pack_spec
        + [vec_spec] * 3
        + [pl.BlockSpec(memory_space=pl.ANY)] * TENSOR,
        [
            row_spec(width),
            row_spec(lanes),
            row_spec(lanes),
            whole((own_seqs, lanes)),
            row_spec(width),
            row_spec(2 * per_f),
            row_spec(width),
            row_spec(width),
            row_spec(4 * per_f),
            vec_spec,
        ],
        [
            shape((rows, width), BF16),
            shape((rows, lanes), BF16),
            shape((rows, lanes), F32),
            shape((own_seqs, lanes), F32),
            shape((rows, width), BF16),
            shape((rows, 2 * per_f), BF16),
            shape((rows, width), BF16),
            shape((rows, width), BF16),
            shape((rows, 4 * per_f), BF16),
            shape((1, width), F32),
        ],
        [
            pltpu.VMEM((lanes, width), BF16),
            pltpu.VMEM((TENSOR * per_f, width), BF16),
            pltpu.VMEM((width, 2 * TENSOR * per_f), BF16),
            pltpu.VMEM((4, 2, TILE, states), F32),
            pltpu.VMEM((2, length, states), F32),
            pltpu.VMEM((own_seqs, lanes), F32),
            pltpu.VMEM((BLOCK, TENSOR * per_f), BF16),
            pltpu.VMEM((BLOCK, 2 * TENSOR * per_f), BF16),
            pltpu.VMEM((BLOCK, width), F32),
            pltpu.VMEM((BLOCK, lanes), F32),
            pltpu.SemaphoreType.DMA((TENSOR, 4)),
        ],
        (2 * rows * width * (2 * lanes + 6 * TENSOR * per_f), rows * width * 24),
    )(
        where,
        lengths,
        tok_rows,
        cot_rows,
        local,
        all_ends,
        *packs_a,
        row(ln_gain),
        row(ln_bias),
        row(skip_gain),
        *packs_b,
    )

    all_back = share_over_dp(back_ends, groups)
    out_other = core_swap(out_own)

    pack_rows = pack_b.shape[0]
    own_b, sent_b = call(
        weight_kernel,
        (1,),
        1,
        [
            whole((rows, 2 * per_f)),
            whole((rows, width)),
            whole((rows, width)),
            whole((rows, 4 * per_f)),
            whole((rows, lanes)),
            whole((rows, width)),
        ],
        [whole((pack_rows, width))] * 2,
        [shape((pack_rows, width), F32), shape((pack_rows, width), BF16)],
        [],
        (4 * rows * width * pack_rows, rows * width * 14),
    )(where, hid_half, cot_m, act, ul_half, state, y_low)
    pair_b = (own_b + core_swap(sent_b).astype(F32)).astype(BF16)
    grads_b = sum_over_dp(pair_b, groups)

    grad_own, own_a, sent_a = call(
        functools.partial(last_kernel, length=length),
        (blocks,),
        1,
        [
            half_spec,
            row_spec(width),
            row_spec(lanes),
            row_spec(lanes),
            row_spec(width),
            whole((groups, own_seqs, lanes)),
            vec_spec,
        ]
        + pack_spec
        + [vec_spec] * 3,
        [row_spec(width), whole(pack_a.shape), whole(pack_a.shape)],
        [shape((rows, width), BF16), shape(pack_a.shape, BF16), shape(pack_a.shape, BF16)],
        [
            pltpu.VMEM((lanes, width), BF16),
            pltpu.VMEM((4, 2, TILE, states), F32),
            pltpu.VMEM((2, length, states), F32),
            pltpu.VMEM((own_seqs, lanes), F32),
            pltpu.VMEM((1, lanes), F32),
            pltpu.VMEM((BLOCK, lanes), BF16),
            pltpu.VMEM((states, width), F32),
            pltpu.VMEM((1, lanes), F32),
            pltpu.VMEM((1, width), F32),
            pltpu.VMEM((1, width), F32),
        ],
        (2 * rows * width * (lanes + states), rows * width * 16),
    )(
        where,
        tok_rows,
        cot_m,
        back,
        state,
        y_low,
        all_back,
        skip_grad,
        *packs_a,
        row(ln_gain),
        row(ln_bias),
        row(skip_gain),
    )
    grad_other = core_swap(grad_own)
    pair_a = (own_a.astype(F32) + core_swap(sent_a).astype(F32)).astype(BF16)
    grads_a = sum_over_dp_small(pair_a, groups)

    def in_order(mine, other):
        first = core == 0
        return jnp.concatenate([jnp.where(first, mine, other), jnp.where(first, other, mine)], axis=0).reshape(
            seqs, length, width
        )

    block_out = in_order(out_own, out_other)
    input_grad = in_order(grad_own, grad_other).astype(F32)

    in_real_grad = grads_a[:per_s].T
    in_imag_grad = grads_a[per_s : 2 * per_s].T
    small = grads_a[2 * per_s :]
    lam_real = lax.dynamic_slice_in_dim(small[3, :states], shard * per_s, per_s)
    lam_imag = lax.dynamic_slice_in_dim(small[3, states:], shard * per_s, per_s)
    cos, sin = jnp.cos(angle), jnp.sin(angle)
    nu_grad = -jnp.exp(nu_log) * modulus * (lam_real * cos + lam_imag * sin)
    theta_grad = angle * modulus * (lam_imag * cos - lam_real * sin)
    gamma_grad = jnp.sum(in_real.astype(F32) * in_real_grad + in_imag.astype(F32) * in_imag_grad, axis=0)
    return (
        block_out,
        input_grad,
        small[0],
        small[1],
        small[2],
        in_real_grad,
        in_imag_grad,
        grads_b[:per_s],
        grads_b[per_s : 2 * per_s],
        nu_grad,
        theta_grad,
        gamma_grad,
        grads_b[2 * per_s + per_f :, :per_f],
        grads_b[2 * per_s + per_f :, per_f:],
        grads_b[2 * per_s : 2 * per_s + per_f],
    )


def solution(mesh):
    rows = P(None, "dp", None)
    columns = P(None, "tensor")
    lines = P("tensor", None)
    vector = P("tensor")
    in_specs = (rows, rows, P(), P(), P(), columns, columns, lines, lines, vector, vector, vector, columns, columns, lines, P())
    out_specs = (rows, rows, P(), P(), P(), columns, columns, lines, lines, vector, vector, vector, columns, columns, lines)
    return jax.shard_map(
        functools.partial(shards, groups=mesh.shape["dp"]),
        mesh=mesh,
        in_specs=in_specs,
        out_specs=out_specs,
        check_vma=False,
    )
```

time: 1540 us -> 186 us (0.12); the launches traced: 1520 us -> 185 us
  waiting for transfers between devices: 587 us -> 70 us
  local copies, waits for them, and re-layouts: 502 us -> 8.27 us
  other arithmetic: 191 us -> 15.7 us
  blocking collectives: 158 us -> 15.2 us
  Pallas kernels: 0 us -> 50.5 us
  matrix products: 39.7 us -> 0 us
    psum x4 -> x0, waiting for transfers between devices: 409 us -> none  [the longest x1 196 us: shards(): lax.psum(jnp.dot(hidden_low, down_weight, preferred_element_type=jnp.floa...]
    slice x196 -> x5, local copies, waits for them, and re-layouts: 287 us -> 3.19 us  [the longest x1 1.05 us: shards(): grads_b[2 * per_s + per_f:, per_f:]]
    all_to_all x4 -> x3, waiting for transfers between devices: 178 us -> 13.7 us  [the longest x2 13.7 us: share_over_dp(): lax.all_to_all(jnp.broadcast_to(value[None], (groups,) + value.shape), 'd...]
    psum x1 -> x0, blocking collectives: 158 us -> none  [shards(): lax.psum((gain_grad, bias_grad, skip_grad, in_real_grad, in_imag_grad, ou...]
    pad x72 -> x0, local copies, waits for them, and re-layouts: 113 us -> none  [linear_scan(): lax.associative_scan(complex_step, elements, reverse=backwards, axis=1)]
    add x77 -> x0, other arithmetic: 95 us -> none  [the longest x31 45.6 us: complex_step(): latter[0] * earlier[3] + latter[1] * earlier[2] + latter[3]]
    ppermute x0 -> x13, waiting for transfers between devices: none -> 56.3 us  [the longest x3 30 us: sum_over_dp_small(): other = lax.ppermute(value, 'dp', [(i, i ^ bit) for i in range(groups)])]
    pallas_call x0 -> x4, Pallas kernels: none -> 50.5 us  [the longest x1 23 us: shards(): call(functools.partial(middle_kernel, length=length), (blocks,), 2, [half...]
  transfers between devices with their start and end apart: 8 -> 16, of which waited for: 7 -> 7; matrix products, arithmetic and copies ran while one was open for 21% -> 9% of each run, Pallas kernels for 0% -> 15%
where the time goes in v1:
time: 186 us; the launch traced here: 185 us
  waiting for transfers between devices  70 us (38%)
  Pallas kernels  50.5 us (27%)
  starting transfers between devices  24.5 us (13%)
  other arithmetic  15.7 us (8%)
  blocking collectives  15.2 us (8%)
  local copies, waits for them, and re-layouts  8.27 us (4%)
    ppermute x3, waiting for transfers between devices, sum_over_dp_small(): other = lax.ppermute(value, 'dp', [(i, i ^ bit) for i in range(groups)])  30 us
    ppermute x2, waiting for transfers between devices, side_swap(): return lax.ppermute(value, 'tensor', [(t, t ^ 2) for t in range(TENSOR)])  24.3 us
    pallas_call x1, Pallas kernels, shards(): call(functools.partial(middle_kernel, length=length), (blocks,), 2, [half...  23 us
    all_to_all x1, blocking collectives, share_over_dp(): lax.all_to_all(jnp.broadcast_to(value[None], (groups,) + value.shape), 'd...  15.2 us
    all_to_all x2, waiting for transfers between devices, share_over_dp(): lax.all_to_all(jnp.broadcast_to(value[None], (groups,) + value.shape), 'd...  13.7 us
    pallas_call x1, Pallas kernels, shards(): call(functools.partial(last_kernel, length=length), (blocks,), 1, [half_s...  10.2 us
    pallas_call x1, Pallas kernels, shards(): call(weight_kernel, (1,), 1, [whole((rows, 2 * per_f)), whole((rows, widt...  8.83 us
    pallas_call x1, Pallas kernels, shards(): call(functools.partial(drive_kernel, length=length), (blocks,), 1, [half_...  8.48 us
  transfers between devices with their start and end apart: 16, of which 7 were waited for; matrix products, arithmetic and copies ran while one was open for 9% of the time, Pallas kernels for 15%

profile of v1, /device:TPU:0, one launch (start us, length us, event | category | flops | bytes accessed | tf_op | source)
XLA Modules:
  0.0 185.2 jit_solution(4424863833158995549)
XLA Ops:
  0.7 1.2 maximum_maximum_fusion.b0
  1.9 3.0 %collective-permute-start.4 = (bf16[896,512]{1,0:T(8,128)(2,1)S(1)}, bf16[896,512]{1,0:T(8,128)(2,1)S(1)}, u32[]{:S(2)}, u32[]{:S(2)}) collective-permute-start(bf16[896,512]{1,0:T(8,128)(2,1)S(1)} %maximum_maximum_fusion.b0), channel_id=1, source_target_pairs={{0,2},{1,3},{2,0},{3,1},{4,6},{5,7},{6,4},{7,5},{8,10},{9,11},{10,... | collective-permute-start | bytes 2752520 | tf_op jit(solution)/shard_map/ppermute | solution.py:450
  5.1 0.1 tile.10
  5.4 20.0 %collective-permute-done.4.b2 = bf16[896,512]{1,0:T(8,128)(2,1)S(1)} collective-permute-done((bf16[896,512]{1,0:T(8,128)(2,1)S(1)}, bf16[896,512]{1,0:T(8,128)(2,1)S(1)}, u32[]{:S(2)}, u32[]{:S(2)}) %collective-permute-start.4) | collective-permute-done | bytes 917536 | tf_op jit(solution)/shard_map/ppermute | solution.py:450
  25.3 0.1 maximum_maximum_fusion.1.a0
  25.4 1.8 collective-permute-start.1
  27.3 0.2 collective-permute-start
  27.5 4.3 %collective-permute-done.1.a2 = bf16[144,512]{1,0:T(8,128)(2,1)S(1)} collective-permute-done((bf16[144,512]{1,0:T(8,128)(2,1)S(1)}, bf16[144,512]{1,0:T(8,128)(2,1)S(1)}, u32[]{:S(2)}, u32[]{:S(2)}) %collective-permute-start.1) | collective-permute-done | bytes 147488 | tf_op jit(solution)/shard_map/ppermute | solution.py:450
  31.8 0.6 pad_add_fusion.where_ref
  32.4 0.8 collective-permute-done.2.a3
  33.2 0.6 copy-done.8
  33.8 8.5 %shard_map.271 = (f32[1536,512]{1,0:T(8,128)}, f32[12,512]{1,0:T(8,128)}) custom-call(s32[3]{0:T(128)} %pad_add_fusion.where_ref, bf16[3072,512]{1,0:T(8,128)(2,1)} %bitcast.63, bf16[144,512]{1,0:T(8,128)(2,1)} %copy-done.3, bf16[144,512]{1,0:T(8,128)(2,1)} %copy-done.7, bf16[144,512]{1,0:T(8,128)(2,1)} %copy-done.6, bf16[144,512]{1,0:T(8,128)(2,1)} %copy-done.8, ...), custom_call_target="tpu_custom_call" | custom-call | flops 805306368 | bytes 6291456 | tf_op jit(solution)/shard_map/pallas_call | solution.py:540
  42.3 0.8 broadcast_in_dim.14
  43.1 15.2 %all_to_all.20.ends_ref = f32[8,12,512]{2,1,0:T(8,128)} all-to-all(f32[8,12,512]{2,1,0:T(8,128)S(1)} %broadcast_in_dim.14), channel_id=1, replica_groups=mesh['dp'=8,'tensor'=4] {'dp'}, dimensions={0} | all-to-all | bytes 393216 | tf_op jit(solution)/shard_map/all_to_all | solution.py:459
  58.2 23.0 %shard_map.272 = (bf16[1536,512]{1,0:T(8,128)(2,1)}, bf16[1536,512]{1,0:T(8,128)(2,1)}, f32[1536,512]{1,0:T(8,128)}, f32[12,512]{1,0:T(8,128)}, bf16[1536,512]{1...) custom-call(s32[3]{0:T(128)} %pad_add_fusion.where_ref, ...), custom_call_target="tpu_custom_call" | custom-call | flops 11274289152 | bytes 18874368 | tf_op jit(solution)/shard_map/pallas_call | solution.py:558
  81.2 1.5 broadcast_in_dim.28
  82.7 3.6 %all-to-all-start.1 = ((f32[8,12,512]{2,1,0:T(8,128)}), f32[8,12,512]{2,1,0:T(8,128)S(1)}, u32[]{:S(2)}, u32[]{:S(2)}) async-start(f32[8,12,512]{2,1,0:T(8,128)} %broadcast_in_dim.28), calls=%async_computation.1 | async-start | bytes 524288 | tf_op jit(solution)/shard_map/all_to_all | solution.py:459
  86.3 8.8 %shard_map.274 = (f32[896,512]{1,0:T(8,128)}, bf16[896,512]{1,0:T(8,128)(2,1)}) custom-call(s32[3]{0:T(128)} %pad_add_fusion.where_ref, bf16[1536,512]{1,0:T(8,128)(2,1)} %get-tuple-element.44.hid_ref, bf16[1536,512]{1,0:T(8,128)(2,1)} %get-tuple-element.35.cotm_ref, bf16[1536,512]{1,0:T(8,128)(2,1)} %get-tuple-element.45.act_ref, ...), custom_call_target="tpu_custom_call" | custom-call | flops 2818572288 | bytes 11010048 | tf_op jit(solution)/shard_map/pallas_call | solution.py:622
  95.1 0.7 copy-done.4
  95.8 10.2 %shard_map.273 = (bf16[1536,512]{1,0:T(8,128)(2,1)}, bf16[144,512]{1,0:T(8,128)(2,1)}, bf16[144,512]{1,0:T(8,128)(2,1)}) custom-call(s32[3]{0:T(128)} %pad_add_fusion.where_ref, bf16[3072,512]{1,0:T(8,128)(2,1)} %bitcast.65, bf16[1536,512]{1,0:T(8,128)(2,1)} %get-tuple-element.35.cotm_ref, f32[1536,512]{1,0:T(8,128)} %get-tuple-element.36.back_ref, ...), custom_call_target="tpu_custom_call" | custom-call | flops 1207959552 | bytes 12582912 | tf_op jit(solution)/shard_map/pallas_call | solution.py:642
  106.1 0.6 collective-permute-start.8
  106.6 1.2 collective-permute-done.8
  107.9 0.9 add_convert_fusion.4
  108.8 2.1 %collective-permute-start.9 = (bf16[144,512]{1,0:T(8,128)(2,1)S(1)}, bf16[144,512]{1,0:T(8,128)(2,1)S(1)}, u32[]{:S(2)}, u32[]{:S(2)}) collective-permute-start(bf16[144,512]{1,0:T(8,128)(2,1)S(1)} %add_convert_fusion.4), channel_id=1, source_target_pairs={{0,4},{4,0},{8,12},{12,8},{16,20},{20,16},{24,28},{28,24},{1,5},{5... | collective-permute-start | bytes 442376 | tf_op jit(solution)/shard_map/ppermute | solution.py:475
  110.9 4.4 %collective-permute-done.9 = bf16[144,512]{1,0:T(8,128)(2,1)S(1)} collective-permute-done((bf16[144,512]{1,0:T(8,128)(2,1)S(1)}, bf16[144,512]{1,0:T(8,128)(2,1)S(1)}, u32[]{:S(2)}, u32[]{:S(2)}) %collective-permute-start.9) | collective-permute-done | bytes 147488 | tf_op jit(solution)/shard_map/ppermute | solution.py:475
  115.3 1.8 collective-permute-start.10
  117.1 1.2 add_convert_fusion
  118.4 4.7 %all-to-all-start.2 = ((bf16[8,112,512]{2,1,0:T(8,128)(2,1)}), bf16[8,112,512]{2,1,0:T(8,128)(2,1)S(1)}, u32[]{:S(2)}, u32[]{:S(2)}) async-start(bf16[8,112,512]{2,1,0:T(8,128)(2,1)} %bitcast.26), calls=%async_computation.2 | async-start | bytes 1835008 | tf_op jit(solution)/shard_map/all_to_all | solution.py:467
  123.2 2.9 %collective-permute-start.11 = (bf16[144,512]{1,0:T(8,128)(2,1)S(1)}, bf16[144,512]{1,0:T(8,128)(2,1)S(1)}, u32[]{:S(2)}, u32[]{:S(2)}) collective-permute-start(bf16[144,512]{1,0:T(8,128)(2,1)S(1)} %add_convert_fusion.2), channel_id=1, source_target_pairs={{0,16},{4,20},{8,24},{12,28},{16,0},{20,4},{24,8},{28,12},{1,17},{... | collective-permute-start | bytes 442376 | tf_op jit(solution)/shard_map/ppermute | solution.py:475
  126.1 0.2 collective-permute-start.7
  126.3 25.7 %collective-permute-done.11 = bf16[144,512]{1,0:T(8,128)(2,1)S(1)} collective-permute-done((bf16[144,512]{1,0:T(8,128)(2,1)S(1)}, bf16[144,512]{1,0:T(8,128)(2,1)S(1)}, u32[]{:S(2)}, u32[]{:S(2)}) %collective-permute-start.11) | collective-permute-done | bytes 147488 | tf_op jit(solution)/shard_map/ppermute | solution.py:475
  152.0 0.6 fusion.10
  152.6 0.6 fusion.14
  153.2 1.4 add_reduce_fusion
  154.6 0.1 reduce_sum.21
  154.7 1.0 broadcast_in_dim.29
  155.7 3.6 %all-to-all-start.3 = ((bf16[8,112,512]{2,1,0:T(8,128)(2,1)}), bf16[8,112,512]{2,1,0:T(8,128)(2,1)S(1)}, u32[]{:S(2)}, u32[]{:S(2)}) async-start(bf16[8,112,512]{2,1,0:T(8,128)(2,1)} %broadcast_in_dim.29), calls=%async_computation.3 | async-start | bytes 1835008 | tf_op jit(solution)/shard_map/all_to_all | solution.py:459
  159.3 1.6 broadcast_select_fusion.3
  160.9 1.9 %pad_maximum_fusion = bf16[3072,512]{1,0:T(8,128)(2,1)} fusion(bf16[1536,512]{1,0:T(8,128)(2,1)S(1)} %get-tuple-element.59, bf16[1536,512]{1,0:T(8,128)(2,1)S(1)} %get-tuple-element.58), kind=kLoop, calls=%fused_computation | loop fusion | flops 6291456 | bytes 6291456 | tf_op jit(solution)/shard_map/concatenate | solution.py:692
  162.8 0.1 copy-done.2
  163.0 1.8 broadcast_select_fusion.1
  164.8 0.2 pad_maximum_fusion.1
  165.0 3.6 %convert.4 = f32[24,128,512]{2,1,0:T(8,128)} convert(bf16[24,128,512]{2,1,0:T(8,128)(2,1)S(1)} %bitcast.62) | non-fusion elementwise | flops 1572864 | bytes 9437184 | tf_op jit(solution)/shard_map/convert_element_type | solution.py:697
  168.6 13.7 %all-to-all-done.3 = bf16[8,112,512]{2,1,0:T(8,128)(2,1)S(1)} async-done(((bf16[8,112,512]{2,1,0:T(8,128)(2,1)}), bf16[8,112,512]{2,1,0:T(8,128)(2,1)S(1)}, u32[]{:S(2)}, u32[]{:S(2)}) %all-to-all-start.3) | async-done | bytes 917536 | tf_op jit(solution)/shard_map/all_to_all | solution.py:459
  182.3 0.3 bitcast_convert_fusion
  182.6 0.7 fusion.12
  183.3 0.8 slice.65
  184.2 1.0 fusion.11
  (55 shorter events, 0.5 us)
Async XLA Ops:
  0.7 4.3 %copy-start.13 = (f32[64]{0:T(128)S(1)}, f32[64]{0:T(128)}, u32[]{:S(2)}) copy-start(f32[64]{0:T(128)} %param.27) | copy-start | bytes 772
  0.7 4.3 %copy-start.11 = (f32[64]{0:T(128)S(1)}, f32[64]{0:T(128)}, u32[]{:S(2)}) copy-start(f32[64]{0:T(128)} %param.26) | copy-start | bytes 772
  0.7 4.3 %copy-start.12 = (f32[64]{0:T(128)S(1)}, f32[64]{0:T(128)}, u32[]{:S(2)}) copy-start(f32[64]{0:T(128)} %param.25) | copy-start | bytes 772
  0.7 24.6 %copy-start.10 = (bf16[512,64]{0,1:T(8,128)(2,1)S(1)}, bf16[512,64]{0,1:T(8,128)(2,1)}, u32[]{:S(2)}) copy-start(bf16[512,64]{0,1:T(8,128)(2,1)} %param.21) | copy-start | bytes 196612
  0.7 24.6 %copy-start.9 = (bf16[512,64]{0,1:T(8,128)(2,1)S(1)}, bf16[512,64]{0,1:T(8,128)(2,1)}, u32[]{:S(2)}) copy-start(bf16[512,64]{0,1:T(8,128)(2,1)} %param.22) | copy-start | bytes 196612
  1.9 56.3 %copy-start.5 = (bf16[896,512]{1,0:T(8,128)(2,1)}, bf16[896,512]{1,0:T(8,128)(2,1)S(1)}, u32[]{:S(2)}) copy-start(bf16[896,512]{1,0:T(8,128)(2,1)S(1)} %maximum_maximum_fusion.b0) | copy-start | bytes 2752516
  1.9 23.4 %collective-permute-start.4 = (bf16[896,512]{1,0:T(8,128)(2,1)S(1)}, bf16[896,512]{1,0:T(8,128)(2,1)S(1)}, u32[]{:S(2)}, u32[]{:S(2)}) collective-permute-start(bf16[896,512]{1,0:T(8,128)(2,1)S(1)} %maximum_maximum_fusion.b0), channel_id=1, source_target_pairs={{0,2},{1,3},{2,0},{3,1},{4,6},{5,7},{6,4},{7,5},{8,10},{9,11},{10,... | collective-permute-start | bytes 2752520 | tf_op jit(solution)/shard_map/ppermute | solution.py:450
  5.0 53.2 %collective-permute-start.3 = (bf16[896,512]{1,0:T(8,128)(2,1)S(1)}, bf16[896,512]{1,0:T(8,128)(2,1)}, u32[]{:S(2)}, u32[]{:S(2)}) collective-permute-start(bf16[896,512]{1,0:T(8,128)(2,1)S(1)} %maximum_maximum_fusion.b0), channel_id=1, source_target_pairs={{0,1},{1,0},{2,3},{3,2},{4,5},{5,4},{6,7},{7,6},{8,9},{9,8},{10,11... | collective-permute-start | bytes 2752520 | tf_op jit(solution)/shard_map/ppermute | solution.py:446
  25.3 32.9 %copy-start.14 = (bf16[896,512]{1,0:T(8,128)(2,1)}, bf16[896,512]{1,0:T(8,128)(2,1)S(1)}, u32[]{:S(2)}) copy-start(bf16[896,512]{1,0:T(8,128)(2,1)S(1)} %collective-permute-done.4.b2) | copy-start | bytes 2752516
  25.3 32.9 %collective-permute-start.5 = (bf16[896,512]{1,0:T(8,128)(2,1)S(1)}, bf16[896,512]{1,0:T(8,128)(2,1)}, u32[]{:S(2)}, u32[]{:S(2)}) collective-permute-start(bf16[896,512]{1,0:T(8,128)(2,1)S(1)} %collective-permute-done.4.b2), channel_id=1, source_target_pairs={{0,1},{1,0},{2,3},{3,2},{4,5},{5,4},{6,7},{7,6},{8,9},{9,8},{10,11... | collective-permute-start | bytes 2752520 | tf_op jit(solution)/shard_map/ppermute | solution.py:446
  25.4 7.7 %copy-start.3 = (bf16[144,512]{1,0:T(8,128)(2,1)}, bf16[144,512]{1,0:T(8,128)(2,1)S(1)}, u32[]{:S(2)}) copy-start(bf16[144,512]{1,0:T(8,128)(2,1)S(1)} %maximum_maximum_fusion.1.a0) | copy-start | bytes 442372
  25.4 6.3 %collective-permute-start.1 = (bf16[144,512]{1,0:T(8,128)(2,1)S(1)}, bf16[144,512]{1,0:T(8,128)(2,1)S(1)}, u32[]{:S(2)}, u32[]{:S(2)}) collective-permute-start(bf16[144,512]{1,0:T(8,128)(2,1)S(1)} %maximum_maximum_fusion.1.a0), channel_id=1, source_target_pairs={{0,2},{1,3},{2,0},{3,1},{4,6},{5,7},{6,4},{7,5},{8,10},{9,11},{10,... | collective-permute-start | bytes 442376 | tf_op jit(solution)/shard_map/ppermute | solution.py:450
  27.3 5.1 %collective-permute-start = (bf16[144,512]{1,0:T(8,128)(2,1)S(1)}, bf16[144,512]{1,0:T(8,128)(2,1)S(1)}, u32[]{:S(2)}, u32[]{:S(2)}) collective-permute-start(bf16[144,512]{1,0:T(8,128)(2,1)S(1)} %maximum_maximum_fusion.1.a0), channel_id=1, source_target_pairs={{0,1},{1,0},{2,3},{3,2},{4,5},{5,4},{6,7},{7,6},{8,9},{9,8},{10,11... | collective-permute-start | bytes 442376 | tf_op jit(solution)/shard_map/ppermute | solution.py:446
  31.8 1.4 copy-start.6
  31.8 1.4 collective-permute-start.2
  32.4 0.8 copy-start.7
  33.1 0.7 copy-start.8
  82.7 12.4 %all-to-all-start.1 = ((f32[8,12,512]{2,1,0:T(8,128)}), f32[8,12,512]{2,1,0:T(8,128)S(1)}, u32[]{:S(2)}, u32[]{:S(2)}) async-start(f32[8,12,512]{2,1,0:T(8,128)} %broadcast_in_dim.28), calls=%async_computation.1 | async-start | bytes 524288 | tf_op jit(solution)/shard_map/all_to_all | solution.py:459
  95.1 22.0 %collective-permute-start.12 = (bf16[896,512]{1,0:T(8,128)(2,1)}, bf16[896,512]{1,0:T(8,128)(2,1)S(1)}, u32[]{:S(2)}, u32[]{:S(2)}) collective-permute-start(bf16[896,512]{1,0:T(8,128)(2,1)} %get-tuple-element.48), channel_id=1, source_target_pairs={{0,1},{1,0},{2,3},{3,2},{4,5},{5,4},{6,7},{7,6},{8,9},{9,8},{10,11... | collective-permute-start | bytes 2752520 | tf_op jit(solution)/shard_map/ppermute | solution.py:446
  95.1 0.7 copy-start.4
  95.8 21.3 %copy-start = (f32[896,512]{1,0:T(8,128)S(1)}, f32[896,512]{1,0:T(8,128)}, u32[]{:S(2)}) copy-start(f32[896,512]{1,0:T(8,128)} %get-tuple-element.47) | copy-start | bytes 5505028
  106.1 1.8 collective-permute-start.8
  108.8 6.5 %collective-permute-start.9 = (bf16[144,512]{1,0:T(8,128)(2,1)S(1)}, bf16[144,512]{1,0:T(8,128)(2,1)S(1)}, u32[]{:S(2)}, u32[]{:S(2)}) collective-permute-start(bf16[144,512]{1,0:T(8,128)(2,1)S(1)} %add_convert_fusion.4), channel_id=1, source_target_pairs={{0,4},{4,0},{8,12},{12,8},{16,20},{20,16},{24,28},{28,24},{1,5},{5... | collective-permute-start | bytes 442376 | tf_op jit(solution)/shard_map/ppermute | solution.py:475
  115.3 7.8 %collective-permute-start.10 = (bf16[144,512]{1,0:T(8,128)(2,1)S(1)}, bf16[144,512]{1,0:T(8,128)(2,1)S(1)}, u32[]{:S(2)}, u32[]{:S(2)}) collective-permute-start(bf16[144,512]{1,0:T(8,128)(2,1)S(1)} %add_convert_fusion.3), channel_id=1, source_target_pairs={{0,8},{4,12},{8,0},{12,4},{16,24},{20,28},{24,16},{28,20},{1,9},{5... | collective-permute-start | bytes 442376 | tf_op jit(solution)/shard_map/ppermute | solution.py:475
  118.4 4.7 %copy-start.1 = (bf16[1536,512]{1,0:T(8,128)(2,1)S(1)}, bf16[1536,512]{1,0:T(8,128)(2,1)}, u32[]{:S(2)}) copy-start(bf16[1536,512]{1,0:T(8,128)(2,1)} %get-tuple-element.34) | copy-start | bytes 4718596
  118.4 36.2 %all-to-all-start.2 = ((bf16[8,112,512]{2,1,0:T(8,128)(2,1)}), bf16[8,112,512]{2,1,0:T(8,128)(2,1)S(1)}, u32[]{:S(2)}, u32[]{:S(2)}) async-start(bf16[8,112,512]{2,1,0:T(8,128)(2,1)} %bitcast.26), calls=%async_computation.2 | async-start | bytes 1835008 | tf_op jit(solution)/shard_map/all_to_all | solution.py:467
  123.0 36.3 %collective-permute-start.6 = (bf16[1536,512]{1,0:T(8,128)(2,1)S(1)}, bf16[1536,512]{1,0:T(8,128)(2,1)}, u32[]{:S(2)}, u32[]{:S(2)}) collective-permute-start(bf16[1536,512]{1,0:T(8,128)(2,1)S(1)} %copy-done.1), channel_id=1, source_target_pairs={{0,1},{1,0},{2,3},{3,2},{4,5},{5,4},{6,7},{7,6},{8,9},{9,8},{10,11... | collective-permute-start | bytes 4718600 | tf_op jit(solution)/shard_map/ppermute | solution.py:446
  123.2 28.8 %collective-permute-start.11 = (bf16[144,512]{1,0:T(8,128)(2,1)S(1)}, bf16[144,512]{1,0:T(8,128)(2,1)S(1)}, u32[]{:S(2)}, u32[]{:S(2)}) collective-permute-start(bf16[144,512]{1,0:T(8,128)(2,1)S(1)} %add_convert_fusion.2), channel_id=1, source_target_pairs={{0,16},{4,20},{8,24},{12,28},{16,0},{20,4},{24,8},{28,12},{1,17},{... | collective-permute-start | bytes 442376 | tf_op jit(solution)/shard_map/ppermute | solution.py:475
  126.1 36.7 %collective-permute-start.7 = (bf16[1536,512]{1,0:T(8,128)(2,1)}, bf16[1536,512]{1,0:T(8,128)(2,1)}, u32[]{:S(2)}, u32[]{:S(2)}) collective-permute-start(bf16[1536,512]{1,0:T(8,128)(2,1)} %get-tuple-element.41), channel_id=1, source_target_pairs={{0,1},{1,0},{2,3},{3,2},{4,5},{5,4},{6,7},{7,6},{8,9},{9,8},{10,11... | collective-permute-start | bytes 4718600 | tf_op jit(solution)/shard_map/ppermute | solution.py:446
  155.7 26.6 %all-to-all-start.3 = ((bf16[8,112,512]{2,1,0:T(8,128)(2,1)}), bf16[8,112,512]{2,1,0:T(8,128)(2,1)S(1)}, u32[]{:S(2)}, u32[]{:S(2)}) async-start(bf16[8,112,512]{2,1,0:T(8,128)(2,1)} %broadcast_in_dim.29), calls=%async_computation.3 | async-start | bytes 1835008 | tf_op jit(solution)/shard_map/all_to_all | solution.py:459
  160.9 2.0 %copy-start.2 = (bf16[1536,512]{1,0:T(8,128)(2,1)S(1)}, bf16[1536,512]{1,0:T(8,128)(2,1)}, u32[]{:S(2)}) copy-start(bf16[1536,512]{1,0:T(8,128)(2,1)} %get-tuple-element.41) | copy-start | bytes 4718596

commit v2 on v1

v2 whole, which is shorter than its diff:
```python
import functools
import math

import jax
import jax.numpy as jnp
from jax import lax
from jax.experimental import pallas as pl
from jax.experimental.pallas import tpu as pltpu
from jax.sharding import PartitionSpec as P

EPSILON = 1e-05
TENSOR = 4
TILE = 8
BLOCK = 256
PARAM_ROWS = 16
F32 = jnp.float32
BF16 = jnp.bfloat16
GELU_K = math.sqrt(2.0 / math.pi)
MIB = 1024 * 1024


def dot(left, right):
    return jnp.dot(left, right, preferred_element_type=F32)


def dot_nt(left, right):
    return lax.dot_general(left, right, (((1,), (1,)), ((), ())), preferred_element_type=F32)


def dot_tn(left, right):
    return lax.dot_general(left, right, (((0,), (0,)), ((), ())), preferred_element_type=F32)


def layer_norm(rows):
    centre = jnp.mean(rows, axis=-1, keepdims=True)
    shifted = rows - centre
    variance = jnp.mean(shifted * shifted, axis=-1, keepdims=True)
    inv_scale = lax.rsqrt(variance + EPSILON)
    return shifted * inv_scale, inv_scale


def cmul(ar, ai, br, bi):
    return ar * br - ai * bi, ar * bi + ai * br


def read_params(packs, row):
    total = None
    for pack in packs:
        rows = pack[row : row + PARAM_ROWS, :].astype(F32)
        total = rows if total is None else total + rows
    states = total.shape[1] // 2
    at = lambda k: total[k : k + 1, :states] + total[k + 3 : k + 4, :states] + total[k + 6 : k + 7, :states]
    return at(0), at(1), at(2)


def powers_of(decay_real, decay_imag, exponent):
    out_r = jnp.ones(exponent.shape, F32)
    out_i = jnp.zeros(exponent.shape, F32)
    br, bi = decay_real, decay_imag
    for bit in range(4):
        mr, mi = cmul(out_r, out_i, br, bi)
        on = ((exponent >> bit) & 1) == 1
        out_r = jnp.where(on, mr, out_r)
        out_i = jnp.where(on, mi, out_i)
        br, bi = cmul(br, bi, br, bi)
    return out_r, out_i


def fill_steps(decay_real, decay_imag, backwards, step_ref):
    states = decay_real.shape[1]
    row = lax.broadcasted_iota(jnp.int32, (TILE, states), 0)
    if backwards:
        row = TILE - 1 - row
    zero = jnp.zeros((TILE, states), F32)
    for k, shift in enumerate((1, 2, 4)):
        pr, pi = powers_of(decay_real, decay_imag, jnp.full((TILE, states), shift, jnp.int32))
        step_ref[k, 0] = jnp.where(row >= shift, pr, zero)
        step_ref[k, 1] = jnp.where(row >= shift, pi, zero)
    step_ref[3, 0], step_ref[3, 1] = powers_of(decay_real, decay_imag, row + 1)


def fill_powers(decay_real, decay_imag, backwards, first, full_ref):
    states = decay_real.shape[1]
    row = lax.broadcasted_iota(jnp.int32, (TILE, states), 0)
    if backwards:
        row = TILE - 1 - row
    pr, pi = powers_of(decay_real, decay_imag, row + first)
    er, ei = powers_of(decay_real, decay_imag, jnp.full((TILE, states), TILE, jnp.int32))
    tiles = full_ref.shape[1] // TILE
    for n in range(tiles):
        at = (tiles - 1 - n if backwards else n) * TILE
        full_ref[0, at : at + TILE, :] = pr
        full_ref[1, at : at + TILE, :] = pi
        pr, pi = cmul(pr, pi, er, ei)


def scan_block(drive_ref, out_ref, step_ref, length, backwards, finish):
    rows, lanes = drive_ref.shape
    states = lanes // 2
    tiles = length // TILE
    table = [(step_ref[k, 0], step_ref[k, 1]) for k in range(4)]
    edge = 0 if backwards else TILE - 1
    for s in range(rows // length):
        cr = ci = None
        for n in range(tiles):
            at = s * length + (tiles - 1 - n if backwards else n) * TILE
            hr = drive_ref[at : at + TILE, :states]
            hi = drive_ref[at : at + TILE, states:]
            for k, shift in enumerate((1, 2, 4)):
                turn = TILE - shift if backwards else shift
                sr = pltpu.roll(hr, turn, 0)
                si = pltpu.roll(hi, turn, 0)
                mr, mi = cmul(table[k][0], table[k][1], sr, si)
                hr, hi = hr + mr, hi + mi
            if cr is not None:
                mr, mi = cmul(table[3][0], table[3][1], cr, ci)
                hr, hi = hr + mr, hi + mi
            out_ref[at : at + TILE, :states] = hr
            out_ref[at : at + TILE, states:] = hi
            cr, ci = hr[edge : edge + 1], hi[edge : edge + 1]
        finish(s, cr, ci)


def incoming(far_refs, beside_ref, odd, powers_ref, backwards, out_ref):
    states = out_ref.shape[1] // 2
    lr, li = powers_ref[0:1, :states], powers_ref[0:1, states:]
    pr, pi = powers_ref[1:2, :states], powers_ref[1:2, states:]
    sr, si = far_refs[-1][:, :states], far_refs[-1][:, states:]
    for ref in far_refs[-2::-1]:
        mr, mi = cmul(pr, pi, sr, si)
        sr, si = mr + ref[:, :states], mi + ref[:, states:]
    mr, mi = cmul(lr, li, sr, si)
    second = odd == (0 if backwards else 1)
    out_ref[:, :states] = jnp.where(second, mr + beside_ref[:, :states], sr)
    out_ref[:, states:] = jnp.where(second, mi + beside_ref[:, states:], si)


def pair_kernel(where_ref, mine_ref, other_ref, powers_ref, out_ref, *, backwards):
    states = out_ref.shape[1] // 2
    second = where_ref[0] % 2 == (0 if backwards else 1)
    lr, li = powers_ref[0:1, :states], powers_ref[0:1, states:]
    pick = lambda first, part: jnp.where(second == first, other_ref[:, part], mine_ref[:, part])
    early, late = slice(0, states), slice(states, None)
    mr, mi = cmul(lr, li, pick(True, early), pick(True, late))
    out_ref[:, :states] = mr + pick(False, early)
    out_ref[:, states:] = mi + pick(False, late)


def assemble_input(packs, shard, out_ref):
    per = packs[0].shape[0] - PARAM_ROWS
    half = per // 2
    states = out_ref.shape[0] // 2
    for k, pack in enumerate(packs):
        at = pl.multiple_of((shard ^ k) * half, half)
        out_ref[pl.ds(at, half), :] = pack[:half, :]
        out_ref[pl.ds(states + at, half), :] = pack[half:per, :]


def norm_kernel(where_ref, lens_ref, tok_ref, cot_ref, gain_ref, bias_ref, low_ref, normed_ref, inv_ref, cotm_ref, *, length, seqs):
    block = pl.program_id(0)
    normed, inv_scale = layer_norm(tok_ref[...].astype(F32))
    normed_ref[...] = normed
    inv_ref[...] = jnp.broadcast_to(inv_scale, inv_ref.shape)
    low_ref[...] = (normed * gain_ref[...] + bias_ref[...]).astype(BF16)
    rows, width = tok_ref.shape
    per_block = rows // length
    for s in range(per_block):
        span = slice(s * length, (s + 1) * length)
        left = lens_ref[where_ref[1] * seqs + block * per_block + s] - where_ref[0] * length
        live = lax.broadcasted_iota(jnp.int32, (length, width), 0) < left
        cotm_ref[span, :] = jnp.where(live, cot_ref[span, :].astype(F32), 0.0).astype(BF16)


def drive_kernel(where_ref, low_ref, a0, a1, a2, a3, drive_ref, ends_ref, powers_ref, in_t, weigh, gam, *, length):
    block = pl.program_id(0)
    packs = (a0, a1, a2, a3)
    states = in_t.shape[0] // 2

    @pl.when(block == 0)
    def _():
        assemble_input(packs, where_ref[2], in_t)
        dr, di, gain = read_params(packs, a0.shape[0] - PARAM_ROWS)
        fill_powers(dr, di, True, 0, weigh)
        gam[...] = jnp.concatenate([gain, gain], axis=1)
        lr, li = cmul(weigh[0, :1, :], weigh[1, :1, :], dr, di)
        powers_ref[...] = jnp.zeros(powers_ref.shape, F32)
        powers_ref[0:1, :] = jnp.concatenate([lr, li], axis=1)
        powers_ref[1:2, :] = jnp.concatenate(cmul(lr, li, lr, li), axis=1)

    drive_ref[...] = dot_nt(low_ref[...], in_t[...]) * gam[...]
    per_block = low_ref.shape[0] // length
    for s in range(per_block):
        er = ei = jnp.zeros((TILE, states), F32)
        for n in range(length // TILE):
            at = s * length + n * TILE
            mr, mi = cmul(
                weigh[0, n * TILE : (n + 1) * TILE, :],
                weigh[1, n * TILE : (n + 1) * TILE, :],
                drive_ref[at : at + TILE, :states],
                drive_ref[at : at + TILE, states:],
            )
            er, ei = er + mr, ei + mi
        ends_ref[pl.ds(block * per_block + s, 1), :states] = jnp.sum(er, axis=0, keepdims=True)
        ends_ref[pl.ds(block * per_block + s, 1), states:] = jnp.sum(ei, axis=0, keepdims=True)


def scan_kernel(drive_ref, a0, a1, a2, a3, local_ref, step, *, length):
    @pl.when(pl.program_id(0) == 0)
    def _():
        dr, di, _ = read_params((a0, a1, a2, a3), a0.shape[0] - PARAM_ROWS)
        fill_steps(dr, di, False, step)

    scan_block(drive_ref, local_ref, step, length, False, lambda *_: None)


def hidden_kernel(where_ref, cotm_ref, b0, b1, b2, b3, hg_ref, *, per_s):
    shard = where_ref[2]
    per_f = hg_ref.shape[1] // TENSOR
    for k, pack in enumerate((b0, b1, b2, b3)):
        at = pl.multiple_of((shard ^ k) * per_f, per_f)
        hg_ref[:, pl.ds(at, per_f)] = dot_nt(cotm_ref[...], pack[2 * per_s :, :]).astype(BF16)


def middle_kernel(where_ref, *refs, length, ways):
    far_refs, refs = refs[: ways - 1], refs[ways - 1 :]
    beside_ref, powers_ref, local_ref, normed_ref, hg_ref, cotm_ref, a0, a1, a2, a3 = refs[:10]
    gain_ref, bias_ref, skip_ref, b0, b1, b2, b3, g0, g1, g2, g3 = refs[10:21]
    state_ref, back_ref, backends_ref, ylow_ref, hid_ref, own_ref, sent_ref = refs[21:28]
    c_all, ug_all, step, full, carry, act_ref, ul, eback, acc_out, acc_down, acc_ug, sems = refs[28:]
    block = pl.program_id(0)
    place, core, shard = where_ref[0], where_ref[1], where_ref[2]
    states = c_all.shape[0] // 2
    rows, width = normed_ref.shape
    per_block = rows // length
    per_s = states // TENSOR
    per_f = hid_ref.shape[1] // TENSOR

    @pl.when(block == 0)
    def _():
        copies = []
        for k, (pack, gates) in enumerate(((b0, g0), (b1, g1), (b2, g2), (b3, g3))):
            t = shard ^ k
            moves = (
                (pack.at[pl.ds(0, per_s), :], c_all.at[pl.ds(pl.multiple_of(t * per_s, per_s), per_s), :]),
                (pack.at[pl.ds(per_s, per_s), :], c_all.at[pl.ds(pl.multiple_of(states + t * per_s, per_s), per_s), :]),
                (gates, ug_all.at[:, pl.ds(pl.multiple_of(t * 2 * per_f, 2 * per_f), 2 * per_f)]),
            )
            for n, (src, dst) in enumerate(moves):
                copies.append(pltpu.make_async_copy(src, dst, sems.at[k, n]))
        for copy in copies:
            copy.start()
        dr, di, _ = read_params((a0, a1, a2, a3), a0.shape[0] - PARAM_ROWS)
        fill_powers(dr, di, False, 1, full)
        incoming(far_refs, beside_ref, place % 2, powers_ref, False, carry)
        fill_steps(dr, di, True, step)
        acc_out[...] = jnp.zeros(acc_out.shape, F32)
        acc_down[...] = jnp.zeros(acc_down.shape, F32)
        acc_ug[...] = jnp.zeros(acc_ug.shape, F32)
        for copy in copies:
            copy.wait()

    for s in range(per_block):
        seq = block * per_block + s
        span = slice(s * length, (s + 1) * length)
        sr = carry[pl.ds(seq, 1), :states]
        si = carry[pl.ds(seq, 1), states:]
        mr, mi = cmul(full[0], full[1], sr, si)
        state_ref[span, :states] = (local_ref[span, :states] + mr).astype(BF16)
        state_ref[span, states:] = (-(local_ref[span, states:] + mi)).astype(BF16)
    skip = skip_ref[...]
    y = dot(state_ref[...], c_all[...]) + (normed_ref[...] * (gain_ref[...] * skip) + bias_ref[...] * skip)
    square = y * y
    th = jnp.tanh(GELU_K * y * (1.0 + 0.044715 * square))
    act_ref[...] = (0.5 * y * (1.0 + th)).astype(BF16)
    slope = 0.5 * (1.0 + th) + (0.5 * GELU_K) * y * (1.0 - th * th) * (1.0 + (3 * 0.044715) * square)
    act = act_ref[...]
    cotm = cotm_ref[...]
    for t in range(TENSOR):
        both = dot(act, ug_all[:, 2 * per_f * t : 2 * per_f * (t + 1)])
        up = both[:, :per_f]
        sig = jax.nn.sigmoid(both[:, per_f:])
        hid_ref[:, per_f * t : per_f * (t + 1)] = (up * sig).astype(BF16)
        up_grad = hg_ref[:, per_f * t : per_f * (t + 1)].astype(F32) * sig
        ul[:, 2 * per_f * t : 2 * per_f * t + per_f] = up_grad.astype(BF16)
        ul[:, 2 * per_f * t + per_f : 2 * per_f * (t + 1)] = (up_grad * up * (1.0 - sig)).astype(BF16)
    y_grad = dot_nt(ul[...], ug_all[...]) * slope
    ylow_ref[...] = y_grad.astype(BF16)
    eback[...] = dot_nt(ylow_ref[...], c_all[...])

    def finish(s, r, i):
        backends_ref[pl.ds(block * per_block + s, 1), :states] = r
        backends_ref[pl.ds(block * per_block + s, 1), states:] = i

    side = shard // 2
    acc_ug[...] += dot_tn(act, ul[:, pl.ds(pl.multiple_of(side * 4 * per_f, 4 * per_f), 4 * per_f)])
    acc_down[...] += dot_tn(hid_ref[:, pl.ds(pl.multiple_of(side * 2 * per_f, 2 * per_f), 2 * per_f)], cotm)
    for k in range(2):
        cols = state_ref[:, pl.ds(pl.multiple_of(k * states + side * 2 * per_s, 2 * per_s), 2 * per_s)]
        acc_out[k * 2 * per_s : (k + 1) * 2 * per_s, :] += dot_tn(cols, ylow_ref[...])
    scan_block(eback, back_ref, step, length, True, finish)

    @pl.when(block == pl.num_programs(0) - 1)
    def _():
        for n, ref in ((core, own_ref), (1 - core, sent_ref)):
            for k in range(2):
                part = acc_out[pl.ds(pl.multiple_of(2 * per_s * k + n * per_s, per_s), per_s), :]
                ref[k * per_s : (k + 1) * per_s, :] = part.astype(ref.dtype)
            part = acc_down[pl.ds(pl.multiple_of(n * per_f, per_f), per_f), :]
            ref[2 * per_s : 2 * per_s + per_f, :] = part.astype(ref.dtype)
            part = acc_ug[:, pl.ds(pl.multiple_of(n * 2 * per_f, 2 * per_f), 2 * per_f)]
            ref[2 * per_s + per_f : 2 * per_s + per_f + width, :] = part.astype(ref.dtype)


def down_kernel(where_ref, lens_ref, tok_ref, hid_ref, b0, b1, b2, b3, out_ref, down_all, *, length, per_s, seqs):
    block = pl.program_id(0)
    shard = where_ref[2]
    rows, width = tok_ref.shape
    per_block = rows // length
    per_f = down_all.shape[0] // TENSOR

    @pl.when(block == 0)
    def _():
        for k, pack in enumerate((b0, b1, b2, b3)):
            down_all[pl.ds(pl.multiple_of((shard ^ k) * per_f, per_f), per_f), :] = pack[2 * per_s :, :]

    added = dot(hid_ref[...], down_all[...])
    for s in range(per_block):
        span = slice(s * length, (s + 1) * length)
        left = lens_ref[where_ref[1] * seqs + block * per_block + s] - where_ref[0] * length
        live = lax.broadcasted_iota(jnp.int32, (length, width), 0) < left
        out_ref[span, :] = jnp.where(live, tok_ref[span, :].astype(F32) + added[span, :], 0.0).astype(BF16)


def last_kernel(where_ref, *refs, length, ways):
    far_refs, refs = refs[: ways - 1], refs[ways - 1 :]
    beside_ref, powers_ref, low_ref, normed_ref, inv_ref, cotm_ref, back_ref, state_ref, ylow_ref = refs[:9]
    a0, a1, a2, a3, gain_ref, bias_ref, skip_ref, grad_ref, own_ref, sent_ref = refs[9:19]
    in_t, full, carry, gam, dlow, in_grad, lam_grad, vec_grad = refs[19:]
    block = pl.program_id(0)
    place, core, shard = where_ref[0], where_ref[1], where_ref[2]
    states = in_t.shape[0] // 2
    rows, width = low_ref.shape
    per_block = rows // length
    per_s = states // TENSOR
    packs = (a0, a1, a2, a3)

    @pl.when(block == 0)
    def _():
        assemble_input(packs, shard, in_t)
        dr, di, gain = read_params(packs, a0.shape[0] - PARAM_ROWS)
        fill_powers(dr, di, True, 1, full)
        incoming(far_refs, beside_ref, place % 2, powers_ref, True, carry)
        gam[...] = jnp.concatenate([gain, -gain], axis=1)
        in_grad[...] = jnp.zeros(in_grad.shape, F32)
        lam_grad[...] = jnp.zeros(lam_grad.shape, F32)
        vec_grad[...] = jnp.zeros(vec_grad.shape, F32)

    for s in range(per_block):
        seq = block * per_block + s
        span = slice(s * length, (s + 1) * length)
        sr = carry[pl.ds(seq, 1), :states]
        si = carry[pl.ds(seq, 1), states:]
        mr, mi = cmul(full[0], full[1], sr, si)
        gr = back_ref[span, :states] + mr
        gi = back_ref[span, states:] + mi
        dlow[span, :states] = (gr * gam[:, :states]).astype(BF16)
        dlow[span, states:] = (gi * gam[:, states:]).astype(BF16)
        nr = jnp.concatenate([gr[1:], sr], axis=0)
        ni = jnp.concatenate([gi[1:], si], axis=0)
        hr = state_ref[span, :states].astype(F32)
        hi = state_ref[span, states:].astype(F32)
        lam_grad[:, :states] += jnp.sum(nr * hr + ni * hi, axis=0, keepdims=True)
        lam_grad[:, states:] += jnp.sum(nr * hi - ni * hr, axis=0, keepdims=True)
    normed = normed_ref[...]
    ylow = ylow_ref[...].astype(F32)
    u_grad = dot(dlow[...], in_t[...]) + ylow * skip_ref[...]
    vec_grad[0:1, :] += jnp.sum(u_grad * normed, axis=0, keepdims=True)
    vec_grad[1:2, :] += jnp.sum(u_grad, axis=0, keepdims=True)
    vec_grad[2:3, :] += jnp.sum(ylow * (normed * gain_ref[...] + bias_ref[...]), axis=0, keepdims=True)
    scaled = u_grad * gain_ref[...]
    grad = (
        scaled
        - jnp.mean(scaled, axis=-1, keepdims=True)
        - normed * jnp.mean(scaled * normed, axis=-1, keepdims=True)
    )
    grad_ref[...] = (cotm_ref[...].astype(F32) + inv_ref[:, :1] * grad).astype(BF16)
    at = pl.multiple_of((shard // 2) * 2 * per_s, 2 * per_s)
    for k in range(2):
        cols = dlow[:, pl.ds(k * states + at, 2 * per_s)]
        in_grad[2 * per_s * k : 2 * per_s * (k + 1), :] += dot_tn(cols, low_ref[...])

    @pl.when(block == pl.num_programs(0) - 1)
    def _():
        small = jnp.concatenate(
            [vec_grad[:3, :], lam_grad[...], jnp.zeros((PARAM_ROWS - 4, width), F32)], axis=0
        ).astype(BF16)
        for n, ref in ((core, own_ref), (1 - core, sent_ref)):
            for k in range(2):
                part = in_grad[pl.ds(pl.multiple_of(2 * per_s * k + n * per_s, per_s), per_s), :]
                ref[k * per_s : (k + 1) * per_s, :] = part.astype(BF16)
            ref[2 * per_s :, :] = small


def fold_kernel(where_ref, own_ref, other_ref, keep_ref, send_ref):
    half = keep_ref.shape[0]
    odd = where_ref[0] % 2
    at = pl.multiple_of(odd * half, 16)
    keep_ref[...] = own_ref[pl.ds(at, half), :] + other_ref[pl.ds(at, half), :].astype(F32)
    at = pl.multiple_of((1 - odd) * half, 16)
    send_ref[...] = (own_ref[pl.ds(at, half), :] + other_ref[pl.ds(at, half), :].astype(F32)).astype(BF16)


def deal_kernel(where_ref, own_ref, other_ref, keep_ref, *send_refs):
    rows = keep_ref.shape[0]
    for k, ref in enumerate((keep_ref,) + send_refs):
        at = pl.multiple_of(((where_ref[0] // 2) ^ k) * rows, 16)
        ref[...] = (own_ref[pl.ds(at, rows), :] + other_ref[pl.ds(at, rows), :].astype(F32)).astype(ref.dtype)


def unpack_kernel(where_ref, *refs, ways):
    mine, other = refs[:ways], refs[ways : 2 * ways]
    real_ref, imag_ref, up_ref, gate_ref, down_ref, total = refs[2 * ways :]
    place = where_ref[0]
    rows = mine[0].shape[0]
    for k in range(ways):
        at = ((place // 2) ^ k) * rows
        total[pl.ds(pl.multiple_of((place % 2) * ways * rows + at, 16), rows), :] = mine[k][...].astype(F32)
        total[pl.ds(pl.multiple_of((1 - place % 2) * ways * rows + at, 16), rows), :] = other[k][...].astype(F32)
    per_s = real_ref.shape[0]
    per_f = down_ref.shape[0]
    real_ref[...] = total[:per_s, :]
    imag_ref[...] = total[per_s : 2 * per_s, :]
    down_ref[...] = total[2 * per_s : 2 * per_s + per_f, :]
    last = 2 * per_s + per_f + up_ref.shape[0]
    up_ref[...] = total[2 * per_s + per_f : last, :per_f]
    gate_ref[...] = total[2 * per_s + per_f : last, per_f:]


def whole(shape):
    return pl.BlockSpec(shape, lambda *_: (0,) * len(shape))


def near(value):
    return pltpu.with_memory_space_constraint(value, pltpu.VMEM)


def far(value):
    return pltpu.with_memory_space_constraint(value, pltpu.HBM)


def call(kernel, grid, prefetch, in_specs, out_specs, out_shape, scratch, cost, vmem):
    return pl.pallas_call(
        kernel,
        grid_spec=pltpu.PrefetchScalarGridSpec(
            num_scalar_prefetch=prefetch,
            grid=grid,
            in_specs=in_specs,
            out_specs=out_specs,
            scratch_shapes=scratch,
        ),
        out_shape=out_shape,
        compiler_params=pltpu.CompilerParams(vmem_limit_bytes=vmem * MIB),
        cost_estimate=pl.CostEstimate(flops=1, bytes_accessed=int(cost * 3.3e6), transcendentals=0),
    )


def split_low(value):
    high = lax.reduce_precision(value, 8, 7)
    middle = lax.reduce_precision(value - high, 8, 7)
    return high, middle, value - high - middle


def core_swap(value):
    return lax.ppermute(value, "tensor", [(t, t ^ 1) for t in range(TENSOR)])


def side_swap(value):
    return lax.ppermute(value, "tensor", [(t, t ^ 2) for t in range(TENSOR)])


def gather_tensor(own, *first):
    across = after(side_swap(own), *first)
    return own, core_swap(own), across, core_swap(across)


def after(value, *first):
    return lax.optimization_barrier((value,) + first)[0]


def flip_dp(value, bits, groups):
    return lax.ppermute(value, "dp", [(i, i ^ bits) for i in range(groups)])


def shift_dp(value, by, groups):
    return lax.ppermute(value, "dp", [(i, i + by) for i in range(groups) if 0 <= i + by < groups])


def shards(
    tokens,
    cotangent,
    ln_gain,
    ln_bias,
    skip_gain,
    in_real,
    in_imag,
    out_real,
    out_imag,
    nu_log,
    theta_log,
    gamma_log,
    up_weight,
    gate_weight,
    down_weight,
    lengths,
    *,
    groups,
):
    seqs, length, width = tokens.shape
    per_s = in_real.shape[1]
    per_f = up_weight.shape[1]
    states = per_s * TENSOR
    own_seqs = seqs // 2
    rows = own_seqs * length
    blocks = rows // BLOCK
    place = lax.axis_index("dp").astype(jnp.int32)
    shard = lax.axis_index("tensor").astype(jnp.int32)
    core = shard % 2
    where = jnp.stack([place, core, shard])

    modulus = jnp.exp(-jnp.exp(nu_log))
    angle = jnp.exp(theta_log)
    gain = jnp.exp(gamma_log)
    parts = [split_low(v) for v in (modulus * jnp.cos(angle), modulus * jnp.sin(angle), gain)]
    table = jnp.stack([parts[v][k] for k in range(3) for v in range(3)])
    placed = jnp.where(
        lax.broadcasted_iota(jnp.int32, (9, width), 1) // per_s == shard, jnp.tile(table, (1, width // per_s)), 0.0
    )
    pack_a = jnp.concatenate(
        [in_real.T, in_imag.T, placed.astype(BF16), jnp.zeros((PARAM_ROWS - 9, width), BF16)], axis=0
    )
    pack_b = after(jnp.concatenate([out_real, out_imag, down_weight], axis=0), pack_a)
    pack_g = after(jnp.concatenate([up_weight, gate_weight], axis=1), pack_b)
    tok_rows = tokens.reshape(seqs * length, width)
    cot_rows = cotangent.reshape(seqs * length, width)
    row = lambda v: v.reshape(1, width)
    gain_row, bias_row, skip_row = row(ln_gain), row(ln_bias), row(skip_gain)
    half_spec = pl.BlockSpec((BLOCK, width), lambda b, w, *_: (w[1] * blocks + b, 0))
    row_spec = lambda lanes: pl.BlockSpec((BLOCK, lanes), lambda b, *_: (b, 0))
    a_spec = [whole(pack_a.shape)] * TENSOR
    b_spec = [whole(pack_b.shape)] * TENSOR
    any_spec = [pl.BlockSpec(memory_space=pl.ANY)] * TENSOR
    vec_spec = whole((1, width))
    shape = jax.ShapeDtypeStruct
    kept = pltpu.VMEM
    lanes = 2 * states
    units = TENSOR * per_f

    low, normed, inv, cot_m = call(
        functools.partial(norm_kernel, length=length, seqs=own_seqs),
        (blocks,),
        2,
        [half_spec, half_spec, vec_spec, vec_spec],
        [row_spec(width), row_spec(width), row_spec(128), row_spec(width)],
        [kept((rows, width), BF16), kept((rows, width), F32), kept((rows, 128), F32), kept((rows, width), BF16)],
        [],
        3,
        8,
    )(where, lengths, far(tok_rows), far(cot_rows), far(gain_row), far(bias_row))

    packs_a = gather_tensor(pack_a, low)
    near_a = tuple(map(near, packs_a))
    drive, ends, powers = call(
        functools.partial(drive_kernel, length=length),
        (blocks,),
        1,
        [row_spec(width)] + a_spec,
        [row_spec(lanes), whole((own_seqs, lanes)), whole((TILE, lanes))],
        [kept((rows, lanes), F32), shape((own_seqs, lanes), F32), shape((TILE, lanes), F32)],
        [
            pltpu.VMEM((lanes, width), BF16),
            pltpu.VMEM((2, length, states), F32),
            pltpu.VMEM((1, lanes), F32),
        ],
        4,
        8,
    )(where, near(low), *near_a)

    local = call(
        functools.partial(scan_kernel, length=length),
        (blocks,),
        0,
        [row_spec(lanes)] + a_spec,
        row_spec(lanes),
        kept((rows, lanes), F32),
        [pltpu.VMEM((4, 2, TILE, states), F32)],
        4,
        8,
    )(near(drive), *near_a)
    ways = groups // 2
    end_spec = whole((own_seqs, lanes))
    power_spec = whole((TILE, lanes))

    def exchange(mine, backwards, beside_work):
        beside = after(flip_dp(mine, 1, groups), beside_work)
        both = call(
            functools.partial(pair_kernel, backwards=backwards),
            (1,),
            1,
            [end_spec, end_spec, power_spec],
            end_spec,
            shape((own_seqs, lanes), F32),
            [],
            1,
            2,
        )(where, mine, beside, powers)
        return [shift_dp(both, (-2 if backwards else 2) * k, groups) for k in range(1, ways)], beside, both

    far_ends, beside_ends, pair_ends = exchange(ends, False, local)
    packs_b = gather_tensor(pack_b, beside_ends)
    near_b = tuple(map(near, packs_b))

    hid_grad = call(
        functools.partial(hidden_kernel, per_s=per_s),
        (blocks,),
        1,
        [row_spec(width)] + b_spec,
        row_spec(units),
        kept((rows, units), BF16),
        [],
        3,
        10,
    )(where, near(after(cot_m, pair_ends)), *near_b)

    packs_g = gather_tensor(pack_g, hid_grad, *far_ends)
    pack_rows = -(-(2 * per_s + per_f + width) // (16 * groups)) * 16 * groups
    state, back, back_ends, y_low, hid, own_b, sent_b = call(
        functools.partial(middle_kernel, length=length, ways=ways),
        (blocks,),
        1,
        [end_spec] * ways
        + [power_spec, row_spec(lanes), row_spec(width), row_spec(units), row_spec(width)]
        + a_spec
        + [vec_spec] * 3
        + any_spec
        + any_spec,
        [
            row_spec(lanes),
            row_spec(lanes),
            end_spec,
            row_spec(width),
            row_spec(units),
            whole((pack_rows, width)),
            whole((pack_rows, width)),
        ],
        [
            kept((rows, lanes), BF16),
            kept((rows, lanes), F32),
            shape((own_seqs, lanes), F32),
            kept((rows, width), BF16),
            kept((rows, units), BF16),
            shape((pack_rows, width), F32),
            shape((pack_rows, width), BF16),
        ],
        [
            pltpu.VMEM((lanes, width), BF16),
            pltpu.VMEM((width, 2 * units), BF16),
            pltpu.VMEM((4, 2, TILE, states), F32),
            pltpu.VMEM((2, length, states), F32),
            pltpu.VMEM((own_seqs, lanes), F32),
            pltpu.VMEM((BLOCK, width), BF16),
            pltpu.VMEM((BLOCK, 2 * units), BF16),
            pltpu.VMEM((BLOCK, lanes), F32),
            pltpu.VMEM((states, width), F32),
            pltpu.VMEM((2 * per_f, width), F32),
            pltpu.VMEM((width, 4 * per_f), F32),
            pltpu.SemaphoreType.DMA((TENSOR, 3)),
        ],
        21,
        20,
    )(
        where,
        *far_ends,
        beside_ends,
        powers,
        *map(near, (local, normed, hid_grad, cot_m)),
        *near_a,
        gain_row,
        bias_row,
        skip_row,
        *near_b,
        *packs_g,
    )

    half, part = pack_rows // 2, pack_rows // groups
    keep_b, send_b = call(
        fold_kernel,
        (1,),
        1,
        [whole((pack_rows, width))] * 2,
        [whole((half, width))] * 2,
        [shape((half, width), F32), shape((half, width), BF16)],
        [],
        2,
        8,
    )(where, own_b, core_swap(sent_b))
    out_own = call(
        functools.partial(down_kernel, length=length, per_s=per_s, seqs=own_seqs),
        (blocks,),
        2,
        [half_spec, row_spec(units)] + b_spec,
        row_spec(width),
        shape((rows, width), BF16),
        [pltpu.VMEM((units, width), BF16)],
        5,
        8,
    )(where, lengths, far(tok_rows), near(after(hid, send_b)), *near_b)
    far_back, beside_back, pair_back = exchange(back_ends, True, out_own)
    half_b = flip_dp(after(send_b, pair_back), 1, groups)

    dealt = call(
        deal_kernel,
        (1,),
        1,
        [whole((half, width))] * 2,
        [whole((part, width))] * ways,
        [shape((part, width), F32)] + [shape((part, width), BF16)] * (ways - 1),
        [],
        2,
        8,
    )(where, after(keep_b, *far_back), half_b)

    grad_own, own_a, sent_a = call(
        functools.partial(last_kernel, length=length, ways=ways),
        (blocks,),
        1,
        [end_spec] * ways
        + [
            power_spec,
            row_spec(width),
            row_spec(width),
            row_spec(128),
            row_spec(width),
            row_spec(lanes),
            row_spec(lanes),
            row_spec(width),
        ]
        + a_spec
        + [vec_spec] * 3,
        [row_spec(width), whole(pack_a.shape), whole(pack_a.shape)],
        [shape((rows, width), BF16), shape(pack_a.shape, BF16), shape(pack_a.shape, BF16)],
        [
            pltpu.VMEM((lanes, width), BF16),
            pltpu.VMEM((2, length, states), F32),
            pltpu.VMEM((own_seqs, lanes), F32),
            pltpu.VMEM((1, lanes), F32),
            pltpu.VMEM((BLOCK, lanes), BF16),
            pltpu.VMEM((states, width), F32),
            pltpu.VMEM((1, lanes), F32),
            pltpu.VMEM((TILE, width), F32),
        ],
        8,
        14,
    )(
        where,
        *far_back,
        after(beside_back, dealt[0]),
        powers,
        *map(near, (low, normed, inv, cot_m, back, state, y_low)),
        *near_a,
        gain_row,
        bias_row,
        skip_row,
    )

    mine_b = dealt[0]
    for k in range(1, ways):
        mine_b = mine_b + flip_dp(dealt[k], 2 * k, groups).astype(F32)
    mine_b = mine_b.astype(BF16)

    grads_a = own_a.astype(F32) + core_swap(after(sent_a, mine_b)).astype(F32)
    bit = 1
    while bit < groups:
        low_a = grads_a.astype(BF16)
        grads_a = low_a.astype(F32) + flip_dp(low_a, bit, groups).astype(F32)
        bit *= 2

    gathered = [mine_b] + [flip_dp(mine_b, 2 * k, groups) for k in range(1, ways)]
    beside = [flip_dp(piece, 1, groups) for piece in gathered]

    out_other = core_swap(out_own)
    grad_other = core_swap(after(grad_own, mine_b))

    def in_order(mine, other):
        first = core == 0
        return jnp.concatenate([jnp.where(first, mine, other), jnp.where(first, other, mine)], axis=0).reshape(
            seqs, length, width
        )

    block_out = in_order(out_own, out_other)
    input_grad = in_order(grad_own, grad_other).astype(F32)
    beside[-1] = after(beside[-1], block_out, input_grad)

    out_real_grad, out_imag_grad, up_grad, gate_grad, down_grad = call(
        functools.partial(unpack_kernel, ways=ways),
        (1,),
        1,
        [whole((part, width))] * groups,
        [whole((per_s, width))] * 2 + [whole((width, per_f))] * 2 + [whole((per_f, width))],
        [shape((per_s, width), F32)] * 2 + [shape((width, per_f), F32)] * 2 + [shape((per_f, width), F32)],
        [pltpu.VMEM((pack_rows, width), F32)],
        2,
        8,
    )(where, *gathered, *beside)

    in_real_grad = grads_a[:per_s].T
    in_imag_grad = grads_a[per_s : 2 * per_s].T
    small = grads_a[2 * per_s :]
    lam_real = lax.dynamic_slice_in_dim(small[3, :states], shard * per_s, per_s)
    lam_imag = lax.dynamic_slice_in_dim(small[3, states:], shard * per_s, per_s)
    cos, sin = jnp.cos(angle), jnp.sin(angle)
    nu_grad = -jnp.exp(nu_log) * modulus * (lam_real * cos + lam_imag * sin)
    theta_grad = angle * modulus * (lam_imag * cos - lam_real * sin)
    gamma_grad = jnp.sum(in_real.astype(F32) * in_real_grad + in_imag.astype(F32) * in_imag_grad, axis=0)
    return (
        block_out,
        input_grad,
        small[0],
        small[1],
        small[2],
        in_real_grad,
        in_imag_grad,
        out_real_grad,
        out_imag_grad,
        nu_grad,
        theta_grad,
        gamma_grad,
        up_grad,
        gate_grad,
        down_grad,
    )


def solution(mesh):
    rows = P(None, "dp", None)
    columns = P(None, "tensor")
    lines = P("tensor", None)
    vector = P("tensor")
    in_specs = (rows, rows, P(), P(), P(), columns, columns, lines, lines, vector, vector, vector, columns, columns, lines, P())
    out_specs = (rows, rows, P(), P(), P(), columns, columns, lines, lines, vector, vector, vector, columns, columns, lines)
    return jax.shard_map(
        functools.partial(shards, groups=mesh.shape["dp"]),
        mesh=mesh,
        in_specs=in_specs,
        out_specs=out_specs,
        check_vma=False,
    )
```

time: 186 us -> 137 us (0.74)
  waiting for transfers between devices: 70 us -> 30.8 us
  starting transfers between devices: 24.5 us -> 42.2 us
  blocking collectives: 15.2 us -> 0 us
  local copies, waits for them, and re-layouts: 8.27 us -> 1.71 us
  Pallas kernels: 50.5 us -> 47.8 us
  other arithmetic: 15.7 us -> 13.1 us
    ppermute x3 -> x22, starting transfers between devices: 6.82 us -> 34.9 us  [the longest x16 21.8 us: flip_dp(): return lax.ppermute(value, 'dp', [(i, i ^ bits) for i in range(groups)])]
    ppermute x2 -> x3, waiting for transfers between devices: 24.3 us -> 0.01 us  [side_swap(): return lax.ppermute(value, 'tensor', [(t, t ^ 2) for t in range(TENSOR)])]
    all_to_all x1 -> x0, blocking collectives: 15.2 us -> none  [share_over_dp(): lax.all_to_all(jnp.broadcast_to(value[None], (groups,) + value.shape), 'd...]
    all_to_all x3 -> x0, waiting for transfers between devices: 13.7 us -> none  [the longest x2 13.7 us: share_over_dp(): lax.all_to_all(jnp.broadcast_to(value[None], (groups,) + value.shape), 'd...]
    all_to_all x3 -> x0, starting transfers between devices: 11.8 us -> none  [the longest x2 7.13 us: share_over_dp(): lax.all_to_all(jnp.broadcast_to(value[None], (groups,) + value.shape), 'd...]
    broadcast_in_dim x3 -> x0, local copies, waits for them, and re-layouts: 3.31 us -> none  [share_over_dp(): jnp.broadcast_to(value[None], (groups,) + value.shape)]
    ppermute x3 -> x22, waiting for transfers between devices: 30 us -> 26.9 us  [the longest x16 22.2 us: flip_dp(): return lax.ppermute(value, 'dp', [(i, i ^ bits) for i in range(groups)])]
    pallas_call x4 -> x12, Pallas kernels: 50.5 us -> 47.8 us  [the longest x1 18.7 us: shards(): call(functools.partial(middle_kernel, length=length, ways=ways), (blocks,...]
  transfers between devices with their start and end apart: 16 -> 35, of which waited for: 7 -> 13; matrix products, arithmetic and copies ran while one was open for 9% -> 8% of each run, Pallas kernels for 15% -> 19%
where the time goes in v2:
time: 137 us
  Pallas kernels  47.8 us (35%)
  starting transfers between devices  42.2 us (31%)
  waiting for transfers between devices  30.8 us (22%)
  other arithmetic  13.1 us (10%)
  local copies, waits for them, and re-layouts  1.71 us (1%)
    ppermute x16, waiting for transfers between devices, flip_dp(): return lax.ppermute(value, 'dp', [(i, i ^ bits) for i in range(groups)])  22.2 us
    ppermute x16, starting transfers between devices, flip_dp(): return lax.ppermute(value, 'dp', [(i, i ^ bits) for i in range(groups)])  21.8 us
    pallas_call x1, Pallas kernels, shards(): call(functools.partial(middle_kernel, length=length, ways=ways), (blocks,...  18.7 us
    ppermute x6, starting transfers between devices, shift_dp(): lax.ppermute(value, 'dp', [(i, i + by) for i in range(groups) if 0 <= i +...  13.1 us
    pallas_call x1, Pallas kernels, shards(): call(functools.partial(last_kernel, length=length, ways=ways), (blocks,),...  5.83 us
    pallas_call x1, Pallas kernels, shards(): call(functools.partial(down_kernel, length=length, per_s=per_s, seqs=own_...  5.33 us
    ppermute x3, starting transfers between devices, side_swap(): return lax.ppermute(value, 'tensor', [(t, t ^ 2) for t in range(TENSOR)])  5.13 us
    pallas_call x1, Pallas kernels, shards(): call(functools.partial(norm_kernel, length=length, seqs=own_seqs), (block...  4.97 us
  transfers between devices with their start and end apart: 35, of which 13 were waited for; matrix products, arithmetic and copies ran while one was open for 8% of the time, Pallas kernels for 19%

profile of v2, /device:TPU:0, one launch (start us, length us, event | category | flops | bytes accessed | tf_op | source)
XLA Modules:
  0.0 136.7 jit_solution(11821795720915944315)
XLA Ops:
  1.3 0.7 fusion.4
  2.3 1.0 maximum_maximum_fusion.a0.refs_9_.refs_12_
  3.3 3.0 %collective-permute-start.1 = (bf16[144,512]{1,0:T(8,128)(2,1)S(1)}, bf16[144,512]{1,0:T(8,128)(2,1)S(1)}, u32[]{:S(2)}, u32[]{:S(2)}) collective-permute-start(bf16[144,512]{1,0:T(8,128)(2,1)S(1)} %maximum_maximum_fusion.a0.refs_9_.refs_12_), channel_id=1, source_target_pairs={{0,2},{1,3},{2,0},{3,1},{4,6},{5,7},{6,4},{7,5},{8,10},{9,11},{10,... | collective-permute-start | bytes 442376 | tf_op jit(solution)/shard_map/ppermute | solution.py:478
  6.3 1.0 pad_maximum_fusion.3.b0.refs_16_
  8.2 5.0 %shard_map.271 = (bf16[1536,512]{1,0:T(8,128)(2,1)S(1)}, f32[1536,512]{1,0:T(8,128)S(1)}, f32[1536,128]{1,0:T(8,128)S(1)}, bf16[1536,512]{1,0:T(8,128)(2,1)S(1)}) custom-call(s32[3]{0:T(128)S(1)} %pad_add_fusion.where_ref, s32[24]{0:T(128)S(1)} %copy-done.5, bf16[3072,512]{1,0:T(8,128)(2,1)} %bitcast.66, bf16[3072,512]{1,0:T(8,128)(2,1)} %bitcast.69, ...), custom_call_target="tpu_custom_call" | custom-call | flops 1 | bytes 9900000 | tf_op jit(solution)/shard_map/pallas_call | solution.py:558
  13.8 2.0 %collective-permute-start.11 = (bf16[512,512]{1,0:T(8,128)(2,1)S(1)}, bf16[512,512]{1,0:T(8,128)(2,1)S(1)}, u32[]{:S(2)}, u32[]{:S(2)}) collective-permute-start(bf16[512,512]{1,0:T(8,128)(2,1)S(1)} %pad_maximum_fusion.2.refs_20_), channel_id=1, source_target_pairs={{0,2},{1,3},{2,0},{3,1},{4,6},{5,7},{6,4},{7,5},{8,10},{9,11},{10,... | collective-permute-start | bytes 1572872 | tf_op jit(solution)/shard_map/ppermute | solution.py:478
  15.8 3.0 %shard_map.272 = (f32[1536,512]{1,0:T(8,128)S(1)}, f32[12,512]{1,0:T(8,128)S(1)}, f32[8,512]{1,0:T(8,128)S(1)}) custom-call(s32[3]{0:T(128)S(1)} %pad_add_fusion.where_ref, bf16[1536,512]{1,0:T(8,128)(2,1)S(1)} %get-tuple-element.58.low_ref.refs_5_, bf16[144,512]{1,0:T(8,128)(2,1)S(1)} %maximum_maximum_fusion.a0.refs_9_.refs_12_, ...), custom_call_target="tpu_custom_call" | custom-call | flops 1 | bytes 13200000 | tf_op jit(solution)/shard_map/pallas_call | solution.py:572
  18.8 1.6 %collective-permute-start.3 = (f32[12,512]{1,0:T(8,128)S(1)}, f32[12,512]{1,0:T(8,128)S(1)}, u32[]{:S(2)}, u32[]{:S(2)}) collective-permute-start(f32[12,512]{1,0:T(8,128)S(1)} %get-tuple-element.60.mine_ref), channel_id=1, source_target_pairs={{0,4},{4,0},{8,12},{12,8},{16,20},{20,16},{24,28},{28,24},{1,5},{5... | collective-permute-start | bytes 73736 | tf_op jit(solution)/shard_map/ppermute | solution.py:491
  20.4 2.1 %shard_map.273.refs_5_ = f32[1536,512]{1,0:T(8,128)S(1)} custom-call(f32[1536,512]{1,0:T(8,128)S(1)} %get-tuple-element.61.drive_ref, bf16[144,512]{1,0:T(8,128)(2,1)S(1)} %maximum_maximum_fusion.a0.refs_9_.refs_12_, bf16[144,512]{1,0:T(8,128)(2,1)S(1)} %collective-permute-done.a1.refs_10_.refs_13_, ...), custom_call_target="tpu_custom_call" | custom-call | flops 1 | bytes 13200000 | tf_op jit(solution)/shard_map/pallas_call | solution.py:588
  23.7 5.5 %collective-permute-start.6 = (f32[12,512]{1,0:T(8,128)S(1)}, f32[12,512]{1,0:T(8,128)S(1)}, u32[]{:S(2)}, u32[]{:S(2)}) collective-permute-start(f32[12,512]{1,0:T(8,128)S(1)} %shard_map.274), channel_id=1, source_target_pairs={{0,24},{4,28},{1,25},{5,29},{2,26},{6,30},{3,27},{7,31}} | collective-permute-start | bytes 73736 | tf_op jit(solution)/shard_map/ppermute | solution.py:495
  29.2 1.3 collective-permute-start.5
  30.5 2.5 %collective-permute-start.4 = (f32[12,512]{1,0:T(8,128)S(1)}, f32[12,512]{1,0:T(8,128)S(1)}, u32[]{:S(2)}, u32[]{:S(2)}) collective-permute-start(f32[12,512]{1,0:T(8,128)S(1)} %shard_map.274), channel_id=1, source_target_pairs={{0,8},{4,12},{8,16},{12,20},{16,24},{20,28},{1,9},{5,13},{9,17},{1... | collective-permute-start | bytes 73736 | tf_op jit(solution)/shard_map/ppermute | solution.py:495
  33.1 3.5 %shard_map.275.refs_7_ = bf16[1536,1024]{1,0:T(8,128)(2,1)S(1)} custom-call(s32[3]{0:T(128)S(1)} %pad_add_fusion.where_ref, bf16[1536,512]{1,0:T(8,128)(2,1)S(1)} %get-tuple-element.66.cotm_ref.refs_8_, bf16[384,512]{1,0:T(8,128)(2,1)S(1)} %pad_maximum_fusion.3.b0.refs_16_, bf16[384,512]{1,0:T(8,128)(2,1)S(1)} %collective-permute-done.7.b1.refs_17_, ...), custom_call_target="tpu_custom_call" | custom-call | flops 1 | bytes 9900000 | tf_op jit(solution)/shard_map/pallas_call | solution.py:622
  37.3 1.5 %collective-permute-done.12.refs_23_ = bf16[512,512]{1,0:T(8,128)(2,1)S(1)} collective-permute-done((bf16[512,512]{1,0:T(8,128)(2,1)S(1)}, bf16[512,512]{1,0:T(8,128)(2,1)S(1)}, u32[]{:S(2)}, u32[]{:S(2)}) %collective-permute-start.12) | collective-permute-done | bytes 524320 | tf_op jit(solution)/shard_map/ppermute | solution.py:474
  38.8 18.7 %shard_map.276 = (bf16[1536,512]{1,0:T(8,128)(2,1)S(1)}, f32[1536,512]{1,0:T(8,128)S(1)}, f32[12,512]{1,0:T(8,128)S(1)}, bf16[1536,512]{1,0:T(8,128)(2,1)S(1)}, ...) custom-call(s32[3]{0:T(128)S(1)} %pad_add_fusion.where_ref, ...), custom_call_target="tpu_custom_call" | custom-call | flops 1 | bytes 69300000 | tf_op jit(solution)/shard_map/pallas_call | solution.py:636
  58.0 1.2 collective-permute-start.15
  59.1 0.9 collective-permute-done.13.other_ref
  60.0 0.7 shard_map.277
  60.8 5.3 %shard_map.278 = bf16[1536,512]{1,0:T(8,128)(2,1)S(1)} custom-call(s32[3]{0:T(128)S(1)} %pad_add_fusion.where_ref, s32[24]{0:T(128)S(1)} %copy-done.6, bf16[3072,512]{1,0:T(8,128)(2,1)} %bitcast.67, bf16[1536,1024]{1,0:T(8,128)(2,1)S(1)} %get-tuple-element.75.hid_ref, bf16[384,512]{1,0:T(8,128)(2,1)S(1)} %pad_maximum_fusion.3.b0.refs_16_, ...), custom_call_target="tpu_custom_call" | custom-call | flops 1 | bytes 16500000 | tf_op jit(solution)/shard_map/pallas_call | solution.py:706
  66.7 1.3 collective-permute-start.19
  67.9 1.3 collective-permute-start.18
  69.2 1.3 collective-permute-start.17
  70.5 1.3 collective-permute-start.16
  71.8 3.8 %collective-permute-done.18.refs_2_ = f32[12,512]{1,0:T(8,128)S(1)} collective-permute-done((f32[12,512]{1,0:T(8,128)S(1)}, f32[12,512]{1,0:T(8,128)S(1)}, u32[]{:S(2)}, u32[]{:S(2)}) %collective-permute-start.18) | collective-permute-done | bytes 24608 | tf_op jit(solution)/shard_map/ppermute | solution.py:495
  75.6 0.7 collective-permute-done.17.refs_1_
  76.6 3.0 %collective-permute-done.19.other_ref = bf16[448,512]{1,0:T(8,128)(2,1)S(1)} collective-permute-done((bf16[448,512]{1,0:T(8,128)(2,1)S(1)}, bf16[448,512]{1,0:T(8,128)(2,1)S(1)}, u32[]{:S(2)}, u32[]{:S(2)}) %collective-permute-start.19) | collective-permute-done | bytes 458784 | tf_op jit(solution)/shard_map/ppermute | solution.py:491
  80.7 4.0 %collective-permute-start.22 = (bf16[112,512]{1,0:T(8,128)(2,1)S(1)}, bf16[112,512]{1,0:T(8,128)(2,1)S(1)}, u32[]{:S(2)}, u32[]{:S(2)}) collective-permute-start(bf16[112,512]{1,0:T(8,128)(2,1)S(1)} %get-tuple-element.90), channel_id=1, source_target_pairs={{0,24},{4,28},{8,16},{12,20},{16,8},{20,12},{24,0},{28,4},{1,25},{... | collective-permute-start | bytes 344072 | tf_op jit(solution)/shard_map/ppermute | solution.py:491
  84.6 5.8 %shard_map.281 = (bf16[1536,512]{1,0:T(8,128)(2,1)S(1)}, bf16[144,512]{1,0:T(8,128)(2,1)S(1)}, bf16[144,512]{1,0:T(8,128)(2,1)S(1)}) custom-call(s32[3]{0:T(128)S(1)} %pad_add_fusion.where_ref, f32[12,512]{1,0:T(8,128)S(1)} %collective-permute-done.16.refs_0_, f32[12,512]{1,0:T(8,128)S(1)} %collective-permute-done.17.refs_1_, ...), custom_call_target="tpu_custom_call" | custom-call | flops 1 | bytes 26400000 | tf_op jit(solution)/shard_map/pallas_call | solution.py:732
  90.5 1.5 %collective-permute-done.21 = bf16[112,512]{1,0:T(8,128)(2,1)S(1)} collective-permute-done((bf16[112,512]{1,0:T(8,128)(2,1)S(1)}, bf16[112,512]{1,0:T(8,128)(2,1)S(1)}, u32[]{:S(2)}, u32[]{:S(2)}) %collective-permute-start.21) | collective-permute-done | bytes 114720 | tf_op jit(solution)/shard_map/ppermute | solution.py:491
  92.2 1.4 collective-permute-done.24
  93.6 1.2 collective-permute-start.25
  94.8 4.7 %collective-permute-done.25 = bf16[144,512]{1,0:T(8,128)(2,1)S(1)} collective-permute-done((bf16[144,512]{1,0:T(8,128)(2,1)S(1)}, bf16[144,512]{1,0:T(8,128)(2,1)S(1)}, u32[]{:S(2)}, u32[]{:S(2)}) %collective-permute-start.25) | collective-permute-done | bytes 147488 | tf_op jit(solution)/shard_map/ppermute | solution.py:491
  99.6 1.9 %collective-permute-start.26 = (bf16[144,512]{1,0:T(8,128)(2,1)S(1)}, bf16[144,512]{1,0:T(8,128)(2,1)S(1)}, u32[]{:S(2)}, u32[]{:S(2)}) collective-permute-start(bf16[144,512]{1,0:T(8,128)(2,1)S(1)} %add_convert_fusion.1), channel_id=1, source_target_pairs={{0,8},{4,12},{8,0},{12,4},{16,24},{20,28},{24,16},{28,20},{1,9},{5... | collective-permute-start | bytes 442376 | tf_op jit(solution)/shard_map/ppermute | solution.py:491
  101.4 3.4 %collective-permute-done.26 = bf16[144,512]{1,0:T(8,128)(2,1)S(1)} collective-permute-done((bf16[144,512]{1,0:T(8,128)(2,1)S(1)}, bf16[144,512]{1,0:T(8,128)(2,1)S(1)}, u32[]{:S(2)}, u32[]{:S(2)}) %collective-permute-start.26) | collective-permute-done | bytes 147488 | tf_op jit(solution)/shard_map/ppermute | solution.py:491
  104.8 1.7 %collective-permute-start.27 = (bf16[144,512]{1,0:T(8,128)(2,1)S(1)}, bf16[144,512]{1,0:T(8,128)(2,1)S(1)}, u32[]{:S(2)}, u32[]{:S(2)}) collective-permute-start(bf16[144,512]{1,0:T(8,128)(2,1)S(1)} %add_convert_fusion), channel_id=1, source_target_pairs={{0,16},{4,20},{8,24},{12,28},{16,0},{20,4},{24,8},{28,12},{1,17},{... | collective-permute-start | bytes 442376 | tf_op jit(solution)/shard_map/ppermute | solution.py:491
  106.6 2.5 %collective-permute-start.30 = (bf16[112,512]{1,0:T(8,128)(2,1)S(1)}, bf16[112,512]{1,0:T(8,128)(2,1)S(1)}, u32[]{:S(2)}, u32[]{:S(2)}) collective-permute-start(bf16[112,512]{1,0:T(8,128)(2,1)S(1)} %add_convert_fusion.3.refs_0_), channel_id=1, source_target_pairs={{0,24},{4,28},{8,16},{12,20},{16,8},{20,12},{24,0},{28,4},{1,25},{... | collective-permute-start | bytes 344072 | tf_op jit(solution)/shard_map/ppermute | solution.py:491
  109.0 1.9 %collective-permute-start.28 = (bf16[112,512]{1,0:T(8,128)(2,1)S(1)}, bf16[112,512]{1,0:T(8,128)(2,1)S(1)}, u32[]{:S(2)}, u32[]{:S(2)}) collective-permute-start(bf16[112,512]{1,0:T(8,128)(2,1)S(1)} %add_convert_fusion.3.refs_0_), channel_id=1, source_target_pairs={{0,8},{4,12},{8,0},{12,4},{16,24},{20,28},{24,16},{28,20},{1,9},{5... | collective-permute-start | bytes 344072 | tf_op jit(solution)/shard_map/ppermute | solution.py:491
  110.9 8.3 %collective-permute-done.27 = bf16[144,512]{1,0:T(8,128)(2,1)S(1)} collective-permute-done((bf16[144,512]{1,0:T(8,128)(2,1)S(1)}, bf16[144,512]{1,0:T(8,128)(2,1)S(1)}, u32[]{:S(2)}, u32[]{:S(2)}) %collective-permute-start.27) | collective-permute-done | bytes 147488 | tf_op jit(solution)/shard_map/ppermute | solution.py:491
  119.9 1.3 add_reduce_fusion
  121.8 1.2 collective-permute-start.31
  123.0 1.0 collective-permute-start.34
  124.0 1.1 collective-permute-start.33
  125.0 1.0 collective-permute-start.32
  126.0 1.6 %broadcast_select_fusion.3 = (bf16[1536,512]{1,0:T(8,128)(2,1)S(1)}, bf16[1536,512]{1,0:T(8,128)(2,1)S(1)}) fusion(bf16[1536,512]{1,0:T(8,128)(2,1)S(1)} %shard_map.278, bf16[1536,512]{1,0:T(8,128)(2,1)} %collective-permute-done.14, pred[]{:T(512)S(6)} %eq.12), kind=kLoop, calls=%fused_computation.5 | loop fusion | flops 1572864 | bytes 6291457 | tf_op jit(solution)/shard_map/jit(_where)/select_n | solution.py:795
  127.6 1.9 %pad_maximum_fusion = bf16[3072,512]{1,0:T(8,128)(2,1)} fusion(bf16[1536,512]{1,0:T(8,128)(2,1)S(1)} %get-tuple-element.111, bf16[1536,512]{1,0:T(8,128)(2,1)S(1)} %get-tuple-element.110), kind=kLoop, calls=%fused_computation | loop fusion | flops 6291456 | bytes 6291456 | tf_op jit(solution)/shard_map/concatenate | solution.py:795
  130.1 3.6 %convert.1 = f32[24,128,512]{2,1,0:T(8,128)} convert(bf16[24,128,512]{2,1,0:T(8,128)(2,1)S(1)} %bitcast.68) | non-fusion elementwise | flops 1572864 | bytes 9437184 | tf_op jit(solution)/shard_map/convert_element_type | solution.py:800
  133.7 1.1 collective-permute-done.32.refs_5_
  134.8 1.9 %shard_map.282 = (f32[64,512]{1,0:T(8,128)}, f32[64,512]{1,0:T(8,128)}, f32[512,256]{1,0:T(8,128)}, f32[512,256]{1,0:T(8,128)}, f32[256,512]{1,0:T(8,128)}) custom-call(s32[3]{0:T(128)S(1)} %pad_add_fusion.where_ref, bf16[112,512]{1,0:T(8,128)(2,1)S(1)} %add_convert_fusion.3.refs_0_, bf16[112,512]{1,0:T(8,128)(2,1)S(1)} %collective-permute-done.28.refs_1_, ...), custom_call_target="tpu_custom_call" | custom-call | flops 1 | bytes 6600000 | tf_op jit(solution)/shard_map/pallas_call | solution.py:803
  (89 shorter events, 8.7 us)
Async XLA Ops:
  3.3 9.9 %collective-permute-start.1 = (bf16[144,512]{1,0:T(8,128)(2,1)S(1)}, bf16[144,512]{1,0:T(8,128)(2,1)S(1)}, u32[]{:S(2)}, u32[]{:S(2)}) collective-permute-start(bf16[144,512]{1,0:T(8,128)(2,1)S(1)} %maximum_maximum_fusion.a0.refs_9_.refs_12_), channel_id=1, source_target_pairs={{0,2},{1,3},{2,0},{3,1},{4,6},{5,7},{6,4},{7,5},{8,10},{9,11},{10,... | collective-permute-start | bytes 442376 | tf_op jit(solution)/shard_map/ppermute | solution.py:478
  7.3 15.5 %collective-permute-start.8 = (bf16[384,512]{1,0:T(8,128)(2,1)S(1)}, bf16[384,512]{1,0:T(8,128)(2,1)S(1)}, u32[]{:S(2)}, u32[]{:S(2)}) collective-permute-start(bf16[384,512]{1,0:T(8,128)(2,1)S(1)} %pad_maximum_fusion.3.b0.refs_16_), channel_id=1, source_target_pairs={{0,2},{1,3},{2,0},{3,1},{4,6},{5,7},{6,4},{7,5},{8,10},{9,11},{10,... | collective-permute-start | bytes 1179656 | tf_op jit(solution)/shard_map/ppermute | solution.py:478
  7.4 8.4 %collective-permute-start = (bf16[144,512]{1,0:T(8,128)(2,1)S(1)}, bf16[144,512]{1,0:T(8,128)(2,1)S(1)}, u32[]{:S(2)}, u32[]{:S(2)}) collective-permute-start(bf16[144,512]{1,0:T(8,128)(2,1)S(1)} %maximum_maximum_fusion.a0.refs_9_.refs_12_), channel_id=1, source_target_pairs={{0,1},{1,0},{2,3},{3,2},{4,5},{5,4},{6,7},{7,6},{8,9},{9,8},{10,11... | collective-permute-start | bytes 442376 | tf_op jit(solution)/shard_map/ppermute | solution.py:474
  7.6 0.7 copy-start.5
  8.2 5.5 %copy-start.9 = (bf16[512,256]{1,0:T(8,128)(2,1)S(1)}, bf16[512,256]{1,0:T(8,128)(2,1)}, u32[]{:S(2)}) copy-start(bf16[512,256]{1,0:T(8,128)(2,1)} %param.29) | copy-start | bytes 786436
  8.2 5.5 %copy-start.10 = (bf16[512,256]{1,0:T(8,128)(2,1)S(1)}, bf16[512,256]{1,0:T(8,128)(2,1)}, u32[]{:S(2)}) copy-start(bf16[512,256]{1,0:T(8,128)(2,1)} %param.28) | copy-start | bytes 786436
  13.2 2.6 %collective-permute-start.2 = (bf16[144,512]{1,0:T(8,128)(2,1)S(1)}, bf16[144,512]{1,0:T(8,128)(2,1)S(1)}, u32[]{:S(2)}, u32[]{:S(2)}) collective-permute-start(bf16[144,512]{1,0:T(8,128)(2,1)S(1)} %collective-permute-done.1.a2.refs_11_.refs_14_), channel_id=1, source_target_pairs={{0,1},{1,0},{2,3},{3,2},{4,5},{5,4},{6,7},{7,6},{8,9},{9,8},{10,11... | collective-permute-start | bytes 442376 | tf_op jit(solution)/shard_map/ppermute | solution.py:474
  13.8 22.9 %collective-permute-start.11 = (bf16[512,512]{1,0:T(8,128)(2,1)S(1)}, bf16[512,512]{1,0:T(8,128)(2,1)S(1)}, u32[]{:S(2)}, u32[]{:S(2)}) collective-permute-start(bf16[512,512]{1,0:T(8,128)(2,1)S(1)} %pad_maximum_fusion.2.refs_20_), channel_id=1, source_target_pairs={{0,2},{1,3},{2,0},{3,1},{4,6},{5,7},{6,4},{7,5},{8,10},{9,11},{10,... | collective-permute-start | bytes 1572872 | tf_op jit(solution)/shard_map/ppermute | solution.py:478
  18.8 4.0 %collective-permute-start.3 = (f32[12,512]{1,0:T(8,128)S(1)}, f32[12,512]{1,0:T(8,128)S(1)}, u32[]{:S(2)}, u32[]{:S(2)}) collective-permute-start(f32[12,512]{1,0:T(8,128)S(1)} %get-tuple-element.60.mine_ref), channel_id=1, source_target_pairs={{0,4},{4,0},{8,12},{12,8},{16,20},{20,16},{24,28},{28,24},{1,5},{5... | collective-permute-start | bytes 73736 | tf_op jit(solution)/shard_map/ppermute | solution.py:491
  20.4 10.1 %collective-permute-start.7 = (bf16[384,512]{1,0:T(8,128)(2,1)S(1)}, bf16[384,512]{1,0:T(8,128)(2,1)S(1)}, u32[]{:S(2)}, u32[]{:S(2)}) collective-permute-start(bf16[384,512]{1,0:T(8,128)(2,1)S(1)} %pad_maximum_fusion.3.b0.refs_16_), channel_id=1, source_target_pairs={{0,1},{1,0},{2,3},{3,2},{4,5},{5,4},{6,7},{7,6},{8,9},{9,8},{10,11... | collective-permute-start | bytes 1179656 | tf_op jit(solution)/shard_map/ppermute | solution.py:474
  22.8 10.2 %collective-permute-start.9 = (bf16[384,512]{1,0:T(8,128)(2,1)S(1)}, bf16[384,512]{1,0:T(8,128)(2,1)S(1)}, u32[]{:S(2)}, u32[]{:S(2)}) collective-permute-start(bf16[384,512]{1,0:T(8,128)(2,1)S(1)} %collective-permute-done.8.b2.refs_18_), channel_id=1, source_target_pairs={{0,1},{1,0},{2,3},{3,2},{4,5},{5,4},{6,7},{7,6},{8,9},{9,8},{10,11... | collective-permute-start | bytes 1179656 | tf_op jit(solution)/shard_map/ppermute | solution.py:474
  23.7 13.0 %collective-permute-start.6 = (f32[12,512]{1,0:T(8,128)S(1)}, f32[12,512]{1,0:T(8,128)S(1)}, u32[]{:S(2)}, u32[]{:S(2)}) collective-permute-start(f32[12,512]{1,0:T(8,128)S(1)} %shard_map.274), channel_id=1, source_target_pairs={{0,24},{4,28},{1,25},{5,29},{2,26},{6,30},{3,27},{7,31}} | collective-permute-start | bytes 73736 | tf_op jit(solution)/shard_map/ppermute | solution.py:495
  29.2 7.5 %collective-permute-start.5 = (f32[12,512]{1,0:T(8,128)S(1)}, f32[12,512]{1,0:T(8,128)S(1)}, u32[]{:S(2)}, u32[]{:S(2)}) collective-permute-start(f32[12,512]{1,0:T(8,128)S(1)} %shard_map.274), channel_id=1, source_target_pairs={{0,16},{4,20},{8,24},{12,28},{1,17},{5,21},{9,25},{13,29},{2,18},{... | collective-permute-start | bytes 73736 | tf_op jit(solution)/shard_map/ppermute | solution.py:495
  30.5 6.2 %collective-permute-start.4 = (f32[12,512]{1,0:T(8,128)S(1)}, f32[12,512]{1,0:T(8,128)S(1)}, u32[]{:S(2)}, u32[]{:S(2)}) collective-permute-start(f32[12,512]{1,0:T(8,128)S(1)} %shard_map.274), channel_id=1, source_target_pairs={{0,8},{4,12},{8,16},{12,20},{16,24},{20,28},{1,9},{5,13},{9,17},{1... | collective-permute-start | bytes 73736 | tf_op jit(solution)/shard_map/ppermute | solution.py:495
  33.0 5.8 %copy-start.2 = (f32[512]{0:T(512)S(1)}, f32[512]{0:T(512)}, u32[]{:S(2)}) copy-start(f32[512]{0:T(512)} %param.18) | copy-start | bytes 6148
  33.0 5.8 %copy-start.3 = (f32[512]{0:T(512)S(1)}, f32[512]{0:T(512)}, u32[]{:S(2)}) copy-start(f32[512]{0:T(512)} %param.19) | copy-start | bytes 6148
  33.0 5.8 %copy-start.4 = (f32[512]{0:T(512)S(1)}, f32[512]{0:T(512)}, u32[]{:S(2)}) copy-start(f32[512]{0:T(512)} %param.20) | copy-start | bytes 6148
  33.0 4.2 %collective-permute-start.10 = (bf16[512,512]{1,0:T(8,128)(2,1)S(1)}, bf16[512,512]{1,0:T(8,128)(2,1)S(1)}, u32[]{:S(2)}, u32[]{:S(2)}) collective-permute-start(bf16[512,512]{1,0:T(8,128)(2,1)S(1)} %pad_maximum_fusion.2.refs_20_), channel_id=1, source_target_pairs={{0,1},{1,0},{2,3},{3,2},{4,5},{5,4},{6,7},{7,6},{8,9},{9,8},{10,11... | collective-permute-start | bytes 1572872 | tf_op jit(solution)/shard_map/ppermute | solution.py:474
  36.7 2.1 %collective-permute-start.12 = (bf16[512,512]{1,0:T(8,128)(2,1)S(1)}, bf16[512,512]{1,0:T(8,128)(2,1)S(1)}, u32[]{:S(2)}, u32[]{:S(2)}) collective-permute-start(bf16[512,512]{1,0:T(8,128)(2,1)S(1)} %collective-permute-done.11.refs_22_), channel_id=1, source_target_pairs={{0,1},{1,0},{2,3},{3,2},{4,5},{5,4},{6,7},{7,6},{8,9},{9,8},{10,11... | collective-permute-start | bytes 1572872 | tf_op jit(solution)/shard_map/ppermute | solution.py:474
  57.5 3.3 %copy-start.6 = (s32[24]{0:T(128)S(1)}, s32[24]{0:T(128)}, u32[]{:S(2)}) copy-start(s32[24]{0:T(128)} %lens_ref.3) | copy-start | bytes 292
  57.5 2.6 %collective-permute-start.13 = (bf16[896,512]{1,0:T(8,128)(2,1)S(1)}, bf16[896,512]{1,0:T(8,128)(2,1)S(1)}, u32[]{:S(2)}, u32[]{:S(2)}) collective-permute-start(bf16[896,512]{1,0:T(8,128)(2,1)S(1)} %get-tuple-element.73), channel_id=1, source_target_pairs={{0,1},{1,0},{2,3},{3,2},{4,5},{5,4},{6,7},{7,6},{8,9},{9,8},{10,11... | collective-permute-start | bytes 2752520 | tf_op jit(solution)/shard_map/ppermute | solution.py:474
  58.0 8.2 %collective-permute-start.15 = (f32[12,512]{1,0:T(8,128)S(1)}, f32[12,512]{1,0:T(8,128)S(1)}, u32[]{:S(2)}, u32[]{:S(2)}) collective-permute-start(f32[12,512]{1,0:T(8,128)S(1)} %get-tuple-element.76.mine_ref), channel_id=1, source_target_pairs={{0,4},{4,0},{8,12},{12,8},{16,20},{20,16},{24,28},{28,24},{1,5},{5... | collective-permute-start | bytes 73736 | tf_op jit(solution)/shard_map/ppermute | solution.py:491
  66.7 12.9 %collective-permute-start.19 = (bf16[448,512]{1,0:T(8,128)(2,1)S(1)}, bf16[448,512]{1,0:T(8,128)(2,1)S(1)}, u32[]{:S(2)}, u32[]{:S(2)}) collective-permute-start(bf16[448,512]{1,0:T(8,128)(2,1)S(1)} %get-tuple-element.80), channel_id=1, source_target_pairs={{0,4},{4,0},{8,12},{12,8},{16,20},{20,16},{24,28},{28,24},{1,5},{5... | collective-permute-start | bytes 1376264 | tf_op jit(solution)/shard_map/ppermute | solution.py:491
  67.9 7.7 %collective-permute-start.18 = (f32[12,512]{1,0:T(8,128)S(1)}, f32[12,512]{1,0:T(8,128)S(1)}, u32[]{:S(2)}, u32[]{:S(2)}) collective-permute-start(f32[12,512]{1,0:T(8,128)S(1)} %shard_map.279), channel_id=1, source_target_pairs={{24,0},{28,4},{25,1},{29,5},{26,2},{30,6},{27,3},{31,7}} | collective-permute-start | bytes 73736 | tf_op jit(solution)/shard_map/ppermute | solution.py:495
  69.2 7.1 %collective-permute-start.17 = (f32[12,512]{1,0:T(8,128)S(1)}, f32[12,512]{1,0:T(8,128)S(1)}, u32[]{:S(2)}, u32[]{:S(2)}) collective-permute-start(f32[12,512]{1,0:T(8,128)S(1)} %shard_map.279), channel_id=1, source_target_pairs={{16,0},{20,4},{24,8},{28,12},{17,1},{21,5},{25,9},{29,13},{18,2},{... | collective-permute-start | bytes 73736 | tf_op jit(solution)/shard_map/ppermute | solution.py:495
  70.5 6.0 %collective-permute-start.16 = (f32[12,512]{1,0:T(8,128)S(1)}, f32[12,512]{1,0:T(8,128)S(1)}, u32[]{:S(2)}, u32[]{:S(2)}) collective-permute-start(f32[12,512]{1,0:T(8,128)S(1)} %shard_map.279), channel_id=1, source_target_pairs={{8,0},{12,4},{16,8},{20,12},{24,16},{28,20},{9,1},{13,5},{17,9},{2... | collective-permute-start | bytes 73736 | tf_op jit(solution)/shard_map/ppermute | solution.py:495
  80.2 10.4 %collective-permute-start.20 = (bf16[112,512]{1,0:T(8,128)(2,1)S(1)}, bf16[112,512]{1,0:T(8,128)(2,1)S(1)}, u32[]{:S(2)}, u32[]{:S(2)}) collective-permute-start(bf16[112,512]{1,0:T(8,128)(2,1)S(1)} %get-tuple-element.88), channel_id=1, source_target_pairs={{0,8},{4,12},{8,0},{12,4},{16,24},{20,28},{24,16},{28,20},{1,9},{5... | collective-permute-start | bytes 344072 | tf_op jit(solution)/shard_map/ppermute | solution.py:491
  80.3 11.8 %collective-permute-start.21 = (bf16[112,512]{1,0:T(8,128)(2,1)S(1)}, bf16[112,512]{1,0:T(8,128)(2,1)S(1)}, u32[]{:S(2)}, u32[]{:S(2)}) collective-permute-start(bf16[112,512]{1,0:T(8,128)(2,1)S(1)} %get-tuple-element.89), channel_id=1, source_target_pairs={{0,16},{4,20},{8,24},{12,28},{16,0},{20,4},{24,8},{28,12},{1,17},{... | collective-permute-start | bytes 344072 | tf_op jit(solution)/shard_map/ppermute | solution.py:491
  80.7 11.4 %collective-permute-start.22 = (bf16[112,512]{1,0:T(8,128)(2,1)S(1)}, bf16[112,512]{1,0:T(8,128)(2,1)S(1)}, u32[]{:S(2)}, u32[]{:S(2)}) collective-permute-start(bf16[112,512]{1,0:T(8,128)(2,1)S(1)} %get-tuple-element.90), channel_id=1, source_target_pairs={{0,24},{4,28},{8,16},{12,20},{16,8},{20,12},{24,0},{28,4},{1,25},{... | collective-permute-start | bytes 344072 | tf_op jit(solution)/shard_map/ppermute | solution.py:491
  90.5 9.1 %copy-start = (bf16[1536,512]{1,0:T(8,128)(2,1)}, bf16[1536,512]{1,0:T(8,128)(2,1)S(1)}, u32[]{:S(2)}) copy-start(bf16[1536,512]{1,0:T(8,128)(2,1)S(1)} %get-tuple-element.91) | copy-start | bytes 4718596
  90.5 29.4 %copy-start.7 = (bf16[512,64]{0,1:T(8,128)(2,1)S(1)}, bf16[512,64]{0,1:T(8,128)(2,1)}, u32[]{:S(2)}) copy-start(bf16[512,64]{0,1:T(8,128)(2,1)} %param.22) | copy-start | bytes 196612
  90.5 29.4 %copy-start.8 = (bf16[512,64]{0,1:T(8,128)(2,1)S(1)}, bf16[512,64]{0,1:T(8,128)(2,1)}, u32[]{:S(2)}) copy-start(bf16[512,64]{0,1:T(8,128)(2,1)} %param.21) | copy-start | bytes 196612
  90.5 30.7 %copy-start.11 = (f32[64]{0:T(128)S(1)}, f32[64]{0:T(128)}, u32[]{:S(2)}) copy-start(f32[64]{0:T(128)} %param.26) | copy-start | bytes 772
  90.5 30.7 %copy-start.12 = (f32[64]{0:T(128)S(1)}, f32[64]{0:T(128)}, u32[]{:S(2)}) copy-start(f32[64]{0:T(128)} %param.25) | copy-start | bytes 772
  92.1 1.4 %collective-permute-start.24 = (bf16[144,512]{1,0:T(8,128)(2,1)S(1)}, bf16[144,512]{1,0:T(8,128)(2,1)S(1)}, u32[]{:S(2)}, u32[]{:S(2)}) collective-permute-start(bf16[144,512]{1,0:T(8,128)(2,1)S(1)} %get-tuple-element.94), channel_id=1, source_target_pairs={{0,1},{1,0},{2,3},{3,2},{4,5},{5,4},{6,7},{7,6},{8,9},{9,8},{10,11... | collective-permute-start | bytes 442376 | tf_op jit(solution)/shard_map/ppermute | solution.py:474
  93.6 6.0 %collective-permute-start.25 = (bf16[144,512]{1,0:T(8,128)(2,1)S(1)}, bf16[144,512]{1,0:T(8,128)(2,1)S(1)}, u32[]{:S(2)}, u32[]{:S(2)}) collective-permute-start(bf16[144,512]{1,0:T(8,128)(2,1)S(1)} %add_convert_fusion.2), channel_id=1, source_target_pairs={{0,4},{4,0},{8,12},{12,8},{16,20},{20,16},{24,28},{28,24},{1,5},{5... | collective-permute-start | bytes 442376 | tf_op jit(solution)/shard_map/ppermute | solution.py:491
  99.6 5.2 %collective-permute-start.26 = (bf16[144,512]{1,0:T(8,128)(2,1)S(1)}, bf16[144,512]{1,0:T(8,128)(2,1)S(1)}, u32[]{:S(2)}, u32[]{:S(2)}) collective-permute-start(bf16[144,512]{1,0:T(8,128)(2,1)S(1)} %add_convert_fusion.1), channel_id=1, source_target_pairs={{0,8},{4,12},{8,0},{12,4},{16,24},{20,28},{24,16},{28,20},{1,9},{5... | collective-permute-start | bytes 442376 | tf_op jit(solution)/shard_map/ppermute | solution.py:491
  101.4 23.6 %collective-permute-start.14 = (bf16[1536,512]{1,0:T(8,128)(2,1)S(1)}, bf16[1536,512]{1,0:T(8,128)(2,1)}, u32[]{:S(2)}, u32[]{:S(2)}) collective-permute-start(bf16[1536,512]{1,0:T(8,128)(2,1)S(1)} %shard_map.278), channel_id=1, source_target_pairs={{0,1},{1,0},{2,3},{3,2},{4,5},{5,4},{6,7},{7,6},{8,9},{9,8},{10,11... | collective-permute-start | bytes 4718600 | tf_op jit(solution)/shard_map/ppermute | solution.py:474
  104.8 14.4 %collective-permute-start.27 = (bf16[144,512]{1,0:T(8,128)(2,1)S(1)}, bf16[144,512]{1,0:T(8,128)(2,1)S(1)}, u32[]{:S(2)}, u32[]{:S(2)}) collective-permute-start(bf16[144,512]{1,0:T(8,128)(2,1)S(1)} %add_convert_fusion), channel_id=1, source_target_pairs={{0,16},{4,20},{8,24},{12,28},{16,0},{20,4},{24,8},{28,12},{1,17},{... | collective-permute-start | bytes 442376 | tf_op jit(solution)/shard_map/ppermute | solution.py:491
  106.6 15.3 %collective-permute-start.30 = (bf16[112,512]{1,0:T(8,128)(2,1)S(1)}, bf16[112,512]{1,0:T(8,128)(2,1)S(1)}, u32[]{:S(2)}, u32[]{:S(2)}) collective-permute-start(bf16[112,512]{1,0:T(8,128)(2,1)S(1)} %add_convert_fusion.3.refs_0_), channel_id=1, source_target_pairs={{0,24},{4,28},{8,16},{12,20},{16,8},{20,12},{24,0},{28,4},{1,25},{... | collective-permute-start | bytes 344072 | tf_op jit(solution)/shard_map/ppermute | solution.py:491
  109.0 14.0 %collective-permute-start.29 = (bf16[112,512]{1,0:T(8,128)(2,1)S(1)}, bf16[112,512]{1,0:T(8,128)(2,1)S(1)}, u32[]{:S(2)}, u32[]{:S(2)}) collective-permute-start(bf16[112,512]{1,0:T(8,128)(2,1)S(1)} %add_convert_fusion.3.refs_0_), channel_id=1, source_target_pairs={{0,16},{4,20},{8,24},{12,28},{16,0},{20,4},{24,8},{28,12},{1,17},{... | collective-permute-start | bytes 344072 | tf_op jit(solution)/shard_map/ppermute | solution.py:491
  109.0 14.9 %collective-permute-start.28 = (bf16[112,512]{1,0:T(8,128)(2,1)S(1)}, bf16[112,512]{1,0:T(8,128)(2,1)S(1)}, u32[]{:S(2)}, u32[]{:S(2)}) collective-permute-start(bf16[112,512]{1,0:T(8,128)(2,1)S(1)} %add_convert_fusion.3.refs_0_), channel_id=1, source_target_pairs={{0,8},{4,12},{8,0},{12,4},{16,24},{20,28},{24,16},{28,20},{1,9},{5... | collective-permute-start | bytes 344072 | tf_op jit(solution)/shard_map/ppermute | solution.py:491
  119.2 10.3 %collective-permute-start.23 = (bf16[1536,512]{1,0:T(8,128)(2,1)}, bf16[1536,512]{1,0:T(8,128)(2,1)S(1)}, u32[]{:S(2)}, u32[]{:S(2)}) collective-permute-start(bf16[1536,512]{1,0:T(8,128)(2,1)} %copy-done), channel_id=1, source_target_pairs={{0,1},{1,0},{2,3},{3,2},{4,5},{5,4},{6,7},{7,6},{8,9},{9,8},{10,11... | collective-permute-start | bytes 4718600 | tf_op jit(solution)/shard_map/ppermute | solution.py:474
  121.8 11.9 %collective-permute-start.31 = (bf16[112,512]{1,0:T(8,128)(2,1)S(1)}, bf16[112,512]{1,0:T(8,128)(2,1)S(1)}, u32[]{:S(2)}, u32[]{:S(2)}) collective-permute-start(bf16[112,512]{1,0:T(8,128)(2,1)S(1)} %add_convert_fusion.3.refs_0_), channel_id=1, source_target_pairs={{0,4},{4,0},{8,12},{12,8},{16,20},{20,16},{24,28},{28,24},{1,5},{5... | collective-permute-start | bytes 344072 | tf_op jit(solution)/shard_map/ppermute | solution.py:491
  123.0 10.7 %collective-permute-start.34 = (bf16[112,512]{1,0:T(8,128)(2,1)S(1)}, bf16[112,512]{1,0:T(8,128)(2,1)S(1)}, u32[]{:S(2)}, u32[]{:S(2)}) collective-permute-start(bf16[112,512]{1,0:T(8,128)(2,1)S(1)} %collective-permute-done.30.refs_3_), channel_id=1, source_target_pairs={{0,4},{4,0},{8,12},{12,8},{16,20},{20,16},{24,28},{28,24},{1,5},{5... | collective-permute-start | bytes 344072 | tf_op jit(solution)/shard_map/ppermute | solution.py:491
  124.0 9.7 %collective-permute-start.33 = (bf16[112,512]{1,0:T(8,128)(2,1)S(1)}, bf16[112,512]{1,0:T(8,128)(2,1)S(1)}, u32[]{:S(2)}, u32[]{:S(2)}) collective-permute-start(bf16[112,512]{1,0:T(8,128)(2,1)S(1)} %collective-permute-done.29.refs_2_), channel_id=1, source_target_pairs={{0,4},{4,0},{8,12},{12,8},{16,20},{20,16},{24,28},{28,24},{1,5},{5... | collective-permute-start | bytes 344072 | tf_op jit(solution)/shard_map/ppermute | solution.py:491
  125.0 9.7 %collective-permute-start.32 = (bf16[112,512]{1,0:T(8,128)(2,1)S(1)}, bf16[112,512]{1,0:T(8,128)(2,1)S(1)}, u32[]{:S(2)}, u32[]{:S(2)}) collective-permute-start(bf16[112,512]{1,0:T(8,128)(2,1)S(1)} %collective-permute-done.28.refs_1_), channel_id=1, source_target_pairs={{0,4},{4,0},{8,12},{12,8},{16,20},{20,16},{24,28},{28,24},{1,5},{5... | collective-permute-start | bytes 344072 | tf_op jit(solution)/shard_map/ppermute | solution.py:491
  127.6 2.0 %copy-start.1 = (bf16[1536,512]{1,0:T(8,128)(2,1)S(1)}, bf16[1536,512]{1,0:T(8,128)(2,1)}, u32[]{:S(2)}) copy-start(bf16[1536,512]{1,0:T(8,128)(2,1)} %copy-done) | copy-start | bytes 4718596

commit v3 on v2

--- a/solution.py
+++ b/solution.py
@@ -123,16 +123,25 @@
 
 def incoming(far_refs, beside_ref, odd, powers_ref, backwards, out_ref):
     states = out_ref.shape[1] // 2
-    lr, li = powers_ref[0:1, :states], powers_ref[0:1, states:]
-    pr, pi = powers_ref[1:2, :states], powers_ref[1:2, states:]
-    sr, si = far_refs[-1][:, :states], far_refs[-1][:, states:]
-    for ref in far_refs[-2::-1]:
-        mr, mi = cmul(pr, pi, sr, si)
-        sr, si = mr + ref[:, :states], mi + ref[:, states:]
-    mr, mi = cmul(lr, li, sr, si)
+    early, late = slice(0, states), slice(states, None)
+    sr, si = far_refs[0][:, early], far_refs[0][:, late]
+    for k in range(1, len(far_refs)):
+        row = slice(4 + k, 5 + k)
+        mr, mi = cmul(powers_ref[row, early], powers_ref[row, late], far_refs[k][:, early], far_refs[k][:, late])
+        sr, si = sr + mr, si + mi
+    mr, mi = cmul(powers_ref[0:1, early], powers_ref[0:1, late], sr, si)
     second = odd == (0 if backwards else 1)
-    out_ref[:, :states] = jnp.where(second, mr + beside_ref[:, :states], sr)
-    out_ref[:, states:] = jnp.where(second, mi + beside_ref[:, states:], si)
+    out_ref[:, early] = jnp.where(second, mr + beside_ref[:, early], sr)
+    out_ref[:, late] = jnp.where(second, mi + beside_ref[:, late], si)
+
+
+def join_kernel(mine_ref, other_ref, powers_ref, out_ref, *, row):
+    states = out_ref.shape[1] // 2
+    early, late = slice(0, states), slice(states, None)
+    row = slice(row, row + 1)
+    mr, mi = cmul(powers_ref[row, early], powers_ref[row, late], other_ref[:, early], other_ref[:, late])
+    out_ref[:, early] = mine_ref[:, early] + mr
+    out_ref[:, late] = mine_ref[:, late] + mi
 
 
 def pair_kernel(where_ref, mine_ref, other_ref, powers_ref, out_ref, *, backwards):
@@ -156,13 +165,41 @@
         out_ref[pl.ds(states + at, half), :] = pack[half:per, :]
 
 
+def input_pack_kernel(where_ref, in_real, in_imag, nu, theta, gamma, a_ref):
+    per_s, width = in_real.shape
+    a_ref[:per_s, :] = in_real[...]
+    a_ref[per_s : 2 * per_s, :] = in_imag[...]
+    modulus = jnp.exp(-jnp.exp(nu[...]))
+    angle = jnp.exp(theta[...])
+    rest = [modulus * jnp.cos(angle), modulus * jnp.sin(angle), jnp.exp(gamma[...])]
+    rows = []
+    for _ in range(3):
+        for n in range(3):
+            high = rest[n].astype(BF16).astype(F32)
+            rows.append(high)
+            rest[n] = rest[n] - high
+    table = jnp.concatenate(rows + [jnp.zeros((PARAM_ROWS - 9, per_s), F32)], axis=0)
+    table = jnp.concatenate([table] * (width // per_s), axis=1)
+    here = lax.broadcasted_iota(jnp.int32, (PARAM_ROWS, width), 1) // per_s == where_ref[2]
+    a_ref[2 * per_s :, :] = jnp.where(here, table, 0.0).astype(BF16)
+
+
+def weight_pack_kernel(out_real, out_imag, up, gate, down, b_ref, g_ref):
+    per_s, per_f = out_real.shape[0], down.shape[0]
+    b_ref[:per_s, :] = out_real[...]
+    b_ref[per_s : 2 * per_s, :] = out_imag[...]
+    b_ref[2 * per_s :, :] = down[...]
+    g_ref[:, :per_f] = up[...]
+    g_ref[:, per_f:] = gate[...]
+
+
 def norm_kernel(where_ref, lens_ref, tok_ref, cot_ref, gain_ref, bias_ref, low_ref, normed_ref, inv_ref, cotm_ref, *, length, seqs):
-    block = pl.program_id(0)
     normed, inv_scale = layer_norm(tok_ref[...].astype(F32))
     normed_ref[...] = normed
     inv_ref[...] = jnp.broadcast_to(inv_scale, inv_ref.shape)
     low_ref[...] = (normed * gain_ref[...] + bias_ref[...]).astype(BF16)
-    rows, width = tok_ref.shape
+    block = pl.program_id(0)
+    rows, width = cot_ref.shape
     per_block = rows // length
     for s in range(per_block):
         span = slice(s * length, (s + 1) * length)
@@ -183,9 +220,14 @@
         fill_powers(dr, di, True, 0, weigh)
         gam[...] = jnp.concatenate([gain, gain], axis=1)
         lr, li = cmul(weigh[0, :1, :], weigh[1, :1, :], dr, di)
-        powers_ref[...] = jnp.zeros(powers_ref.shape, F32)
-        powers_ref[0:1, :] = jnp.concatenate([lr, li], axis=1)
-        powers_ref[1:2, :] = jnp.concatenate(cmul(lr, li, lr, li), axis=1)
+        rows = [(lr, li)] + [cmul(lr, li, lr, li)]
+        for _ in range(2):
+            rows.append(cmul(*rows[-1], *rows[-1]))
+        rows.append((jnp.ones_like(lr), jnp.zeros_like(lr)))
+        for _ in range(3):
+            rows.append(cmul(*cmul(*rows[-1], *rows[-1]), *rows[1]))
+        for k, (lr, li) in enumerate(rows):
+            powers_ref[k : k + 1, :] = jnp.concatenate([lr, li], axis=1)
 
     drive_ref[...] = dot_nt(low_ref[...], in_t[...]) * gam[...]
     per_block = low_ref.shape[0] // length
@@ -221,8 +263,8 @@
         hg_ref[:, pl.ds(at, per_f)] = dot_nt(cotm_ref[...], pack[2 * per_s :, :]).astype(BF16)
 
 
-def middle_kernel(where_ref, *refs, length, ways):
-    far_refs, refs = refs[: ways - 1], refs[ways - 1 :]
+def middle_kernel(where_ref, *refs, length, levels):
+    far_refs, refs = refs[:levels], refs[levels:]
     beside_ref, powers_ref, local_ref, normed_ref, hg_ref, cotm_ref, a0, a1, a2, a3 = refs[:10]
     gain_ref, bias_ref, skip_ref, b0, b1, b2, b3, g0, g1, g2, g3 = refs[10:21]
     state_ref, back_ref, backends_ref, ylow_ref, hid_ref, own_ref, sent_ref = refs[21:28]
@@ -311,7 +353,7 @@
             ref[2 * per_s + per_f : 2 * per_s + per_f + width, :] = part.astype(ref.dtype)
 
 
-def down_kernel(where_ref, lens_ref, tok_ref, hid_ref, b0, b1, b2, b3, out_ref, down_all, *, length, per_s, seqs):
+def down_kernel(where_ref, lens_ref, tok_ref, hid_ref, b0, b1, b2, b3, all_ref, out_ref, down_all, *, length, per_s, seqs):
     block = pl.program_id(0)
     shard = where_ref[2]
     rows, width = tok_ref.shape
@@ -329,13 +371,14 @@
         left = lens_ref[where_ref[1] * seqs + block * per_block + s] - where_ref[0] * length
         live = lax.broadcasted_iota(jnp.int32, (length, width), 0) < left
         out_ref[span, :] = jnp.where(live, tok_ref[span, :].astype(F32) + added[span, :], 0.0).astype(BF16)
-
-
-def last_kernel(where_ref, *refs, length, ways):
-    far_refs, refs = refs[: ways - 1], refs[ways - 1 :]
+    all_ref[...] = out_ref[...]
+
+
+def last_kernel(where_ref, *refs, length, levels):
+    far_refs, refs = refs[:levels], refs[levels:]
     beside_ref, powers_ref, low_ref, normed_ref, inv_ref, cotm_ref, back_ref, state_ref, ylow_ref = refs[:9]
-    a0, a1, a2, a3, gain_ref, bias_ref, skip_ref, grad_ref, own_ref, sent_ref = refs[9:19]
-    in_t, full, carry, gam, dlow, in_grad, lam_grad, vec_grad = refs[19:]
+    a0, a1, a2, a3, gain_ref, bias_ref, skip_ref, all_ref, grad_ref, own_ref, sent_ref = refs[9:20]
+    in_t, full, carry, gam, dlow, in_grad, lam_grad, vec_grad = refs[20:]
     block = pl.program_id(0)
     place, core, shard = where_ref[0], where_ref[1], where_ref[2]
     states = in_t.shape[0] // 2
@@ -384,6 +427,7 @@
         - normed * jnp.mean(scaled * normed, axis=-1, keepdims=True)
     )
     grad_ref[...] = (cotm_ref[...].astype(F32) + inv_ref[:, :1] * grad).astype(BF16)
+    all_ref[...] = grad_ref[...].astype(F32)
     at = pl.multiple_of((shard // 2) * 2 * per_s, 2 * per_s)
     for k in range(2):
         cols = dlow[:, pl.ds(k * states + at, 2 * per_s)]
@@ -417,24 +461,50 @@
         ref[...] = (own_ref[pl.ds(at, rows), :] + other_ref[pl.ds(at, rows), :].astype(F32)).astype(ref.dtype)
 
 
-def unpack_kernel(where_ref, *refs, ways):
-    mine, other = refs[:ways], refs[ways : 2 * ways]
-    real_ref, imag_ref, up_ref, gate_ref, down_ref, total = refs[2 * ways :]
+def place_kernel(where_ref, all_ref, other_ref, out_ref):
+    out_ref[...] = other_ref[...].astype(out_ref.dtype)
+
+
+def finish_kernel(where_ref, *refs, ways):
+    parts, refs = refs[: 2 * ways], refs[2 * ways :]
+    mine_ref, other_ref, in_real, in_imag, nu, theta = refs[:6]
+    vec_refs, (in_real_ref, in_imag_ref, nu_ref, theta_ref, gamma_ref) = refs[6:9], refs[9:14]
+    real_ref, imag_ref, up_ref, gate_ref, down_ref, total = refs[14:]
     place = where_ref[0]
-    rows = mine[0].shape[0]
-    for k in range(ways):
-        at = ((place // 2) ^ k) * rows
-        total[pl.ds(pl.multiple_of((place % 2) * ways * rows + at, 16), rows), :] = mine[k][...].astype(F32)
-        total[pl.ds(pl.multiple_of((1 - place % 2) * ways * rows + at, 16), rows), :] = other[k][...].astype(F32)
+    rows = parts[0].shape[0]
+    for n, part in enumerate(parts):
+        half = place % 2 if n < ways else 1 - place % 2
+        at = (half * ways + ((place // 2) ^ (n % ways))) * rows
+        total[pl.ds(pl.multiple_of(at, 16), rows), :] = part[...].astype(F32)
     per_s = real_ref.shape[0]
     per_f = down_ref.shape[0]
+    last = 2 * per_s + per_f + up_ref.shape[0]
     real_ref[...] = total[:per_s, :]
     imag_ref[...] = total[per_s : 2 * per_s, :]
     down_ref[...] = total[2 * per_s : 2 * per_s + per_f, :]
-    last = 2 * per_s + per_f + up_ref.shape[0]
     up_ref[...] = total[2 * per_s + per_f : last, :per_f]
     gate_ref[...] = total[2 * per_s + per_f : last, per_f:]
 
+    grads = mine_ref[...].astype(F32) + other_ref[...].astype(F32)
+    in_real_ref[...] = grads[:per_s, :]
+    in_imag_ref[...] = grads[per_s : 2 * per_s, :]
+    for n in range(3):
+        vec_refs[n][...] = grads[2 * per_s + n : 2 * per_s + n + 1, :]
+    lam = [jnp.zeros((1, per_s), F32), jnp.zeros((1, per_s), F32)]
+    for t in range(TENSOR):
+        for n in range(2):
+            at = (n * TENSOR + t) * per_s
+            part = grads[2 * per_s + 3 : 2 * per_s + 4, at : at + per_s]
+            lam[n] = jnp.where(where_ref[2] == t, part, lam[n])
+    decay = jnp.exp(nu[...])
+    modulus = jnp.exp(-decay)
+    angle = jnp.exp(theta[...])
+    cos, sin = jnp.cos(angle), jnp.sin(angle)
+    nu_ref[...] = -decay * modulus * (lam[0] * cos + lam[1] * sin)
+    theta_ref[...] = angle * modulus * (lam[1] * cos - lam[0] * sin)
+    terms = in_real[...].astype(F32) * grads[:per_s, :] + in_imag[...].astype(F32) * grads[per_s : 2 * per_s, :]
+    gamma_ref[...] = jnp.sum(terms.T, axis=0, keepdims=True)
+
 
 def whole(shape):
     return pl.BlockSpec(shape, lambda *_: (0,) * len(shape))
@@ -448,7 +518,7 @@
     return pltpu.with_memory_space_constraint(value, pltpu.HBM)
 
 
-def call(kernel, grid, prefetch, in_specs, out_specs, out_shape, scratch, cost, vmem):
+def call(kernel, grid, prefetch, in_specs, out_specs, out_shape, scratch, cost, vmem, aliases=None):
     return pl.pallas_call(
         kernel,
         grid_spec=pltpu.PrefetchScalarGridSpec(
@@ -459,15 +529,10 @@
             scratch_shapes=scratch,
         ),
         out_shape=out_shape,
+        input_output_aliases=aliases or {},
         compiler_params=pltpu.CompilerParams(vmem_limit_bytes=vmem * MIB),
         cost_estimate=pl.CostEstimate(flops=1, bytes_accessed=int(cost * 3.3e6), transcendentals=0),
     )
-
-
-def split_low(value):
-    high = lax.reduce_precision(value, 8, 7)
-    middle = lax.reduce_precision(value - high, 8, 7)
-    return high, middle, value - high - middle
 
 
 def core_swap(value):
@@ -527,27 +592,16 @@
     core = shard % 2
     where = jnp.stack([place, core, shard])
 
-    modulus = jnp.exp(-jnp.exp(nu_log))
-    angle = jnp.exp(theta_log)
-    gain = jnp.exp(gamma_log)
-    parts = [split_low(v) for v in (modulus * jnp.cos(angle), modulus * jnp.sin(angle), gain)]
-    table = jnp.stack([parts[v][k] for k in range(3) for v in range(3)])
-    placed = jnp.where(
-        lax.broadcasted_iota(jnp.int32, (9, width), 1) // per_s == shard, jnp.tile(table, (1, width // per_s)), 0.0
-    )
-    pack_a = jnp.concatenate(
-        [in_real.T, in_imag.T, placed.astype(BF16), jnp.zeros((PARAM_ROWS - 9, width), BF16)], axis=0
-    )
-    pack_b = after(jnp.concatenate([out_real, out_imag, down_weight], axis=0), pack_a)
-    pack_g = after(jnp.concatenate([up_weight, gate_weight], axis=1), pack_b)
     tok_rows = tokens.reshape(seqs * length, width)
     cot_rows = cotangent.reshape(seqs * length, width)
     row = lambda v: v.reshape(1, width)
     gain_row, bias_row, skip_row = row(ln_gain), row(ln_bias), row(skip_gain)
     half_spec = pl.BlockSpec((BLOCK, width), lambda b, w, *_: (w[1] * blocks + b, 0))
     row_spec = lambda lanes: pl.BlockSpec((BLOCK, lanes), lambda b, *_: (b, 0))
-    a_spec = [whole(pack_a.shape)] * TENSOR
-    b_spec = [whole(pack_b.shape)] * TENSOR
+    a_shape = (2 * per_s + PARAM_ROWS, width)
+    b_shape = (2 * per_s + per_f, width)
+    a_spec = [whole(a_shape)] * TENSOR
+    b_spec = [whole(b_shape)] * TENSOR
     any_spec = [pl.BlockSpec(memory_space=pl.ANY)] * TENSOR
     vec_spec = whole((1, width))
     shape = jax.ShapeDtypeStruct
@@ -555,6 +609,18 @@
     lanes = 2 * states
     units = TENSOR * per_f
 
+    line = lambda v: v.reshape(1, per_s)
+    pack_a = call(
+        input_pack_kernel,
+        (1,),
+        1,
+        [whole((per_s, width))] * 2 + [whole((1, per_s))] * 3,
+        whole(a_shape),
+        shape(a_shape, BF16),
+        [],
+        1,
+        4,
+    )(where, *map(far, (in_real.T, in_imag.T, line(nu_log), line(theta_log), line(gamma_log))))
     low, normed, inv, cot_m = call(
         functools.partial(norm_kernel, length=length, seqs=own_seqs),
         (blocks,),
@@ -565,9 +631,20 @@
         [],
         3,
         8,
-    )(where, lengths, far(tok_rows), far(cot_rows), far(gain_row), far(bias_row))
+    )(where, lengths, far(after(tok_rows, pack_a)), far(cot_rows), far(gain_row), far(bias_row))
 
     packs_a = gather_tensor(pack_a, low)
+    pack_b, pack_g = call(
+        weight_pack_kernel,
+        (1,),
+        0,
+        [whole((per_s, width))] * 2 + [whole((width, per_f))] * 2 + [whole((per_f, width))],
+        [whole(b_shape), whole((width, 2 * per_f))],
+        [shape(b_shape, BF16), shape((width, 2 * per_f), BF16)],
+        [],
+        2,
+        10,
+    )(*map(far, (after(out_real, packs_a[2]), out_imag, up_weight, gate_weight, down_weight)))
     near_a = tuple(map(near, packs_a))
     drive, ends, powers = call(
         functools.partial(drive_kernel, length=length),
@@ -597,28 +674,37 @@
         8,
     )(near(drive), *near_a)
     ways = groups // 2
+    levels = (ways - 1).bit_length()
     end_spec = whole((own_seqs, lanes))
     power_spec = whole((TILE, lanes))
 
-    def exchange(mine, backwards, beside_work):
-        beside = after(flip_dp(mine, 1, groups), beside_work)
-        both = call(
-            functools.partial(pair_kernel, backwards=backwards),
+    def small(kernel, prefetch, inputs):
+        return call(
+            kernel,
             (1,),
-            1,
+            prefetch,
             [end_spec, end_spec, power_spec],
             end_spec,
             shape((own_seqs, lanes), F32),
             [],
             1,
             2,
-        )(where, mine, beside, powers)
-        return [shift_dp(both, (-2 if backwards else 2) * k, groups) for k in range(1, ways)], beside, both
-
-    far_ends, beside_ends, pair_ends = exchange(ends, False, local)
-    packs_b = gather_tensor(pack_b, beside_ends)
-    near_b = tuple(map(near, packs_b))
-
+        )(*inputs)
+
+    def exchange(mine, backwards, beside_work):
+        beside = after(flip_dp(mine, 1, groups), beside_work)
+        both = small(functools.partial(pair_kernel, backwards=backwards), 1, (where, mine, beside, powers))
+        found = [both]
+        from_far = []
+        for k in range(levels):
+            step = 2 << k
+            from_far.append(shift_dp(found[-1], -step if backwards else step, groups))
+            if k + 1 < levels:
+                found.append(small(functools.partial(join_kernel, row=1 + k), 0, (found[-1], from_far[-1], powers)))
+        return from_far, beside, found
+
+    far_ends, beside_ends, found_ends = exchange(ends, False, local)
+    near_b = tuple(map(near, gather_tensor(pack_b, far_ends[0])))
     hid_grad = call(
         functools.partial(hidden_kernel, per_s=per_s),
         (blocks,),
@@ -629,15 +715,14 @@
         [],
         3,
         10,
-    )(where, near(after(cot_m, pair_ends)), *near_b)
-
+    )(where, near(after(cot_m, found_ends[-1])), *near_b)
     packs_g = gather_tensor(pack_g, hid_grad, *far_ends)
     pack_rows = -(-(2 * per_s + per_f + width) // (16 * groups)) * 16 * groups
     state, back, back_ends, y_low, hid, own_b, sent_b = call(
-        functools.partial(middle_kernel, length=length, ways=ways),
+        functools.partial(middle_kernel, length=length, levels=levels),
         (blocks,),
         1,
-        [end_spec] * ways
+        [end_spec] * (levels + 1)
         + [power_spec, row_spec(lanes), row_spec(width), row_spec(units), row_spec(width)]
         + a_spec
         + [vec_spec] * 3
@@ -703,19 +788,20 @@
         2,
         8,
     )(where, own_b, core_swap(sent_b))
-    out_own = call(
+    far_back, beside_back, found_back = exchange(back_ends, True, send_b)
+    half_b = flip_dp(after(send_b, found_back[0]), 1, groups)
+
+    all_out, out_own = call(
         functools.partial(down_kernel, length=length, per_s=per_s, seqs=own_seqs),
         (blocks,),
         2,
         [half_spec, row_spec(units)] + b_spec,
-        row_spec(width),
-        shape((rows, width), BF16),
+        [half_spec, row_spec(width)],
+        [shape((seqs * length, width), BF16), shape((rows, width), BF16)],
         [pltpu.VMEM((units, width), BF16)],
         5,
         8,
-    )(where, lengths, far(tok_rows), near(after(hid, send_b)), *near_b)
-    far_back, beside_back, pair_back = exchange(back_ends, True, out_own)
-    half_b = flip_dp(after(send_b, pair_back), 1, groups)
+    )(where, lengths, far(tok_rows), near(after(hid, found_back[-1])), *near_b)
 
     dealt = call(
         deal_kernel,
@@ -727,13 +813,13 @@
         [],
         2,
         8,
-    )(where, after(keep_b, *far_back), half_b)
-
-    grad_own, own_a, sent_a = call(
-        functools.partial(last_kernel, length=length, ways=ways),
+    )(where, after(keep_b, out_own, *far_back), half_b)
+
+    all_grad, grad_own, own_a, sent_a = call(
+        functools.partial(last_kernel, length=length, levels=levels),
         (blocks,),
         1,
-        [end_spec] * ways
+        [end_spec] * (levels + 1)
         + [
             power_spec,
             row_spec(width),
@@ -746,8 +832,13 @@
         ]
         + a_spec
         + [vec_spec] * 3,
-        [row_spec(width), whole(pack_a.shape), whole(pack_a.shape)],
-        [shape((rows, width), BF16), shape(pack_a.shape, BF16), shape(pack_a.shape, BF16)],
+        [half_spec, row_spec(width), whole(a_shape), whole(a_shape)],
+        [
+            shape((seqs * length, width), F32),
+            shape((rows, width), BF16),
+            shape(a_shape, BF16),
+            shape(a_shape, BF16),
+        ],
         [
             pltpu.VMEM((lanes, width), BF16),
             pltpu.VMEM((2, length, states), F32),
@@ -763,7 +854,7 @@
     )(
         where,
         *far_back,
-        after(beside_back, dealt[0]),
+        after(beside_back, dealt[0], out_own),
         powers,
         *map(near, (low, normed, inv, cot_m, back, state, y_low)),
         *near_a,
@@ -777,66 +868,82 @@
         mine_b = mine_b + flip_dp(dealt[k], 2 * k, groups).astype(F32)
     mine_b = mine_b.astype(BF16)
 
-    grads_a = own_a.astype(F32) + core_swap(after(sent_a, mine_b)).astype(F32)
-    bit = 1
-    while bit < groups:
-        low_a = grads_a.astype(BF16)
-        grads_a = low_a.astype(F32) + flip_dp(low_a, bit, groups).astype(F32)
-        bit *= 2
-
     gathered = [mine_b] + [flip_dp(mine_b, 2 * k, groups) for k in range(1, ways)]
     beside = [flip_dp(piece, 1, groups) for piece in gathered]
 
-    out_other = core_swap(out_own)
-    grad_other = core_swap(after(grad_own, mine_b))
-
-    def in_order(mine, other):
-        first = core == 0
-        return jnp.concatenate([jnp.where(first, mine, other), jnp.where(first, other, mine)], axis=0).reshape(
-            seqs, length, width
-        )
-
-    block_out = in_order(out_own, out_other)
-    input_grad = in_order(grad_own, grad_other).astype(F32)
-    beside[-1] = after(beside[-1], block_out, input_grad)
-
-    out_real_grad, out_imag_grad, up_grad, gate_grad, down_grad = call(
-        functools.partial(unpack_kernel, ways=ways),
+    grads_a = own_a.astype(F32) + core_swap(after(sent_a, mine_b)).astype(F32)
+    low_a = grads_a.astype(BF16)
+    other_a = flip_dp(low_a, 1, groups)
+
+    def complete(partly, other):
+        steps = blocks // 2
+        spec = pl.BlockSpec((rows // steps, width), lambda b, w, *_: ((1 - w[1]) * steps + b, 0))
+        return call(
+            place_kernel,
+            (steps,),
+            1,
+            [pl.BlockSpec(memory_space=pl.ANY), pl.BlockSpec((rows // steps, width), lambda b, *_: (b, 0))],
+            spec,
+            shape(partly.shape, partly.dtype),
+            [],
+            2,
+            8,
+            {1: 0},
+        )(where, partly, other).reshape(seqs, length, width)
+
+    block_out = complete(all_out, core_swap(out_own))
+    input_grad = complete(all_grad, core_swap(after(grad_own, low_a)))
+    bit = 2
+    while bit < groups:
+        low_a = (low_a.astype(F32) + other_a.astype(F32)).astype(BF16)
+        if bit == 2:
+            low_a = after(low_a, block_out, input_grad, *gathered)
+        elif bit == 4:
+            low_a = after(low_a, *beside[:2])
+        other_a = flip_dp(low_a, bit, groups)
+        bit *= 2
+
+    state_shape = shape((per_s, width), F32)
+    finished = call(
+        functools.partial(finish_kernel, ways=ways),
         (1,),
         1,
-        [whole((part, width))] * groups,
-        [whole((per_s, width))] * 2 + [whole((width, per_f))] * 2 + [whole((per_f, width))],
-        [shape((per_s, width), F32)] * 2 + [shape((width, per_f), F32)] * 2 + [shape((per_f, width), F32)],
+        [whole((part, width))] * groups
+        + [whole(a_shape)] * 2
+        + [whole((per_s, width))] * 2
+        + [whole((1, per_s))] * 2,
+        [vec_spec] * 3
+        + [whole((per_s, width))] * 2
+        + [whole((1, per_s))] * 3
+        + [whole((per_s, width))] * 2
+        + [whole((width, per_f))] * 2
+        + [whole((per_f, width))],
+        [shape((1, width), F32)] * 3
+        + [state_shape] * 2
+        + [shape((1, per_s), F32)] * 3
+        + [state_shape] * 2
+        + [shape((width, per_f), F32)] * 2
+        + [shape((per_f, width), F32)],
         [pltpu.VMEM((pack_rows, width), F32)],
-        2,
-        8,
-    )(where, *gathered, *beside)
-
-    in_real_grad = grads_a[:per_s].T
-    in_imag_grad = grads_a[per_s : 2 * per_s].T
-    small = grads_a[2 * per_s :]
-    lam_real = lax.dynamic_slice_in_dim(small[3, :states], shard * per_s, per_s)
-    lam_imag = lax.dynamic_slice_in_dim(small[3, states:], shard * per_s, per_s)
-    cos, sin = jnp.cos(angle), jnp.sin(angle)
-    nu_grad = -jnp.exp(nu_log) * modulus * (lam_real * cos + lam_imag * sin)
-    theta_grad = angle * modulus * (lam_imag * cos - lam_real * sin)
-    gamma_grad = jnp.sum(in_real.astype(F32) * in_real_grad + in_imag.astype(F32) * in_imag_grad, axis=0)
+        3,
+        12,
+    )(
+        where,
+        *gathered,
+        *beside,
+        low_a,
+        other_a,
+        *map(far, (in_real.T, in_imag.T, line(nu_log), line(theta_log))),
+    )
+    vectors, in_grads, logs = finished[:3], finished[3:5], finished[5:8]
     return (
         block_out,
         input_grad,
-        small[0],
-        small[1],
-        small[2],
-        in_real_grad,
-        in_imag_grad,
-        out_real_grad,
-        out_imag_grad,
-        nu_grad,
-        theta_grad,
-        gamma_grad,
-        up_grad,
-        gate_grad,
-        down_grad,
+        *[v.reshape(width) for v in vectors],
+        *[v.T for v in in_grads],
+        *finished[8:10],
+        *[v.reshape(per_s) for v in logs],
+        *finished[10:],
     )
 
 

time: 137 us -> 125 us (0.912)
  other arithmetic: 13.1 us -> 0.25 us
  Pallas kernels: 47.8 us -> 58.5 us
  waiting for transfers between devices: 30.8 us -> 23.5 us
    pallas_call x5 -> x11, Pallas kernels: 27.5 us -> 37.2 us  [the longest x1 18.7 us: shards(): call(functools.partial(middle_kernel, length=length, levels=levels), (blo...]
    ppermute x16, waiting for transfers between devices: 22.2 us -> 14.3 us  [flip_dp(): return lax.ppermute(value, 'dp', [(i, i ^ bits) for i in range(groups)])]
    concatenate x5 -> x0, other arithmetic: 4.04 us -> none  [the longest x2 2.07 us: in_order(): jnp.concatenate([jnp.where(first, mine, other), jnp.where(first, other, m...]
    convert_element_type x2, other arithmetic: 3.61 us -> 0.07 us  [shards(): low_a = (low_a.astype(F32) + other_a.astype(F32)).astype(BF16)]
    ppermute x6 -> x4, starting transfers between devices: 13.1 us -> 11.3 us  [shift_dp(): lax.ppermute(value, 'dp', [(i, i + by) for i in range(groups) if 0 <= i +...]
    select_n x2 -> x0, other arithmetic: 1.82 us -> none  [in_order(): jnp.where(first, mine, other)]
    another operation x3 -> x0, other arithmetic: 1.4 us -> none  [shards(): table = jnp.stack([parts[v][k] for k in range(3) for v in range(3)])]
    ppermute x6 -> x4, waiting for transfers between devices: 4.76 us -> 6.01 us  [shift_dp(): lax.ppermute(value, 'dp', [(i, i + by) for i in range(groups) if 0 <= i +...]
  transfers between devices with their start and end apart: 35 -> 33, of which waited for: 13 -> 15; matrix products, arithmetic and copies ran while one was open for 8% -> 0% of each run, Pallas kernels for 19% -> 26%
where the time goes in v3:
time: 125 us
  Pallas kernels  58.5 us (47%)
  starting transfers between devices  41 us (33%)
  waiting for transfers between devices  23.5 us (19%)
    ppermute x16, starting transfers between devices, flip_dp(): return lax.ppermute(value, 'dp', [(i, i ^ bits) for i in range(groups)])  22.3 us
    pallas_call x1, Pallas kernels, shards(): call(functools.partial(middle_kernel, length=length, levels=levels), (blo...  18.7 us
    ppermute x16, waiting for transfers between devices, flip_dp(): return lax.ppermute(value, 'dp', [(i, i ^ bits) for i in range(groups)])  14.3 us
    ppermute x4, starting transfers between devices, shift_dp(): lax.ppermute(value, 'dp', [(i, i + by) for i in range(groups) if 0 <= i +...  11.3 us
    pallas_call x1, Pallas kernels, shards(): call(functools.partial(last_kernel, length=length, levels=levels), (block...  6.71 us
    pallas_call x1, Pallas kernels, shards(): call(functools.partial(down_kernel, length=length, per_s=per_s, seqs=own_...  6.36 us
    ppermute x4, waiting for transfers between devices, shift_dp(): lax.ppermute(value, 'dp', [(i, i + by) for i in range(groups) if 0 <= i +...  6.01 us
    ppermute x3, starting transfers between devices, side_swap(): return lax.ppermute(value, 'tensor', [(t, t ^ 2) for t in range(TENSOR)])  5 us
  transfers between devices with their start and end apart: 33, of which 15 were waited for; matrix products, arithmetic and copies ran while one was open for 0% of the time, Pallas kernels for 26%

profile of v3, /device:TPU:0, one launch (start us, length us, event | category | flops | bytes accessed | tf_op | source)
XLA Modules:
  0.0 124.8 jit_solution(9330415104509858080)
XLA Ops:
  0.7 1.6 %shard_map.271.a0.refs_8_.refs_11_ = bf16[144,512]{1,0:T(8,128)(2,1)S(1)} custom-call(s32[3]{0:T(128)S(1)} %pad_add_fusion.where_ref, bf16[64,512]{1,0:T(8,128)(2,1)} %bitcast.36, bf16[64,512]{1,0:T(8,128)(2,1)} %bitcast.38, f32[1,64]{1,0:T(1,128)} %bitcast.40, f32[1,64]{1,0:T(1,128)} %bitcast.42, f32[1,64]{1,0:T(1,128)} %bitcast.44), custom_call_target="tpu_custom_call" | custom-call | flops 1 | bytes 3300000 | tf_op jit(solution)/shard_map/pallas_call | solution.py:613
  2.3 3.0 %collective-permute-start.1 = (bf16[144,512]{1,0:T(8,128)(2,1)S(1)}, bf16[144,512]{1,0:T(8,128)(2,1)S(1)}, u32[]{:S(2)}, u32[]{:S(2)}) collective-permute-start(bf16[144,512]{1,0:T(8,128)(2,1)S(1)} %shard_map.271.a0.refs_8_.refs_11_), channel_id=1, source_target_pairs={{0,2},{1,3},{2,0},{3,1},{4,6},{5,7},{6,4},{7,5},{8,10},{9,11},{10,... | collective-permute-start | bytes 442376 | tf_op jit(solution)/shard_map/ppermute | solution.py:543
  5.3 0.7 copy-done.3
  5.9 5.0 %shard_map.272 = (bf16[1536,512]{1,0:T(8,128)(2,1)S(1)}, f32[1536,512]{1,0:T(8,128)S(1)}, f32[1536,128]{1,0:T(8,128)S(1)}, bf16[1536,512]{1,0:T(8,128)(2,1)S(1)}) custom-call(s32[3]{0:T(128)S(1)} %pad_add_fusion.where_ref, s32[24]{0:T(128)S(1)} %copy-done.3, bf16[3072,512]{1,0:T(8,128)(2,1)} %bitcast.31, bf16[3072,512]{1,0:T(8,128)(2,1)} %bitcast.34, ...), custom_call_target="tpu_custom_call" | custom-call | flops 1 | bytes 9900000 | tf_op jit(solution)/shard_map/pallas_call | solution.py:624
  10.9 1.2 shard_map.277
  12.8 1.9 %collective-permute-start.10 = (bf16[512,512]{1,0:T(8,128)(2,1)S(1)}, bf16[512,512]{1,0:T(8,128)(2,1)S(1)}, u32[]{:S(2)}, u32[]{:S(2)}) collective-permute-start(bf16[512,512]{1,0:T(8,128)(2,1)S(1)} %get-tuple-element.85.refs_19_), channel_id=1, source_target_pairs={{0,2},{1,3},{2,0},{3,1},{4,6},{5,7},{6,4},{7,5},{8,10},{9,11},{10,... | collective-permute-start | bytes 1572872 | tf_op jit(solution)/shard_map/ppermute | solution.py:543
  14.8 3.0 %shard_map.273 = (f32[1536,512]{1,0:T(8,128)S(1)}, f32[12,512]{1,0:T(8,128)S(1)}, f32[8,512]{1,0:T(8,128)S(1)}) custom-call(s32[3]{0:T(128)S(1)} %pad_add_fusion.where_ref, bf16[1536,512]{1,0:T(8,128)(2,1)S(1)} %get-tuple-element.73.low_ref.refs_4_, bf16[144,512]{1,0:T(8,128)(2,1)S(1)} %shard_map.271.a0.refs_8_.refs_11_, ...), custom_call_target="tpu_custom_call" | custom-call | flops 1 | bytes 13200000 | tf_op jit(solution)/shard_map/pallas_call | solution.py:649
  17.7 1.6 %collective-permute-start.3 = (f32[12,512]{1,0:T(8,128)S(1)}, f32[12,512]{1,0:T(8,128)S(1)}, u32[]{:S(2)}, u32[]{:S(2)}) collective-permute-start(f32[12,512]{1,0:T(8,128)S(1)} %get-tuple-element.75.mine_ref), channel_id=1, source_target_pairs={{0,4},{4,0},{8,12},{12,8},{16,20},{20,16},{24,28},{28,24},{1,5},{5... | collective-permute-start | bytes 73736 | tf_op jit(solution)/shard_map/ppermute | solution.py:556
  19.3 2.1 %shard_map.274.refs_4_ = f32[1536,512]{1,0:T(8,128)S(1)} custom-call(f32[1536,512]{1,0:T(8,128)S(1)} %get-tuple-element.76.drive_ref, bf16[144,512]{1,0:T(8,128)(2,1)S(1)} %shard_map.271.a0.refs_8_.refs_11_, bf16[144,512]{1,0:T(8,128)(2,1)S(1)} %collective-permute-done.a1.refs_9_.refs_12_, bf16[144,512]{1,0:T(8,128)(2,1)S(1)} %collective-permute-done.1.a2.refs_10_.refs_13_, ...), custom_call_target="tpu_custom_call" | custom-call | flops 1 | bytes 13200000 | tf_op jit(solution)/shard_map/pallas_call | solution.py:665
  21.7 0.6 shard_map.275.mine_ref
  22.3 3.5 %collective-permute-start.4 = (f32[12,512]{1,0:T(8,128)S(1)}, f32[12,512]{1,0:T(8,128)S(1)}, u32[]{:S(2)}, u32[]{:S(2)}) collective-permute-start(f32[12,512]{1,0:T(8,128)S(1)} %shard_map.275.mine_ref), channel_id=1, source_target_pairs={{0,8},{4,12},{8,16},{12,20},{16,24},{20,28},{1,9},{5,13},{9,17},{1... | collective-permute-start | bytes 73736 | tf_op jit(solution)/shard_map/ppermute | solution.py:560
  25.9 1.5 %collective-permute-done.4.other_ref.refs_0_ = f32[12,512]{1,0:T(8,128)S(1)} collective-permute-done((f32[12,512]{1,0:T(8,128)S(1)}, f32[12,512]{1,0:T(8,128)S(1)}, u32[]{:S(2)}, u32[]{:S(2)}) %collective-permute-start.4) | collective-permute-done | bytes 24608 | tf_op jit(solution)/shard_map/ppermute | solution.py:560
  27.4 5.2 %collective-permute-start.5 = (f32[12,512]{1,0:T(8,128)S(1)}, f32[12,512]{1,0:T(8,128)S(1)}, u32[]{:S(2)}, u32[]{:S(2)}) collective-permute-start(f32[12,512]{1,0:T(8,128)S(1)} %shard_map.276), channel_id=1, source_target_pairs={{0,16},{4,20},{8,24},{12,28},{1,17},{5,21},{9,25},{13,29},{2,18},{... | collective-permute-start | bytes 73736 | tf_op jit(solution)/shard_map/ppermute | solution.py:560
  32.9 3.5 %shard_map.278.refs_6_ = bf16[1536,1024]{1,0:T(8,128)(2,1)S(1)} custom-call(s32[3]{0:T(128)S(1)} %pad_add_fusion.where_ref, bf16[1536,512]{1,0:T(8,128)(2,1)S(1)} %get-tuple-element.81.cotm_ref.refs_7_, bf16[384,512]{1,0:T(8,128)(2,1)S(1)} %get-tuple-element.83.b0.refs_15_, bf16[384,512]{1,0:T(8,128)(2,1)S(1)} %collective-permute-done.6.b1.refs_16_, ...), custom_call_target="tpu_custom_call" | custom-call | flops 1 | bytes 9900000 | tf_op jit(solution)/shard_map/pallas_call | solution.py:708
  36.8 1.6 %collective-permute-done.11.refs_22_ = bf16[512,512]{1,0:T(8,128)(2,1)S(1)} collective-permute-done((bf16[512,512]{1,0:T(8,128)(2,1)S(1)}, bf16[512,512]{1,0:T(8,128)(2,1)S(1)}, u32[]{:S(2)}, u32[]{:S(2)}) %collective-permute-start.11) | collective-permute-done | bytes 524320 | tf_op jit(solution)/shard_map/ppermute | solution.py:539
  38.5 18.7 %shard_map.279 = (bf16[1536,512]{1,0:T(8,128)(2,1)S(1)}, f32[1536,512]{1,0:T(8,128)S(1)}, f32[12,512]{1,0:T(8,128)S(1)}, bf16[1536,512]{1,0:T(8,128)(2,1)S(1)}, ...) custom-call(s32[3]{0:T(128)S(1)} %pad_add_fusion.where_ref, ...), custom_call_target="tpu_custom_call" | custom-call | flops 1 | bytes 69300000 | tf_op jit(solution)/shard_map/pallas_call | solution.py:721
  57.5 1.5 %collective-permute-start.12 = (f32[12,512]{1,0:T(8,128)S(1)}, f32[12,512]{1,0:T(8,128)S(1)}, u32[]{:S(2)}, u32[]{:S(2)}) collective-permute-start(f32[12,512]{1,0:T(8,128)S(1)} %get-tuple-element.88.mine_ref), channel_id=1, source_target_pairs={{0,4},{4,0},{8,12},{12,8},{16,20},{20,16},{24,28},{28,24},{1,5},{5... | collective-permute-start | bytes 73736 | tf_op jit(solution)/shard_map/ppermute | solution.py:556
  59.0 0.7 collective-permute-done.13.other_ref
  59.7 0.7 shard_map.280
  60.4 1.0 collective-permute-done.12.other_ref.refs_2_
  61.4 0.6 shard_map.281.mine_ref
  62.0 1.6 %collective-permute-start.17 = (bf16[448,512]{1,0:T(8,128)(2,1)S(1)}, bf16[448,512]{1,0:T(8,128)(2,1)S(1)}, u32[]{:S(2)}, u32[]{:S(2)}) collective-permute-start(bf16[448,512]{1,0:T(8,128)(2,1)S(1)} %get-tuple-element.98), channel_id=1, source_target_pairs={{0,4},{4,0},{8,12},{12,8},{16,20},{20,16},{24,28},{28,24},{1,5},{5... | collective-permute-start | bytes 1376264 | tf_op jit(solution)/shard_map/ppermute | solution.py:556
  63.5 1.3 %collective-permute-start.14 = (f32[12,512]{1,0:T(8,128)S(1)}, f32[12,512]{1,0:T(8,128)S(1)}, u32[]{:S(2)}, u32[]{:S(2)}) collective-permute-start(f32[12,512]{1,0:T(8,128)S(1)} %shard_map.281.mine_ref), channel_id=1, source_target_pairs={{8,0},{12,4},{16,8},{20,12},{24,16},{28,20},{9,1},{13,5},{17,9},{2... | collective-permute-start | bytes 73736 | tf_op jit(solution)/shard_map/ppermute | solution.py:560
  64.8 4.5 %collective-permute-done.14.other_ref.refs_0_ = f32[12,512]{1,0:T(8,128)S(1)} collective-permute-done((f32[12,512]{1,0:T(8,128)S(1)}, f32[12,512]{1,0:T(8,128)S(1)}, u32[]{:S(2)}, u32[]{:S(2)}) %collective-permute-start.14) | collective-permute-done | bytes 24608 | tf_op jit(solution)/shard_map/ppermute | solution.py:560
  69.4 1.3 %collective-permute-start.16 = (f32[12,512]{1,0:T(8,128)S(1)}, f32[12,512]{1,0:T(8,128)S(1)}, u32[]{:S(2)}, u32[]{:S(2)}) collective-permute-start(f32[12,512]{1,0:T(8,128)S(1)} %shard_map.282), channel_id=1, source_target_pairs={{16,0},{20,4},{24,8},{28,12},{17,1},{21,5},{25,9},{29,13},{18,2},{... | collective-permute-start | bytes 73736 | tf_op jit(solution)/shard_map/ppermute | solution.py:560
  70.7 6.4 %shard_map.283 = (bf16[3072,512]{1,0:T(8,128)(2,1)}, bf16[1536,512]{1,0:T(8,128)(2,1)S(1)}) custom-call(s32[3]{0:T(128)S(1)} %pad_add_fusion.where_ref, s32[24]{0:T(128)S(1)} %copy-done.3, bf16[3072,512]{1,0:T(8,128)(2,1)} %bitcast.32, bf16[1536,1024]{1,0:T(8,128)(2,1)S(1)} %get-tuple-element.93.hid_ref, bf16[384,512]{1,0:T(8,128)(2,1)S(1)} %get-tuple-element.83.b0.refs_15_, ...), custom_call_target="tpu_custom_call" | custom-call | flops 1 | bytes 16500000 | tf_op jit(solution)/shard_map/pallas_call | solution.py:794
  77.0 0.7 shard_map.285
  77.7 1.6 %collective-permute-start.18 = (bf16[112,512]{1,0:T(8,128)(2,1)S(1)}, bf16[112,512]{1,0:T(8,128)(2,1)S(1)}, u32[]{:S(2)}, u32[]{:S(2)}) collective-permute-start(bf16[112,512]{1,0:T(8,128)(2,1)S(1)} %get-tuple-element.109), channel_id=1, source_target_pairs={{0,8},{4,12},{8,0},{12,4},{16,24},{20,28},{24,16},{28,20},{1,9},{5... | collective-permute-start | bytes 344072 | tf_op jit(solution)/shard_map/ppermute | solution.py:556
  79.3 3.5 %collective-permute-start.19 = (bf16[112,512]{1,0:T(8,128)(2,1)S(1)}, bf16[112,512]{1,0:T(8,128)(2,1)S(1)}, u32[]{:S(2)}, u32[]{:S(2)}) collective-permute-start(bf16[112,512]{1,0:T(8,128)(2,1)S(1)} %get-tuple-element.110), channel_id=1, source_target_pairs={{0,16},{4,20},{8,24},{12,28},{16,0},{20,4},{24,8},{28,12},{1,17},{... | collective-permute-start | bytes 344072 | tf_op jit(solution)/shard_map/ppermute | solution.py:556
  82.9 6.7 %shard_map.286 = (f32[3072,512]{1,0:T(8,128)}, bf16[1536,512]{1,0:T(8,128)(2,1)S(1)}, bf16[144,512]{1,0:T(8,128)(2,1)S(1)}, bf16[144,512]{1,0:T(8,128)(2,1)S(1)}) custom-call(s32[3]{0:T(128)S(1)} %pad_add_fusion.where_ref, f32[12,512]{1,0:T(8,128)S(1)} %collective-permute-done.14.other_ref.refs_0_, f32[12,512]{1,0:T(8,128)S(1)} %collective-permute-done.16.refs_1_, ...), custom_call_target="tpu_custom_call" | custom-call | flops 1 | bytes 26400000 | tf_op jit(solution)/shard_map/pallas_call | solution.py:818
  90.5 0.9 collective-permute-done.21
  91.6 0.6 collective-permute-start.30
  92.2 3.5 %collective-permute-start.25 = (bf16[112,512]{1,0:T(8,128)(2,1)S(1)}, bf16[112,512]{1,0:T(8,128)(2,1)S(1)}, u32[]{:S(2)}, u32[]{:S(2)}) collective-permute-start(bf16[112,512]{1,0:T(8,128)(2,1)S(1)} %add_convert_fusion.3.refs_0_), channel_id=1, source_target_pairs={{0,24},{4,28},{8,16},{12,20},{16,8},{20,12},{24,0},{28,4},{1,25},{... | collective-permute-start | bytes 344072 | tf_op jit(solution)/shard_map/ppermute | solution.py:556
  95.7 2.0 %collective-permute-done.30 = bf16[144,512]{1,0:T(8,128)(2,1)S(1)} collective-permute-done((bf16[144,512]{1,0:T(8,128)(2,1)S(1)}, bf16[144,512]{1,0:T(8,128)(2,1)S(1)}, u32[]{:S(2)}, u32[]{:S(2)}) %collective-permute-start.30) | collective-permute-done | bytes 147488 | tf_op jit(solution)/shard_map/ppermute | solution.py:556
  97.8 1.8 %collective-permute-start.23 = (bf16[112,512]{1,0:T(8,128)(2,1)S(1)}, bf16[112,512]{1,0:T(8,128)(2,1)S(1)}, u32[]{:S(2)}, u32[]{:S(2)}) collective-permute-start(bf16[112,512]{1,0:T(8,128)(2,1)S(1)} %add_convert_fusion.3.refs_0_), channel_id=1, source_target_pairs={{0,8},{4,12},{8,0},{12,4},{16,24},{20,28},{24,16},{28,20},{1,9},{5... | collective-permute-start | bytes 344072 | tf_op jit(solution)/shard_map/ppermute | solution.py:556
  99.6 2.2 %shard_map.284 = bf16[3072,512]{1,0:T(8,128)(2,1)} custom-call(s32[3]{0:T(128)S(1)} %pad_add_fusion.where_ref, bf16[3072,512]{1,0:T(8,128)(2,1)} %get-tuple-element.94.all_ref, bf16[1536,512]{1,0:T(8,128)(2,1)S(1)} %collective-permute-done.15.other_ref), custom_call_target="tpu_custom_call", output_to_operand_aliasing={{}: (1, {})} | custom-call | flops 1 | bytes 6600000 | tf_op jit(solution)/shard_map/pallas_call | solution.py:881
  101.8 2.6 %shard_map.287 = f32[3072,512]{1,0:T(8,128)} custom-call(s32[3]{0:T(128)S(1)} %pad_add_fusion.where_ref, f32[3072,512]{1,0:T(8,128)} %get-tuple-element.105.all_ref, bf16[1536,512]{1,0:T(8,128)(2,1)S(1)} %collective-permute-done.22.other_ref), custom_call_target="tpu_custom_call", output_to_operand_aliasing={{}: (1, {})} | custom-call | flops 1 | bytes 6600000 | tf_op jit(solution)/shard_map/pallas_call | solution.py:881
  104.5 1.4 %collective-permute-done.24.refs_2_ = bf16[112,512]{1,0:T(8,128)(2,1)S(1)} collective-permute-done((bf16[112,512]{1,0:T(8,128)(2,1)S(1)}, bf16[112,512]{1,0:T(8,128)(2,1)S(1)}, u32[]{:S(2)}, u32[]{:S(2)}) %collective-permute-start.24) | collective-permute-done | bytes 114720 | tf_op jit(solution)/shard_map/ppermute | solution.py:556
  105.9 1.5 %collective-permute-start.26 = (bf16[112,512]{1,0:T(8,128)(2,1)S(1)}, bf16[112,512]{1,0:T(8,128)(2,1)S(1)}, u32[]{:S(2)}, u32[]{:S(2)}) collective-permute-start(bf16[112,512]{1,0:T(8,128)(2,1)S(1)} %add_convert_fusion.3.refs_0_), channel_id=1, source_target_pairs={{0,4},{4,0},{8,12},{12,8},{16,20},{20,16},{24,28},{28,24},{1,5},{5... | collective-permute-start | bytes 344072 | tf_op jit(solution)/shard_map/ppermute | solution.py:556
  107.4 0.5 collective-permute-start.27
  108.0 3.2 %collective-permute-done.31 = bf16[144,512]{1,0:T(8,128)(2,1)S(1)} collective-permute-done((bf16[144,512]{1,0:T(8,128)(2,1)S(1)}, bf16[144,512]{1,0:T(8,128)(2,1)S(1)}, u32[]{:S(2)}, u32[]{:S(2)}) %collective-permute-start.31) | collective-permute-done | bytes 147488 | tf_op jit(solution)/shard_map/ppermute | solution.py:556
  111.7 1.2 collective-permute-done.27.refs_5_
  112.9 2.6 %collective-permute-start.32 = (bf16[144,512]{1,0:T(8,128)(2,1)S(1)}, bf16[144,512]{1,0:T(8,128)(2,1)S(1)}, u32[]{:S(2)}, u32[]{:S(2)}) collective-permute-start(bf16[144,512]{1,0:T(8,128)(2,1)S(1)} %add_convert_fusion.refs_8_), channel_id=1, source_target_pairs={{0,16},{4,20},{8,24},{12,28},{16,0},{20,4},{24,8},{28,12},{1,17},{... | collective-permute-start | bytes 442376 | tf_op jit(solution)/shard_map/ppermute | solution.py:556
  115.5 1.5 %collective-permute-start.29 = (bf16[112,512]{1,0:T(8,128)(2,1)S(1)}, bf16[112,512]{1,0:T(8,128)(2,1)S(1)}, u32[]{:S(2)}, u32[]{:S(2)}) collective-permute-start(bf16[112,512]{1,0:T(8,128)(2,1)S(1)} %collective-permute-done.25.refs_3_), channel_id=1, source_target_pairs={{0,4},{4,0},{8,12},{12,8},{16,20},{20,16},{24,28},{28,24},{1,5},{5... | collective-permute-start | bytes 344072 | tf_op jit(solution)/shard_map/ppermute | solution.py:556
  117.0 0.5 collective-permute-start.28
  117.5 2.8 %collective-permute-done.29.refs_7_ = bf16[112,512]{1,0:T(8,128)(2,1)S(1)} collective-permute-done((bf16[112,512]{1,0:T(8,128)(2,1)S(1)}, bf16[112,512]{1,0:T(8,128)(2,1)S(1)}, u32[]{:S(2)}, u32[]{:S(2)}) %collective-permute-start.29) | collective-permute-done | bytes 114720 | tf_op jit(solution)/shard_map/ppermute | solution.py:556
  120.3 1.5 %collective-permute-done.28.refs_6_ = bf16[112,512]{1,0:T(8,128)(2,1)S(1)} collective-permute-done((bf16[112,512]{1,0:T(8,128)(2,1)S(1)}, bf16[112,512]{1,0:T(8,128)(2,1)S(1)}, u32[]{:S(2)}, u32[]{:S(2)}) %collective-permute-start.28) | collective-permute-done | bytes 114720 | tf_op jit(solution)/shard_map/ppermute | solution.py:556
  121.8 3.0 %shard_map.288 = (f32[1,512]{1,0:T(1,128)}, f32[1,512]{1,0:T(1,128)}, f32[1,512]{1,0:T(1,128)}, f32[64,512]{1,0:T(8,128)}, f32[64,512]{1,0:T(8,128)}, /*index=5*...) custom-call(s32[3]{0:T(128)S(1)} %pad_add_fusion.where_ref, ...), custom_call_target="tpu_custom_call" | custom-call | flops 1 | bytes 9900000 | tf_op jit(solution)/shard_map/pallas_call | solution.py:907
  (49 shorter events, 3.9 us)
Async XLA Ops:
  2.3 8.6 %collective-permute-start.1 = (bf16[144,512]{1,0:T(8,128)(2,1)S(1)}, bf16[144,512]{1,0:T(8,128)(2,1)S(1)}, u32[]{:S(2)}, u32[]{:S(2)}) collective-permute-start(bf16[144,512]{1,0:T(8,128)(2,1)S(1)} %shard_map.271.a0.refs_8_.refs_11_), channel_id=1, source_target_pairs={{0,2},{1,3},{2,0},{3,1},{4,6},{5,7},{6,4},{7,5},{8,10},{9,11},{10,... | collective-permute-start | bytes 442376 | tf_op jit(solution)/shard_map/ppermute | solution.py:543
  5.3 0.7 copy-start.3
  12.2 15.2 %collective-permute-start.7 = (bf16[384,512]{1,0:T(8,128)(2,1)S(1)}, bf16[384,512]{1,0:T(8,128)(2,1)S(1)}, u32[]{:S(2)}, u32[]{:S(2)}) collective-permute-start(bf16[384,512]{1,0:T(8,128)(2,1)S(1)} %get-tuple-element.83.b0.refs_15_), channel_id=1, source_target_pairs={{0,2},{1,3},{2,0},{3,1},{4,6},{5,7},{6,4},{7,5},{8,10},{9,11},{10,... | collective-permute-start | bytes 1179656 | tf_op jit(solution)/shard_map/ppermute | solution.py:543
  12.2 2.5 %collective-permute-start = (bf16[144,512]{1,0:T(8,128)(2,1)S(1)}, bf16[144,512]{1,0:T(8,128)(2,1)S(1)}, u32[]{:S(2)}, u32[]{:S(2)}) collective-permute-start(bf16[144,512]{1,0:T(8,128)(2,1)S(1)} %shard_map.271.a0.refs_8_.refs_11_), channel_id=1, source_target_pairs={{0,1},{1,0},{2,3},{3,2},{4,5},{5,4},{6,7},{7,6},{8,9},{9,8},{10,11... | collective-permute-start | bytes 442376 | tf_op jit(solution)/shard_map/ppermute | solution.py:539
  12.3 2.5 %collective-permute-start.2 = (bf16[144,512]{1,0:T(8,128)(2,1)S(1)}, bf16[144,512]{1,0:T(8,128)(2,1)S(1)}, u32[]{:S(2)}, u32[]{:S(2)}) collective-permute-start(bf16[144,512]{1,0:T(8,128)(2,1)S(1)} %collective-permute-done.1.a2.refs_10_.refs_13_), channel_id=1, source_target_pairs={{0,1},{1,0},{2,3},{3,2},{4,5},{5,4},{6,7},{7,6},{8,9},{9,8},{10,11... | collective-permute-start | bytes 442376 | tf_op jit(solution)/shard_map/ppermute | solution.py:539
  12.8 23.7 %collective-permute-start.10 = (bf16[512,512]{1,0:T(8,128)(2,1)S(1)}, bf16[512,512]{1,0:T(8,128)(2,1)S(1)}, u32[]{:S(2)}, u32[]{:S(2)}) collective-permute-start(bf16[512,512]{1,0:T(8,128)(2,1)S(1)} %get-tuple-element.85.refs_19_), channel_id=1, source_target_pairs={{0,2},{1,3},{2,0},{3,1},{4,6},{5,7},{6,4},{7,5},{8,10},{9,11},{10,... | collective-permute-start | bytes 1572872 | tf_op jit(solution)/shard_map/ppermute | solution.py:543
  17.7 4.0 %collective-permute-start.3 = (f32[12,512]{1,0:T(8,128)S(1)}, f32[12,512]{1,0:T(8,128)S(1)}, u32[]{:S(2)}, u32[]{:S(2)}) collective-permute-start(f32[12,512]{1,0:T(8,128)S(1)} %get-tuple-element.75.mine_ref), channel_id=1, source_target_pairs={{0,4},{4,0},{8,12},{12,8},{16,20},{20,16},{24,28},{28,24},{1,5},{5... | collective-permute-start | bytes 73736 | tf_op jit(solution)/shard_map/ppermute | solution.py:556
  22.3 5.1 %collective-permute-start.4 = (f32[12,512]{1,0:T(8,128)S(1)}, f32[12,512]{1,0:T(8,128)S(1)}, u32[]{:S(2)}, u32[]{:S(2)}) collective-permute-start(f32[12,512]{1,0:T(8,128)S(1)} %shard_map.275.mine_ref), channel_id=1, source_target_pairs={{0,8},{4,12},{8,16},{12,20},{16,24},{20,28},{1,9},{5,13},{9,17},{1... | collective-permute-start | bytes 73736 | tf_op jit(solution)/shard_map/ppermute | solution.py:560
  25.8 7.1 %collective-permute-start.6 = (bf16[384,512]{1,0:T(8,128)(2,1)S(1)}, bf16[384,512]{1,0:T(8,128)(2,1)S(1)}, u32[]{:S(2)}, u32[]{:S(2)}) collective-permute-start(bf16[384,512]{1,0:T(8,128)(2,1)S(1)} %get-tuple-element.83.b0.refs_15_), channel_id=1, source_target_pairs={{0,1},{1,0},{2,3},{3,2},{4,5},{5,4},{6,7},{7,6},{8,9},{9,8},{10,11... | collective-permute-start | bytes 1179656 | tf_op jit(solution)/shard_map/ppermute | solution.py:539
  27.4 5.6 %collective-permute-start.8 = (bf16[384,512]{1,0:T(8,128)(2,1)S(1)}, bf16[384,512]{1,0:T(8,128)(2,1)S(1)}, u32[]{:S(2)}, u32[]{:S(2)}) collective-permute-start(bf16[384,512]{1,0:T(8,128)(2,1)S(1)} %collective-permute-done.7.b2.refs_17_), channel_id=1, source_target_pairs={{0,1},{1,0},{2,3},{3,2},{4,5},{5,4},{6,7},{7,6},{8,9},{9,8},{10,11... | collective-permute-start | bytes 1179656 | tf_op jit(solution)/shard_map/ppermute | solution.py:539
  27.4 9.1 %collective-permute-start.5 = (f32[12,512]{1,0:T(8,128)S(1)}, f32[12,512]{1,0:T(8,128)S(1)}, u32[]{:S(2)}, u32[]{:S(2)}) collective-permute-start(f32[12,512]{1,0:T(8,128)S(1)} %shard_map.276), channel_id=1, source_target_pairs={{0,16},{4,20},{8,24},{12,28},{1,17},{5,21},{9,25},{13,29},{2,18},{... | collective-permute-start | bytes 73736 | tf_op jit(solution)/shard_map/ppermute | solution.py:560
  32.6 4.2 %collective-permute-start.9 = (bf16[512,512]{1,0:T(8,128)(2,1)S(1)}, bf16[512,512]{1,0:T(8,128)(2,1)S(1)}, u32[]{:S(2)}, u32[]{:S(2)}) collective-permute-start(bf16[512,512]{1,0:T(8,128)(2,1)S(1)} %get-tuple-element.85.refs_19_), channel_id=1, source_target_pairs={{0,1},{1,0},{2,3},{3,2},{4,5},{5,4},{6,7},{7,6},{8,9},{9,8},{10,11... | collective-permute-start | bytes 1572872 | tf_op jit(solution)/shard_map/ppermute | solution.py:539
  32.9 5.6 %copy-start = (f32[512]{0:T(512)S(1)}, f32[512]{0:T(512)}, u32[]{:S(2)}) copy-start(f32[512]{0:T(512)} %param.18) | copy-start | bytes 6148
  32.9 5.6 %copy-start.1 = (f32[512]{0:T(512)S(1)}, f32[512]{0:T(512)}, u32[]{:S(2)}) copy-start(f32[512]{0:T(512)} %param.19) | copy-start | bytes 6148
  32.9 5.6 %copy-start.2 = (f32[512]{0:T(512)S(1)}, f32[512]{0:T(512)}, u32[]{:S(2)}) copy-start(f32[512]{0:T(512)} %param.20) | copy-start | bytes 6148
  36.5 2.0 %collective-permute-start.11 = (bf16[512,512]{1,0:T(8,128)(2,1)S(1)}, bf16[512,512]{1,0:T(8,128)(2,1)S(1)}, u32[]{:S(2)}, u32[]{:S(2)}) collective-permute-start(bf16[512,512]{1,0:T(8,128)(2,1)S(1)} %collective-permute-done.10.refs_21_), channel_id=1, source_target_pairs={{0,1},{1,0},{2,3},{3,2},{4,5},{5,4},{6,7},{7,6},{8,9},{9,8},{10,11... | collective-permute-start | bytes 1572872 | tf_op jit(solution)/shard_map/ppermute | solution.py:539
  57.2 2.5 %collective-permute-start.13 = (bf16[896,512]{1,0:T(8,128)(2,1)S(1)}, bf16[896,512]{1,0:T(8,128)(2,1)S(1)}, u32[]{:S(2)}, u32[]{:S(2)}) collective-permute-start(bf16[896,512]{1,0:T(8,128)(2,1)S(1)} %get-tuple-element.90), channel_id=1, source_target_pairs={{0,1},{1,0},{2,3},{3,2},{4,5},{5,4},{6,7},{7,6},{8,9},{9,8},{10,11... | collective-permute-start | bytes 2752520 | tf_op jit(solution)/shard_map/ppermute | solution.py:539
  57.5 3.9 %collective-permute-start.12 = (f32[12,512]{1,0:T(8,128)S(1)}, f32[12,512]{1,0:T(8,128)S(1)}, u32[]{:S(2)}, u32[]{:S(2)}) collective-permute-start(f32[12,512]{1,0:T(8,128)S(1)} %get-tuple-element.88.mine_ref), channel_id=1, source_target_pairs={{0,4},{4,0},{8,12},{12,8},{16,20},{20,16},{24,28},{28,24},{1,5},{5... | collective-permute-start | bytes 73736 | tf_op jit(solution)/shard_map/ppermute | solution.py:556
  62.0 15.0 %collective-permute-start.17 = (bf16[448,512]{1,0:T(8,128)(2,1)S(1)}, bf16[448,512]{1,0:T(8,128)(2,1)S(1)}, u32[]{:S(2)}, u32[]{:S(2)}) collective-permute-start(bf16[448,512]{1,0:T(8,128)(2,1)S(1)} %get-tuple-element.98), channel_id=1, source_target_pairs={{0,4},{4,0},{8,12},{12,8},{16,20},{20,16},{24,28},{28,24},{1,5},{5... | collective-permute-start | bytes 1376264 | tf_op jit(solution)/shard_map/ppermute | solution.py:556
  63.5 5.8 %collective-permute-start.14 = (f32[12,512]{1,0:T(8,128)S(1)}, f32[12,512]{1,0:T(8,128)S(1)}, u32[]{:S(2)}, u32[]{:S(2)}) collective-permute-start(f32[12,512]{1,0:T(8,128)S(1)} %shard_map.281.mine_ref), channel_id=1, source_target_pairs={{8,0},{12,4},{16,8},{20,12},{24,16},{28,20},{9,1},{13,5},{17,9},{2... | collective-permute-start | bytes 73736 | tf_op jit(solution)/shard_map/ppermute | solution.py:560
  69.4 7.7 %collective-permute-start.16 = (f32[12,512]{1,0:T(8,128)S(1)}, f32[12,512]{1,0:T(8,128)S(1)}, u32[]{:S(2)}, u32[]{:S(2)}) collective-permute-start(f32[12,512]{1,0:T(8,128)S(1)} %shard_map.282), channel_id=1, source_target_pairs={{16,0},{20,4},{24,8},{28,12},{17,1},{21,5},{25,9},{29,13},{18,2},{... | collective-permute-start | bytes 73736 | tf_op jit(solution)/shard_map/ppermute | solution.py:560
  77.7 11.9 %collective-permute-start.18 = (bf16[112,512]{1,0:T(8,128)(2,1)S(1)}, bf16[112,512]{1,0:T(8,128)(2,1)S(1)}, u32[]{:S(2)}, u32[]{:S(2)}) collective-permute-start(bf16[112,512]{1,0:T(8,128)(2,1)S(1)} %get-tuple-element.109), channel_id=1, source_target_pairs={{0,8},{4,12},{8,0},{12,4},{16,24},{20,28},{24,16},{28,20},{1,9},{5... | collective-permute-start | bytes 344072 | tf_op jit(solution)/shard_map/ppermute | solution.py:556
  79.3 10.6 %collective-permute-start.19 = (bf16[112,512]{1,0:T(8,128)(2,1)S(1)}, bf16[112,512]{1,0:T(8,128)(2,1)S(1)}, u32[]{:S(2)}, u32[]{:S(2)}) collective-permute-start(bf16[112,512]{1,0:T(8,128)(2,1)S(1)} %get-tuple-element.110), channel_id=1, source_target_pairs={{0,16},{4,20},{8,24},{12,28},{16,0},{20,4},{24,8},{28,12},{1,17},{... | collective-permute-start | bytes 344072 | tf_op jit(solution)/shard_map/ppermute | solution.py:556
  82.9 7.0 %collective-permute-start.20 = (bf16[112,512]{1,0:T(8,128)(2,1)S(1)}, bf16[112,512]{1,0:T(8,128)(2,1)S(1)}, u32[]{:S(2)}, u32[]{:S(2)}) collective-permute-start(bf16[112,512]{1,0:T(8,128)(2,1)S(1)} %get-tuple-element.111), channel_id=1, source_target_pairs={{0,24},{4,28},{8,16},{12,20},{16,8},{20,12},{24,0},{28,4},{1,25},{... | collective-permute-start | bytes 344072 | tf_op jit(solution)/shard_map/ppermute | solution.py:556
  90.0 1.4 %collective-permute-start.21 = (bf16[144,512]{1,0:T(8,128)(2,1)S(1)}, bf16[144,512]{1,0:T(8,128)(2,1)S(1)}, u32[]{:S(2)}, u32[]{:S(2)}) collective-permute-start(bf16[144,512]{1,0:T(8,128)(2,1)S(1)} %get-tuple-element.112), channel_id=1, source_target_pairs={{0,1},{1,0},{2,3},{3,2},{4,5},{5,4},{6,7},{7,6},{8,9},{9,8},{10,11... | collective-permute-start | bytes 442376 | tf_op jit(solution)/shard_map/ppermute | solution.py:539
  90.0 9.6 %collective-permute-start.15 = (bf16[1536,512]{1,0:T(8,128)(2,1)S(1)}, bf16[1536,512]{1,0:T(8,128)(2,1)S(1)}, u32[]{:S(2)}, u32[]{:S(2)}) collective-permute-start(bf16[1536,512]{1,0:T(8,128)(2,1)S(1)} %get-tuple-element.95), channel_id=1, source_target_pairs={{0,1},{1,0},{2,3},{3,2},{4,5},{5,4},{6,7},{7,6},{8,9},{9,8},{10,11... | collective-permute-start | bytes 4718600 | tf_op jit(solution)/shard_map/ppermute | solution.py:539
  91.4 10.4 %collective-permute-start.22 = (bf16[1536,512]{1,0:T(8,128)(2,1)S(1)}, bf16[1536,512]{1,0:T(8,128)(2,1)S(1)}, u32[]{:S(2)}, u32[]{:S(2)}) collective-permute-start(bf16[1536,512]{1,0:T(8,128)(2,1)S(1)} %get-tuple-element.113), channel_id=1, source_target_pairs={{0,1},{1,0},{2,3},{3,2},{4,5},{5,4},{6,7},{7,6},{8,9},{9,8},{10,11... | collective-permute-start | bytes 4718600 | tf_op jit(solution)/shard_map/ppermute | solution.py:539
  91.6 6.1 %collective-permute-start.30 = (bf16[144,512]{1,0:T(8,128)(2,1)S(1)}, bf16[144,512]{1,0:T(8,128)(2,1)S(1)}, u32[]{:S(2)}, u32[]{:S(2)}) collective-permute-start(bf16[144,512]{1,0:T(8,128)(2,1)S(1)} %add_convert_fusion.2), channel_id=1, source_target_pairs={{0,4},{4,0},{8,12},{12,8},{16,20},{20,16},{24,28},{28,24},{1,5},{5... | collective-permute-start | bytes 442376 | tf_op jit(solution)/shard_map/ppermute | solution.py:556
  92.2 12.3 %collective-permute-start.25 = (bf16[112,512]{1,0:T(8,128)(2,1)S(1)}, bf16[112,512]{1,0:T(8,128)(2,1)S(1)}, u32[]{:S(2)}, u32[]{:S(2)}) collective-permute-start(bf16[112,512]{1,0:T(8,128)(2,1)S(1)} %add_convert_fusion.3.refs_0_), channel_id=1, source_target_pairs={{0,24},{4,28},{8,16},{12,20},{16,8},{20,12},{24,0},{28,4},{1,25},{... | collective-permute-start | bytes 344072 | tf_op jit(solution)/shard_map/ppermute | solution.py:556
  95.7 10.2 %collective-permute-start.24 = (bf16[112,512]{1,0:T(8,128)(2,1)S(1)}, bf16[112,512]{1,0:T(8,128)(2,1)S(1)}, u32[]{:S(2)}, u32[]{:S(2)}) collective-permute-start(bf16[112,512]{1,0:T(8,128)(2,1)S(1)} %add_convert_fusion.3.refs_0_), channel_id=1, source_target_pairs={{0,16},{4,20},{8,24},{12,28},{16,0},{20,4},{24,8},{28,12},{1,17},{... | collective-permute-start | bytes 344072 | tf_op jit(solution)/shard_map/ppermute | solution.py:556
  97.8 8.2 %collective-permute-start.23 = (bf16[112,512]{1,0:T(8,128)(2,1)S(1)}, bf16[112,512]{1,0:T(8,128)(2,1)S(1)}, u32[]{:S(2)}, u32[]{:S(2)}) collective-permute-start(bf16[112,512]{1,0:T(8,128)(2,1)S(1)} %add_convert_fusion.3.refs_0_), channel_id=1, source_target_pairs={{0,8},{4,12},{8,0},{12,4},{16,24},{20,28},{24,16},{28,20},{1,9},{5... | collective-permute-start | bytes 344072 | tf_op jit(solution)/shard_map/ppermute | solution.py:556
  105.9 5.2 %collective-permute-start.31 = (bf16[144,512]{1,0:T(8,128)(2,1)S(1)}, bf16[144,512]{1,0:T(8,128)(2,1)S(1)}, u32[]{:S(2)}, u32[]{:S(2)}) collective-permute-start(bf16[144,512]{1,0:T(8,128)(2,1)S(1)} %add_convert_fusion.1), channel_id=1, source_target_pairs={{0,8},{4,12},{8,0},{12,4},{16,24},{20,28},{24,16},{28,20},{1,9},{5... | collective-permute-start | bytes 442376 | tf_op jit(solution)/shard_map/ppermute | solution.py:556
  105.9 5.7 %collective-permute-start.26 = (bf16[112,512]{1,0:T(8,128)(2,1)S(1)}, bf16[112,512]{1,0:T(8,128)(2,1)S(1)}, u32[]{:S(2)}, u32[]{:S(2)}) collective-permute-start(bf16[112,512]{1,0:T(8,128)(2,1)S(1)} %add_convert_fusion.3.refs_0_), channel_id=1, source_target_pairs={{0,4},{4,0},{8,12},{12,8},{16,20},{20,16},{24,28},{28,24},{1,5},{5... | collective-permute-start | bytes 344072 | tf_op jit(solution)/shard_map/ppermute | solution.py:556
  107.4 5.5 %collective-permute-start.27 = (bf16[112,512]{1,0:T(8,128)(2,1)S(1)}, bf16[112,512]{1,0:T(8,128)(2,1)S(1)}, u32[]{:S(2)}, u32[]{:S(2)}) collective-permute-start(bf16[112,512]{1,0:T(8,128)(2,1)S(1)} %collective-permute-done.23.refs_1_), channel_id=1, source_target_pairs={{0,4},{4,0},{8,12},{12,8},{16,20},{20,16},{24,28},{28,24},{1,5},{5... | collective-permute-start | bytes 344072 | tf_op jit(solution)/shard_map/ppermute | solution.py:556
  112.9 8.9 %collective-permute-start.32 = (bf16[144,512]{1,0:T(8,128)(2,1)S(1)}, bf16[144,512]{1,0:T(8,128)(2,1)S(1)}, u32[]{:S(2)}, u32[]{:S(2)}) collective-permute-start(bf16[144,512]{1,0:T(8,128)(2,1)S(1)} %add_convert_fusion.refs_8_), channel_id=1, source_target_pairs={{0,16},{4,20},{8,24},{12,28},{16,0},{20,4},{24,8},{28,12},{1,17},{... | collective-permute-start | bytes 442376 | tf_op jit(solution)/shard_map/ppermute | solution.py:556
  115.5 4.8 %collective-permute-start.29 = (bf16[112,512]{1,0:T(8,128)(2,1)S(1)}, bf16[112,512]{1,0:T(8,128)(2,1)S(1)}, u32[]{:S(2)}, u32[]{:S(2)}) collective-permute-start(bf16[112,512]{1,0:T(8,128)(2,1)S(1)} %collective-permute-done.25.refs_3_), channel_id=1, source_target_pairs={{0,4},{4,0},{8,12},{12,8},{16,20},{20,16},{24,28},{28,24},{1,5},{5... | collective-permute-start | bytes 344072 | tf_op jit(solution)/shard_map/ppermute | solution.py:556
  117.0 4.8 %collective-permute-start.28 = (bf16[112,512]{1,0:T(8,128)(2,1)S(1)}, bf16[112,512]{1,0:T(8,128)(2,1)S(1)}, u32[]{:S(2)}, u32[]{:S(2)}) collective-permute-start(bf16[112,512]{1,0:T(8,128)(2,1)S(1)} %collective-permute-done.24.refs_2_), channel_id=1, source_target_pairs={{0,4},{4,0},{8,12},{12,8},{16,20},{20,16},{24,28},{28,24},{1,5},{5... | collective-permute-start | bytes 344072 | tf_op jit(solution)/shard_map/ppermute | solution.py:556

commit v4 on v3

v4 whole, which is shorter than its diff:
```python
import functools
import math

import jax
import jax.numpy as jnp
from jax import lax
from jax.experimental import pallas as pl
from jax.experimental.pallas import tpu as pltpu
from jax.sharding import PartitionSpec as P

EPSILON = 1e-05
TENSOR = 4
TILE = 8
BLOCK = 256
PARAM_ROWS = 16
F32 = jnp.float32
BF16 = jnp.bfloat16
GELU_K = math.sqrt(2.0 / math.pi)
MIB = 1024 * 1024


def dot(left, right):
    return jnp.dot(left, right, preferred_element_type=F32)


def dot_nt(left, right):
    return lax.dot_general(left, right, (((1,), (1,)), ((), ())), preferred_element_type=F32)


def dot_tn(left, right):
    return lax.dot_general(left, right, (((0,), (0,)), ((), ())), preferred_element_type=F32)


def layer_norm(rows):
    centre = jnp.mean(rows, axis=-1, keepdims=True)
    shifted = rows - centre
    variance = jnp.mean(shifted * shifted, axis=-1, keepdims=True)
    inv_scale = lax.rsqrt(variance + EPSILON)
    return shifted * inv_scale, inv_scale


def cmul(ar, ai, br, bi):
    return ar * br - ai * bi, ar * bi + ai * br


def read_params(packs, row):
    total = None
    for pack in packs:
        rows = pack[row : row + PARAM_ROWS, :].astype(F32)
        total = rows if total is None else total + rows
    states = total.shape[1] // 2
    at = lambda k: total[k : k + 1, :states] + total[k + 3 : k + 4, :states] + total[k + 6 : k + 7, :states]
    return at(0), at(1), at(2)


def powers_of(decay_real, decay_imag, exponent):
    out_r = jnp.ones(exponent.shape, F32)
    out_i = jnp.zeros(exponent.shape, F32)
    br, bi = decay_real, decay_imag
    for bit in range(4):
        mr, mi = cmul(out_r, out_i, br, bi)
        on = ((exponent >> bit) & 1) == 1
        out_r = jnp.where(on, mr, out_r)
        out_i = jnp.where(on, mi, out_i)
        br, bi = cmul(br, bi, br, bi)
    return out_r, out_i


def fill_steps(decay_real, decay_imag, backwards, step_ref):
    states = decay_real.shape[1]
    row = lax.broadcasted_iota(jnp.int32, (TILE, states), 0)
    if backwards:
        row = TILE - 1 - row
    zero = jnp.zeros((TILE, states), F32)
    for k, shift in enumerate((1, 2, 4)):
        pr, pi = powers_of(decay_real, decay_imag, jnp.full((TILE, states), shift, jnp.int32))
        step_ref[k, 0] = jnp.where(row >= shift, pr, zero)
        step_ref[k, 1] = jnp.where(row >= shift, pi, zero)
    step_ref[3, 0], step_ref[3, 1] = powers_of(decay_real, decay_imag, row + 1)


def fill_powers(decay_real, decay_imag, backwards, first, full_ref):
    states = decay_real.shape[1]
    row = lax.broadcasted_iota(jnp.int32, (TILE, states), 0)
    if backwards:
        row = TILE - 1 - row
    pr, pi = powers_of(decay_real, decay_imag, row + first)
    er, ei = powers_of(decay_real, decay_imag, jnp.full((TILE, states), TILE, jnp.int32))
    tiles = full_ref.shape[1] // TILE
    for n in range(tiles):
        at = (tiles - 1 - n if backwards else n) * TILE
        full_ref[0, at : at + TILE, :] = pr
        full_ref[1, at : at + TILE, :] = pi
        pr, pi = cmul(pr, pi, er, ei)


def scan_block(drive_ref, out_ref, step_ref, length, backwards):
    rows, lanes = drive_ref.shape
    states = lanes // 2
    tiles = length // TILE
    table = [(step_ref[k, 0], step_ref[k, 1]) for k in range(4)]
    edge = 0 if backwards else TILE - 1
    for s in range(rows // length):
        cr = ci = None
        for n in range(tiles):
            at = s * length + (tiles - 1 - n if backwards else n) * TILE
            hr = drive_ref[at : at + TILE, :states]
            hi = drive_ref[at : at + TILE, states:]
            for k, shift in enumerate((1, 2, 4)):
                turn = TILE - shift if backwards else shift
                sr = pltpu.roll(hr, turn, 0)
                si = pltpu.roll(hi, turn, 0)
                mr, mi = cmul(table[k][0], table[k][1], sr, si)
                hr, hi = hr + mr, hi + mi
            if cr is not None:
                mr, mi = cmul(table[3][0], table[3][1], cr, ci)
                hr, hi = hr + mr, hi + mi
            out_ref[at : at + TILE, :states] = hr
            out_ref[at : at + TILE, states:] = hi
            cr, ci = hr[edge : edge + 1], hi[edge : edge + 1]


def each_block(rows, body):
    def step(block, carry):
        at = pl.multiple_of(block * BLOCK, BLOCK)
        body(block, lambda ref: ref.at[pl.ds(at, BLOCK), :])
        return carry

    lax.fori_loop(0, rows // BLOCK, step, 0)


def fetch(pairs, sems):
    copies = [pltpu.make_async_copy(src, dst, sems.at[n]) for n, (src, dst) in enumerate(pairs)]
    for copy in copies:
        copy.start()
    for copy in copies:
        copy.wait()


def half_copies(where_ref, src, dst, sems):
    rows = dst.shape[0]
    first = where_ref[1] * rows
    return [
        pltpu.make_async_copy(
            src.at[pl.ds(pl.multiple_of(first + n * BLOCK, BLOCK), BLOCK), :],
            dst.at[pl.ds(n * BLOCK, BLOCK), :],
            sems.at[n],
        )
        for n in range(rows // BLOCK)
    ]


def incoming(far_refs, beside_ref, odd, powers_ref, backwards, out_ref):
    states = out_ref.shape[1] // 2
    early, late = slice(0, states), slice(states, None)
    sr, si = far_refs[0][:, early], far_refs[0][:, late]
    for k in range(1, len(far_refs)):
        row = slice(4 + k, 5 + k)
        mr, mi = cmul(powers_ref[row, early], powers_ref[row, late], far_refs[k][:, early], far_refs[k][:, late])
        sr, si = sr + mr, si + mi
    mr, mi = cmul(powers_ref[0:1, early], powers_ref[0:1, late], sr, si)
    second = odd == (0 if backwards else 1)
    out_ref[:, early] = jnp.where(second, mr + beside_ref[:, early], sr)
    out_ref[:, late] = jnp.where(second, mi + beside_ref[:, late], si)


def join_kernel(mine_ref, other_ref, powers_ref, out_ref, *, row):
    states = out_ref.shape[1] // 2
    early, late = slice(0, states), slice(states, None)
    row = slice(row, row + 1)
    mr, mi = cmul(powers_ref[row, early], powers_ref[row, late], other_ref[:, early], other_ref[:, late])
    out_ref[:, early] = mine_ref[:, early] + mr
    out_ref[:, late] = mine_ref[:, late] + mi


def pair_kernel(where_ref, mine_ref, other_ref, powers_ref, out_ref, *, backwards):
    states = out_ref.shape[1] // 2
    second = where_ref[0] % 2 == (0 if backwards else 1)
    lr, li = powers_ref[0:1, :states], powers_ref[0:1, states:]
    pick = lambda first, part: jnp.where(second == first, other_ref[:, part], mine_ref[:, part])
    early, late = slice(0, states), slice(states, None)
    mr, mi = cmul(lr, li, pick(True, early), pick(True, late))
    out_ref[:, :states] = mr + pick(False, early)
    out_ref[:, states:] = mi + pick(False, late)


def assemble_input(packs, shard, out_ref):
    per = packs[0].shape[0] - PARAM_ROWS
    half = per // 2
    states = out_ref.shape[0] // 2
    for k, pack in enumerate(packs):
        at = pl.multiple_of((shard ^ k) * half, half)
        out_ref[pl.ds(at, half), :] = pack[:half, :]
        out_ref[pl.ds(states + at, half), :] = pack[half:per, :]


def input_pack_kernel(where_ref, in_real, in_imag, nu, theta, gamma, a_ref, logs, sems):
    per_s, width = in_real.shape
    fetch(
        [(in_real, a_ref.at[pl.ds(0, per_s), :]), (in_imag, a_ref.at[pl.ds(per_s, per_s), :])]
        + [(ref, logs.at[n]) for n, ref in enumerate((nu, theta, gamma))],
        sems,
    )
    modulus = jnp.exp(-jnp.exp(logs[0]))
    angle = jnp.exp(logs[1])
    rest = [modulus * jnp.cos(angle), modulus * jnp.sin(angle), jnp.exp(logs[2])]
    rows = []
    for _ in range(3):
        for n in range(3):
            high = rest[n].astype(BF16).astype(F32)
            rows.append(high)
            rest[n] = rest[n] - high
    table = jnp.concatenate(rows + [jnp.zeros((PARAM_ROWS - 9, per_s), F32)], axis=0)
    table = jnp.concatenate([table] * (width // per_s), axis=1)
    here = lax.broadcasted_iota(jnp.int32, (PARAM_ROWS, width), 1) // per_s == where_ref[2]
    a_ref[2 * per_s :, :] = jnp.where(here, table, 0.0).astype(BF16)


def weight_pack_kernel(out_real, out_imag, up, gate, down, b_ref, g_ref, sems):
    per_s, per_f = out_real.shape[0], down.shape[0]
    fetch(
        [
            (out_real, b_ref.at[pl.ds(0, per_s), :]),
            (out_imag, b_ref.at[pl.ds(per_s, per_s), :]),
            (down, b_ref.at[pl.ds(2 * per_s, per_f), :]),
            (up, g_ref.at[:, pl.ds(0, per_f)]),
            (gate, g_ref.at[:, pl.ds(per_f, per_f)]),
        ],
        sems,
    )


def mask_rows(lens_ref, where_ref, seq, seqs, length, width):
    left = lens_ref[where_ref[1] * seqs + seq] - where_ref[0] * length
    return lax.broadcasted_iota(jnp.int32, (length, width), 0) < left


def norm_kernel(
    where_ref, tok_all, cot_all, gain_all, bias_all, lens_all, low_ref, normed_ref, inv_ref, cotm_ref,
    tok, cot, gain_ref, bias_ref, lens_ref, sems, small_sems, *, length
):
    rows, width = low_ref.shape
    per_block = BLOCK // length
    halves = [half_copies(where_ref, src, dst, sems.at[n]) for n, (src, dst) in enumerate(((tok_all, tok), (cot_all, cot)))]
    for copies in zip(*halves):
        for copy in copies:
            copy.start()
    fetch([(gain_all, gain_ref), (bias_all, bias_ref), (lens_all, lens_ref)], small_sems)
    for block, copies in enumerate(zip(*halves)):
        for copy in copies:
            copy.wait()
        span = slice(block * BLOCK, (block + 1) * BLOCK)
        normed, inv_scale = layer_norm(tok[span, :].astype(F32))
        normed_ref[span, :] = normed
        inv_ref[span, :] = jnp.broadcast_to(inv_scale, (BLOCK, inv_ref.shape[1]))
        low_ref[span, :] = (normed * gain_ref[...] + bias_ref[...]).astype(BF16)
        for s in range(per_block):
            seq = block * per_block + s
            span = slice(seq * length, (seq + 1) * length)
            live = mask_rows(lens_ref, where_ref, seq, rows // length, length, width)
            cotm_ref[span, :] = jnp.where(live, cot[span, :].astype(F32), 0.0).astype(BF16)


def weighted_ends(drive_ref, weigh, length, first, ends_ref):
    rows, lanes = drive_ref.shape
    states = lanes // 2
    for s in range(rows // length):
        er = ei = jnp.zeros((TILE, states), F32)
        for n in range(length // TILE):
            at = s * length + n * TILE
            mr, mi = cmul(
                weigh[0, n * TILE : (n + 1) * TILE, :],
                weigh[1, n * TILE : (n + 1) * TILE, :],
                drive_ref[at : at + TILE, :states],
                drive_ref[at : at + TILE, states:],
            )
            er, ei = er + mr, ei + mi
        ends_ref[pl.ds(first + s, 1), :states] = jnp.sum(er, axis=0, keepdims=True)
        ends_ref[pl.ds(first + s, 1), states:] = jnp.sum(ei, axis=0, keepdims=True)


def drive_kernel(where_ref, low_all, a0, a1, a2, a3, drive_all, ends_ref, powers_ref, in_t, weigh, *, length):
    packs = (a0, a1, a2, a3)
    states = in_t.shape[0] // 2
    assemble_input(packs, where_ref[2], in_t)
    dr, di, gain = read_params(packs, a0.shape[0] - PARAM_ROWS)
    fill_powers(dr, di, True, 0, weigh)
    gam = jnp.concatenate([gain, gain], axis=1)
    lr, li = cmul(weigh[0, :1, :], weigh[1, :1, :], dr, di)
    rows = [(lr, li)] + [cmul(lr, li, lr, li)]
    for _ in range(2):
        rows.append(cmul(*rows[-1], *rows[-1]))
    rows.append((jnp.ones_like(lr), jnp.zeros_like(lr)))
    for _ in range(3):
        rows.append(cmul(*cmul(*rows[-1], *rows[-1]), *rows[1]))
    for k, (lr, li) in enumerate(rows):
        powers_ref[k : k + 1, :] = jnp.concatenate([lr, li], axis=1)
    per_block = BLOCK // length

    def body(block, view):
        low_ref, drive_ref = view(low_all), view(drive_all)
        drive_ref[...] = dot_nt(low_ref[...], in_t[...]) * gam
        weighted_ends(drive_ref, weigh, length, block * per_block, ends_ref)

    each_block(low_all.shape[0], body)


def scan_kernel(drive_all, a0, a1, a2, a3, local_all, step, *, length, backwards):
    dr, di, _ = read_params((a0, a1, a2, a3), a0.shape[0] - PARAM_ROWS)
    fill_steps(dr, di, backwards, step)
    each_block(
        drive_all.shape[0],
        lambda block, view: scan_block(view(drive_all), view(local_all), step, length, backwards),
    )


def hidden_kernel(where_ref, cotm_all, b0, b1, b2, b3, hg_all, *, per_s):
    shard = where_ref[2]
    per_f = hg_all.shape[1] // TENSOR

    def body(block, view):
        hg_ref, cotm = view(hg_all), view(cotm_all)[...]
        for k, pack in enumerate((b0, b1, b2, b3)):
            at = pl.multiple_of((shard ^ k) * per_f, per_f)
            hg_ref[:, pl.ds(at, per_f)] = dot_nt(cotm, pack[2 * per_s :, :]).astype(BF16)

    each_block(cotm_all.shape[0], body)


def middle_kernel(where_ref, *refs, length, levels):
    far_refs, refs = refs[:levels], refs[levels:]
    beside_ref, powers_ref, local_all, normed_all, hg_all, cotm_all, a0, a1, a2, a3 = refs[:10]
    gain_ref, bias_ref, skip_ref, b0, b1, b2, b3, g0, g1, g2, g3 = refs[10:21]
    state_all, back_all, backends_ref, ylow_all, hid_all, act_all, ul_half_all = refs[21:28]
    c_all, ug_all, weigh, full, carry, ul, sems = refs[28:]
    place, core, shard = where_ref[0], where_ref[1], where_ref[2]
    states = c_all.shape[0] // 2
    rows, width = normed_all.shape
    per_block = BLOCK // length
    per_s = states // TENSOR
    per_f = hid_all.shape[1] // TENSOR
    side = shard // 2

    copies = []
    for k, (pack, gates) in enumerate(((b0, g0), (b1, g1), (b2, g2), (b3, g3))):
        t = shard ^ k
        moves = (
            (pack.at[pl.ds(0, per_s), :], c_all.at[pl.ds(pl.multiple_of(t * per_s, per_s), per_s), :]),
            (pack.at[pl.ds(per_s, per_s), :], c_all.at[pl.ds(pl.multiple_of(states + t * per_s, per_s), per_s), :]),
            (gates, ug_all.at[:, pl.ds(pl.multiple_of(t * 2 * per_f, 2 * per_f), 2 * per_f)]),
        )
        for n, (src, dst) in enumerate(moves):
            copies.append(pltpu.make_async_copy(src, dst, sems.at[k, n]))
    for copy in copies:
        copy.start()
    dr, di, _ = read_params((a0, a1, a2, a3), a0.shape[0] - PARAM_ROWS)
    fill_powers(dr, di, False, 1, full)
    incoming(far_refs, beside_ref, place % 2, powers_ref, False, carry)
    fill_powers(dr, di, False, 0, weigh)
    for copy in copies:
        copy.wait()
    skip = skip_ref[...]
    skip_gain, skip_bias = gain_ref[...] * skip, bias_ref[...] * skip

    def body(block, view):
        local_ref, state_ref, hid_ref, ylow_ref = view(local_all), view(state_all), view(hid_all), view(ylow_all)
        hg_ref, act_ref, back_ref = view(hg_all), view(act_all), view(back_all)
        for s in range(per_block):
            seq = block * per_block + s
            span = slice(s * length, (s + 1) * length)
            sr = carry[pl.ds(seq, 1), :states]
            si = carry[pl.ds(seq, 1), states:]
            mr, mi = cmul(full[0], full[1], sr, si)
            state_ref[span, :states] = (local_ref[span, :states] + mr).astype(BF16)
            state_ref[span, states:] = (-(local_ref[span, states:] + mi)).astype(BF16)
        y = dot(state_ref[...], c_all[...]) + (view(normed_all)[...] * skip_gain + skip_bias)
        square = y * y
        th = jnp.tanh(y * (GELU_K + (GELU_K * 0.044715) * square))
        half_y = 0.5 * y
        act_ref[...] = (half_y + half_y * th).astype(BF16)
        slope = (0.5 + 0.5 * th) + half_y * (1.0 - th * th) * (GELU_K + (GELU_K * 3 * 0.044715) * square)
        act = act_ref[...]
        for t in range(TENSOR):
            both = dot(act, ug_all[:, 2 * per_f * t : 2 * per_f * (t + 1)])
            up = both[:, :per_f]
            th = 0.5 * jnp.tanh(0.5 * both[:, per_f:])
            sig = 0.5 + th
            hid_ref[:, per_f * t : per_f * (t + 1)] = (up * sig).astype(BF16)
            up_grad = hg_ref[:, per_f * t : per_f * (t + 1)].astype(F32) * sig
            ul[:, 2 * per_f * t : 2 * per_f * t + per_f] = up_grad.astype(BF16)
            ul[:, 2 * per_f * t + per_f : 2 * per_f * (t + 1)] = (up_grad * up * (0.5 - th)).astype(BF16)
        y_grad = dot_nt(ul[...], ug_all[...]) * slope
        ylow_ref[...] = y_grad.astype(BF16)
        back_ref[...] = dot_nt(ylow_ref[...], c_all[...])
        weighted_ends(back_ref, weigh, length, block * per_block, backends_ref)
        view(ul_half_all)[...] = ul[:, pl.ds(pl.multiple_of(side * 4 * per_f, 4 * per_f), 4 * per_f)]

    each_block(rows, body)


def weight_kernel(where_ref, hid_ref, cotm_ref, act_ref, ul_ref, state_ref, ylow_ref, own_ref, sent_ref):
    core, side = where_ref[1], where_ref[2] // 2
    states = state_ref.shape[1] // 2
    per_s = states // TENSOR
    per_f = hid_ref.shape[1] // TENSOR
    width = act_ref.shape[1]
    cols = [
        state_ref[:, pl.ds(pl.multiple_of(k * states + side * 2 * per_s, 2 * per_s), 2 * per_s)] for k in range(2)
    ]
    out_grad = dot_tn(jnp.concatenate(cols, axis=1), ylow_ref[...])
    act, cotm = act_ref[...], cotm_ref[...]
    for n, ref in ((1 - core, sent_ref), (core, own_ref)):
        ul = ul_ref[:, pl.ds(pl.multiple_of(n * 2 * per_f, 2 * per_f), 2 * per_f)]
        ref[2 * per_s + per_f : 2 * per_s + per_f + width, :] = dot_tn(act, ul).astype(ref.dtype)
        hid = hid_ref[:, pl.ds(pl.multiple_of((2 * side + n) * per_f, per_f), per_f)]
        ref[2 * per_s : 2 * per_s + per_f, :] = dot_tn(hid, cotm).astype(ref.dtype)
        for k in range(2):
            at = 2 * per_s * k
            part = jnp.where(n == 0, out_grad[at : at + per_s, :], out_grad[at + per_s : at + 2 * per_s, :])
            ref[k * per_s : (k + 1) * per_s, :] = part.astype(ref.dtype)


def down_kernel(where_ref, lens_ref, tok_all, hid_all, b0, b1, b2, b3, out_all, down_all, tok, sems, *, length, per_s):
    shard = where_ref[2]
    rows, width = out_all.shape
    per_block = BLOCK // length
    per_f = down_all.shape[0] // TENSOR
    copies = half_copies(where_ref, tok_all, tok, sems)
    for copy in copies:
        copy.start()
    for k, pack in enumerate((b0, b1, b2, b3)):
        down_all[pl.ds(pl.multiple_of((shard ^ k) * per_f, per_f), per_f), :] = pack[2 * per_s :, :]
    for copy in copies:
        copy.wait()

    def body(block, view):
        added = dot(view(hid_all)[...], down_all[...])
        out_ref, tok_ref = view(out_all), view(tok)
        for s in range(per_block):
            span = slice(s * length, (s + 1) * length)
            live = mask_rows(lens_ref, where_ref, block * per_block + s, rows // length, length, width)
            out_ref[span, :] = jnp.where(live, tok_ref[span, :].astype(F32) + added[span, :], 0.0).astype(BF16)

    each_block(rows, body)


def last_kernel(where_ref, *refs, length, levels):
    far_refs, refs = refs[:levels], refs[levels:]
    beside_ref, powers_ref, low_all, normed_all, inv_all, cotm_all, back_all, state_all, ylow_all = refs[:9]
    a0, a1, a2, a3, gain_ref, bias_ref, skip_ref, grad_all, own_ref, sent_ref = refs[9:19]
    in_t, full, carry, dlow, in_grad, lam_grad, vec_grad = refs[19:]
    place, core, shard = where_ref[0], where_ref[1], where_ref[2]
    states = in_t.shape[0] // 2
    rows, width = low_all.shape
    per_block = BLOCK // length
    per_s = states // TENSOR
    packs = (a0, a1, a2, a3)

    assemble_input(packs, shard, in_t)
    dr, di, gain = read_params(packs, a0.shape[0] - PARAM_ROWS)
    fill_powers(dr, di, True, 1, full)
    incoming(far_refs, beside_ref, place % 2, powers_ref, True, carry)
    in_grad[...] = jnp.zeros(in_grad.shape, F32)
    lam_grad[...] = jnp.zeros(lam_grad.shape, F32)
    vec_grad[...] = jnp.zeros(vec_grad.shape, F32)
    at = pl.multiple_of((shard // 2) * 2 * per_s, 2 * per_s)

    def body(block, view):
        back_ref, state_ref = view(back_all), view(state_all)
        for s in range(per_block):
            seq = block * per_block + s
            span = slice(s * length, (s + 1) * length)
            sr = carry[pl.ds(seq, 1), :states]
            si = carry[pl.ds(seq, 1), states:]
            mr, mi = cmul(full[0], full[1], sr, si)
            gr = back_ref[span, :states] + mr
            gi = back_ref[span, states:] + mi
            dlow[span, :states] = (gr * gain).astype(BF16)
            dlow[span, states:] = (gi * -gain).astype(BF16)
            nr = jnp.concatenate([gr[1:], sr], axis=0)
            ni = jnp.concatenate([gi[1:], si], axis=0)
            hr = state_ref[span, :states].astype(F32)
            hi = state_ref[span, states:].astype(F32)
            lam_grad[:, :states] += jnp.sum(nr * hr + ni * hi, axis=0, keepdims=True)
            lam_grad[:, states:] += jnp.sum(nr * hi - ni * hr, axis=0, keepdims=True)
        normed = view(normed_all)[...]
        ylow = view(ylow_all)[...].astype(F32)
        low = view(low_all)[...]
        u_grad = dot(dlow[...], in_t[...]) + ylow * skip_ref[...]
        vec_grad[0:1, :] += jnp.sum(u_grad * normed, axis=0, keepdims=True)
        vec_grad[1:2, :] += jnp.sum(u_grad, axis=0, keepdims=True)
        vec_grad[2:3, :] += jnp.sum(ylow * (normed * gain_ref[...] + bias_ref[...]), axis=0, keepdims=True)
        scaled = u_grad * gain_ref[...]
        grad = (
            scaled
            - jnp.mean(scaled, axis=-1, keepdims=True)
            - normed * jnp.mean(scaled * normed, axis=-1, keepdims=True)
        )
        view(grad_all)[...] = (view(cotm_all)[...].astype(F32) + view(inv_all)[:, :1] * grad).astype(BF16)
        for k in range(2):
            cols = dlow[:, pl.ds(k * states + at, 2 * per_s)]
            in_grad[2 * per_s * k : 2 * per_s * (k + 1), :] += dot_tn(cols, low)

    each_block(rows, body)
    small = jnp.concatenate(
        [vec_grad[:3, :], lam_grad[...], jnp.zeros((PARAM_ROWS - 4, width), F32)], axis=0
    ).astype(BF16)
    for n, ref in ((core, own_ref), (1 - core, sent_ref)):
        for k in range(2):
            part = in_grad[pl.ds(pl.multiple_of(2 * per_s * k + n * per_s, per_s), per_s), :]
            ref[k * per_s : (k + 1) * per_s, :] = part.astype(BF16)
        ref[2 * per_s :, :] = small


def join_halves_kernel(where_ref, own_ref, other_ref, out_ref, sems):
    rows = own_ref.shape[0]
    copies = [
        pltpu.make_async_copy(ref, out_ref.at[pl.ds(pl.multiple_of(n * rows, BLOCK), rows), :], sems.at[k])
        for k, (n, ref) in enumerate(((where_ref[1], own_ref), (1 - where_ref[1], other_ref)))
    ]
    for copy in copies:
        copy.start()
    for copy in copies:
        copy.wait()


def widen_halves_kernel(where_ref, own_ref, other_ref, out_ref, wide, sems):
    rows = own_ref.shape[0]
    slots = wide.shape[0]
    flying = []
    for n in range(2 * rows // BLOCK):
        slot = n % slots
        if n >= slots:
            flying[n - slots].wait()
        at = (n // 2) * BLOCK
        half, ref = ((where_ref[1], own_ref), (1 - where_ref[1], other_ref))[n % 2]
        wide[slot] = ref[at : at + BLOCK, :].astype(F32)
        copy = pltpu.make_async_copy(
            wide.at[slot], out_ref.at[pl.ds(pl.multiple_of(half * rows + at, BLOCK), BLOCK), :], sems.at[slot]
        )
        copy.start()
        flying.append(copy)
    for copy in flying[-slots:]:
        copy.wait()


def fold_kernel(where_ref, own_ref, other_ref, keep_ref, send_ref):
    half = keep_ref.shape[0]
    odd = where_ref[0] % 2
    at = pl.multiple_of(odd * half, 16)
    keep_ref[...] = own_ref[pl.ds(at, half), :] + other_ref[pl.ds(at, half), :].astype(F32)
    at = pl.multiple_of((1 - odd) * half, 16)
    send_ref[...] = (own_ref[pl.ds(at, half), :] + other_ref[pl.ds(at, half), :].astype(F32)).astype(BF16)


def deal_kernel(where_ref, own_ref, other_ref, keep_ref, *send_refs):
    rows = keep_ref.shape[0]
    for k, ref in enumerate((keep_ref,) + send_refs):
        at = pl.multiple_of(((where_ref[0] // 2) ^ k) * rows, 16)
        ref[...] = (own_ref[pl.ds(at, rows), :] + other_ref[pl.ds(at, rows), :].astype(F32)).astype(ref.dtype)


def finish_kernel(where_ref, *refs, ways):
    parts, refs = refs[: 2 * ways], refs[2 * ways :]
    mine_ref, other_ref, in_real, in_imag, nu, theta = refs[:6]
    vec_outs, (in_real_out, in_imag_out), log_outs = refs[6:9], refs[9:11], refs[11:14]
    real_ref, imag_ref, up_ref, gate_ref, down_ref, total, grads_ref, logs, fetched, sems, fetch_sems = refs[14:]
    fetch([(ref, fetched.at[n]) for n, ref in enumerate((nu, theta))], fetch_sems)
    nu, theta = fetched.at[0], fetched.at[1]
    place = where_ref[0]
    rows = parts[0].shape[0]
    for n, part in enumerate(parts):
        half = place % 2 if n < ways else 1 - place % 2
        at = (half * ways + ((place // 2) ^ (n % ways))) * rows
        total[pl.ds(pl.multiple_of(at, 16), rows), :] = part[...].astype(F32)
    per_s = real_ref.shape[0]
    per_f = down_ref.shape[0]
    moves = [
        (total.at[pl.ds(0, per_s), :], real_ref),
        (total.at[pl.ds(per_s, per_s), :], imag_ref),
        (total.at[pl.ds(2 * per_s, per_f), :], down_ref),
        (total.at[pl.ds(2 * per_s + per_f, up_ref.shape[0]), pl.ds(0, per_f)], up_ref),
        (total.at[pl.ds(2 * per_s + per_f, up_ref.shape[0]), pl.ds(per_f, per_f)], gate_ref),
    ]
    copies = [pltpu.make_async_copy(src, dst, sems.at[n]) for n, (src, dst) in enumerate(moves)]
    for copy in copies:
        copy.start()

    grads = mine_ref[...].astype(F32) + other_ref[...].astype(F32)
    grads_ref[...] = grads
    moves = [
        (grads_ref.at[pl.ds(0, per_s), :], in_real_out),
        (grads_ref.at[pl.ds(per_s, per_s), :], in_imag_out),
    ]
    moves += [(grads_ref.at[pl.ds(2 * per_s + n, 1), :], vec_outs[n]) for n in range(3)]
    more = [pltpu.make_async_copy(src, dst, sems.at[5 + n]) for n, (src, dst) in enumerate(moves)]
    for copy in more:
        copy.start()
    lam = [jnp.zeros((1, per_s), F32), jnp.zeros((1, per_s), F32)]
    for t in range(TENSOR):
        for n in range(2):
            at = (n * TENSOR + t) * per_s
            part = grads[2 * per_s + 3 : 2 * per_s + 4, at : at + per_s]
            lam[n] = jnp.where(where_ref[2] == t, part, lam[n])
    decay = jnp.exp(nu[...])
    modulus = jnp.exp(-decay)
    angle = jnp.exp(theta[...])
    cos, sin = jnp.cos(angle), jnp.sin(angle)
    logs[0] = -decay * modulus * (lam[0] * cos + lam[1] * sin)
    logs[1] = angle * modulus * (lam[1] * cos - lam[0] * sin)
    terms = in_real[...].astype(F32) * grads[:per_s, :] + in_imag[...].astype(F32) * grads[per_s : 2 * per_s, :]
    logs[2] = jnp.sum(terms.T, axis=0, keepdims=True)
    rest = [pltpu.make_async_copy(logs.at[n], log_outs[n], sems.at[10 + n]) for n in range(3)]
    for copy in rest:
        copy.start()
    for copy in copies + more + rest:
        copy.wait()


def near(value):
    return pltpu.with_memory_space_constraint(value, pltpu.VMEM)


def call(kernel, scalars, inputs, outs, scratch, vmem, far_inputs=(), far_outs=()):
    here, anywhere = pl.BlockSpec(memory_space=pltpu.VMEM), pl.BlockSpec(memory_space=pl.ANY)
    single = not isinstance(outs, list)
    listed = [outs] if single else outs
    shapes = [
        jax.ShapeDtypeStruct(*out) if n in far_outs else pltpu.VMEM(*out) for n, out in enumerate(listed)
    ]
    out_specs = [anywhere if n in far_outs else here for n in range(len(listed))]
    return pl.pallas_call(
        kernel,
        in_specs=[pl.BlockSpec(memory_space=pltpu.SMEM)] * len(scalars)
        + [anywhere if n in far_inputs else here for n in range(len(inputs))],
        out_specs=out_specs[0] if single else out_specs,
        out_shape=shapes[0] if single else shapes,
        scratch_shapes=scratch,
        compiler_params=pltpu.CompilerParams(vmem_limit_bytes=vmem * MIB),
    )(
        *scalars,
        *[
            pltpu.with_memory_space_constraint(v, pltpu.HBM) if n in far_inputs else near(v)
            for n, v in enumerate(inputs)
        ],
    )


def core_swap(value):
    return lax.ppermute(value, "tensor", [(t, t ^ 1) for t in range(TENSOR)])


def side_swap(value):
    return lax.ppermute(value, "tensor", [(t, t ^ 2) for t in range(TENSOR)])


def gather_tensor(own, *first):
    across = after(side_swap(own), *first)
    return own, core_swap(own), across, core_swap(across)


def after(value, *first):
    return lax.optimization_barrier((value,) + first)[0]


def flip_dp(value, bits, groups):
    return lax.ppermute(value, "dp", [(i, i ^ bits) for i in range(groups)])


def shift_dp(value, by, groups):
    return lax.ppermute(value, "dp", [(i, i + by) for i in range(groups) if 0 <= i + by < groups])


def shards(
    tokens,
    cotangent,
    ln_gain,
    ln_bias,
    skip_gain,
    in_real,
    in_imag,
    out_real,
    out_imag,
    nu_log,
    theta_log,
    gamma_log,
    up_weight,
    gate_weight,
    down_weight,
    lengths,
    *,
    groups,
):
    seqs, length, width = tokens.shape
    per_s = in_real.shape[1]
    per_f = up_weight.shape[1]
    states = per_s * TENSOR
    own_seqs = seqs // 2
    rows = own_seqs * length
    blocks = rows // BLOCK
    place = lax.axis_index("dp").astype(jnp.int32)
    shard = lax.axis_index("tensor").astype(jnp.int32)
    core = shard % 2
    where = jnp.stack([place, core, shard])

    tok_rows = tokens.reshape(seqs * length, width)
    cot_rows = cotangent.reshape(seqs * length, width)
    row = lambda v: v.reshape(1, width)
    gain_row, bias_row, skip_row = row(ln_gain), row(ln_bias), row(skip_gain)
    a_shape = (2 * per_s + PARAM_ROWS, width)
    b_shape = (2 * per_s + per_f, width)
    lanes = 2 * states
    units = TENSOR * per_f
    ends_shape = ((own_seqs, lanes), F32)
    dma = pltpu.SemaphoreType.DMA
    line = lambda v: v.reshape(1, per_s)

    pack_a = call(
        input_pack_kernel,
        [where],
        [in_real.T, in_imag.T, line(nu_log), line(theta_log), line(gamma_log)],
        (a_shape, BF16),
        [pltpu.VMEM((3, 1, per_s), F32), dma((5,))],
        4,
        far_inputs=range(5),
    )
    low, normed, inv, cot_m = call(
        functools.partial(norm_kernel, length=length),
        [where],
        [after(tok_rows, pack_a), cot_rows, gain_row, bias_row, lengths],
        [((rows, width), BF16), ((rows, width), F32), ((rows, 128), F32), ((rows, width), BF16)],
        [
            pltpu.VMEM((rows, width), BF16),
            pltpu.VMEM((rows, width), BF16),
            pltpu.VMEM((1, width), F32),
            pltpu.VMEM((1, width), F32),
            pltpu.SMEM((seqs,), jnp.int32),
            dma((2, blocks)),
            dma((3,)),
        ],
        8,
        far_inputs=range(5),
    )
    packs_a = gather_tensor(pack_a, low)
    pack_b, pack_g = call(
        weight_pack_kernel,
        [],
        [after(out_real, packs_a[2]), out_imag, up_weight, gate_weight, down_weight],
        [(b_shape, BF16), ((width, 2 * per_f), BF16)],
        [dma((5,))],
        4,
        far_inputs=range(5),
    )
    drive, ends, powers = call(
        functools.partial(drive_kernel, length=length),
        [where],
        [low, *packs_a],
        [((rows, lanes), F32), ends_shape, ((TILE, lanes), F32)],
        [pltpu.VMEM((lanes, width), BF16), pltpu.VMEM((2, length, states), F32)],
        8,
    )
    local = call(
        functools.partial(scan_kernel, length=length, backwards=False),
        [],
        [drive, *packs_a],
        ((rows, lanes), F32),
        [pltpu.VMEM((4, 2, TILE, states), F32)],
        8,
    )

    ways = groups // 2
    levels = (ways - 1).bit_length()

    def exchange(mine, backwards, beside_work, first_work=None):
        beside = after(flip_dp(mine, 1, groups), beside_work)
        both = call(
            functools.partial(pair_kernel, backwards=backwards), [where], [mine, beside, powers], ends_shape, [], 2
        )
        found = [both]
        from_far = []
        for k in range(levels):
            step = 2 << k
            from_far.append(shift_dp(found[-1], -step if backwards else step, groups))
            if k == 0 and first_work is not None:
                from_far[0] = after(from_far[0], first_work(both))
            if k + 1 < levels:
                found.append(
                    call(functools.partial(join_kernel, row=1 + k), [], [found[-1], from_far[-1], powers], ends_shape, [], 2)
                )
        return from_far, beside, found

    far_ends, beside_ends, found_ends = exchange(ends, False, local)
    packs_b = gather_tensor(pack_b, far_ends[0])
    hid_grad = call(
        functools.partial(hidden_kernel, per_s=per_s),
        [where],
        [after(cot_m, found_ends[-1]), *packs_b],
        ((rows, units), BF16),
        [],
        8,
    )
    packs_g = gather_tensor(pack_g, hid_grad, *far_ends)

    pack_rows = -(-(2 * per_s + per_f + width) // (16 * groups)) * 16 * groups
    state, back_drive, back_ends, y_low, hid, act, ul_half = call(
        functools.partial(middle_kernel, length=length, levels=levels),
        [where],
        [
            *far_ends,
            beside_ends,
            powers,
            local,
            normed,
            hid_grad,
            cot_m,
            *packs_a,
            gain_row,
            bias_row,
            skip_row,
            *packs_b,
            *packs_g,
        ],
        [
            ((rows, lanes), BF16),
            ((rows, lanes), F32),
            ends_shape,
            ((rows, width), BF16),
            ((rows, units), BF16),
            ((rows, width), BF16),
            ((rows, units), BF16),
        ],
        [
            pltpu.VMEM((lanes, width), BF16),
            pltpu.VMEM((width, 2 * units), BF16),
            pltpu.VMEM((2, length, states), F32),
            pltpu.VMEM((2, length, states), F32),
            pltpu.VMEM((own_seqs, lanes), F32),
            pltpu.VMEM((BLOCK, 2 * units), BF16),
            dma((TENSOR, 3)),
        ],
        14,
    )
    own_b, sent_b = call(
        weight_kernel,
        [where],
        [hid, cot_m, act, ul_half, state, y_low],
        [((pack_rows, width), F32), ((pack_rows, width), BF16)],
        [],
        10,
    )

    half, part = pack_rows // 2, pack_rows // groups
    keep_b, send_b = call(
        fold_kernel,
        [where],
        [own_b, core_swap(sent_b)],
        [((half, width), F32), ((half, width), BF16)],
        [],
        4,
    )
    made = []

    def scan_work(pair_back):
        made.append(
            call(
                functools.partial(scan_kernel, length=length, backwards=True),
                [],
                [after(back_drive, pair_back), *packs_a],
                ((rows, lanes), F32),
                [pltpu.VMEM((4, 2, TILE, states), F32)],
                8,
            )
        )
        return made[0]

    far_back, beside_back, found_back = exchange(back_ends, True, send_b, scan_work)
    back = made[0]
    half_b = flip_dp(after(send_b, found_back[0]), 1, groups)
    out_own = call(
        functools.partial(down_kernel, length=length, per_s=per_s),
        [where, lengths],
        [tok_rows, after(hid, found_back[-1]), *packs_b],
        ((rows, width), BF16),
        [pltpu.VMEM((units, width), BF16), pltpu.VMEM((rows, width), BF16), dma((blocks,))],
        8,
        far_inputs=(0,),
    )
    dealt = call(
        deal_kernel,
        [where],
        [after(keep_b, out_own, *far_back), half_b],
        [((part, width), F32)] + [((part, width), BF16)] * (ways - 1),
        [],
        4,
    )

    grad_own, own_a, sent_a = call(
        functools.partial(last_kernel, length=length, levels=levels),
        [where],
        [
            *far_back,
            after(beside_back, dealt[0]),
            powers,
            low,
            normed,
            inv,
            cot_m,
            back,
            state,
            y_low,
            *packs_a,
            gain_row,
            bias_row,
            skip_row,
        ],
        [((rows, width), BF16), (a_shape, BF16), (a_shape, BF16)],
        [
            pltpu.VMEM((lanes, width), BF16),
            pltpu.VMEM((2, length, states), F32),
            pltpu.VMEM((own_seqs, lanes), F32),
            pltpu.VMEM((BLOCK, lanes), BF16),
            pltpu.VMEM((states, width), F32),
            pltpu.VMEM((1, lanes), F32),
            pltpu.VMEM((TILE, width), F32),
        ],
        12,
    )

    mine_b = dealt[0]
    for k in range(1, ways):
        mine_b = mine_b + flip_dp(dealt[k], 2 * k, groups).astype(F32)
    mine_b = mine_b.astype(BF16)
    gathered = [mine_b] + [flip_dp(mine_b, 2 * k, groups) for k in range(1, ways)]
    beside = [flip_dp(piece, 1, groups) for piece in gathered]

    grads_a = own_a.astype(F32) + core_swap(after(sent_a, mine_b)).astype(F32)
    low_a = grads_a.astype(BF16)
    other_a = flip_dp(low_a, 1, groups)

    block_out = call(
        join_halves_kernel,
        [where],
        [out_own, core_swap(out_own)],
        [((seqs * length, width), BF16)],
        [dma((2,))],
        2,
        far_outs=(0,),
    )[0].reshape(seqs, length, width)
    input_grad = call(
        widen_halves_kernel,
        [where],
        [grad_own, core_swap(after(grad_own, low_a))],
        [((seqs * length, width), F32)],
        [pltpu.VMEM((4, BLOCK, width), F32), dma((4,))],
        4,
        far_outs=(0,),
    )[0].reshape(seqs, length, width)

    works = {1: [beside[0], block_out, input_grad], 2: [beside[1]]}
    other_a = after(other_a, *works[1])
    bit = 2
    while bit < groups:
        low_a = (low_a.astype(F32) + other_a.astype(F32)).astype(BF16)
        if bit == 2:
            low_a = after(low_a, *gathered)
        other_a = flip_dp(low_a, bit, groups)
        if bit in works:
            other_a = after(other_a, *works[bit])
        bit *= 2

    state_shape = ((per_s, width), F32)
    finished = call(
        functools.partial(finish_kernel, ways=ways),
        [where],
        [*gathered, *beside, low_a, other_a, in_real.T, in_imag.T, line(nu_log), line(theta_log)],
        [((1, width), F32)] * 3
        + [state_shape] * 2
        + [((1, per_s), F32)] * 3
        + [state_shape] * 2
        + [((width, per_f), F32)] * 2
        + [((per_f, width), F32)],
        [
            pltpu.VMEM((pack_rows, width), F32),
            pltpu.VMEM(a_shape, F32),
            pltpu.VMEM((3, 1, per_s), F32),
            pltpu.VMEM((2, 1, per_s), F32),
            dma((13,)),
            dma((2,)),
        ],
        8,
        far_inputs=(groups + 4, groups + 5),
        far_outs=range(13),
    )
    vectors, in_grads, logs = finished[:3], finished[3:5], finished[5:8]
    return (
        block_out,
        input_grad,
        *[v.reshape(width) for v in vectors],
        *[v.T for v in in_grads],
        *finished[8:10],
        *[v.reshape(per_s) for v in logs],
        *finished[10:],
    )


def solution(mesh):
    rows = P(None, "dp", None)
    columns = P(None, "tensor")
    lines = P("tensor", None)
    vector = P("tensor")
    in_specs = (rows, rows, P(), P(), P(), columns, columns, lines, lines, vector, vector, vector, columns, columns, lines, P())
    out_specs = (rows, rows, P(), P(), P(), columns, columns, lines, lines, vector, vector, vector, columns, columns, lines)
    return jax.shard_map(
        functools.partial(shards, groups=mesh.shape["dp"]),
        mesh=mesh,
        in_specs=in_specs,
        out_specs=out_specs,
        check_vma=False,
    )
```

time: 125 us -> 121 us (0.968)
  Pallas kernels: 58.5 us -> 57 us
    pallas_call x18 -> x20, Pallas kernels: 58.5 us -> 57 us  [call(): pl.pallas_call(kernel, in_specs=[pl.BlockSpec(memory_space=pltpu.SMEM)] *...]
    ppermute x4, waiting for transfers between devices: 6.01 us -> 4.55 us  [shift_dp(): lax.ppermute(value, 'dp', [(i, i + by) for i in range(groups) if 0 <= i +...]
  transfers between devices with their start and end apart: 33 -> 33, of which waited for: 15 -> 16; matrix products, arithmetic and copies ran while one was open for 0% -> 0% of each run, Pallas kernels for 26% -> 26%
where the time goes in v4:
time: 121 us
  Pallas kernels  57 us (47%)
  starting transfers between devices  40 us (33%)
  waiting for transfers between devices  22.6 us (19%)
    pallas_call x20, Pallas kernels, call(): pl.pallas_call(kernel, in_specs=[pl.BlockSpec(memory_space=pltpu.SMEM)] *...  57 us
    ppermute x16, starting transfers between devices, flip_dp(): return lax.ppermute(value, 'dp', [(i, i ^ bits) for i in range(groups)])  21.1 us
    ppermute x16, waiting for transfers between devices, flip_dp(): return lax.ppermute(value, 'dp', [(i, i ^ bits) for i in range(groups)])  14.4 us
    ppermute x4, starting transfers between devices, shift_dp(): lax.ppermute(value, 'dp', [(i, i + by) for i in range(groups) if 0 <= i +...  11.5 us
    ppermute x3, starting transfers between devices, side_swap(): return lax.ppermute(value, 'tensor', [(t, t ^ 2) for t in range(TENSOR)])  5.12 us
    ppermute x4, waiting for transfers between devices, shift_dp(): lax.ppermute(value, 'dp', [(i, i + by) for i in range(groups) if 0 <= i +...  4.55 us
    ppermute x10, waiting for transfers between devices, core_swap(): return lax.ppermute(value, 'tensor', [(t, t ^ 1) for t in range(TENSOR)])  3.61 us
  transfers between devices with their start and end apart: 33, of which 16 were waited for; matrix products, arithmetic and copies ran while one was open for 0% of the time, Pallas kernels for 26%

profile of v4, /device:TPU:0, one launch (start us, length us, event | category | flops | bytes accessed | tf_op | source)
XLA Modules:
  0.0 121.0 jit_solution(14700732428014839916)
XLA Ops:
  0.7 1.6 %shard_map.271.a0.refs_8_.refs_11_ = bf16[144,512]{1,0:T(8,128)(2,1)S(1)} custom-call(s32[3]{0:T(128)S(1)} %pad_add_fusion.where_ref, bf16[64,512]{1,0:T(8,128)(2,1)} %bitcast.23, bf16[64,512]{1,0:T(8,128)(2,1)} %bitcast.25, f32[1,64]{1,0:T(1,128)} %bitcast.40, f32[1,64]{1,0:T(1,128)} %bitcast.42, f32[1,64]{1,0:T(1,128)} %bitcast.44), custom_call_target="tpu_custom_call" | custom-call | tf_op jit(solution)/shard_map/pallas_call | solution.py:632
  2.3 3.0 %collective-permute-start.1 = (bf16[144,512]{1,0:T(8,128)(2,1)S(1)}, bf16[144,512]{1,0:T(8,128)(2,1)S(1)}, u32[]{:S(2)}, u32[]{:S(2)}) collective-permute-start(bf16[144,512]{1,0:T(8,128)(2,1)S(1)} %shard_map.271.a0.refs_8_.refs_11_), channel_id=1, source_target_pairs={{0,2},{1,3},{2,0},{3,1},{4,6},{5,7},{6,4},{7,5},{8,10},{9,11},{10,... | collective-permute-start | bytes 442376 | tf_op jit(solution)/shard_map/ppermute | solution.py:654
  5.4 4.2 %shard_map.272 = (bf16[1536,512]{1,0:T(8,128)(2,1)S(1)}, f32[1536,512]{1,0:T(8,128)S(1)}, f32[1536,128]{1,0:T(8,128)S(1)}, bf16[1536,512]{1,0:T(8,128)(2,1)S(1)}) custom-call(s32[3]{0:T(128)S(1)} %pad_add_fusion.where_ref, bf16[3072,512]{1,0:T(8,128)(2,1)} %bitcast.35, bf16[3072,512]{1,0:T(8,128)(2,1)} %bitcast.38, f32[1,512]{1,0:T(1,128)} %bitcast.27, ...), custom_call_target="tpu_custom_call" | custom-call | tf_op jit(solution)/shard_map/pallas_call | solution.py:632
  9.5 1.2 %shard_map.277 = (bf16[384,512]{1,0:T(8,128)(2,1)S(1)}, bf16[512,512]{1,0:T(8,128)(2,1)S(1)}) custom-call(bf16[64,512]{1,0:T(8,128)(2,1)} %out_real, bf16[64,512]{1,0:T(8,128)(2,1)} %out_imag.1, bf16[512,256]{1,0:T(8,128)(2,1)} %up.1, bf16[512,256]{1,0:T(8,128)(2,1)} %gate.1, bf16[256,512]{1,0:T(8,128)(2,1)} %down.1), custom_call_target="tpu_custom_call" | custom-call | tf_op jit(solution)/shard_map/pallas_call | solution.py:632
  10.8 1.5 %collective-permute-start.7 = (bf16[384,512]{1,0:T(8,128)(2,1)S(1)}, bf16[384,512]{1,0:T(8,128)(2,1)S(1)}, u32[]{:S(2)}, u32[]{:S(2)}) collective-permute-start(bf16[384,512]{1,0:T(8,128)(2,1)S(1)} %get-tuple-element.85.b0.refs_15_), channel_id=1, source_target_pairs={{0,2},{1,3},{2,0},{3,1},{4,6},{5,7},{6,4},{7,5},{8,10},{9,11},{10,... | collective-permute-start | bytes 1179656 | tf_op jit(solution)/shard_map/ppermute | solution.py:654
  12.8 0.6 collective-permute-start.10
  13.8 2.9 %shard_map.273 = (f32[1536,512]{1,0:T(8,128)S(1)}, f32[12,512]{1,0:T(8,128)S(1)}, f32[8,512]{1,0:T(8,128)S(1)}) custom-call(s32[3]{0:T(128)S(1)} %pad_add_fusion.where_ref, bf16[1536,512]{1,0:T(8,128)(2,1)S(1)} %get-tuple-element.75.low_all.refs_4_, bf16[144,512]{1,0:T(8,128)(2,1)S(1)} %shard_map.271.a0.refs_8_.refs_11_, ...), custom_call_target="tpu_custom_call" | custom-call | tf_op jit(solution)/shard_map/pallas_call | solution.py:632
  16.7 1.6 %collective-permute-start.3 = (f32[12,512]{1,0:T(8,128)S(1)}, f32[12,512]{1,0:T(8,128)S(1)}, u32[]{:S(2)}, u32[]{:S(2)}) collective-permute-start(f32[12,512]{1,0:T(8,128)S(1)} %get-tuple-element.77.mine_ref), channel_id=1, source_target_pairs={{0,4},{4,0},{8,12},{12,8},{16,20},{20,16},{24,28},{28,24},{1,5},{5... | collective-permute-start | bytes 73736 | tf_op jit(solution)/shard_map/ppermute | solution.py:667
  18.3 2.1 %shard_map.274.refs_4_ = f32[1536,512]{1,0:T(8,128)S(1)} custom-call(f32[1536,512]{1,0:T(8,128)S(1)} %get-tuple-element.78.drive_all, bf16[144,512]{1,0:T(8,128)(2,1)S(1)} %shard_map.271.a0.refs_8_.refs_11_, bf16[144,512]{1,0:T(8,128)(2,1)S(1)} %collective-permute-done.a1.refs_9_.refs_12_, bf16[144,512]{1,0:T(8,128)(2,1)S(1)} %collective-permute-done.1.a2.refs_10_.refs_13_, ...), custom_call_target="tpu_custom_call" | custom-call | tf_op jit(solution)/shard_map/pallas_call | solution.py:632
  20.7 0.6 shard_map.275.mine_ref
  21.3 3.5 %collective-permute-start.4 = (f32[12,512]{1,0:T(8,128)S(1)}, f32[12,512]{1,0:T(8,128)S(1)}, u32[]{:S(2)}, u32[]{:S(2)}) collective-permute-start(f32[12,512]{1,0:T(8,128)S(1)} %shard_map.275.mine_ref), channel_id=1, source_target_pairs={{0,8},{4,12},{8,16},{12,20},{16,24},{20,28},{1,9},{5,13},{9,17},{1... | collective-permute-start | bytes 73736 | tf_op jit(solution)/shard_map/ppermute | solution.py:671
  24.9 1.5 %collective-permute-done.4.other_ref.refs_0_ = f32[12,512]{1,0:T(8,128)S(1)} collective-permute-done((f32[12,512]{1,0:T(8,128)S(1)}, f32[12,512]{1,0:T(8,128)S(1)}, u32[]{:S(2)}, u32[]{:S(2)}) %collective-permute-start.4) | collective-permute-done | bytes 24608 | tf_op jit(solution)/shard_map/ppermute | solution.py:671
  26.4 5.2 %collective-permute-start.5 = (f32[12,512]{1,0:T(8,128)S(1)}, f32[12,512]{1,0:T(8,128)S(1)}, u32[]{:S(2)}, u32[]{:S(2)}) collective-permute-start(f32[12,512]{1,0:T(8,128)S(1)} %shard_map.276), channel_id=1, source_target_pairs={{0,16},{4,20},{8,24},{12,28},{1,17},{5,21},{9,25},{13,29},{2,18},{... | collective-permute-start | bytes 73736 | tf_op jit(solution)/shard_map/ppermute | solution.py:671
  31.9 3.5 %shard_map.278.refs_6_ = bf16[1536,1024]{1,0:T(8,128)(2,1)S(1)} custom-call(s32[3]{0:T(128)S(1)} %pad_add_fusion.where_ref, bf16[1536,512]{1,0:T(8,128)(2,1)S(1)} %get-tuple-element.83.cotm_all.refs_7_.cotm_ref, bf16[384,512]{1,0:T(8,128)(2,1)S(1)} %get-tuple-element.85.b0.refs_15_, bf16[384,512]{1,0:T(8,128)(2,1)S(1)} %collective-permute-done.6.b1.refs_16_, ...), custom_call_target="tpu_custom_call" | custom-call | tf_op jit(solution)/shard_map/pallas_call | solution.py:632
  35.8 1.6 %collective-permute-done.11.refs_22_ = bf16[512,512]{1,0:T(8,128)(2,1)S(1)} collective-permute-done((bf16[512,512]{1,0:T(8,128)(2,1)S(1)}, bf16[512,512]{1,0:T(8,128)(2,1)S(1)}, u32[]{:S(2)}, u32[]{:S(2)}) %collective-permute-start.11) | collective-permute-done | bytes 524320 | tf_op jit(solution)/shard_map/ppermute | solution.py:650
  37.4 14.3 %shard_map.279 = (bf16[1536,512]{1,0:T(8,128)(2,1)S(1)}, f32[1536,512]{1,0:T(8,128)S(1)}, f32[12,512]{1,0:T(8,128)S(1)}, bf16[1536,512]{1,0:T(8,128)(2,1)S(1)}, ...) custom-call(s32[3]{0:T(128)S(1)} %pad_add_fusion.where_ref, ...), custom_call_target="tpu_custom_call" | custom-call | tf_op jit(solution)/shard_map/pallas_call | solution.py:632
  51.7 3.6 %shard_map.280 = (f32[896,512]{1,0:T(8,128)S(1)}, bf16[896,512]{1,0:T(8,128)(2,1)S(1)}) custom-call(s32[3]{0:T(128)S(1)} %pad_add_fusion.where_ref, bf16[1536,1024]{1,0:T(8,128)(2,1)S(1)} %get-tuple-element.102.hid_ref.hid_all, bf16[1536,512]{1,0:T(8,128)(2,1)S(1)} %get-tuple-element.83.cotm_all.refs_7_.cotm_ref, ...), custom_call_target="tpu_custom_call" | custom-call | tf_op jit(solution)/shard_map/pallas_call | solution.py:632
  55.7 1.5 %collective-permute-start.12 = (f32[12,512]{1,0:T(8,128)S(1)}, f32[12,512]{1,0:T(8,128)S(1)}, u32[]{:S(2)}, u32[]{:S(2)}) collective-permute-start(f32[12,512]{1,0:T(8,128)S(1)} %get-tuple-element.90.mine_ref), channel_id=1, source_target_pairs={{0,4},{4,0},{8,12},{12,8},{16,20},{20,16},{24,28},{28,24},{1,5},{5... | collective-permute-start | bytes 73736 | tf_op jit(solution)/shard_map/ppermute | solution.py:667
  57.2 0.7 collective-permute-done.13.other_ref
  57.9 0.7 shard_map.281
  58.6 1.0 collective-permute-done.12.other_ref.refs_2_
  59.6 0.6 shard_map.282.mine_ref
  60.2 1.6 %collective-permute-start.17 = (bf16[448,512]{1,0:T(8,128)(2,1)S(1)}, bf16[448,512]{1,0:T(8,128)(2,1)S(1)}, u32[]{:S(2)}, u32[]{:S(2)}) collective-permute-start(bf16[448,512]{1,0:T(8,128)(2,1)S(1)} %get-tuple-element.105), channel_id=1, source_target_pairs={{0,4},{4,0},{8,12},{12,8},{16,20},{20,16},{24,28},{28,24},{1,5},{5... | collective-permute-start | bytes 1376264 | tf_op jit(solution)/shard_map/ppermute | solution.py:667
  61.7 1.3 %collective-permute-start.14 = (f32[12,512]{1,0:T(8,128)S(1)}, f32[12,512]{1,0:T(8,128)S(1)}, u32[]{:S(2)}, u32[]{:S(2)}) collective-permute-start(f32[12,512]{1,0:T(8,128)S(1)} %shard_map.282.mine_ref), channel_id=1, source_target_pairs={{8,0},{12,4},{16,8},{20,12},{24,16},{28,20},{9,1},{13,5},{17,9},{2... | collective-permute-start | bytes 73736 | tf_op jit(solution)/shard_map/ppermute | solution.py:671
  63.0 2.1 %shard_map.283.refs_8_ = f32[1536,512]{1,0:T(8,128)S(1)} custom-call(f32[1536,512]{1,0:T(8,128)S(1)} %get-tuple-element.100.drive_all, bf16[144,512]{1,0:T(8,128)(2,1)S(1)} %shard_map.271.a0.refs_8_.refs_11_, bf16[144,512]{1,0:T(8,128)(2,1)S(1)} %collective-permute-done.a1.refs_9_.refs_12_, bf16[144,512]{1,0:T(8,128)(2,1)S(1)} %collective-permute-done.1.a2.refs_10_.refs_13_, ...), custom_call_target="tpu_custom_call" | custom-call | tf_op jit(solution)/shard_map/pallas_call | solution.py:632
  65.1 2.4 %collective-permute-done.14.other_ref.refs_0_ = f32[12,512]{1,0:T(8,128)S(1)} collective-permute-done((f32[12,512]{1,0:T(8,128)S(1)}, f32[12,512]{1,0:T(8,128)S(1)}, u32[]{:S(2)}, u32[]{:S(2)}) %collective-permute-start.14) | collective-permute-done | bytes 24608 | tf_op jit(solution)/shard_map/ppermute | solution.py:671
  67.6 1.5 %collective-permute-start.16 = (f32[12,512]{1,0:T(8,128)S(1)}, f32[12,512]{1,0:T(8,128)S(1)}, u32[]{:S(2)}, u32[]{:S(2)}) collective-permute-start(f32[12,512]{1,0:T(8,128)S(1)} %shard_map.284), channel_id=1, source_target_pairs={{16,0},{20,4},{24,8},{28,12},{17,1},{21,5},{25,9},{29,13},{18,2},{... | collective-permute-start | bytes 73736 | tf_op jit(solution)/shard_map/ppermute | solution.py:671
  69.0 4.6 %shard_map.285.own_ref = bf16[1536,512]{1,0:T(8,128)(2,1)S(1)} custom-call(s32[3]{0:T(128)S(1)} %pad_add_fusion.where_ref, s32[24]{0:T(128)S(1)} %copy-done.5, bf16[3072,512]{1,0:T(8,128)(2,1)} %bitcast.36, bf16[1536,1024]{1,0:T(8,128)(2,1)S(1)} %get-tuple-element.102.hid_ref.hid_all, bf16[384,512]{1,0:T(8,128)(2,1)S(1)} %get-tuple-element.85.b0.refs_15_, ...), custom_call_target="tpu_custom_call" | custom-call | tf_op jit(solution)/shard_map/pallas_call | solution.py:632
  73.6 0.6 collective-permute-done.16.refs_1_
  74.3 0.7 shard_map.287
  74.9 1.6 %collective-permute-start.18 = (bf16[112,512]{1,0:T(8,128)(2,1)S(1)}, bf16[112,512]{1,0:T(8,128)(2,1)S(1)}, u32[]{:S(2)}, u32[]{:S(2)}) collective-permute-start(bf16[112,512]{1,0:T(8,128)(2,1)S(1)} %get-tuple-element.112), channel_id=1, source_target_pairs={{0,8},{4,12},{8,0},{12,4},{16,24},{20,28},{24,16},{28,20},{1,9},{5... | collective-permute-start | bytes 344072 | tf_op jit(solution)/shard_map/ppermute | solution.py:667
  76.6 2.9 %collective-permute-start.19 = (bf16[112,512]{1,0:T(8,128)(2,1)S(1)}, bf16[112,512]{1,0:T(8,128)(2,1)S(1)}, u32[]{:S(2)}, u32[]{:S(2)}) collective-permute-start(bf16[112,512]{1,0:T(8,128)(2,1)S(1)} %get-tuple-element.113), channel_id=1, source_target_pairs={{0,16},{4,20},{8,24},{12,28},{16,0},{20,4},{24,8},{28,12},{1,17},{... | collective-permute-start | bytes 344072 | tf_op jit(solution)/shard_map/ppermute | solution.py:667
  79.5 5.7 %shard_map.288 = (bf16[1536,512]{1,0:T(8,128)(2,1)S(1)}, bf16[144,512]{1,0:T(8,128)(2,1)S(1)}, bf16[144,512]{1,0:T(8,128)(2,1)S(1)}) custom-call(s32[3]{0:T(128)S(1)} %pad_add_fusion.where_ref, f32[12,512]{1,0:T(8,128)S(1)} %collective-permute-done.14.other_ref.refs_0_, f32[12,512]{1,0:T(8,128)S(1)} %collective-permute-done.16.refs_1_, ...), custom_call_target="tpu_custom_call" | custom-call | tf_op jit(solution)/shard_map/pallas_call | solution.py:632
  85.2 1.3 %collective-permute-done.19 = bf16[112,512]{1,0:T(8,128)(2,1)S(1)} collective-permute-done((bf16[112,512]{1,0:T(8,128)(2,1)S(1)}, bf16[112,512]{1,0:T(8,128)(2,1)S(1)}, u32[]{:S(2)}, u32[]{:S(2)}) %collective-permute-start.19) | collective-permute-done | bytes 114720 | tf_op jit(solution)/shard_map/ppermute | solution.py:667
  87.2 0.9 collective-permute-done.21
  88.8 1.5 %collective-permute-start.26 = (bf16[112,512]{1,0:T(8,128)(2,1)S(1)}, bf16[112,512]{1,0:T(8,128)(2,1)S(1)}, u32[]{:S(2)}, u32[]{:S(2)}) collective-permute-start(bf16[112,512]{1,0:T(8,128)(2,1)S(1)} %add_convert_fusion.3.refs_0_), channel_id=1, source_target_pairs={{0,4},{4,0},{8,12},{12,8},{16,20},{20,16},{24,28},{28,24},{1,5},{5... | collective-permute-start | bytes 344072 | tf_op jit(solution)/shard_map/ppermute | solution.py:667
  90.3 2.6 %collective-permute-start.25 = (bf16[112,512]{1,0:T(8,128)(2,1)S(1)}, bf16[112,512]{1,0:T(8,128)(2,1)S(1)}, u32[]{:S(2)}, u32[]{:S(2)}) collective-permute-start(bf16[112,512]{1,0:T(8,128)(2,1)S(1)} %add_convert_fusion.3.refs_0_), channel_id=1, source_target_pairs={{0,24},{4,28},{8,16},{12,20},{16,8},{20,12},{24,0},{28,4},{1,25},{... | collective-permute-start | bytes 344072 | tf_op jit(solution)/shard_map/ppermute | solution.py:667
  92.9 0.7 collective-permute-start.24
  93.6 2.2 %shard_map.286 = bf16[3072,512]{1,0:T(8,128)(2,1)} custom-call(s32[3]{0:T(128)S(1)} %pad_add_fusion.where_ref, bf16[1536,512]{1,0:T(8,128)(2,1)S(1)} %shard_map.285.own_ref, bf16[1536,512]{1,0:T(8,128)(2,1)S(1)} %collective-permute-done.15.other_ref), custom_call_target="tpu_custom_call" | custom-call | tf_op jit(solution)/shard_map/pallas_call | solution.py:632
  95.9 1.2 collective-permute-start.23
  97.1 3.6 %shard_map.289 = f32[3072,512]{1,0:T(8,128)} custom-call(s32[3]{0:T(128)S(1)} %pad_add_fusion.where_ref, bf16[1536,512]{1,0:T(8,128)(2,1)S(1)} %get-tuple-element.116.own_ref, bf16[1536,512]{1,0:T(8,128)(2,1)S(1)} %collective-permute-done.22.other_ref), custom_call_target="tpu_custom_call" | custom-call | tf_op jit(solution)/shard_map/pallas_call | solution.py:632
  100.7 3.1 %collective-permute-done.24.refs_2_ = bf16[112,512]{1,0:T(8,128)(2,1)S(1)} collective-permute-done((bf16[112,512]{1,0:T(8,128)(2,1)S(1)}, bf16[112,512]{1,0:T(8,128)(2,1)S(1)}, u32[]{:S(2)}, u32[]{:S(2)}) %collective-permute-start.24) | collective-permute-done | bytes 114720 | tf_op jit(solution)/shard_map/ppermute | solution.py:667
  104.3 4.3 %collective-permute-done.27.refs_5_ = bf16[112,512]{1,0:T(8,128)(2,1)S(1)} collective-permute-done((bf16[112,512]{1,0:T(8,128)(2,1)S(1)}, bf16[112,512]{1,0:T(8,128)(2,1)S(1)}, u32[]{:S(2)}, u32[]{:S(2)}) %collective-permute-start.27) | collective-permute-done | bytes 114720 | tf_op jit(solution)/shard_map/ppermute | solution.py:667
  109.0 2.8 %collective-permute-start.32 = (bf16[144,512]{1,0:T(8,128)(2,1)S(1)}, bf16[144,512]{1,0:T(8,128)(2,1)S(1)}, u32[]{:S(2)}, u32[]{:S(2)}) collective-permute-start(bf16[144,512]{1,0:T(8,128)(2,1)S(1)} %add_convert_fusion.refs_8_), channel_id=1, source_target_pairs={{0,16},{4,20},{8,24},{12,28},{16,0},{20,4},{24,8},{28,12},{1,17},{... | collective-permute-start | bytes 442376 | tf_op jit(solution)/shard_map/ppermute | solution.py:667
  112.4 1.5 %collective-permute-start.28 = (bf16[112,512]{1,0:T(8,128)(2,1)S(1)}, bf16[112,512]{1,0:T(8,128)(2,1)S(1)}, u32[]{:S(2)}, u32[]{:S(2)}) collective-permute-start(bf16[112,512]{1,0:T(8,128)(2,1)S(1)} %collective-permute-done.24.refs_2_), channel_id=1, source_target_pairs={{0,4},{4,0},{8,12},{12,8},{16,20},{20,16},{24,28},{28,24},{1,5},{5... | collective-permute-start | bytes 344072 | tf_op jit(solution)/shard_map/ppermute | solution.py:667
  113.9 2.8 %collective-permute-done.29.refs_7_ = bf16[112,512]{1,0:T(8,128)(2,1)S(1)} collective-permute-done((bf16[112,512]{1,0:T(8,128)(2,1)S(1)}, bf16[112,512]{1,0:T(8,128)(2,1)S(1)}, u32[]{:S(2)}, u32[]{:S(2)}) %collective-permute-start.29) | collective-permute-done | bytes 114720 | tf_op jit(solution)/shard_map/ppermute | solution.py:667
  116.6 1.2 %collective-permute-done.28.refs_6_ = bf16[112,512]{1,0:T(8,128)(2,1)S(1)} collective-permute-done((bf16[112,512]{1,0:T(8,128)(2,1)S(1)}, bf16[112,512]{1,0:T(8,128)(2,1)S(1)}, u32[]{:S(2)}, u32[]{:S(2)}) %collective-permute-start.28) | collective-permute-done | bytes 114720 | tf_op jit(solution)/shard_map/ppermute | solution.py:667
  117.9 3.0 %shard_map.290 = (f32[1,512]{1,0:T(1,128)}, f32[1,512]{1,0:T(1,128)}, f32[1,512]{1,0:T(1,128)}, f32[64,512]{1,0:T(8,128)}, f32[64,512]{1,0:T(8,128)}, /*index=5*...) custom-call(s32[3]{0:T(128)S(1)} %pad_add_fusion.where_ref, ...), custom_call_target="tpu_custom_call" | custom-call | tf_op jit(solution)/shard_map/pallas_call | solution.py:632
  (55 shorter events, 5.5 us)
Async XLA Ops:
  2.3 7.2 %collective-permute-start.1 = (bf16[144,512]{1,0:T(8,128)(2,1)S(1)}, bf16[144,512]{1,0:T(8,128)(2,1)S(1)}, u32[]{:S(2)}, u32[]{:S(2)}) collective-permute-start(bf16[144,512]{1,0:T(8,128)(2,1)S(1)} %shard_map.271.a0.refs_8_.refs_11_), channel_id=1, source_target_pairs={{0,2},{1,3},{2,0},{3,1},{4,6},{5,7},{6,4},{7,5},{8,10},{9,11},{10,... | collective-permute-start | bytes 442376 | tf_op jit(solution)/shard_map/ppermute | solution.py:654
  10.8 15.6 %collective-permute-start.7 = (bf16[384,512]{1,0:T(8,128)(2,1)S(1)}, bf16[384,512]{1,0:T(8,128)(2,1)S(1)}, u32[]{:S(2)}, u32[]{:S(2)}) collective-permute-start(bf16[384,512]{1,0:T(8,128)(2,1)S(1)} %get-tuple-element.85.b0.refs_15_), channel_id=1, source_target_pairs={{0,2},{1,3},{2,0},{3,1},{4,6},{5,7},{6,4},{7,5},{8,10},{9,11},{10,... | collective-permute-start | bytes 1179656 | tf_op jit(solution)/shard_map/ppermute | solution.py:654
  12.3 1.4 %collective-permute-start = (bf16[144,512]{1,0:T(8,128)(2,1)S(1)}, bf16[144,512]{1,0:T(8,128)(2,1)S(1)}, u32[]{:S(2)}, u32[]{:S(2)}) collective-permute-start(bf16[144,512]{1,0:T(8,128)(2,1)S(1)} %shard_map.271.a0.refs_8_.refs_11_), channel_id=1, source_target_pairs={{0,1},{1,0},{2,3},{3,2},{4,5},{5,4},{6,7},{7,6},{8,9},{9,8},{10,11... | collective-permute-start | bytes 442376 | tf_op jit(solution)/shard_map/ppermute | solution.py:650
  12.3 1.6 %collective-permute-start.2 = (bf16[144,512]{1,0:T(8,128)(2,1)S(1)}, bf16[144,512]{1,0:T(8,128)(2,1)S(1)}, u32[]{:S(2)}, u32[]{:S(2)}) collective-permute-start(bf16[144,512]{1,0:T(8,128)(2,1)S(1)} %collective-permute-done.1.a2.refs_10_.refs_13_), channel_id=1, source_target_pairs={{0,1},{1,0},{2,3},{3,2},{4,5},{5,4},{6,7},{7,6},{8,9},{9,8},{10,11... | collective-permute-start | bytes 442376 | tf_op jit(solution)/shard_map/ppermute | solution.py:650
  12.8 22.7 %collective-permute-start.10 = (bf16[512,512]{1,0:T(8,128)(2,1)S(1)}, bf16[512,512]{1,0:T(8,128)(2,1)S(1)}, u32[]{:S(2)}, u32[]{:S(2)}) collective-permute-start(bf16[512,512]{1,0:T(8,128)(2,1)S(1)} %get-tuple-element.87.refs_19_), channel_id=1, source_target_pairs={{0,2},{1,3},{2,0},{3,1},{4,6},{5,7},{6,4},{7,5},{8,10},{9,11},{10,... | collective-permute-start | bytes 1572872 | tf_op jit(solution)/shard_map/ppermute | solution.py:654
  16.7 4.0 %collective-permute-start.3 = (f32[12,512]{1,0:T(8,128)S(1)}, f32[12,512]{1,0:T(8,128)S(1)}, u32[]{:S(2)}, u32[]{:S(2)}) collective-permute-start(f32[12,512]{1,0:T(8,128)S(1)} %get-tuple-element.77.mine_ref), channel_id=1, source_target_pairs={{0,4},{4,0},{8,12},{12,8},{16,20},{20,16},{24,28},{28,24},{1,5},{5... | collective-permute-start | bytes 73736 | tf_op jit(solution)/shard_map/ppermute | solution.py:667
  21.3 5.1 %collective-permute-start.4 = (f32[12,512]{1,0:T(8,128)S(1)}, f32[12,512]{1,0:T(8,128)S(1)}, u32[]{:S(2)}, u32[]{:S(2)}) collective-permute-start(f32[12,512]{1,0:T(8,128)S(1)} %shard_map.275.mine_ref), channel_id=1, source_target_pairs={{0,8},{4,12},{8,16},{12,20},{16,24},{20,28},{1,9},{5,13},{9,17},{1... | collective-permute-start | bytes 73736 | tf_op jit(solution)/shard_map/ppermute | solution.py:671
  24.8 7.1 %collective-permute-start.6 = (bf16[384,512]{1,0:T(8,128)(2,1)S(1)}, bf16[384,512]{1,0:T(8,128)(2,1)S(1)}, u32[]{:S(2)}, u32[]{:S(2)}) collective-permute-start(bf16[384,512]{1,0:T(8,128)(2,1)S(1)} %get-tuple-element.85.b0.refs_15_), channel_id=1, source_target_pairs={{0,1},{1,0},{2,3},{3,2},{4,5},{5,4},{6,7},{7,6},{8,9},{9,8},{10,11... | collective-permute-start | bytes 1179656 | tf_op jit(solution)/shard_map/ppermute | solution.py:650
  26.4 5.6 %collective-permute-start.8 = (bf16[384,512]{1,0:T(8,128)(2,1)S(1)}, bf16[384,512]{1,0:T(8,128)(2,1)S(1)}, u32[]{:S(2)}, u32[]{:S(2)}) collective-permute-start(bf16[384,512]{1,0:T(8,128)(2,1)S(1)} %collective-permute-done.7.b2.refs_17_), channel_id=1, source_target_pairs={{0,1},{1,0},{2,3},{3,2},{4,5},{5,4},{6,7},{7,6},{8,9},{9,8},{10,11... | collective-permute-start | bytes 1179656 | tf_op jit(solution)/shard_map/ppermute | solution.py:650
  26.4 9.0 %collective-permute-start.5 = (f32[12,512]{1,0:T(8,128)S(1)}, f32[12,512]{1,0:T(8,128)S(1)}, u32[]{:S(2)}, u32[]{:S(2)}) collective-permute-start(f32[12,512]{1,0:T(8,128)S(1)} %shard_map.276), channel_id=1, source_target_pairs={{0,16},{4,20},{8,24},{12,28},{1,17},{5,21},{9,25},{13,29},{2,18},{... | collective-permute-start | bytes 73736 | tf_op jit(solution)/shard_map/ppermute | solution.py:671
  31.6 4.2 %collective-permute-start.9 = (bf16[512,512]{1,0:T(8,128)(2,1)S(1)}, bf16[512,512]{1,0:T(8,128)(2,1)S(1)}, u32[]{:S(2)}, u32[]{:S(2)}) collective-permute-start(bf16[512,512]{1,0:T(8,128)(2,1)S(1)} %get-tuple-element.87.refs_19_), channel_id=1, source_target_pairs={{0,1},{1,0},{2,3},{3,2},{4,5},{5,4},{6,7},{7,6},{8,9},{9,8},{10,11... | collective-permute-start | bytes 1572872 | tf_op jit(solution)/shard_map/ppermute | solution.py:650
  31.9 5.5 %copy-start.2 = (f32[512]{0:T(512)S(1)}, f32[512]{0:T(512)}, u32[]{:S(2)}) copy-start(f32[512]{0:T(512)} %param.18) | copy-start | bytes 6148
  31.9 5.5 %copy-start.3 = (f32[512]{0:T(512)S(1)}, f32[512]{0:T(512)}, u32[]{:S(2)}) copy-start(f32[512]{0:T(512)} %param.19) | copy-start | bytes 6148
  31.9 5.5 %copy-start.4 = (f32[512]{0:T(512)S(1)}, f32[512]{0:T(512)}, u32[]{:S(2)}) copy-start(f32[512]{0:T(512)} %param.20) | copy-start | bytes 6148
  35.4 2.0 %collective-permute-start.11 = (bf16[512,512]{1,0:T(8,128)(2,1)S(1)}, bf16[512,512]{1,0:T(8,128)(2,1)S(1)}, u32[]{:S(2)}, u32[]{:S(2)}) collective-permute-start(bf16[512,512]{1,0:T(8,128)(2,1)S(1)} %collective-permute-done.10.refs_21_), channel_id=1, source_target_pairs={{0,1},{1,0},{2,3},{3,2},{4,5},{5,4},{6,7},{7,6},{8,9},{9,8},{10,11... | collective-permute-start | bytes 1572872 | tf_op jit(solution)/shard_map/ppermute | solution.py:650
  55.3 2.5 %collective-permute-start.13 = (bf16[896,512]{1,0:T(8,128)(2,1)S(1)}, bf16[896,512]{1,0:T(8,128)(2,1)S(1)}, u32[]{:S(2)}, u32[]{:S(2)}) collective-permute-start(bf16[896,512]{1,0:T(8,128)(2,1)S(1)} %get-tuple-element.96), channel_id=1, source_target_pairs={{0,1},{1,0},{2,3},{3,2},{4,5},{5,4},{6,7},{7,6},{8,9},{9,8},{10,11... | collective-permute-start | bytes 2752520 | tf_op jit(solution)/shard_map/ppermute | solution.py:650
  55.7 3.9 %collective-permute-start.12 = (f32[12,512]{1,0:T(8,128)S(1)}, f32[12,512]{1,0:T(8,128)S(1)}, u32[]{:S(2)}, u32[]{:S(2)}) collective-permute-start(f32[12,512]{1,0:T(8,128)S(1)} %get-tuple-element.90.mine_ref), channel_id=1, source_target_pairs={{0,4},{4,0},{8,12},{12,8},{16,20},{20,16},{24,28},{28,24},{1,5},{5... | collective-permute-start | bytes 73736 | tf_op jit(solution)/shard_map/ppermute | solution.py:667
  60.2 14.1 %collective-permute-start.17 = (bf16[448,512]{1,0:T(8,128)(2,1)S(1)}, bf16[448,512]{1,0:T(8,128)(2,1)S(1)}, u32[]{:S(2)}, u32[]{:S(2)}) collective-permute-start(bf16[448,512]{1,0:T(8,128)(2,1)S(1)} %get-tuple-element.105), channel_id=1, source_target_pairs={{0,4},{4,0},{8,12},{12,8},{16,20},{20,16},{24,28},{28,24},{1,5},{5... | collective-permute-start | bytes 1376264 | tf_op jit(solution)/shard_map/ppermute | solution.py:667
  61.7 5.8 %collective-permute-start.14 = (f32[12,512]{1,0:T(8,128)S(1)}, f32[12,512]{1,0:T(8,128)S(1)}, u32[]{:S(2)}, u32[]{:S(2)}) collective-permute-start(f32[12,512]{1,0:T(8,128)S(1)} %shard_map.282.mine_ref), channel_id=1, source_target_pairs={{8,0},{12,4},{16,8},{20,12},{24,16},{28,20},{9,1},{13,5},{17,9},{2... | collective-permute-start | bytes 73736 | tf_op jit(solution)/shard_map/ppermute | solution.py:671
  63.0 6.0 %copy-start.5 = (s32[24]{0:T(128)S(1)}, s32[24]{0:T(128)}, u32[]{:S(2)}) copy-start(s32[24]{0:T(128)} %lens_ref.1) | copy-start | bytes 292
  67.6 6.7 %collective-permute-start.16 = (f32[12,512]{1,0:T(8,128)S(1)}, f32[12,512]{1,0:T(8,128)S(1)}, u32[]{:S(2)}, u32[]{:S(2)}) collective-permute-start(f32[12,512]{1,0:T(8,128)S(1)} %shard_map.284), channel_id=1, source_target_pairs={{16,0},{20,4},{24,8},{28,12},{17,1},{21,5},{25,9},{29,13},{18,2},{... | collective-permute-start | bytes 73736 | tf_op jit(solution)/shard_map/ppermute | solution.py:671
  74.9 10.3 %collective-permute-start.18 = (bf16[112,512]{1,0:T(8,128)(2,1)S(1)}, bf16[112,512]{1,0:T(8,128)(2,1)S(1)}, u32[]{:S(2)}, u32[]{:S(2)}) collective-permute-start(bf16[112,512]{1,0:T(8,128)(2,1)S(1)} %get-tuple-element.112), channel_id=1, source_target_pairs={{0,8},{4,12},{8,0},{12,4},{16,24},{20,28},{24,16},{28,20},{1,9},{5... | collective-permute-start | bytes 344072 | tf_op jit(solution)/shard_map/ppermute | solution.py:667
  76.6 10.0 %collective-permute-start.19 = (bf16[112,512]{1,0:T(8,128)(2,1)S(1)}, bf16[112,512]{1,0:T(8,128)(2,1)S(1)}, u32[]{:S(2)}, u32[]{:S(2)}) collective-permute-start(bf16[112,512]{1,0:T(8,128)(2,1)S(1)} %get-tuple-element.113), channel_id=1, source_target_pairs={{0,16},{4,20},{8,24},{12,28},{16,0},{20,4},{24,8},{28,12},{1,17},{... | collective-permute-start | bytes 344072 | tf_op jit(solution)/shard_map/ppermute | solution.py:667
  79.5 7.0 %collective-permute-start.20 = (bf16[112,512]{1,0:T(8,128)(2,1)S(1)}, bf16[112,512]{1,0:T(8,128)(2,1)S(1)}, u32[]{:S(2)}, u32[]{:S(2)}) collective-permute-start(bf16[112,512]{1,0:T(8,128)(2,1)S(1)} %get-tuple-element.114), channel_id=1, source_target_pairs={{0,24},{4,28},{8,16},{12,20},{16,8},{20,12},{24,0},{28,4},{1,25},{... | collective-permute-start | bytes 344072 | tf_op jit(solution)/shard_map/ppermute | solution.py:667
  86.6 1.4 %collective-permute-start.21 = (bf16[144,512]{1,0:T(8,128)(2,1)S(1)}, bf16[144,512]{1,0:T(8,128)(2,1)S(1)}, u32[]{:S(2)}, u32[]{:S(2)}) collective-permute-start(bf16[144,512]{1,0:T(8,128)(2,1)S(1)} %get-tuple-element.115), channel_id=1, source_target_pairs={{0,1},{1,0},{2,3},{3,2},{4,5},{5,4},{6,7},{7,6},{8,9},{9,8},{10,11... | collective-permute-start | bytes 442376 | tf_op jit(solution)/shard_map/ppermute | solution.py:650
  86.7 6.2 %collective-permute-start.15 = (bf16[1536,512]{1,0:T(8,128)(2,1)S(1)}, bf16[1536,512]{1,0:T(8,128)(2,1)S(1)}, u32[]{:S(2)}, u32[]{:S(2)}) collective-permute-start(bf16[1536,512]{1,0:T(8,128)(2,1)S(1)} %shard_map.285.own_ref), channel_id=1, source_target_pairs={{0,1},{1,0},{2,3},{3,2},{4,5},{5,4},{6,7},{7,6},{8,9},{9,8},{10,11... | collective-permute-start | bytes 4718600 | tf_op jit(solution)/shard_map/ppermute | solution.py:650
  88.1 7.8 %collective-permute-start.22 = (bf16[1536,512]{1,0:T(8,128)(2,1)S(1)}, bf16[1536,512]{1,0:T(8,128)(2,1)S(1)}, u32[]{:S(2)}, u32[]{:S(2)}) collective-permute-start(bf16[1536,512]{1,0:T(8,128)(2,1)S(1)} %get-tuple-element.116.own_ref), channel_id=1, source_target_pairs={{0,1},{1,0},{2,3},{3,2},{4,5},{5,4},{6,7},{7,6},{8,9},{9,8},{10,11... | collective-permute-start | bytes 4718600 | tf_op jit(solution)/shard_map/ppermute | solution.py:650
  88.3 12.4 %collective-permute-start.30 = (bf16[144,512]{1,0:T(8,128)(2,1)S(1)}, bf16[144,512]{1,0:T(8,128)(2,1)S(1)}, u32[]{:S(2)}, u32[]{:S(2)}) collective-permute-start(bf16[144,512]{1,0:T(8,128)(2,1)S(1)} %add_convert_fusion.2), channel_id=1, source_target_pairs={{0,4},{4,0},{8,12},{12,8},{16,20},{20,16},{24,28},{28,24},{1,5},{5... | collective-permute-start | bytes 442376 | tf_op jit(solution)/shard_map/ppermute | solution.py:667
  88.8 11.8 %collective-permute-start.26 = (bf16[112,512]{1,0:T(8,128)(2,1)S(1)}, bf16[112,512]{1,0:T(8,128)(2,1)S(1)}, u32[]{:S(2)}, u32[]{:S(2)}) collective-permute-start(bf16[112,512]{1,0:T(8,128)(2,1)S(1)} %add_convert_fusion.3.refs_0_), channel_id=1, source_target_pairs={{0,4},{4,0},{8,12},{12,8},{16,20},{20,16},{24,28},{28,24},{1,5},{5... | collective-permute-start | bytes 344072 | tf_op jit(solution)/shard_map/ppermute | solution.py:667
  90.3 10.4 %collective-permute-start.25 = (bf16[112,512]{1,0:T(8,128)(2,1)S(1)}, bf16[112,512]{1,0:T(8,128)(2,1)S(1)}, u32[]{:S(2)}, u32[]{:S(2)}) collective-permute-start(bf16[112,512]{1,0:T(8,128)(2,1)S(1)} %add_convert_fusion.3.refs_0_), channel_id=1, source_target_pairs={{0,24},{4,28},{8,16},{12,20},{16,8},{20,12},{24,0},{28,4},{1,25},{... | collective-permute-start | bytes 344072 | tf_op jit(solution)/shard_map/ppermute | solution.py:667
  92.9 10.9 %collective-permute-start.24 = (bf16[112,512]{1,0:T(8,128)(2,1)S(1)}, bf16[112,512]{1,0:T(8,128)(2,1)S(1)}, u32[]{:S(2)}, u32[]{:S(2)}) collective-permute-start(bf16[112,512]{1,0:T(8,128)(2,1)S(1)} %add_convert_fusion.3.refs_0_), channel_id=1, source_target_pairs={{0,16},{4,20},{8,24},{12,28},{16,0},{20,4},{24,8},{28,12},{1,17},{... | collective-permute-start | bytes 344072 | tf_op jit(solution)/shard_map/ppermute | solution.py:667
  95.8 22.0 %copy-start = (bf16[512,64]{0,1:T(8,128)(2,1)S(1)}, bf16[512,64]{0,1:T(8,128)(2,1)}, u32[]{:S(2)}) copy-start(bf16[512,64]{0,1:T(8,128)(2,1)} %param.21) | copy-start | bytes 196612
  95.8 22.0 %copy-start.1 = (bf16[512,64]{0,1:T(8,128)(2,1)S(1)}, bf16[512,64]{0,1:T(8,128)(2,1)}, u32[]{:S(2)}) copy-start(bf16[512,64]{0,1:T(8,128)(2,1)} %param.22) | copy-start | bytes 196612
  95.9 7.9 %collective-permute-start.23 = (bf16[112,512]{1,0:T(8,128)(2,1)S(1)}, bf16[112,512]{1,0:T(8,128)(2,1)S(1)}, u32[]{:S(2)}, u32[]{:S(2)}) collective-permute-start(bf16[112,512]{1,0:T(8,128)(2,1)S(1)} %add_convert_fusion.3.refs_0_), channel_id=1, source_target_pairs={{0,8},{4,12},{8,0},{12,4},{16,24},{20,28},{24,16},{28,20},{1,9},{5... | collective-permute-start | bytes 344072 | tf_op jit(solution)/shard_map/ppermute | solution.py:667
  103.8 5.2 %collective-permute-start.31 = (bf16[144,512]{1,0:T(8,128)(2,1)S(1)}, bf16[144,512]{1,0:T(8,128)(2,1)S(1)}, u32[]{:S(2)}, u32[]{:S(2)}) collective-permute-start(bf16[144,512]{1,0:T(8,128)(2,1)S(1)} %add_convert_fusion.1), channel_id=1, source_target_pairs={{0,8},{4,12},{8,0},{12,4},{16,24},{20,28},{24,16},{28,20},{1,9},{5... | collective-permute-start | bytes 442376 | tf_op jit(solution)/shard_map/ppermute | solution.py:667
  103.8 4.8 %collective-permute-start.27 = (bf16[112,512]{1,0:T(8,128)(2,1)S(1)}, bf16[112,512]{1,0:T(8,128)(2,1)S(1)}, u32[]{:S(2)}, u32[]{:S(2)}) collective-permute-start(bf16[112,512]{1,0:T(8,128)(2,1)S(1)} %collective-permute-done.23.refs_1_), channel_id=1, source_target_pairs={{0,4},{4,0},{8,12},{12,8},{16,20},{20,16},{24,28},{28,24},{1,5},{5... | collective-permute-start | bytes 344072 | tf_op jit(solution)/shard_map/ppermute | solution.py:667
  109.0 8.9 %collective-permute-start.32 = (bf16[144,512]{1,0:T(8,128)(2,1)S(1)}, bf16[144,512]{1,0:T(8,128)(2,1)S(1)}, u32[]{:S(2)}, u32[]{:S(2)}) collective-permute-start(bf16[144,512]{1,0:T(8,128)(2,1)S(1)} %add_convert_fusion.refs_8_), channel_id=1, source_target_pairs={{0,16},{4,20},{8,24},{12,28},{16,0},{20,4},{24,8},{28,12},{1,17},{... | collective-permute-start | bytes 442376 | tf_op jit(solution)/shard_map/ppermute | solution.py:667
  111.8 4.8 %collective-permute-start.29 = (bf16[112,512]{1,0:T(8,128)(2,1)S(1)}, bf16[112,512]{1,0:T(8,128)(2,1)S(1)}, u32[]{:S(2)}, u32[]{:S(2)}) collective-permute-start(bf16[112,512]{1,0:T(8,128)(2,1)S(1)} %collective-permute-done.25.refs_3_), channel_id=1, source_target_pairs={{0,4},{4,0},{8,12},{12,8},{16,20},{20,16},{24,28},{28,24},{1,5},{5... | collective-permute-start | bytes 344072 | tf_op jit(solution)/shard_map/ppermute | solution.py:667
  112.4 5.5 %collective-permute-start.28 = (bf16[112,512]{1,0:T(8,128)(2,1)S(1)}, bf16[112,512]{1,0:T(8,128)(2,1)S(1)}, u32[]{:S(2)}, u32[]{:S(2)}) collective-permute-start(bf16[112,512]{1,0:T(8,128)(2,1)S(1)} %collective-permute-done.24.refs_2_), channel_id=1, source_target_pairs={{0,4},{4,0},{8,12},{12,8},{16,20},{20,16},{24,28},{28,24},{1,5},{5... | collective-permute-start | bytes 344072 | tf_op jit(solution)/shard_map/ppermute | solution.py:667

commit v5 on v4

--- a/solution.py
+++ b/solution.py
@@ -12,6 +12,7 @@
 TENSOR = 4
 TILE = 8
 BLOCK = 256
+LARGE = 512
 PARAM_ROWS = 16
 F32 = jnp.float32
 BF16 = jnp.bfloat16
@@ -120,13 +121,13 @@
             cr, ci = hr[edge : edge + 1], hi[edge : edge + 1]
 
 
-def each_block(rows, body):
+def each_block(rows, size, body):
     def step(block, carry):
-        at = pl.multiple_of(block * BLOCK, BLOCK)
-        body(block, lambda ref: ref.at[pl.ds(at, BLOCK), :])
+        at = pl.multiple_of(block * size, size)
+        body(block, lambda ref: ref.at[pl.ds(at, size), :])
         return carry
 
-    lax.fori_loop(0, rows // BLOCK, step, 0)
+    lax.fori_loop(0, rows // size, step, 0)
 
 
 def fetch(pairs, sems):
@@ -295,14 +296,14 @@
         rows.append(cmul(*cmul(*rows[-1], *rows[-1]), *rows[1]))
     for k, (lr, li) in enumerate(rows):
         powers_ref[k : k + 1, :] = jnp.concatenate([lr, li], axis=1)
-    per_block = BLOCK // length
+    per_block = LARGE // length
 
     def body(block, view):
         low_ref, drive_ref = view(low_all), view(drive_all)
         drive_ref[...] = dot_nt(low_ref[...], in_t[...]) * gam
         weighted_ends(drive_ref, weigh, length, block * per_block, ends_ref)
 
-    each_block(low_all.shape[0], body)
+    each_block(low_all.shape[0], LARGE, body)
 
 
 def scan_kernel(drive_all, a0, a1, a2, a3, local_all, step, *, length, backwards):
@@ -310,6 +311,7 @@
     fill_steps(dr, di, backwards, step)
     each_block(
         drive_all.shape[0],
+        BLOCK,
         lambda block, view: scan_block(view(drive_all), view(local_all), step, length, backwards),
     )
 
@@ -324,22 +326,21 @@
             at = pl.multiple_of((shard ^ k) * per_f, per_f)
             hg_ref[:, pl.ds(at, per_f)] = dot_nt(cotm, pack[2 * per_s :, :]).astype(BF16)
 
-    each_block(cotm_all.shape[0], body)
+    each_block(cotm_all.shape[0], LARGE, body)
 
 
 def middle_kernel(where_ref, *refs, length, levels):
     far_refs, refs = refs[:levels], refs[levels:]
     beside_ref, powers_ref, local_all, normed_all, hg_all, cotm_all, a0, a1, a2, a3 = refs[:10]
     gain_ref, bias_ref, skip_ref, b0, b1, b2, b3, g0, g1, g2, g3 = refs[10:21]
-    state_all, back_all, backends_ref, ylow_all, hid_all, act_all, ul_half_all = refs[21:28]
-    c_all, ug_all, weigh, full, carry, ul, sems = refs[28:]
+    state_all, back_all, backends_ref, ylow_all, hid_all, act_all, ul_all = refs[21:28]
+    c_all, ug_all, weigh, full, carry, sems = refs[28:]
     place, core, shard = where_ref[0], where_ref[1], where_ref[2]
     states = c_all.shape[0] // 2
     rows, width = normed_all.shape
-    per_block = BLOCK // length
+    per_block = LARGE // length
     per_s = states // TENSOR
     per_f = hid_all.shape[1] // TENSOR
-    side = shard // 2
 
     copies = []
     for k, (pack, gates) in enumerate(((b0, g0), (b1, g1), (b2, g2), (b3, g3))):
@@ -364,7 +365,7 @@
 
     def body(block, view):
         local_ref, state_ref, hid_ref, ylow_ref = view(local_all), view(state_all), view(hid_all), view(ylow_all)
-        hg_ref, act_ref, back_ref = view(hg_all), view(act_all), view(back_all)
+        hg_ref, act_ref, back_ref, ul = view(hg_all), view(act_all), view(back_all), view(ul_all)
         for s in range(per_block):
             seq = block * per_block + s
             span = slice(s * length, (s + 1) * length)
@@ -393,9 +394,8 @@
         ylow_ref[...] = y_grad.astype(BF16)
         back_ref[...] = dot_nt(ylow_ref[...], c_all[...])
         weighted_ends(back_ref, weigh, length, block * per_block, backends_ref)
-        view(ul_half_all)[...] = ul[:, pl.ds(pl.multiple_of(side * 4 * per_f, 4 * per_f), 4 * per_f)]
-
-    each_block(rows, body)
+
+    each_block(rows, LARGE, body)
 
 
 def weight_kernel(where_ref, hid_ref, cotm_ref, act_ref, ul_ref, state_ref, ylow_ref, own_ref, sent_ref):
@@ -410,7 +410,7 @@
     out_grad = dot_tn(jnp.concatenate(cols, axis=1), ylow_ref[...])
     act, cotm = act_ref[...], cotm_ref[...]
     for n, ref in ((1 - core, sent_ref), (core, own_ref)):
-        ul = ul_ref[:, pl.ds(pl.multiple_of(n * 2 * per_f, 2 * per_f), 2 * per_f)]
+        ul = ul_ref[:, pl.ds(pl.multiple_of((2 * side + n) * 2 * per_f, 2 * per_f), 2 * per_f)]
         ref[2 * per_s + per_f : 2 * per_s + per_f + width, :] = dot_tn(act, ul).astype(ref.dtype)
         hid = hid_ref[:, pl.ds(pl.multiple_of((2 * side + n) * per_f, per_f), per_f)]
         ref[2 * per_s : 2 * per_s + per_f, :] = dot_tn(hid, cotm).astype(ref.dtype)
@@ -423,7 +423,7 @@
 def down_kernel(where_ref, lens_ref, tok_all, hid_all, b0, b1, b2, b3, out_all, down_all, tok, sems, *, length, per_s):
     shard = where_ref[2]
     rows, width = out_all.shape
-    per_block = BLOCK // length
+    per_block = LARGE // length
     per_f = down_all.shape[0] // TENSOR
     copies = half_copies(where_ref, tok_all, tok, sems)
     for copy in copies:
@@ -441,7 +441,7 @@
             live = mask_rows(lens_ref, where_ref, block * per_block + s, rows // length, length, width)
             out_ref[span, :] = jnp.where(live, tok_ref[span, :].astype(F32) + added[span, :], 0.0).astype(BF16)
 
-    each_block(rows, body)
+    each_block(rows, LARGE, body)
 
 
 def last_kernel(where_ref, *refs, length, levels):
@@ -501,7 +501,7 @@
             cols = dlow[:, pl.ds(k * states + at, 2 * per_s)]
             in_grad[2 * per_s * k : 2 * per_s * (k + 1), :] += dot_tn(cols, low)
 
-    each_block(rows, body)
+    each_block(rows, BLOCK, body)
     small = jnp.concatenate(
         [vec_grad[:3, :], lam_grad[...], jnp.zeros((PARAM_ROWS - 4, width), F32)], axis=0
     ).astype(BF16)
@@ -560,61 +560,55 @@
         ref[...] = (own_ref[pl.ds(at, rows), :] + other_ref[pl.ds(at, rows), :].astype(F32)).astype(ref.dtype)
 
 
-def finish_kernel(where_ref, *refs, ways):
-    parts, refs = refs[: 2 * ways], refs[2 * ways :]
-    mine_ref, other_ref, in_real, in_imag, nu, theta = refs[:6]
-    vec_outs, (in_real_out, in_imag_out), log_outs = refs[6:9], refs[9:11], refs[11:14]
-    real_ref, imag_ref, up_ref, gate_ref, down_ref, total, grads_ref, logs, fetched, sems, fetch_sems = refs[14:]
-    fetch([(ref, fetched.at[n]) for n, ref in enumerate((nu, theta))], fetch_sems)
-    nu, theta = fetched.at[0], fetched.at[1]
+def unpack_kernel(where_ref, *refs, ways):
+    parts, (real_ref, imag_ref, up_ref, gate_ref, down_ref, total, sems) = refs[: ways + 2], refs[ways + 2 :]
     place = where_ref[0]
     rows = parts[0].shape[0]
-    for n, part in enumerate(parts):
+    for n in range(2 * ways):
+        k = n % ways
         half = place % 2 if n < ways else 1 - place % 2
-        at = (half * ways + ((place // 2) ^ (n % ways))) * rows
-        total[pl.ds(pl.multiple_of(at, 16), rows), :] = part[...].astype(F32)
-    per_s = real_ref.shape[0]
-    per_f = down_ref.shape[0]
+        at = (half * ways + ((place // 2) ^ k)) * rows
+        if n <= ways:
+            part = parts[n][...]
+        else:
+            part = parts[-1][(k - 1) * rows : k * rows, :]
+        total[pl.ds(pl.multiple_of(at, 16), rows), :] = part.astype(F32)
+    per_s, per_f, width = real_ref.shape[0], down_ref.shape[0], up_ref.shape[0]
+    first = 2 * per_s + per_f
     moves = [
+        (total.at[pl.ds(first, width), pl.ds(0, per_f)], up_ref),
+        (total.at[pl.ds(first, width), pl.ds(per_f, per_f)], gate_ref),
+        (total.at[pl.ds(2 * per_s, per_f), :], down_ref),
         (total.at[pl.ds(0, per_s), :], real_ref),
         (total.at[pl.ds(per_s, per_s), :], imag_ref),
-        (total.at[pl.ds(2 * per_s, per_f), :], down_ref),
-        (total.at[pl.ds(2 * per_s + per_f, up_ref.shape[0]), pl.ds(0, per_f)], up_ref),
-        (total.at[pl.ds(2 * per_s + per_f, up_ref.shape[0]), pl.ds(per_f, per_f)], gate_ref),
     ]
-    copies = [pltpu.make_async_copy(src, dst, sems.at[n]) for n, (src, dst) in enumerate(moves)]
-    for copy in copies:
-        copy.start()
-
+    fetch(moves, sems)
+
+
+def finish_kernel(where_ref, mine_ref, other_ref, a_ref, logs_ref, *refs):
+    outs, (grads_ref, logs, sems) = refs[:8], refs[8:]
+    width = grads_ref.shape[1]
+    per_s = logs_ref.shape[2]
     grads = mine_ref[...].astype(F32) + other_ref[...].astype(F32)
     grads_ref[...] = grads
-    moves = [
-        (grads_ref.at[pl.ds(0, per_s), :], in_real_out),
-        (grads_ref.at[pl.ds(per_s, per_s), :], in_imag_out),
-    ]
-    moves += [(grads_ref.at[pl.ds(2 * per_s + n, 1), :], vec_outs[n]) for n in range(3)]
-    more = [pltpu.make_async_copy(src, dst, sems.at[5 + n]) for n, (src, dst) in enumerate(moves)]
-    for copy in more:
-        copy.start()
     lam = [jnp.zeros((1, per_s), F32), jnp.zeros((1, per_s), F32)]
     for t in range(TENSOR):
         for n in range(2):
             at = (n * TENSOR + t) * per_s
             part = grads[2 * per_s + 3 : 2 * per_s + 4, at : at + per_s]
             lam[n] = jnp.where(where_ref[2] == t, part, lam[n])
-    decay = jnp.exp(nu[...])
+    decay = jnp.exp(logs_ref[0])
     modulus = jnp.exp(-decay)
-    angle = jnp.exp(theta[...])
+    angle = jnp.exp(logs_ref[1])
     cos, sin = jnp.cos(angle), jnp.sin(angle)
     logs[0] = -decay * modulus * (lam[0] * cos + lam[1] * sin)
     logs[1] = angle * modulus * (lam[1] * cos - lam[0] * sin)
-    terms = in_real[...].astype(F32) * grads[:per_s, :] + in_imag[...].astype(F32) * grads[per_s : 2 * per_s, :]
+    terms = a_ref[:per_s, :].astype(F32) * grads[:per_s, :] + a_ref[per_s : 2 * per_s, :].astype(F32) * grads[per_s : 2 * per_s, :]
     logs[2] = jnp.sum(terms.T, axis=0, keepdims=True)
-    rest = [pltpu.make_async_copy(logs.at[n], log_outs[n], sems.at[10 + n]) for n in range(3)]
-    for copy in rest:
-        copy.start()
-    for copy in copies + more + rest:
-        copy.wait()
+    moves = [(grads_ref.at[pl.ds(2 * per_s + n, 1), :], outs[n]) for n in range(3)]
+    moves += [(grads_ref.at[pl.ds(n * per_s, per_s), :], outs[3 + n]) for n in range(2)]
+    moves += [(logs.at[n], outs[5 + n]) for n in range(3)]
+    fetch(moves, sems)
 
 
 def near(value):
@@ -715,12 +709,12 @@
     dma = pltpu.SemaphoreType.DMA
     line = lambda v: v.reshape(1, per_s)
 
-    pack_a = call(
+    pack_a, logs = call(
         input_pack_kernel,
         [where],
         [in_real.T, in_imag.T, line(nu_log), line(theta_log), line(gamma_log)],
-        (a_shape, BF16),
-        [pltpu.VMEM((3, 1, per_s), F32), dma((5,))],
+        [(a_shape, BF16), ((3, 1, per_s), F32)],
+        [dma((5,))],
         4,
         far_inputs=range(5),
     )
@@ -802,7 +796,7 @@
     packs_g = gather_tensor(pack_g, hid_grad, *far_ends)
 
     pack_rows = -(-(2 * per_s + per_f + width) // (16 * groups)) * 16 * groups
-    state, back_drive, back_ends, y_low, hid, act, ul_half = call(
+    state, back_drive, back_ends, y_low, hid, act, ul = call(
         functools.partial(middle_kernel, length=length, levels=levels),
         [where],
         [
@@ -827,7 +821,7 @@
             ((rows, width), BF16),
             ((rows, units), BF16),
             ((rows, width), BF16),
-            ((rows, units), BF16),
+            ((rows, 2 * units), BF16),
         ],
         [
             pltpu.VMEM((lanes, width), BF16),
@@ -835,29 +829,20 @@
             pltpu.VMEM((2, length, states), F32),
             pltpu.VMEM((2, length, states), F32),
             pltpu.VMEM((own_seqs, lanes), F32),
-            pltpu.VMEM((BLOCK, 2 * units), BF16),
             dma((TENSOR, 3)),
         ],
-        14,
+        16,
     )
     own_b, sent_b = call(
         weight_kernel,
         [where],
-        [hid, cot_m, act, ul_half, state, y_low],
+        [hid, cot_m, act, ul, state, y_low],
         [((pack_rows, width), F32), ((pack_rows, width), BF16)],
         [],
         10,
     )
 
     half, part = pack_rows // 2, pack_rows // groups
-    keep_b, send_b = call(
-        fold_kernel,
-        [where],
-        [own_b, core_swap(sent_b)],
-        [((half, width), F32), ((half, width), BF16)],
-        [],
-        4,
-    )
     made = []
 
     def scan_work(pair_back):
@@ -873,8 +858,16 @@
         )
         return made[0]
 
-    far_back, beside_back, found_back = exchange(back_ends, True, send_b, scan_work)
+    far_back, beside_back, found_back = exchange(back_ends, True, own_b, scan_work)
     back = made[0]
+    keep_b, send_b = call(
+        fold_kernel,
+        [where],
+        [own_b, core_swap(after(sent_b, beside_back))],
+        [((half, width), F32), ((half, width), BF16)],
+        [],
+        4,
+    )
     half_b = flip_dp(after(send_b, found_back[0]), 1, groups)
     out_own = call(
         functools.partial(down_kernel, length=length, per_s=per_s),
@@ -931,11 +924,10 @@
         mine_b = mine_b + flip_dp(dealt[k], 2 * k, groups).astype(F32)
     mine_b = mine_b.astype(BF16)
     gathered = [mine_b] + [flip_dp(mine_b, 2 * k, groups) for k in range(1, ways)]
-    beside = [flip_dp(piece, 1, groups) for piece in gathered]
+    beside = [flip_dp(mine_b, 1, groups), flip_dp(jnp.concatenate(gathered[1:], axis=0), 1, groups)]
 
     grads_a = own_a.astype(F32) + core_swap(after(sent_a, mine_b)).astype(F32)
     low_a = grads_a.astype(BF16)
-    other_a = flip_dp(low_a, 1, groups)
 
     block_out = call(
         join_halves_kernel,
@@ -956,50 +948,43 @@
         far_outs=(0,),
     )[0].reshape(seqs, length, width)
 
-    works = {1: [beside[0], block_out, input_grad], 2: [beside[1]]}
-    other_a = after(other_a, *works[1])
-    bit = 2
+    state_shape = ((per_s, width), F32)
+    unpacked = call(
+        functools.partial(unpack_kernel, ways=ways),
+        [where],
+        [*gathered, *beside],
+        [state_shape] * 2 + [((width, per_f), F32)] * 2 + [((per_f, width), F32)],
+        [pltpu.VMEM((pack_rows, width), F32), dma((5,))],
+        8,
+        far_outs=range(5),
+    )
+    works = {1: [block_out], 2: [input_grad, beside[0]], 4: unpacked}
+    bit = 1
     while bit < groups:
-        low_a = (low_a.astype(F32) + other_a.astype(F32)).astype(BF16)
-        if bit == 2:
+        other_a = after(flip_dp(low_a, bit, groups), *works.get(bit, []))
+        bit *= 2
+        if bit < groups:
+            low_a = (low_a.astype(F32) + other_a.astype(F32)).astype(BF16)
+        if bit == 4:
             low_a = after(low_a, *gathered)
-        other_a = flip_dp(low_a, bit, groups)
-        if bit in works:
-            other_a = after(other_a, *works[bit])
-        bit *= 2
-
-    state_shape = ((per_s, width), F32)
+
     finished = call(
-        functools.partial(finish_kernel, ways=ways),
-        [where],
-        [*gathered, *beside, low_a, other_a, in_real.T, in_imag.T, line(nu_log), line(theta_log)],
-        [((1, width), F32)] * 3
-        + [state_shape] * 2
-        + [((1, per_s), F32)] * 3
-        + [state_shape] * 2
-        + [((width, per_f), F32)] * 2
-        + [((per_f, width), F32)],
-        [
-            pltpu.VMEM((pack_rows, width), F32),
-            pltpu.VMEM(a_shape, F32),
-            pltpu.VMEM((3, 1, per_s), F32),
-            pltpu.VMEM((2, 1, per_s), F32),
-            dma((13,)),
-            dma((2,)),
-        ],
-        8,
-        far_inputs=(groups + 4, groups + 5),
-        far_outs=range(13),
-    )
-    vectors, in_grads, logs = finished[:3], finished[3:5], finished[5:8]
+        finish_kernel,
+        [where],
+        [low_a, other_a, pack_a, logs],
+        [((1, width), F32)] * 3 + [state_shape] * 2 + [((1, per_s), F32)] * 3,
+        [pltpu.VMEM(a_shape, F32), pltpu.VMEM((3, 1, per_s), F32), dma((8,))],
+        4,
+        far_outs=range(8),
+    )
     return (
         block_out,
         input_grad,
-        *[v.reshape(width) for v in vectors],
-        *[v.T for v in in_grads],
-        *finished[8:10],
-        *[v.reshape(per_s) for v in logs],
-        *finished[10:],
+        *[v.reshape(width) for v in finished[:3]],
+        *[v.T for v in finished[3:5]],
+        *unpacked[:2],
+        *[v.reshape(per_s) for v in finished[5:]],
+        *unpacked[2:],
     )
 
 

time: 121 us -> 116 us (0.959)
  starting transfers between devices: 40 us -> 36.6 us
  Pallas kernels: 57 us -> 54.3 us
    ppermute x16 -> x14, starting transfers between devices: 21.1 us -> 17.9 us  [flip_dp(): return lax.ppermute(value, 'dp', [(i, i ^ bits) for i in range(groups)])]
    pallas_call x20 -> x21, Pallas kernels: 57 us -> 54.3 us  [call(): pl.pallas_call(kernel, in_specs=[pl.BlockSpec(memory_space=pltpu.SMEM)] *...]
    ppermute x16 -> x14, waiting for transfers between devices: 14.4 us -> 13.1 us  [flip_dp(): return lax.ppermute(value, 'dp', [(i, i ^ bits) for i in range(groups)])]
    ppermute x10, waiting for transfers between devices: 3.61 us -> 4.83 us  [core_swap(): return lax.ppermute(value, 'tensor', [(t, t ^ 1) for t in range(TENSOR)])]
  transfers between devices with their start and end apart: 33 -> 31, of which waited for: 16 -> 14; matrix products, arithmetic and copies ran while one was open for 0% -> 0% of each run, Pallas kernels for 26% -> 31%
where the time goes in v5:
time: 116 us; the launch traced here: 115 us
  Pallas kernels  54.3 us (47%)
  starting transfers between devices  36.6 us (32%)
  waiting for transfers between devices  23 us (20%)
    pallas_call x21, Pallas kernels, call(): pl.pallas_call(kernel, in_specs=[pl.BlockSpec(memory_space=pltpu.SMEM)] *...  54.3 us
    ppermute x14, starting transfers between devices, flip_dp(): return lax.ppermute(value, 'dp', [(i, i ^ bits) for i in range(groups)])  17.9 us
    ppermute x14, waiting for transfers between devices, flip_dp(): return lax.ppermute(value, 'dp', [(i, i ^ bits) for i in range(groups)])  13.1 us
    ppermute x4, starting transfers between devices, shift_dp(): lax.ppermute(value, 'dp', [(i, i + by) for i in range(groups) if 0 <= i +...  11.5 us
    ppermute x3, starting transfers between devices, side_swap(): return lax.ppermute(value, 'tensor', [(t, t ^ 2) for t in range(TENSOR)])  5.12 us
    ppermute x4, waiting for transfers between devices, shift_dp(): lax.ppermute(value, 'dp', [(i, i + by) for i in range(groups) if 0 <= i +...  5.05 us
    ppermute x10, waiting for transfers between devices, core_swap(): return lax.ppermute(value, 'tensor', [(t, t ^ 1) for t in range(TENSOR)])  4.83 us
  transfers between devices with their start and end apart: 31, of which 14 were waited for; matrix products, arithmetic and copies ran while one was open for 0% of the time, Pallas kernels for 31%

profile of v5, /device:TPU:0, one launch (start us, length us, event | category | flops | bytes accessed | tf_op | source)
XLA Modules:
  0.0 115.3 jit_solution(17759237306077787051)
XLA Ops:
  0.7 1.6 %shard_map.271 = (bf16[144,512]{1,0:T(8,128)(2,1)S(1)}, f32[3,1,64]{2,1,0:T(1,128)S(1)}) custom-call(s32[3]{0:T(128)S(1)} %pad_add_fusion.where_ref, bf16[64,512]{1,0:T(8,128)(2,1)} %bitcast.36, bf16[64,512]{1,0:T(8,128)(2,1)} %bitcast.37, f32[1,64]{1,0:T(1,128)} %bitcast.38, f32[1,64]{1,0:T(1,128)} %bitcast.39, f32[1,64]{1,0:T(1,128)} %bitcast.40), custom_call_target="tpu_custom_call" | custom-call | tf_op jit(solution)/shard_map/pallas_call | solution.py:626
  2.3 3.0 %collective-permute-start.1 = (bf16[144,512]{1,0:T(8,128)(2,1)S(1)}, bf16[144,512]{1,0:T(8,128)(2,1)S(1)}, u32[]{:S(2)}, u32[]{:S(2)}) collective-permute-start(bf16[144,512]{1,0:T(8,128)(2,1)S(1)} %get-tuple-element.78.a0.refs_8_.refs_11_.a_ref), channel_id=1, source_target_pairs={{0,2},{1,3},{2,0},{3,1},{4,6},{5,7},{6,4},{7,5},{8,10},{9,11},{10,... | collective-permute-start | bytes 442376 | tf_op jit(solution)/shard_map/ppermute | solution.py:648
  5.4 4.2 %shard_map.272 = (bf16[1536,512]{1,0:T(8,128)(2,1)S(1)}, f32[1536,512]{1,0:T(8,128)S(1)}, f32[1536,128]{1,0:T(8,128)S(1)}, bf16[1536,512]{1,0:T(8,128)(2,1)S(1)}) custom-call(s32[3]{0:T(128)S(1)} %pad_add_fusion.where_ref, bf16[3072,512]{1,0:T(8,128)(2,1)} %bitcast.31, bf16[3072,512]{1,0:T(8,128)(2,1)} %bitcast.34, f32[1,512]{1,0:T(1,128)} %bitcast.23, ...), custom_call_target="tpu_custom_call" | custom-call | tf_op jit(solution)/shard_map/pallas_call | solution.py:626
  9.6 1.2 %shard_map.277 = (bf16[384,512]{1,0:T(8,128)(2,1)S(1)}, bf16[512,512]{1,0:T(8,128)(2,1)S(1)}) custom-call(bf16[64,512]{1,0:T(8,128)(2,1)} %out_real, bf16[64,512]{1,0:T(8,128)(2,1)} %out_imag.1, bf16[512,256]{1,0:T(8,128)(2,1)} %up.1, bf16[512,256]{1,0:T(8,128)(2,1)} %gate.1, bf16[256,512]{1,0:T(8,128)(2,1)} %down.1), custom_call_target="tpu_custom_call" | custom-call | tf_op jit(solution)/shard_map/pallas_call | solution.py:626
  10.8 1.5 %collective-permute-start.7 = (bf16[384,512]{1,0:T(8,128)(2,1)S(1)}, bf16[384,512]{1,0:T(8,128)(2,1)S(1)}, u32[]{:S(2)}, u32[]{:S(2)}) collective-permute-start(bf16[384,512]{1,0:T(8,128)(2,1)S(1)} %get-tuple-element.90.b0.refs_15_), channel_id=1, source_target_pairs={{0,2},{1,3},{2,0},{3,1},{4,6},{5,7},{6,4},{7,5},{8,10},{9,11},{10,... | collective-permute-start | bytes 1179656 | tf_op jit(solution)/shard_map/ppermute | solution.py:648
  12.8 0.6 collective-permute-start.10
  13.8 2.3 %shard_map.273 = (f32[1536,512]{1,0:T(8,128)S(1)}, f32[12,512]{1,0:T(8,128)S(1)}, f32[8,512]{1,0:T(8,128)S(1)}) custom-call(s32[3]{0:T(128)S(1)} %pad_add_fusion.where_ref, bf16[1536,512]{1,0:T(8,128)(2,1)S(1)} %get-tuple-element.80.low_all.refs_4_, bf16[144,512]{1,0:T(8,128)(2,1)S(1)} %get-tuple-element.78.a0.refs_8_.refs_11_.a_ref, ...), custom_call_target="tpu_custom_call" | custom-call | tf_op jit(solution)/shard_map/pallas_call | solution.py:626
  16.1 1.6 %collective-permute-start.3 = (f32[12,512]{1,0:T(8,128)S(1)}, f32[12,512]{1,0:T(8,128)S(1)}, u32[]{:S(2)}, u32[]{:S(2)}) collective-permute-start(f32[12,512]{1,0:T(8,128)S(1)} %get-tuple-element.82.mine_ref), channel_id=1, source_target_pairs={{0,4},{4,0},{8,12},{12,8},{16,20},{20,16},{24,28},{28,24},{1,5},{5... | collective-permute-start | bytes 73736 | tf_op jit(solution)/shard_map/ppermute | solution.py:661
  17.7 2.1 %shard_map.274.refs_4_ = f32[1536,512]{1,0:T(8,128)S(1)} custom-call(f32[1536,512]{1,0:T(8,128)S(1)} %get-tuple-element.83.drive_all, bf16[144,512]{1,0:T(8,128)(2,1)S(1)} %get-tuple-element.78.a0.refs_8_.refs_11_.a_ref, bf16[144,512]{1,0:T(8,128)(2,1)S(1)} %collective-permute-done.a1.refs_9_.refs_12_, ...), custom_call_target="tpu_custom_call" | custom-call | tf_op jit(solution)/shard_map/pallas_call | solution.py:626
  20.1 0.6 shard_map.275.mine_ref
  20.7 3.5 %collective-permute-start.4 = (f32[12,512]{1,0:T(8,128)S(1)}, f32[12,512]{1,0:T(8,128)S(1)}, u32[]{:S(2)}, u32[]{:S(2)}) collective-permute-start(f32[12,512]{1,0:T(8,128)S(1)} %shard_map.275.mine_ref), channel_id=1, source_target_pairs={{0,8},{4,12},{8,16},{12,20},{16,24},{20,28},{1,9},{5,13},{9,17},{1... | collective-permute-start | bytes 73736 | tf_op jit(solution)/shard_map/ppermute | solution.py:665
  24.2 1.5 %collective-permute-done.4.other_ref.refs_0_ = f32[12,512]{1,0:T(8,128)S(1)} collective-permute-done((f32[12,512]{1,0:T(8,128)S(1)}, f32[12,512]{1,0:T(8,128)S(1)}, u32[]{:S(2)}, u32[]{:S(2)}) %collective-permute-start.4) | collective-permute-done | bytes 24608 | tf_op jit(solution)/shard_map/ppermute | solution.py:665
  25.8 5.2 %collective-permute-start.5 = (f32[12,512]{1,0:T(8,128)S(1)}, f32[12,512]{1,0:T(8,128)S(1)}, u32[]{:S(2)}, u32[]{:S(2)}) collective-permute-start(f32[12,512]{1,0:T(8,128)S(1)} %shard_map.276), channel_id=1, source_target_pairs={{0,16},{4,20},{8,24},{12,28},{1,17},{5,21},{9,25},{13,29},{2,18},{... | collective-permute-start | bytes 73736 | tf_op jit(solution)/shard_map/ppermute | solution.py:665
  31.3 3.0 %shard_map.278.refs_6_ = bf16[1536,1024]{1,0:T(8,128)(2,1)S(1)} custom-call(s32[3]{0:T(128)S(1)} %pad_add_fusion.where_ref, bf16[1536,512]{1,0:T(8,128)(2,1)S(1)} %get-tuple-element.88.cotm_all.refs_7_.cotm_ref, bf16[384,512]{1,0:T(8,128)(2,1)S(1)} %get-tuple-element.90.b0.refs_15_, bf16[384,512]{1,0:T(8,128)(2,1)S(1)} %collective-permute-done.6.b1.refs_16_, ...), custom_call_target="tpu_custom_call" | custom-call | tf_op jit(solution)/shard_map/pallas_call | solution.py:626
  34.7 1.6 %collective-permute-done.11.refs_22_ = bf16[512,512]{1,0:T(8,128)(2,1)S(1)} collective-permute-done((bf16[512,512]{1,0:T(8,128)(2,1)S(1)}, bf16[512,512]{1,0:T(8,128)(2,1)S(1)}, u32[]{:S(2)}, u32[]{:S(2)}) %collective-permute-start.11) | collective-permute-done | bytes 524320 | tf_op jit(solution)/shard_map/ppermute | solution.py:644
  36.4 12.8 %shard_map.279 = (bf16[1536,512]{1,0:T(8,128)(2,1)S(1)}, f32[1536,512]{1,0:T(8,128)S(1)}, f32[12,512]{1,0:T(8,128)S(1)}, bf16[1536,512]{1,0:T(8,128)(2,1)S(1)}, ...) custom-call(s32[3]{0:T(128)S(1)} %pad_add_fusion.where_ref, ...), custom_call_target="tpu_custom_call" | custom-call | tf_op jit(solution)/shard_map/pallas_call | solution.py:626
  49.2 1.6 %collective-permute-start.12 = (f32[12,512]{1,0:T(8,128)S(1)}, f32[12,512]{1,0:T(8,128)S(1)}, u32[]{:S(2)}, u32[]{:S(2)}) collective-permute-start(f32[12,512]{1,0:T(8,128)S(1)} %get-tuple-element.95.mine_ref), channel_id=1, source_target_pairs={{0,4},{4,0},{8,12},{12,8},{16,20},{20,16},{24,28},{28,24},{1,5},{5... | collective-permute-start | bytes 73736 | tf_op jit(solution)/shard_map/ppermute | solution.py:661
  50.8 3.6 %shard_map.280 = (f32[896,512]{1,0:T(8,128)S(1)}, bf16[896,512]{1,0:T(8,128)(2,1)S(1)}) custom-call(s32[3]{0:T(128)S(1)} %pad_add_fusion.where_ref, bf16[1536,1024]{1,0:T(8,128)(2,1)S(1)} %get-tuple-element.105.hid_ref.hid_all, bf16[1536,512]{1,0:T(8,128)(2,1)S(1)} %get-tuple-element.88.cotm_all.refs_7_.cotm_ref, ...), custom_call_target="tpu_custom_call" | custom-call | tf_op jit(solution)/shard_map/pallas_call | solution.py:626
  55.0 1.9 %collective-permute-done.16.other_ref = bf16[896,512]{1,0:T(8,128)(2,1)S(1)} collective-permute-done((bf16[896,512]{1,0:T(8,128)(2,1)S(1)}, bf16[896,512]{1,0:T(8,128)(2,1)S(1)}, u32[]{:S(2)}, u32[]{:S(2)}) %collective-permute-start.16) | collective-permute-done | bytes 917536 | tf_op jit(solution)/shard_map/ppermute | solution.py:644
  56.9 0.7 shard_map.286
  57.6 0.6 collective-permute-start.17
  58.2 1.3 %collective-permute-start.13 = (f32[12,512]{1,0:T(8,128)S(1)}, f32[12,512]{1,0:T(8,128)S(1)}, u32[]{:S(2)}, u32[]{:S(2)}) collective-permute-start(f32[12,512]{1,0:T(8,128)S(1)} %shard_map.281.mine_ref), channel_id=1, source_target_pairs={{8,0},{12,4},{16,8},{20,12},{24,16},{28,20},{9,1},{13,5},{17,9},{2... | collective-permute-start | bytes 73736 | tf_op jit(solution)/shard_map/ppermute | solution.py:665
  59.5 2.1 %shard_map.282.refs_8_ = f32[1536,512]{1,0:T(8,128)S(1)} custom-call(f32[1536,512]{1,0:T(8,128)S(1)} %get-tuple-element.103.drive_all, bf16[144,512]{1,0:T(8,128)(2,1)S(1)} %get-tuple-element.78.a0.refs_8_.refs_11_.a_ref, bf16[144,512]{1,0:T(8,128)(2,1)S(1)} %collective-permute-done.a1.refs_9_.refs_12_, ...), custom_call_target="tpu_custom_call" | custom-call | tf_op jit(solution)/shard_map/pallas_call | solution.py:626
  61.6 2.4 %collective-permute-done.13.other_ref.refs_0_ = f32[12,512]{1,0:T(8,128)S(1)} collective-permute-done((f32[12,512]{1,0:T(8,128)S(1)}, f32[12,512]{1,0:T(8,128)S(1)}, u32[]{:S(2)}, u32[]{:S(2)}) %collective-permute-start.13) | collective-permute-done | bytes 24608 | tf_op jit(solution)/shard_map/ppermute | solution.py:665
  64.0 1.5 %collective-permute-start.15 = (f32[12,512]{1,0:T(8,128)S(1)}, f32[12,512]{1,0:T(8,128)S(1)}, u32[]{:S(2)}, u32[]{:S(2)}) collective-permute-start(f32[12,512]{1,0:T(8,128)S(1)} %shard_map.283), channel_id=1, source_target_pairs={{16,0},{20,4},{24,8},{28,12},{17,1},{21,5},{25,9},{29,13},{18,2},{... | collective-permute-start | bytes 73736 | tf_op jit(solution)/shard_map/ppermute | solution.py:665
  65.5 4.1 %shard_map.284.own_ref = bf16[1536,512]{1,0:T(8,128)(2,1)S(1)} custom-call(s32[3]{0:T(128)S(1)} %pad_add_fusion.where_ref, s32[24]{0:T(128)S(1)} %copy-done.3, bf16[3072,512]{1,0:T(8,128)(2,1)} %bitcast.32, bf16[1536,1024]{1,0:T(8,128)(2,1)S(1)} %get-tuple-element.105.hid_ref.hid_all, bf16[384,512]{1,0:T(8,128)(2,1)S(1)} %get-tuple-element.90.b0.refs_15_, ...), custom_call_target="tpu_custom_call" | custom-call | tf_op jit(solution)/shard_map/pallas_call | solution.py:626
  69.6 1.1 collective-permute-done.15.refs_1_
  70.7 0.7 shard_map.287
  71.4 1.6 %collective-permute-start.18 = (bf16[112,512]{1,0:T(8,128)(2,1)S(1)}, bf16[112,512]{1,0:T(8,128)(2,1)S(1)}, u32[]{:S(2)}, u32[]{:S(2)}) collective-permute-start(bf16[112,512]{1,0:T(8,128)(2,1)S(1)} %get-tuple-element.118), channel_id=1, source_target_pairs={{0,8},{4,12},{8,0},{12,4},{16,24},{20,28},{24,16},{28,20},{1,9},{5... | collective-permute-start | bytes 344072 | tf_op jit(solution)/shard_map/ppermute | solution.py:661
  73.0 2.4 %collective-permute-start.19 = (bf16[112,512]{1,0:T(8,128)(2,1)S(1)}, bf16[112,512]{1,0:T(8,128)(2,1)S(1)}, u32[]{:S(2)}, u32[]{:S(2)}) collective-permute-start(bf16[112,512]{1,0:T(8,128)(2,1)S(1)} %get-tuple-element.119), channel_id=1, source_target_pairs={{0,16},{4,20},{8,24},{12,28},{16,0},{20,4},{24,8},{28,12},{1,17},{... | collective-permute-start | bytes 344072 | tf_op jit(solution)/shard_map/ppermute | solution.py:661
  75.8 5.6 %shard_map.288 = (bf16[1536,512]{1,0:T(8,128)(2,1)S(1)}, bf16[144,512]{1,0:T(8,128)(2,1)S(1)}, bf16[144,512]{1,0:T(8,128)(2,1)S(1)}) custom-call(s32[3]{0:T(128)S(1)} %pad_add_fusion.where_ref, f32[12,512]{1,0:T(8,128)S(1)} %collective-permute-done.13.other_ref.refs_0_, f32[12,512]{1,0:T(8,128)S(1)} %collective-permute-done.15.refs_1_, ...), custom_call_target="tpu_custom_call" | custom-call | tf_op jit(solution)/shard_map/pallas_call | solution.py:626
  81.5 2.2 %collective-permute-done.19 = bf16[112,512]{1,0:T(8,128)(2,1)S(1)} collective-permute-done((bf16[112,512]{1,0:T(8,128)(2,1)S(1)}, bf16[112,512]{1,0:T(8,128)(2,1)S(1)}, u32[]{:S(2)}, u32[]{:S(2)}) %collective-permute-start.19) | collective-permute-done | bytes 114720 | tf_op jit(solution)/shard_map/ppermute | solution.py:661
  84.3 0.9 collective-permute-done.21
  85.4 1.2 %collective-permute-start.23 = (bf16[144,512]{1,0:T(8,128)(2,1)S(1)}, bf16[144,512]{1,0:T(8,128)(2,1)S(1)}, u32[]{:S(2)}, u32[]{:S(2)}) collective-permute-start(bf16[144,512]{1,0:T(8,128)(2,1)S(1)} %add_convert_fusion.2), channel_id=1, source_target_pairs={{0,4},{4,0},{8,12},{12,8},{16,20},{20,16},{24,28},{28,24},{1,5},{5... | collective-permute-start | bytes 442376 | tf_op jit(solution)/shard_map/ppermute | solution.py:661
  86.6 2.6 %collective-permute-start.28 = (bf16[112,512]{1,0:T(8,128)(2,1)S(1)}, bf16[112,512]{1,0:T(8,128)(2,1)S(1)}, u32[]{:S(2)}, u32[]{:S(2)}) collective-permute-start(bf16[112,512]{1,0:T(8,128)(2,1)S(1)} %add_convert_fusion.3.refs_0_), channel_id=1, source_target_pairs={{0,24},{4,28},{8,16},{12,20},{16,8},{20,12},{24,0},{28,4},{1,25},{... | collective-permute-start | bytes 344072 | tf_op jit(solution)/shard_map/ppermute | solution.py:661
  89.2 0.7 collective-permute-start.27
  89.9 1.1 collective-permute-start.26
  91.0 2.2 %shard_map.285 = bf16[3072,512]{1,0:T(8,128)(2,1)} custom-call(s32[3]{0:T(128)S(1)} %pad_add_fusion.where_ref, bf16[1536,512]{1,0:T(8,128)(2,1)S(1)} %shard_map.284.own_ref, bf16[1536,512]{1,0:T(8,128)(2,1)S(1)} %collective-permute-done.14.other_ref), custom_call_target="tpu_custom_call" | custom-call | tf_op jit(solution)/shard_map/pallas_call | solution.py:626
  93.3 1.0 collective-permute-start.24
  94.4 0.9 collective-permute-start.25
  95.4 5.1 %collective-permute-done.27.refs_2_ = bf16[112,512]{1,0:T(8,128)(2,1)S(1)} collective-permute-done((bf16[112,512]{1,0:T(8,128)(2,1)S(1)}, bf16[112,512]{1,0:T(8,128)(2,1)S(1)}, u32[]{:S(2)}, u32[]{:S(2)}) %collective-permute-start.27) | collective-permute-done | bytes 114720 | tf_op jit(solution)/shard_map/ppermute | solution.py:661
  100.5 0.9 collective-permute-start.30
  101.4 3.6 %shard_map.289 = f32[3072,512]{1,0:T(8,128)} custom-call(s32[3]{0:T(128)S(1)} %pad_add_fusion.where_ref, bf16[1536,512]{1,0:T(8,128)(2,1)S(1)} %get-tuple-element.122.own_ref, bf16[1536,512]{1,0:T(8,128)(2,1)S(1)} %collective-permute-done.22.other_ref), custom_call_target="tpu_custom_call" | custom-call | tf_op jit(solution)/shard_map/pallas_call | solution.py:626
  105.0 1.4 %collective-permute-start.29 = (bf16[144,512]{1,0:T(8,128)(2,1)S(1)}, bf16[144,512]{1,0:T(8,128)(2,1)S(1)}, u32[]{:S(2)}, u32[]{:S(2)}) collective-permute-start(bf16[144,512]{1,0:T(8,128)(2,1)S(1)} %add_convert_fusion.mine_ref), channel_id=1, source_target_pairs={{0,16},{4,20},{8,24},{12,28},{16,0},{20,4},{24,8},{28,12},{1,17},{... | collective-permute-start | bytes 442376 | tf_op jit(solution)/shard_map/ppermute | solution.py:661
  106.4 3.5 %collective-permute-done.30.refs_5_ = bf16[336,512]{1,0:T(8,128)(2,1)S(1)} collective-permute-done((bf16[336,512]{1,0:T(8,128)(2,1)S(1)}, bf16[336,512]{1,0:T(8,128)(2,1)S(1)}, u32[]{:S(2)}, u32[]{:S(2)}) %collective-permute-start.30) | collective-permute-done | bytes 344096 | tf_op jit(solution)/shard_map/ppermute | solution.py:661
  109.9 1.9 %shard_map.290 = (f32[64,512]{1,0:T(8,128)}, f32[64,512]{1,0:T(8,128)}, f32[512,256]{1,0:T(8,128)}, f32[512,256]{1,0:T(8,128)}, f32[256,512]{1,0:T(8,128)}) custom-call(s32[3]{0:T(128)S(1)} %pad_add_fusion.where_ref, bf16[112,512]{1,0:T(8,128)(2,1)S(1)} %add_convert_fusion.3.refs_0_, bf16[112,512]{1,0:T(8,128)(2,1)S(1)} %collective-permute-done.26.refs_1_, ...), custom_call_target="tpu_custom_call" | custom-call | tf_op jit(solution)/shard_map/pallas_call | solution.py:626
  111.8 1.8 %collective-permute-done.29.other_ref = bf16[144,512]{1,0:T(8,128)(2,1)S(1)} collective-permute-done((bf16[144,512]{1,0:T(8,128)(2,1)S(1)}, bf16[144,512]{1,0:T(8,128)(2,1)S(1)}, u32[]{:S(2)}, u32[]{:S(2)}) %collective-permute-start.29) | collective-permute-done | bytes 147488 | tf_op jit(solution)/shard_map/ppermute | solution.py:661
  113.6 1.5 %shard_map.291 = (f32[1,512]{1,0:T(1,128)}, f32[1,512]{1,0:T(1,128)}, f32[1,512]{1,0:T(1,128)}, f32[64,512]{1,0:T(8,128)}, f32[64,512]{1,0:T(8,128)}, /*index=5*...) custom-call(s32[3]{0:T(128)S(1)} %pad_add_fusion.where_ref, bf16[144,512]{1,0:T(8,128)(2,1)S(1)} %add_convert_fusion.mine_ref, ...), custom_call_target="tpu_custom_call" | custom-call | tf_op jit(solution)/shard_map/pallas_call | solution.py:626
  (49 shorter events, 4.4 us)
Async XLA Ops:
  2.3 7.2 %collective-permute-start.1 = (bf16[144,512]{1,0:T(8,128)(2,1)S(1)}, bf16[144,512]{1,0:T(8,128)(2,1)S(1)}, u32[]{:S(2)}, u32[]{:S(2)}) collective-permute-start(bf16[144,512]{1,0:T(8,128)(2,1)S(1)} %get-tuple-element.78.a0.refs_8_.refs_11_.a_ref), channel_id=1, source_target_pairs={{0,2},{1,3},{2,0},{3,1},{4,6},{5,7},{6,4},{7,5},{8,10},{9,11},{10,... | collective-permute-start | bytes 442376 | tf_op jit(solution)/shard_map/ppermute | solution.py:648
  10.8 14.9 %collective-permute-start.7 = (bf16[384,512]{1,0:T(8,128)(2,1)S(1)}, bf16[384,512]{1,0:T(8,128)(2,1)S(1)}, u32[]{:S(2)}, u32[]{:S(2)}) collective-permute-start(bf16[384,512]{1,0:T(8,128)(2,1)S(1)} %get-tuple-element.90.b0.refs_15_), channel_id=1, source_target_pairs={{0,2},{1,3},{2,0},{3,1},{4,6},{5,7},{6,4},{7,5},{8,10},{9,11},{10,... | collective-permute-start | bytes 1179656 | tf_op jit(solution)/shard_map/ppermute | solution.py:648
  12.3 1.4 %collective-permute-start = (bf16[144,512]{1,0:T(8,128)(2,1)S(1)}, bf16[144,512]{1,0:T(8,128)(2,1)S(1)}, u32[]{:S(2)}, u32[]{:S(2)}) collective-permute-start(bf16[144,512]{1,0:T(8,128)(2,1)S(1)} %get-tuple-element.78.a0.refs_8_.refs_11_.a_ref), channel_id=1, source_target_pairs={{0,1},{1,0},{2,3},{3,2},{4,5},{5,4},{6,7},{7,6},{8,9},{9,8},{10,11... | collective-permute-start | bytes 442376 | tf_op jit(solution)/shard_map/ppermute | solution.py:644
  12.3 1.6 %collective-permute-start.2 = (bf16[144,512]{1,0:T(8,128)(2,1)S(1)}, bf16[144,512]{1,0:T(8,128)(2,1)S(1)}, u32[]{:S(2)}, u32[]{:S(2)}) collective-permute-start(bf16[144,512]{1,0:T(8,128)(2,1)S(1)} %collective-permute-done.1.a2.refs_10_.refs_13_), channel_id=1, source_target_pairs={{0,1},{1,0},{2,3},{3,2},{4,5},{5,4},{6,7},{7,6},{8,9},{9,8},{10,11... | collective-permute-start | bytes 442376 | tf_op jit(solution)/shard_map/ppermute | solution.py:644
  12.8 21.6 %collective-permute-start.10 = (bf16[512,512]{1,0:T(8,128)(2,1)S(1)}, bf16[512,512]{1,0:T(8,128)(2,1)S(1)}, u32[]{:S(2)}, u32[]{:S(2)}) collective-permute-start(bf16[512,512]{1,0:T(8,128)(2,1)S(1)} %get-tuple-element.92.refs_19_), channel_id=1, source_target_pairs={{0,2},{1,3},{2,0},{3,1},{4,6},{5,7},{6,4},{7,5},{8,10},{9,11},{10,... | collective-permute-start | bytes 1572872 | tf_op jit(solution)/shard_map/ppermute | solution.py:648
  16.1 4.0 %collective-permute-start.3 = (f32[12,512]{1,0:T(8,128)S(1)}, f32[12,512]{1,0:T(8,128)S(1)}, u32[]{:S(2)}, u32[]{:S(2)}) collective-permute-start(f32[12,512]{1,0:T(8,128)S(1)} %get-tuple-element.82.mine_ref), channel_id=1, source_target_pairs={{0,4},{4,0},{8,12},{12,8},{16,20},{20,16},{24,28},{28,24},{1,5},{5... | collective-permute-start | bytes 73736 | tf_op jit(solution)/shard_map/ppermute | solution.py:661
  20.7 5.1 %collective-permute-start.4 = (f32[12,512]{1,0:T(8,128)S(1)}, f32[12,512]{1,0:T(8,128)S(1)}, u32[]{:S(2)}, u32[]{:S(2)}) collective-permute-start(f32[12,512]{1,0:T(8,128)S(1)} %shard_map.275.mine_ref), channel_id=1, source_target_pairs={{0,8},{4,12},{8,16},{12,20},{16,24},{20,28},{1,9},{5,13},{9,17},{1... | collective-permute-start | bytes 73736 | tf_op jit(solution)/shard_map/ppermute | solution.py:665
  24.2 7.1 %collective-permute-start.6 = (bf16[384,512]{1,0:T(8,128)(2,1)S(1)}, bf16[384,512]{1,0:T(8,128)(2,1)S(1)}, u32[]{:S(2)}, u32[]{:S(2)}) collective-permute-start(bf16[384,512]{1,0:T(8,128)(2,1)S(1)} %get-tuple-element.90.b0.refs_15_), channel_id=1, source_target_pairs={{0,1},{1,0},{2,3},{3,2},{4,5},{5,4},{6,7},{7,6},{8,9},{9,8},{10,11... | collective-permute-start | bytes 1179656 | tf_op jit(solution)/shard_map/ppermute | solution.py:644
  25.7 5.6 %collective-permute-start.8 = (bf16[384,512]{1,0:T(8,128)(2,1)S(1)}, bf16[384,512]{1,0:T(8,128)(2,1)S(1)}, u32[]{:S(2)}, u32[]{:S(2)}) collective-permute-start(bf16[384,512]{1,0:T(8,128)(2,1)S(1)} %collective-permute-done.7.b2.refs_17_), channel_id=1, source_target_pairs={{0,1},{1,0},{2,3},{3,2},{4,5},{5,4},{6,7},{7,6},{8,9},{9,8},{10,11... | collective-permute-start | bytes 1179656 | tf_op jit(solution)/shard_map/ppermute | solution.py:644
  25.8 8.6 %collective-permute-start.5 = (f32[12,512]{1,0:T(8,128)S(1)}, f32[12,512]{1,0:T(8,128)S(1)}, u32[]{:S(2)}, u32[]{:S(2)}) collective-permute-start(f32[12,512]{1,0:T(8,128)S(1)} %shard_map.276), channel_id=1, source_target_pairs={{0,16},{4,20},{8,24},{12,28},{1,17},{5,21},{9,25},{13,29},{2,18},{... | collective-permute-start | bytes 73736 | tf_op jit(solution)/shard_map/ppermute | solution.py:665
  31.0 3.7 %collective-permute-start.9 = (bf16[512,512]{1,0:T(8,128)(2,1)S(1)}, bf16[512,512]{1,0:T(8,128)(2,1)S(1)}, u32[]{:S(2)}, u32[]{:S(2)}) collective-permute-start(bf16[512,512]{1,0:T(8,128)(2,1)S(1)} %get-tuple-element.92.refs_19_), channel_id=1, source_target_pairs={{0,1},{1,0},{2,3},{3,2},{4,5},{5,4},{6,7},{7,6},{8,9},{9,8},{10,11... | collective-permute-start | bytes 1572872 | tf_op jit(solution)/shard_map/ppermute | solution.py:644
  31.3 5.1 %copy-start = (f32[512]{0:T(512)S(1)}, f32[512]{0:T(512)}, u32[]{:S(2)}) copy-start(f32[512]{0:T(512)} %param.18) | copy-start | bytes 6148
  31.3 5.1 %copy-start.1 = (f32[512]{0:T(512)S(1)}, f32[512]{0:T(512)}, u32[]{:S(2)}) copy-start(f32[512]{0:T(512)} %param.19) | copy-start | bytes 6148
  31.3 5.1 %copy-start.2 = (f32[512]{0:T(512)S(1)}, f32[512]{0:T(512)}, u32[]{:S(2)}) copy-start(f32[512]{0:T(512)} %param.20) | copy-start | bytes 6148
  34.4 2.0 %collective-permute-start.11 = (bf16[512,512]{1,0:T(8,128)(2,1)S(1)}, bf16[512,512]{1,0:T(8,128)(2,1)S(1)}, u32[]{:S(2)}, u32[]{:S(2)}) collective-permute-start(bf16[512,512]{1,0:T(8,128)(2,1)S(1)} %collective-permute-done.10.refs_21_), channel_id=1, source_target_pairs={{0,1},{1,0},{2,3},{3,2},{4,5},{5,4},{6,7},{7,6},{8,9},{9,8},{10,11... | collective-permute-start | bytes 1572872 | tf_op jit(solution)/shard_map/ppermute | solution.py:644
  49.2 5.2 %collective-permute-start.12 = (f32[12,512]{1,0:T(8,128)S(1)}, f32[12,512]{1,0:T(8,128)S(1)}, u32[]{:S(2)}, u32[]{:S(2)}) collective-permute-start(f32[12,512]{1,0:T(8,128)S(1)} %get-tuple-element.95.mine_ref), channel_id=1, source_target_pairs={{0,4},{4,0},{8,12},{12,8},{16,20},{20,16},{24,28},{28,24},{1,5},{5... | collective-permute-start | bytes 73736 | tf_op jit(solution)/shard_map/ppermute | solution.py:661
  54.4 2.5 %collective-permute-start.16 = (bf16[896,512]{1,0:T(8,128)(2,1)S(1)}, bf16[896,512]{1,0:T(8,128)(2,1)S(1)}, u32[]{:S(2)}, u32[]{:S(2)}) collective-permute-start(bf16[896,512]{1,0:T(8,128)(2,1)S(1)} %get-tuple-element.107), channel_id=1, source_target_pairs={{0,1},{1,0},{2,3},{3,2},{4,5},{5,4},{6,7},{7,6},{8,9},{9,8},{10,11... | collective-permute-start | bytes 2752520 | tf_op jit(solution)/shard_map/ppermute | solution.py:644
  57.6 13.1 %collective-permute-start.17 = (bf16[448,512]{1,0:T(8,128)(2,1)S(1)}, bf16[448,512]{1,0:T(8,128)(2,1)S(1)}, u32[]{:S(2)}, u32[]{:S(2)}) collective-permute-start(bf16[448,512]{1,0:T(8,128)(2,1)S(1)} %get-tuple-element.111), channel_id=1, source_target_pairs={{0,4},{4,0},{8,12},{12,8},{16,20},{20,16},{24,28},{28,24},{1,5},{5... | collective-permute-start | bytes 1376264 | tf_op jit(solution)/shard_map/ppermute | solution.py:661
  58.2 5.8 %collective-permute-start.13 = (f32[12,512]{1,0:T(8,128)S(1)}, f32[12,512]{1,0:T(8,128)S(1)}, u32[]{:S(2)}, u32[]{:S(2)}) collective-permute-start(f32[12,512]{1,0:T(8,128)S(1)} %shard_map.281.mine_ref), channel_id=1, source_target_pairs={{8,0},{12,4},{16,8},{20,12},{24,16},{28,20},{9,1},{13,5},{17,9},{2... | collective-permute-start | bytes 73736 | tf_op jit(solution)/shard_map/ppermute | solution.py:665
  59.5 6.0 %copy-start.3 = (s32[24]{0:T(128)S(1)}, s32[24]{0:T(128)}, u32[]{:S(2)}) copy-start(s32[24]{0:T(128)} %lens_ref.1) | copy-start | bytes 292
  64.0 6.7 %collective-permute-start.15 = (f32[12,512]{1,0:T(8,128)S(1)}, f32[12,512]{1,0:T(8,128)S(1)}, u32[]{:S(2)}, u32[]{:S(2)}) collective-permute-start(f32[12,512]{1,0:T(8,128)S(1)} %shard_map.283), channel_id=1, source_target_pairs={{16,0},{20,4},{24,8},{28,12},{17,1},{21,5},{25,9},{29,13},{18,2},{... | collective-permute-start | bytes 73736 | tf_op jit(solution)/shard_map/ppermute | solution.py:665
  71.4 10.1 %collective-permute-start.18 = (bf16[112,512]{1,0:T(8,128)(2,1)S(1)}, bf16[112,512]{1,0:T(8,128)(2,1)S(1)}, u32[]{:S(2)}, u32[]{:S(2)}) collective-permute-start(bf16[112,512]{1,0:T(8,128)(2,1)S(1)} %get-tuple-element.118), channel_id=1, source_target_pairs={{0,8},{4,12},{8,0},{12,4},{16,24},{20,28},{24,16},{28,20},{1,9},{5... | collective-permute-start | bytes 344072 | tf_op jit(solution)/shard_map/ppermute | solution.py:661
  73.0 10.6 %collective-permute-start.19 = (bf16[112,512]{1,0:T(8,128)(2,1)S(1)}, bf16[112,512]{1,0:T(8,128)(2,1)S(1)}, u32[]{:S(2)}, u32[]{:S(2)}) collective-permute-start(bf16[112,512]{1,0:T(8,128)(2,1)S(1)} %get-tuple-element.119), channel_id=1, source_target_pairs={{0,16},{4,20},{8,24},{12,28},{16,0},{20,4},{24,8},{28,12},{1,17},{... | collective-permute-start | bytes 344072 | tf_op jit(solution)/shard_map/ppermute | solution.py:661
  75.5 8.2 %collective-permute-start.20 = (bf16[112,512]{1,0:T(8,128)(2,1)S(1)}, bf16[112,512]{1,0:T(8,128)(2,1)S(1)}, u32[]{:S(2)}, u32[]{:S(2)}) collective-permute-start(bf16[112,512]{1,0:T(8,128)(2,1)S(1)} %get-tuple-element.120), channel_id=1, source_target_pairs={{0,24},{4,28},{8,16},{12,20},{16,8},{20,12},{24,0},{28,4},{1,25},{... | collective-permute-start | bytes 344072 | tf_op jit(solution)/shard_map/ppermute | solution.py:661
  83.7 1.4 %collective-permute-start.21 = (bf16[144,512]{1,0:T(8,128)(2,1)S(1)}, bf16[144,512]{1,0:T(8,128)(2,1)S(1)}, u32[]{:S(2)}, u32[]{:S(2)}) collective-permute-start(bf16[144,512]{1,0:T(8,128)(2,1)S(1)} %get-tuple-element.121), channel_id=1, source_target_pairs={{0,1},{1,0},{2,3},{3,2},{4,5},{5,4},{6,7},{7,6},{8,9},{9,8},{10,11... | collective-permute-start | bytes 442376 | tf_op jit(solution)/shard_map/ppermute | solution.py:644
  83.8 6.1 %collective-permute-start.14 = (bf16[1536,512]{1,0:T(8,128)(2,1)S(1)}, bf16[1536,512]{1,0:T(8,128)(2,1)S(1)}, u32[]{:S(2)}, u32[]{:S(2)}) collective-permute-start(bf16[1536,512]{1,0:T(8,128)(2,1)S(1)} %shard_map.284.own_ref), channel_id=1, source_target_pairs={{0,1},{1,0},{2,3},{3,2},{4,5},{5,4},{6,7},{7,6},{8,9},{9,8},{10,11... | collective-permute-start | bytes 4718600 | tf_op jit(solution)/shard_map/ppermute | solution.py:644
  85.2 16.2 %collective-permute-start.22 = (bf16[1536,512]{1,0:T(8,128)(2,1)S(1)}, bf16[1536,512]{1,0:T(8,128)(2,1)S(1)}, u32[]{:S(2)}, u32[]{:S(2)}) collective-permute-start(bf16[1536,512]{1,0:T(8,128)(2,1)S(1)} %get-tuple-element.122.own_ref), channel_id=1, source_target_pairs={{0,1},{1,0},{2,3},{3,2},{4,5},{5,4},{6,7},{7,6},{8,9},{9,8},{10,11... | collective-permute-start | bytes 4718600 | tf_op jit(solution)/shard_map/ppermute | solution.py:644
  85.4 7.8 %collective-permute-start.23 = (bf16[144,512]{1,0:T(8,128)(2,1)S(1)}, bf16[144,512]{1,0:T(8,128)(2,1)S(1)}, u32[]{:S(2)}, u32[]{:S(2)}) collective-permute-start(bf16[144,512]{1,0:T(8,128)(2,1)S(1)} %add_convert_fusion.2), channel_id=1, source_target_pairs={{0,4},{4,0},{8,12},{12,8},{16,20},{20,16},{24,28},{28,24},{1,5},{5... | collective-permute-start | bytes 442376 | tf_op jit(solution)/shard_map/ppermute | solution.py:661
  86.6 7.8 %collective-permute-start.28 = (bf16[112,512]{1,0:T(8,128)(2,1)S(1)}, bf16[112,512]{1,0:T(8,128)(2,1)S(1)}, u32[]{:S(2)}, u32[]{:S(2)}) collective-permute-start(bf16[112,512]{1,0:T(8,128)(2,1)S(1)} %add_convert_fusion.3.refs_0_), channel_id=1, source_target_pairs={{0,24},{4,28},{8,16},{12,20},{16,8},{20,12},{24,0},{28,4},{1,25},{... | collective-permute-start | bytes 344072 | tf_op jit(solution)/shard_map/ppermute | solution.py:661
  89.2 11.3 %collective-permute-start.27 = (bf16[112,512]{1,0:T(8,128)(2,1)S(1)}, bf16[112,512]{1,0:T(8,128)(2,1)S(1)}, u32[]{:S(2)}, u32[]{:S(2)}) collective-permute-start(bf16[112,512]{1,0:T(8,128)(2,1)S(1)} %add_convert_fusion.3.refs_0_), channel_id=1, source_target_pairs={{0,16},{4,20},{8,24},{12,28},{16,0},{20,4},{24,8},{28,12},{1,17},{... | collective-permute-start | bytes 344072 | tf_op jit(solution)/shard_map/ppermute | solution.py:661
  89.9 10.6 %collective-permute-start.26 = (bf16[112,512]{1,0:T(8,128)(2,1)S(1)}, bf16[112,512]{1,0:T(8,128)(2,1)S(1)}, u32[]{:S(2)}, u32[]{:S(2)}) collective-permute-start(bf16[112,512]{1,0:T(8,128)(2,1)S(1)} %add_convert_fusion.3.refs_0_), channel_id=1, source_target_pairs={{0,8},{4,12},{8,0},{12,4},{16,24},{20,28},{24,16},{28,20},{1,9},{5... | collective-permute-start | bytes 344072 | tf_op jit(solution)/shard_map/ppermute | solution.py:661
  93.3 11.7 %collective-permute-start.24 = (bf16[144,512]{1,0:T(8,128)(2,1)S(1)}, bf16[144,512]{1,0:T(8,128)(2,1)S(1)}, u32[]{:S(2)}, u32[]{:S(2)}) collective-permute-start(bf16[144,512]{1,0:T(8,128)(2,1)S(1)} %add_convert_fusion.1), channel_id=1, source_target_pairs={{0,8},{4,12},{8,0},{12,4},{16,24},{20,28},{24,16},{28,20},{1,9},{5... | collective-permute-start | bytes 442376 | tf_op jit(solution)/shard_map/ppermute | solution.py:661
  94.4 10.5 %collective-permute-start.25 = (bf16[112,512]{1,0:T(8,128)(2,1)S(1)}, bf16[112,512]{1,0:T(8,128)(2,1)S(1)}, u32[]{:S(2)}, u32[]{:S(2)}) collective-permute-start(bf16[112,512]{1,0:T(8,128)(2,1)S(1)} %add_convert_fusion.3.refs_0_), channel_id=1, source_target_pairs={{0,4},{4,0},{8,12},{12,8},{16,20},{20,16},{24,28},{28,24},{1,5},{5... | collective-permute-start | bytes 344072 | tf_op jit(solution)/shard_map/ppermute | solution.py:661
  100.5 9.4 %collective-permute-start.30 = (bf16[336,512]{1,0:T(8,128)(2,1)S(1)}, bf16[336,512]{1,0:T(8,128)(2,1)S(1)}, u32[]{:S(2)}, u32[]{:S(2)}) collective-permute-start(bf16[336,512]{1,0:T(8,128)(2,1)S(1)} %pad_maximum_fusion), channel_id=1, source_target_pairs={{0,4},{4,0},{8,12},{12,8},{16,20},{20,16},{24,28},{28,24},{1,5},{5... | collective-permute-start | bytes 1032200 | tf_op jit(solution)/shard_map/ppermute | solution.py:661
  105.0 8.6 %collective-permute-start.29 = (bf16[144,512]{1,0:T(8,128)(2,1)S(1)}, bf16[144,512]{1,0:T(8,128)(2,1)S(1)}, u32[]{:S(2)}, u32[]{:S(2)}) collective-permute-start(bf16[144,512]{1,0:T(8,128)(2,1)S(1)} %add_convert_fusion.mine_ref), channel_id=1, source_target_pairs={{0,16},{4,20},{8,24},{12,28},{16,0},{20,4},{24,8},{28,12},{1,17},{... | collective-permute-start | bytes 442376 | tf_op jit(solution)/shard_map/ppermute | solution.py:661

commit v6 on v5

--- a/solution.py
+++ b/solution.py
@@ -130,25 +130,12 @@
     lax.fori_loop(0, rows // size, step, 0)
 
 
-def fetch(pairs, sems):
+def fetch(pairs, sems, behind=()):
     copies = [pltpu.make_async_copy(src, dst, sems.at[n]) for n, (src, dst) in enumerate(pairs)]
-    for copy in copies:
+    for copy in copies + list(behind):
         copy.start()
     for copy in copies:
         copy.wait()
-
-
-def half_copies(where_ref, src, dst, sems):
-    rows = dst.shape[0]
-    first = where_ref[1] * rows
-    return [
-        pltpu.make_async_copy(
-            src.at[pl.ds(pl.multiple_of(first + n * BLOCK, BLOCK), BLOCK), :],
-            dst.at[pl.ds(n * BLOCK, BLOCK), :],
-            sems.at[n],
-        )
-        for n in range(rows // BLOCK)
-    ]
 
 
 def incoming(far_refs, beside_ref, odd, powers_ref, backwards, out_ref):
@@ -195,12 +182,20 @@
         out_ref[pl.ds(states + at, half), :] = pack[half:per, :]
 
 
-def input_pack_kernel(where_ref, in_real, in_imag, nu, theta, gamma, a_ref, logs, sems):
+def input_pack_kernel(
+    where_ref, in_real, in_imag, nu, theta, gamma, tok_all, cot_all, a_ref, logs, tok, cot, sems, row_sems
+):
     per_s, width = in_real.shape
+    rows = tok.shape[0]
+    mine = pl.ds(pl.multiple_of(where_ref[1] * rows, BLOCK), rows)
+    halves = [
+        pltpu.make_async_copy(src.at[mine, :], dst, row_sems.at[n]) for n, (src, dst) in enumerate(((tok_all, tok), (cot_all, cot)))
+    ]
     fetch(
         [(in_real, a_ref.at[pl.ds(0, per_s), :]), (in_imag, a_ref.at[pl.ds(per_s, per_s), :])]
         + [(ref, logs.at[n]) for n, ref in enumerate((nu, theta, gamma))],
         sems,
+        halves,
     )
     modulus = jnp.exp(-jnp.exp(logs[0]))
     angle = jnp.exp(logs[1])
@@ -215,6 +210,8 @@
     table = jnp.concatenate([table] * (width // per_s), axis=1)
     here = lax.broadcasted_iota(jnp.int32, (PARAM_ROWS, width), 1) // per_s == where_ref[2]
     a_ref[2 * per_s :, :] = jnp.where(here, table, 0.0).astype(BF16)
+    for copy in halves:
+        copy.wait()
 
 
 def weight_pack_kernel(out_real, out_imag, up, gate, down, b_ref, g_ref, sems):
@@ -237,26 +234,18 @@
 
 
 def norm_kernel(
-    where_ref, tok_all, cot_all, gain_all, bias_all, lens_all, low_ref, normed_ref, inv_ref, cotm_ref,
-    tok, cot, gain_ref, bias_ref, lens_ref, sems, small_sems, *, length
+    where_ref, tok, cot, gain_all, bias_all, lens_all, low_ref, normed_ref, inv_ref, cotm_ref,
+    gain_ref, bias_ref, lens_ref, sems, *, length
 ):
     rows, width = low_ref.shape
-    per_block = BLOCK // length
-    halves = [half_copies(where_ref, src, dst, sems.at[n]) for n, (src, dst) in enumerate(((tok_all, tok), (cot_all, cot)))]
-    for copies in zip(*halves):
-        for copy in copies:
-            copy.start()
-    fetch([(gain_all, gain_ref), (bias_all, bias_ref), (lens_all, lens_ref)], small_sems)
-    for block, copies in enumerate(zip(*halves)):
-        for copy in copies:
-            copy.wait()
+    fetch([(gain_all, gain_ref), (bias_all, bias_ref), (lens_all, lens_ref)], sems)
+    for block in range(rows // BLOCK):
         span = slice(block * BLOCK, (block + 1) * BLOCK)
         normed, inv_scale = layer_norm(tok[span, :].astype(F32))
         normed_ref[span, :] = normed
         inv_ref[span, :] = jnp.broadcast_to(inv_scale, (BLOCK, inv_ref.shape[1]))
         low_ref[span, :] = (normed * gain_ref[...] + bias_ref[...]).astype(BF16)
-        for s in range(per_block):
-            seq = block * per_block + s
+        for seq in range(block * BLOCK // length, (block + 1) * BLOCK // length):
             span = slice(seq * length, (seq + 1) * length)
             live = mask_rows(lens_ref, where_ref, seq, rows // length, length, width)
             cotm_ref[span, :] = jnp.where(live, cot[span, :].astype(F32), 0.0).astype(BF16)
@@ -420,18 +409,13 @@
             ref[k * per_s : (k + 1) * per_s, :] = part.astype(ref.dtype)
 
 
-def down_kernel(where_ref, lens_ref, tok_all, hid_all, b0, b1, b2, b3, out_all, down_all, tok, sems, *, length, per_s):
+def down_kernel(where_ref, lens_ref, tok, hid_all, b0, b1, b2, b3, out_all, down_all, *, length, per_s):
     shard = where_ref[2]
     rows, width = out_all.shape
     per_block = LARGE // length
     per_f = down_all.shape[0] // TENSOR
-    copies = half_copies(where_ref, tok_all, tok, sems)
-    for copy in copies:
-        copy.start()
     for k, pack in enumerate((b0, b1, b2, b3)):
         down_all[pl.ds(pl.multiple_of((shard ^ k) * per_f, per_f), per_f), :] = pack[2 * per_s :, :]
-    for copy in copies:
-        copy.wait()
 
     def body(block, view):
         added = dot(view(hid_all)[...], down_all[...])
@@ -452,7 +436,7 @@
     place, core, shard = where_ref[0], where_ref[1], where_ref[2]
     states = in_t.shape[0] // 2
     rows, width = low_all.shape
-    per_block = BLOCK // length
+    per_block = LARGE // length
     per_s = states // TENSOR
     packs = (a0, a1, a2, a3)
 
@@ -501,7 +485,7 @@
             cols = dlow[:, pl.ds(k * states + at, 2 * per_s)]
             in_grad[2 * per_s * k : 2 * per_s * (k + 1), :] += dot_tn(cols, low)
 
-    each_block(rows, BLOCK, body)
+    each_block(rows, LARGE, body)
     small = jnp.concatenate(
         [vec_grad[:3, :], lam_grad[...], jnp.zeros((PARAM_ROWS - 4, width), F32)], axis=0
     ).astype(BF16)
@@ -709,42 +693,40 @@
     dma = pltpu.SemaphoreType.DMA
     line = lambda v: v.reshape(1, per_s)
 
-    pack_a, logs = call(
+    pack_a, logs, own_tok, own_cot = call(
         input_pack_kernel,
         [where],
-        [in_real.T, in_imag.T, line(nu_log), line(theta_log), line(gamma_log)],
-        [(a_shape, BF16), ((3, 1, per_s), F32)],
-        [dma((5,))],
+        [in_real.T, in_imag.T, line(nu_log), line(theta_log), line(gamma_log), tok_rows, cot_rows],
+        [(a_shape, BF16), ((3, 1, per_s), F32), ((rows, width), BF16), ((rows, width), BF16)],
+        [dma((5,)), dma((2,))],
         4,
-        far_inputs=range(5),
-    )
-    low, normed, inv, cot_m = call(
-        functools.partial(norm_kernel, length=length),
-        [where],
-        [after(tok_rows, pack_a), cot_rows, gain_row, bias_row, lengths],
-        [((rows, width), BF16), ((rows, width), F32), ((rows, 128), F32), ((rows, width), BF16)],
-        [
-            pltpu.VMEM((rows, width), BF16),
-            pltpu.VMEM((rows, width), BF16),
-            pltpu.VMEM((1, width), F32),
-            pltpu.VMEM((1, width), F32),
-            pltpu.SMEM((seqs,), jnp.int32),
-            dma((2, blocks)),
-            dma((3,)),
-        ],
-        8,
-        far_inputs=range(5),
-    )
-    packs_a = gather_tensor(pack_a, low)
+        far_inputs=range(7),
+    )
     pack_b, pack_g = call(
         weight_pack_kernel,
         [],
-        [after(out_real, packs_a[2]), out_imag, up_weight, gate_weight, down_weight],
+        [after(out_real, pack_a), out_imag, up_weight, gate_weight, down_weight],
         [(b_shape, BF16), ((width, 2 * per_f), BF16)],
         [dma((5,))],
         4,
         far_inputs=range(5),
     )
+    low, normed, inv, cot_m = call(
+        functools.partial(norm_kernel, length=length),
+        [where],
+        [own_tok, after(own_cot, pack_b), gain_row, bias_row, lengths],
+        [((rows, width), BF16), ((rows, width), F32), ((rows, 128), F32), ((rows, width), BF16)],
+        [
+            pltpu.VMEM((1, width), F32),
+            pltpu.VMEM((1, width), F32),
+            pltpu.SMEM((seqs,), jnp.int32),
+            dma((3,)),
+        ],
+        8,
+        far_inputs=(2, 3, 4),
+    )
+    packs_a = gather_tensor(pack_a, low)
+    pack_b, pack_g = after((pack_b, pack_g), packs_a[2])
     drive, ends, powers = call(
         functools.partial(drive_kernel, length=length),
         [where],
@@ -872,11 +854,10 @@
     out_own = call(
         functools.partial(down_kernel, length=length, per_s=per_s),
         [where, lengths],
-        [tok_rows, after(hid, found_back[-1]), *packs_b],
+        [own_tok, after(hid, found_back[-1]), *packs_b],
         ((rows, width), BF16),
-        [pltpu.VMEM((units, width), BF16), pltpu.VMEM((rows, width), BF16), dma((blocks,))],
+        [pltpu.VMEM((units, width), BF16)],
         8,
-        far_inputs=(0,),
     )
     dealt = call(
         deal_kernel,
@@ -911,7 +892,7 @@
             pltpu.VMEM((lanes, width), BF16),
             pltpu.VMEM((2, length, states), F32),
             pltpu.VMEM((own_seqs, lanes), F32),
-            pltpu.VMEM((BLOCK, lanes), BF16),
+            pltpu.VMEM((LARGE, lanes), BF16),
             pltpu.VMEM((states, width), F32),
             pltpu.VMEM((1, lanes), F32),
             pltpu.VMEM((TILE, width), F32),
@@ -926,13 +907,13 @@
     gathered = [mine_b] + [flip_dp(mine_b, 2 * k, groups) for k in range(1, ways)]
     beside = [flip_dp(mine_b, 1, groups), flip_dp(jnp.concatenate(gathered[1:], axis=0), 1, groups)]
 
-    grads_a = own_a.astype(F32) + core_swap(after(sent_a, mine_b)).astype(F32)
+    grads_a = own_a.astype(F32) + after(core_swap(sent_a), mine_b).astype(F32)
     low_a = grads_a.astype(BF16)
 
     block_out = call(
         join_halves_kernel,
         [where],
-        [out_own, core_swap(out_own)],
+        [out_own, core_swap(after(out_own, low_a))],
         [((seqs * length, width), BF16)],
         [dma((2,))],
         2,
@@ -952,13 +933,13 @@
     unpacked = call(
         functools.partial(unpack_kernel, ways=ways),
         [where],
-        [*gathered, *beside],
+        [*gathered, beside[0], after(beside[1], input_grad)],
         [state_shape] * 2 + [((width, per_f), F32)] * 2 + [((per_f, width), F32)],
         [pltpu.VMEM((pack_rows, width), F32), dma((5,))],
         8,
         far_outs=range(5),
     )
-    works = {1: [block_out], 2: [input_grad, beside[0]], 4: unpacked}
+    works = {1: [block_out], 2: [beside[0]], 4: unpacked}
     bit = 1
     while bit < groups:
         other_a = after(flip_dp(low_a, bit, groups), *works.get(bit, []))

time: 116 us -> 111 us (0.957)
  waiting for transfers between devices: 23 us -> 17.9 us
  starting transfers between devices: 36.6 us -> 39.4 us
  Pallas kernels: 54.3 us -> 52.4 us
    ppermute x14, waiting for transfers between devices: 13.1 us -> 7.51 us  [flip_dp(): return lax.ppermute(value, 'dp', [(i, i ^ bits) for i in range(groups)])]
    ppermute x14, starting transfers between devices: 17.9 us -> 20.9 us  [flip_dp(): return lax.ppermute(value, 'dp', [(i, i ^ bits) for i in range(groups)])]
    pallas_call x21, Pallas kernels: 54.3 us -> 52.4 us  [call(): pl.pallas_call(kernel, in_specs=[pl.BlockSpec(memory_space=pltpu.SMEM)] *...]
    ppermute x4, waiting for transfers between devices: 5.05 us -> 6.39 us  [shift_dp(): lax.ppermute(value, 'dp', [(i, i + by) for i in range(groups) if 0 <= i +...]
  transfers between devices with their start and end apart: 31 -> 31, of which waited for: 14 -> 12; matrix products, arithmetic and copies ran while one was open for 0% -> 0% of each run, Pallas kernels for 31% -> 31%
where the time goes in v6:
time: 111 us
  Pallas kernels  52.4 us (47%)
  starting transfers between devices  39.4 us (35%)
  waiting for transfers between devices  17.9 us (16%)
  between operations  1.16 us (1%)
    pallas_call x21, Pallas kernels, call(): pl.pallas_call(kernel, in_specs=[pl.BlockSpec(memory_space=pltpu.SMEM)] *...  52.4 us
    ppermute x14, starting transfers between devices, flip_dp(): return lax.ppermute(value, 'dp', [(i, i ^ bits) for i in range(groups)])  20.9 us
    ppermute x4, starting transfers between devices, shift_dp(): lax.ppermute(value, 'dp', [(i, i + by) for i in range(groups) if 0 <= i +...  11.5 us
    ppermute x14, waiting for transfers between devices, flip_dp(): return lax.ppermute(value, 'dp', [(i, i ^ bits) for i in range(groups)])  7.51 us
    ppermute x4, waiting for transfers between devices, shift_dp(): lax.ppermute(value, 'dp', [(i, i + by) for i in range(groups) if 0 <= i +...  6.39 us
    ppermute x3, starting transfers between devices, side_swap(): return lax.ppermute(value, 'tensor', [(t, t ^ 2) for t in range(TENSOR)])  5.12 us
    ppermute x10, waiting for transfers between devices, core_swap(): return lax.ppermute(value, 'tensor', [(t, t ^ 1) for t in range(TENSOR)])  3.95 us
  transfers between devices with their start and end apart: 31, of which 12 were waited for; matrix products, arithmetic and copies ran while one was open for 0% of the time, Pallas kernels for 31%

profile of v6, /device:TPU:0, one launch (start us, length us, event | category | flops | bytes accessed | tf_op | source)
XLA Modules:
  0.0 111.1 jit_solution(2510189451206207824)
XLA Ops:
  0.7 2.6 %shard_map.271 = (bf16[144,512]{1,0:T(8,128)(2,1)S(1)}, f32[3,1,64]{2,1,0:T(1,128)S(1)}, bf16[1536,512]{1,0:T(8,128)(2,1)S(1)}, bf16[1536,512]{1,0:T(8,128)(2,1)S(1)}) custom-call(s32[3]{0:T(128)S(1)} %pad_add_fusion.where_ref, bf16[64,512]{1,0:T(8,128)(2,1)} %bitcast.35, bf16[64,512]{1,0:T(8,128)(2,1)} %bitcast.36, f32[1,64]{1,0:T(1,128)} %bitcast.37, ...), custom_call_target="tpu_custom_call" | custom-call | tf_op jit(solution)/shard_map/pallas_call | solution.py:610
  3.3 3.0 %collective-permute-start.1 = (bf16[144,512]{1,0:T(8,128)(2,1)S(1)}, bf16[144,512]{1,0:T(8,128)(2,1)S(1)}, u32[]{:S(2)}, u32[]{:S(2)}) collective-permute-start(bf16[144,512]{1,0:T(8,128)(2,1)S(1)} %get-tuple-element.86.a0.refs_8_.refs_11_.a_ref), channel_id=1, source_target_pairs={{0,2},{1,3},{2,0},{3,1},{4,6},{5,7},{6,4},{7,5},{8,10},{9,11},{10,... | collective-permute-start | bytes 442376 | tf_op jit(solution)/shard_map/ppermute | solution.py:632
  6.4 1.2 %shard_map.272 = (bf16[384,512]{1,0:T(8,128)(2,1)S(1)}, bf16[512,512]{1,0:T(8,128)(2,1)S(1)}) custom-call(bf16[64,512]{1,0:T(8,128)(2,1)} %out_real, bf16[64,512]{1,0:T(8,128)(2,1)} %out_imag.1, bf16[512,256]{1,0:T(8,128)(2,1)} %up.1, bf16[512,256]{1,0:T(8,128)(2,1)} %gate.1, bf16[256,512]{1,0:T(8,128)(2,1)} %down.1), custom_call_target="tpu_custom_call" | custom-call | tf_op jit(solution)/shard_map/pallas_call | solution.py:610
  7.6 2.9 %shard_map.273 = (bf16[1536,512]{1,0:T(8,128)(2,1)S(1)}, f32[1536,512]{1,0:T(8,128)S(1)}, f32[1536,128]{1,0:T(8,128)S(1)}, bf16[1536,512]{1,0:T(8,128)(2,1)S(1)}) custom-call(s32[3]{0:T(128)S(1)} %pad_add_fusion.where_ref, bf16[1536,512]{1,0:T(8,128)(2,1)S(1)} %get-tuple-element.84.tok, bf16[1536,512]{1,0:T(8,128)(2,1)S(1)} %get-tuple-element.89.cot, ...), custom_call_target="tpu_custom_call" | custom-call | tf_op jit(solution)/shard_map/pallas_call | solution.py:610
  10.5 1.4 %collective-permute-start.7 = (bf16[384,512]{1,0:T(8,128)(2,1)S(1)}, bf16[384,512]{1,0:T(8,128)(2,1)S(1)}, u32[]{:S(2)}, u32[]{:S(2)}) collective-permute-start(bf16[384,512]{1,0:T(8,128)(2,1)S(1)} %get-tuple-element.100.b0.refs_15_), channel_id=1, source_target_pairs={{0,2},{1,3},{2,0},{3,1},{4,6},{5,7},{6,4},{7,5},{8,10},{9,11},{10,... | collective-permute-start | bytes 1179656 | tf_op jit(solution)/shard_map/ppermute | solution.py:632
  12.0 0.5 collective-permute-start.2
  12.5 0.6 collective-permute-start.10
  13.6 2.3 %shard_map.274 = (f32[1536,512]{1,0:T(8,128)S(1)}, f32[12,512]{1,0:T(8,128)S(1)}, f32[8,512]{1,0:T(8,128)S(1)}) custom-call(s32[3]{0:T(128)S(1)} %pad_add_fusion.where_ref, bf16[1536,512]{1,0:T(8,128)(2,1)S(1)} %get-tuple-element.90.low_all.refs_4_, bf16[144,512]{1,0:T(8,128)(2,1)S(1)} %get-tuple-element.86.a0.refs_8_.refs_11_.a_ref, ...), custom_call_target="tpu_custom_call" | custom-call | tf_op jit(solution)/shard_map/pallas_call | solution.py:610
  15.8 1.6 %collective-permute-start.3 = (f32[12,512]{1,0:T(8,128)S(1)}, f32[12,512]{1,0:T(8,128)S(1)}, u32[]{:S(2)}, u32[]{:S(2)}) collective-permute-start(f32[12,512]{1,0:T(8,128)S(1)} %get-tuple-element.92.mine_ref), channel_id=1, source_target_pairs={{0,4},{4,0},{8,12},{12,8},{16,20},{20,16},{24,28},{28,24},{1,5},{5... | collective-permute-start | bytes 73736 | tf_op jit(solution)/shard_map/ppermute | solution.py:645
  17.4 2.1 %shard_map.275.refs_4_ = f32[1536,512]{1,0:T(8,128)S(1)} custom-call(f32[1536,512]{1,0:T(8,128)S(1)} %get-tuple-element.93.drive_all, bf16[144,512]{1,0:T(8,128)(2,1)S(1)} %get-tuple-element.86.a0.refs_8_.refs_11_.a_ref, bf16[144,512]{1,0:T(8,128)(2,1)S(1)} %collective-permute-done.a1.refs_9_.refs_12_, ...), custom_call_target="tpu_custom_call" | custom-call | tf_op jit(solution)/shard_map/pallas_call | solution.py:610
  19.8 0.6 shard_map.276.mine_ref
  20.4 3.5 %collective-permute-start.4 = (f32[12,512]{1,0:T(8,128)S(1)}, f32[12,512]{1,0:T(8,128)S(1)}, u32[]{:S(2)}, u32[]{:S(2)}) collective-permute-start(f32[12,512]{1,0:T(8,128)S(1)} %shard_map.276.mine_ref), channel_id=1, source_target_pairs={{0,8},{4,12},{8,16},{12,20},{16,24},{20,28},{1,9},{5,13},{9,17},{1... | collective-permute-start | bytes 73736 | tf_op jit(solution)/shard_map/ppermute | solution.py:649
  23.9 1.5 %collective-permute-done.4.other_ref.refs_0_ = f32[12,512]{1,0:T(8,128)S(1)} collective-permute-done((f32[12,512]{1,0:T(8,128)S(1)}, f32[12,512]{1,0:T(8,128)S(1)}, u32[]{:S(2)}, u32[]{:S(2)}) %collective-permute-start.4) | collective-permute-done | bytes 24608 | tf_op jit(solution)/shard_map/ppermute | solution.py:649
  25.5 5.2 %collective-permute-start.5 = (f32[12,512]{1,0:T(8,128)S(1)}, f32[12,512]{1,0:T(8,128)S(1)}, u32[]{:S(2)}, u32[]{:S(2)}) collective-permute-start(f32[12,512]{1,0:T(8,128)S(1)} %shard_map.277), channel_id=1, source_target_pairs={{0,16},{4,20},{8,24},{12,28},{1,17},{5,21},{9,25},{13,29},{2,18},{... | collective-permute-start | bytes 73736 | tf_op jit(solution)/shard_map/ppermute | solution.py:649
  31.0 3.0 %shard_map.278.refs_6_ = bf16[1536,1024]{1,0:T(8,128)(2,1)S(1)} custom-call(s32[3]{0:T(128)S(1)} %pad_add_fusion.where_ref, bf16[1536,512]{1,0:T(8,128)(2,1)S(1)} %get-tuple-element.98.cotm_all.refs_7_.cotm_ref, bf16[384,512]{1,0:T(8,128)(2,1)S(1)} %get-tuple-element.100.b0.refs_15_, bf16[384,512]{1,0:T(8,128)(2,1)S(1)} %collective-permute-done.6.b1.refs_16_, ...), custom_call_target="tpu_custom_call" | custom-call | tf_op jit(solution)/shard_map/pallas_call | solution.py:610
  34.4 1.6 %collective-permute-done.11.refs_22_ = bf16[512,512]{1,0:T(8,128)(2,1)S(1)} collective-permute-done((bf16[512,512]{1,0:T(8,128)(2,1)S(1)}, bf16[512,512]{1,0:T(8,128)(2,1)S(1)}, u32[]{:S(2)}, u32[]{:S(2)}) %collective-permute-start.11) | collective-permute-done | bytes 524320 | tf_op jit(solution)/shard_map/ppermute | solution.py:628
  36.0 12.8 %shard_map.279 = (bf16[1536,512]{1,0:T(8,128)(2,1)S(1)}, f32[1536,512]{1,0:T(8,128)S(1)}, f32[12,512]{1,0:T(8,128)S(1)}, bf16[1536,512]{1,0:T(8,128)(2,1)S(1)}, ...) custom-call(s32[3]{0:T(128)S(1)} %pad_add_fusion.where_ref, ...), custom_call_target="tpu_custom_call" | custom-call | tf_op jit(solution)/shard_map/pallas_call | solution.py:610
  48.9 1.6 %collective-permute-start.12 = (f32[12,512]{1,0:T(8,128)S(1)}, f32[12,512]{1,0:T(8,128)S(1)}, u32[]{:S(2)}, u32[]{:S(2)}) collective-permute-start(f32[12,512]{1,0:T(8,128)S(1)} %get-tuple-element.105.mine_ref), channel_id=1, source_target_pairs={{0,4},{4,0},{8,12},{12,8},{16,20},{20,16},{24,28},{28,24},{1,5},{5... | collective-permute-start | bytes 73736 | tf_op jit(solution)/shard_map/ppermute | solution.py:645
  50.4 3.6 %shard_map.280 = (f32[896,512]{1,0:T(8,128)S(1)}, bf16[896,512]{1,0:T(8,128)(2,1)S(1)}) custom-call(s32[3]{0:T(128)S(1)} %pad_add_fusion.where_ref, bf16[1536,1024]{1,0:T(8,128)(2,1)S(1)} %get-tuple-element.115.hid_ref.hid_all, bf16[1536,512]{1,0:T(8,128)(2,1)S(1)} %get-tuple-element.98.cotm_all.refs_7_.cotm_ref, ...), custom_call_target="tpu_custom_call" | custom-call | tf_op jit(solution)/shard_map/pallas_call | solution.py:610
  54.1 0.6 shard_map.281.mine_ref
  54.7 1.9 %collective-permute-done.15.other_ref = bf16[896,512]{1,0:T(8,128)(2,1)S(1)} collective-permute-done((bf16[896,512]{1,0:T(8,128)(2,1)S(1)}, bf16[896,512]{1,0:T(8,128)(2,1)S(1)}, u32[]{:S(2)}, u32[]{:S(2)}) %collective-permute-start.15) | collective-permute-done | bytes 917536 | tf_op jit(solution)/shard_map/ppermute | solution.py:628
  56.6 0.7 shard_map.285
  57.3 0.6 collective-permute-start.16
  57.9 1.3 %collective-permute-start.13 = (f32[12,512]{1,0:T(8,128)S(1)}, f32[12,512]{1,0:T(8,128)S(1)}, u32[]{:S(2)}, u32[]{:S(2)}) collective-permute-start(f32[12,512]{1,0:T(8,128)S(1)} %shard_map.281.mine_ref), channel_id=1, source_target_pairs={{8,0},{12,4},{16,8},{20,12},{24,16},{28,20},{9,1},{13,5},{17,9},{2... | collective-permute-start | bytes 73736 | tf_op jit(solution)/shard_map/ppermute | solution.py:649
  59.2 2.1 %shard_map.282.refs_8_ = f32[1536,512]{1,0:T(8,128)S(1)} custom-call(f32[1536,512]{1,0:T(8,128)S(1)} %get-tuple-element.113.drive_all, bf16[144,512]{1,0:T(8,128)(2,1)S(1)} %get-tuple-element.86.a0.refs_8_.refs_11_.a_ref, bf16[144,512]{1,0:T(8,128)(2,1)S(1)} %collective-permute-done.a1.refs_9_.refs_12_, ...), custom_call_target="tpu_custom_call" | custom-call | tf_op jit(solution)/shard_map/pallas_call | solution.py:610
  61.3 2.4 %collective-permute-done.13.other_ref.refs_0_ = f32[12,512]{1,0:T(8,128)S(1)} collective-permute-done((f32[12,512]{1,0:T(8,128)S(1)}, f32[12,512]{1,0:T(8,128)S(1)}, u32[]{:S(2)}, u32[]{:S(2)}) %collective-permute-start.13) | collective-permute-done | bytes 24608 | tf_op jit(solution)/shard_map/ppermute | solution.py:649
  63.7 1.5 %collective-permute-start.14 = (f32[12,512]{1,0:T(8,128)S(1)}, f32[12,512]{1,0:T(8,128)S(1)}, u32[]{:S(2)}, u32[]{:S(2)}) collective-permute-start(f32[12,512]{1,0:T(8,128)S(1)} %shard_map.283), channel_id=1, source_target_pairs={{16,0},{20,4},{24,8},{28,12},{17,1},{21,5},{25,9},{29,13},{18,2},{... | collective-permute-start | bytes 73736 | tf_op jit(solution)/shard_map/ppermute | solution.py:649
  65.2 2.7 %shard_map.284.own_ref = bf16[1536,512]{1,0:T(8,128)(2,1)S(1)} custom-call(s32[3]{0:T(128)S(1)} %pad_add_fusion.where_ref, s32[24]{0:T(128)S(1)} %copy-done.3, bf16[1536,512]{1,0:T(8,128)(2,1)S(1)} %get-tuple-element.84.tok, bf16[1536,1024]{1,0:T(8,128)(2,1)S(1)} %get-tuple-element.115.hid_ref.hid_all, bf16[384,512]{1,0:T(8,128)(2,1)S(1)} %get-tuple-element.100.b0.refs_15_, ...), custom_call_target="tpu_custom_call" | custom-call | tf_op jit(solution)/shard_map/pallas_call | solution.py:610
  67.9 2.5 %collective-permute-done.14.refs_1_ = f32[12,512]{1,0:T(8,128)S(1)} collective-permute-done((f32[12,512]{1,0:T(8,128)S(1)}, f32[12,512]{1,0:T(8,128)S(1)}, u32[]{:S(2)}, u32[]{:S(2)}) %collective-permute-start.14) | collective-permute-done | bytes 24608 | tf_op jit(solution)/shard_map/ppermute | solution.py:649
  70.4 0.6 shard_map.286
  71.0 1.6 %collective-permute-start.18 = (bf16[112,512]{1,0:T(8,128)(2,1)S(1)}, bf16[112,512]{1,0:T(8,128)(2,1)S(1)}, u32[]{:S(2)}, u32[]{:S(2)}) collective-permute-start(bf16[112,512]{1,0:T(8,128)(2,1)S(1)} %get-tuple-element.127), channel_id=1, source_target_pairs={{0,8},{4,12},{8,0},{12,4},{16,24},{20,28},{24,16},{28,20},{1,9},{5... | collective-permute-start | bytes 344072 | tf_op jit(solution)/shard_map/ppermute | solution.py:645
  72.7 1.4 %collective-permute-start.19 = (bf16[112,512]{1,0:T(8,128)(2,1)S(1)}, bf16[112,512]{1,0:T(8,128)(2,1)S(1)}, u32[]{:S(2)}, u32[]{:S(2)}) collective-permute-start(bf16[112,512]{1,0:T(8,128)(2,1)S(1)} %get-tuple-element.128), channel_id=1, source_target_pairs={{0,16},{4,20},{8,24},{12,28},{16,0},{20,4},{24,8},{28,12},{1,17},{... | collective-permute-start | bytes 344072 | tf_op jit(solution)/shard_map/ppermute | solution.py:645
  74.1 1.4 %collective-permute-start.20 = (bf16[112,512]{1,0:T(8,128)(2,1)S(1)}, bf16[112,512]{1,0:T(8,128)(2,1)S(1)}, u32[]{:S(2)}, u32[]{:S(2)}) collective-permute-start(bf16[112,512]{1,0:T(8,128)(2,1)S(1)} %get-tuple-element.129), channel_id=1, source_target_pairs={{0,24},{4,28},{8,16},{12,20},{16,8},{20,12},{24,0},{28,4},{1,25},{... | collective-permute-start | bytes 344072 | tf_op jit(solution)/shard_map/ppermute | solution.py:645
  75.5 5.4 %shard_map.287 = (bf16[1536,512]{1,0:T(8,128)(2,1)S(1)}, bf16[144,512]{1,0:T(8,128)(2,1)S(1)}, bf16[144,512]{1,0:T(8,128)(2,1)S(1)}) custom-call(s32[3]{0:T(128)S(1)} %pad_add_fusion.where_ref, f32[12,512]{1,0:T(8,128)S(1)} %collective-permute-done.13.other_ref.refs_0_, f32[12,512]{1,0:T(8,128)S(1)} %collective-permute-done.14.refs_1_, ...), custom_call_target="tpu_custom_call" | custom-call | tf_op jit(solution)/shard_map/pallas_call | solution.py:610
  81.0 2.3 %collective-permute-done.19 = bf16[112,512]{1,0:T(8,128)(2,1)S(1)} collective-permute-done((bf16[112,512]{1,0:T(8,128)(2,1)S(1)}, bf16[112,512]{1,0:T(8,128)(2,1)S(1)}, u32[]{:S(2)}, u32[]{:S(2)}) %collective-permute-start.19) | collective-permute-done | bytes 114720 | tf_op jit(solution)/shard_map/ppermute | solution.py:645
  84.0 0.5 collective-permute-start.23
  84.6 2.0 %collective-permute-start.28 = (bf16[112,512]{1,0:T(8,128)(2,1)S(1)}, bf16[112,512]{1,0:T(8,128)(2,1)S(1)}, u32[]{:S(2)}, u32[]{:S(2)}) collective-permute-start(bf16[112,512]{1,0:T(8,128)(2,1)S(1)} %add_convert_fusion.3.refs_0_), channel_id=1, source_target_pairs={{0,24},{4,28},{8,16},{12,20},{16,8},{20,12},{24,0},{28,4},{1,25},{... | collective-permute-start | bytes 344072 | tf_op jit(solution)/shard_map/ppermute | solution.py:645
  86.6 1.3 %collective-permute-start.27 = (bf16[112,512]{1,0:T(8,128)(2,1)S(1)}, bf16[112,512]{1,0:T(8,128)(2,1)S(1)}, u32[]{:S(2)}, u32[]{:S(2)}) collective-permute-start(bf16[112,512]{1,0:T(8,128)(2,1)S(1)} %add_convert_fusion.3.refs_0_), channel_id=1, source_target_pairs={{0,16},{4,20},{8,24},{12,28},{16,0},{20,4},{24,8},{28,12},{1,17},{... | collective-permute-start | bytes 344072 | tf_op jit(solution)/shard_map/ppermute | solution.py:645
  87.8 1.1 %collective-permute-start.26 = (bf16[112,512]{1,0:T(8,128)(2,1)S(1)}, bf16[112,512]{1,0:T(8,128)(2,1)S(1)}, u32[]{:S(2)}, u32[]{:S(2)}) collective-permute-start(bf16[112,512]{1,0:T(8,128)(2,1)S(1)} %add_convert_fusion.3.refs_0_), channel_id=1, source_target_pairs={{0,8},{4,12},{8,0},{12,4},{16,24},{20,28},{24,16},{28,20},{1,9},{5... | collective-permute-start | bytes 344072 | tf_op jit(solution)/shard_map/ppermute | solution.py:645
  88.9 2.2 %shard_map.288 = bf16[3072,512]{1,0:T(8,128)(2,1)} custom-call(s32[3]{0:T(128)S(1)} %pad_add_fusion.where_ref, bf16[1536,512]{1,0:T(8,128)(2,1)S(1)} %shard_map.284.own_ref, bf16[1536,512]{1,0:T(8,128)(2,1)S(1)} %collective-permute-done.21.other_ref), custom_call_target="tpu_custom_call" | custom-call | tf_op jit(solution)/shard_map/pallas_call | solution.py:610
  91.2 1.0 collective-permute-start.24
  92.4 1.5 %collective-permute-start.25 = (bf16[112,512]{1,0:T(8,128)(2,1)S(1)}, bf16[112,512]{1,0:T(8,128)(2,1)S(1)}, u32[]{:S(2)}, u32[]{:S(2)}) collective-permute-start(bf16[112,512]{1,0:T(8,128)(2,1)S(1)} %add_convert_fusion.3.refs_0_), channel_id=1, source_target_pairs={{0,4},{4,0},{8,12},{12,8},{16,20},{20,16},{24,28},{28,24},{1,5},{5... | collective-permute-start | bytes 344072 | tf_op jit(solution)/shard_map/ppermute | solution.py:645
  93.9 4.2 %collective-permute-done.27.refs_2_ = bf16[112,512]{1,0:T(8,128)(2,1)S(1)} collective-permute-done((bf16[112,512]{1,0:T(8,128)(2,1)S(1)}, bf16[112,512]{1,0:T(8,128)(2,1)S(1)}, u32[]{:S(2)}, u32[]{:S(2)}) %collective-permute-start.27) | collective-permute-done | bytes 114720 | tf_op jit(solution)/shard_map/ppermute | solution.py:645
  98.1 1.6 %collective-permute-start.30 = (bf16[336,512]{1,0:T(8,128)(2,1)S(1)}, bf16[336,512]{1,0:T(8,128)(2,1)S(1)}, u32[]{:S(2)}, u32[]{:S(2)}) collective-permute-start(bf16[336,512]{1,0:T(8,128)(2,1)S(1)} %pad_maximum_fusion), channel_id=1, source_target_pairs={{0,4},{4,0},{8,12},{12,8},{16,20},{20,16},{24,28},{28,24},{1,5},{5... | collective-permute-start | bytes 1032200 | tf_op jit(solution)/shard_map/ppermute | solution.py:645
  99.7 3.8 %collective-permute-start.29 = (bf16[144,512]{1,0:T(8,128)(2,1)S(1)}, bf16[144,512]{1,0:T(8,128)(2,1)S(1)}, u32[]{:S(2)}, u32[]{:S(2)}) collective-permute-start(bf16[144,512]{1,0:T(8,128)(2,1)S(1)} %add_convert_fusion.mine_ref), channel_id=1, source_target_pairs={{0,16},{4,20},{8,24},{12,28},{16,0},{20,4},{24,8},{28,12},{1,17},{... | collective-permute-start | bytes 442376 | tf_op jit(solution)/shard_map/ppermute | solution.py:645
  103.6 3.6 %shard_map.289 = f32[3072,512]{1,0:T(8,128)} custom-call(s32[3]{0:T(128)S(1)} %pad_add_fusion.where_ref, bf16[1536,512]{1,0:T(8,128)(2,1)S(1)} %get-tuple-element.133.own_ref, bf16[1536,512]{1,0:T(8,128)(2,1)S(1)} %collective-permute-done.22.other_ref), custom_call_target="tpu_custom_call" | custom-call | tf_op jit(solution)/shard_map/pallas_call | solution.py:610
  107.5 1.9 %shard_map.290 = (f32[64,512]{1,0:T(8,128)}, f32[64,512]{1,0:T(8,128)}, f32[512,256]{1,0:T(8,128)}, f32[512,256]{1,0:T(8,128)}, f32[256,512]{1,0:T(8,128)}) custom-call(s32[3]{0:T(128)S(1)} %pad_add_fusion.where_ref, bf16[112,512]{1,0:T(8,128)(2,1)S(1)} %add_convert_fusion.3.refs_0_, bf16[112,512]{1,0:T(8,128)(2,1)S(1)} %collective-permute-done.26.refs_1_, ...), custom_call_target="tpu_custom_call" | custom-call | tf_op jit(solution)/shard_map/pallas_call | solution.py:610
  109.5 1.5 %shard_map.291 = (f32[1,512]{1,0:T(1,128)}, f32[1,512]{1,0:T(1,128)}, f32[1,512]{1,0:T(1,128)}, f32[64,512]{1,0:T(8,128)}, f32[64,512]{1,0:T(8,128)}, /*index=5*...) custom-call(s32[3]{0:T(128)S(1)} %pad_add_fusion.where_ref, bf16[144,512]{1,0:T(8,128)(2,1)S(1)} %add_convert_fusion.mine_ref, ...), custom_call_target="tpu_custom_call" | custom-call | tf_op jit(solution)/shard_map/pallas_call | solution.py:610
  (49 shorter events, 3.2 us)
Async XLA Ops:
  3.3 7.2 %collective-permute-start.1 = (bf16[144,512]{1,0:T(8,128)(2,1)S(1)}, bf16[144,512]{1,0:T(8,128)(2,1)S(1)}, u32[]{:S(2)}, u32[]{:S(2)}) collective-permute-start(bf16[144,512]{1,0:T(8,128)(2,1)S(1)} %get-tuple-element.86.a0.refs_8_.refs_11_.a_ref), channel_id=1, source_target_pairs={{0,2},{1,3},{2,0},{3,1},{4,6},{5,7},{6,4},{7,5},{8,10},{9,11},{10,... | collective-permute-start | bytes 442376 | tf_op jit(solution)/shard_map/ppermute | solution.py:632
  10.5 14.9 %collective-permute-start.7 = (bf16[384,512]{1,0:T(8,128)(2,1)S(1)}, bf16[384,512]{1,0:T(8,128)(2,1)S(1)}, u32[]{:S(2)}, u32[]{:S(2)}) collective-permute-start(bf16[384,512]{1,0:T(8,128)(2,1)S(1)} %get-tuple-element.100.b0.refs_15_), channel_id=1, source_target_pairs={{0,2},{1,3},{2,0},{3,1},{4,6},{5,7},{6,4},{7,5},{8,10},{9,11},{10,... | collective-permute-start | bytes 1179656 | tf_op jit(solution)/shard_map/ppermute | solution.py:632
  12.0 1.4 %collective-permute-start = (bf16[144,512]{1,0:T(8,128)(2,1)S(1)}, bf16[144,512]{1,0:T(8,128)(2,1)S(1)}, u32[]{:S(2)}, u32[]{:S(2)}) collective-permute-start(bf16[144,512]{1,0:T(8,128)(2,1)S(1)} %get-tuple-element.86.a0.refs_8_.refs_11_.a_ref), channel_id=1, source_target_pairs={{0,1},{1,0},{2,3},{3,2},{4,5},{5,4},{6,7},{7,6},{8,9},{9,8},{10,11... | collective-permute-start | bytes 442376 | tf_op jit(solution)/shard_map/ppermute | solution.py:628
  12.0 1.6 %collective-permute-start.2 = (bf16[144,512]{1,0:T(8,128)(2,1)S(1)}, bf16[144,512]{1,0:T(8,128)(2,1)S(1)}, u32[]{:S(2)}, u32[]{:S(2)}) collective-permute-start(bf16[144,512]{1,0:T(8,128)(2,1)S(1)} %collective-permute-done.1.a2.refs_10_.refs_13_), channel_id=1, source_target_pairs={{0,1},{1,0},{2,3},{3,2},{4,5},{5,4},{6,7},{7,6},{8,9},{9,8},{10,11... | collective-permute-start | bytes 442376 | tf_op jit(solution)/shard_map/ppermute | solution.py:628
  12.5 21.6 %collective-permute-start.10 = (bf16[512,512]{1,0:T(8,128)(2,1)S(1)}, bf16[512,512]{1,0:T(8,128)(2,1)S(1)}, u32[]{:S(2)}, u32[]{:S(2)}) collective-permute-start(bf16[512,512]{1,0:T(8,128)(2,1)S(1)} %get-tuple-element.102.refs_19_), channel_id=1, source_target_pairs={{0,2},{1,3},{2,0},{3,1},{4,6},{5,7},{6,4},{7,5},{8,10},{9,11},{10,... | collective-permute-start | bytes 1572872 | tf_op jit(solution)/shard_map/ppermute | solution.py:632
  15.8 4.0 %collective-permute-start.3 = (f32[12,512]{1,0:T(8,128)S(1)}, f32[12,512]{1,0:T(8,128)S(1)}, u32[]{:S(2)}, u32[]{:S(2)}) collective-permute-start(f32[12,512]{1,0:T(8,128)S(1)} %get-tuple-element.92.mine_ref), channel_id=1, source_target_pairs={{0,4},{4,0},{8,12},{12,8},{16,20},{20,16},{24,28},{28,24},{1,5},{5... | collective-permute-start | bytes 73736 | tf_op jit(solution)/shard_map/ppermute | solution.py:645
  20.4 5.1 %collective-permute-start.4 = (f32[12,512]{1,0:T(8,128)S(1)}, f32[12,512]{1,0:T(8,128)S(1)}, u32[]{:S(2)}, u32[]{:S(2)}) collective-permute-start(f32[12,512]{1,0:T(8,128)S(1)} %shard_map.276.mine_ref), channel_id=1, source_target_pairs={{0,8},{4,12},{8,16},{12,20},{16,24},{20,28},{1,9},{5,13},{9,17},{1... | collective-permute-start | bytes 73736 | tf_op jit(solution)/shard_map/ppermute | solution.py:649
  23.9 7.1 %collective-permute-start.6 = (bf16[384,512]{1,0:T(8,128)(2,1)S(1)}, bf16[384,512]{1,0:T(8,128)(2,1)S(1)}, u32[]{:S(2)}, u32[]{:S(2)}) collective-permute-start(bf16[384,512]{1,0:T(8,128)(2,1)S(1)} %get-tuple-element.100.b0.refs_15_), channel_id=1, source_target_pairs={{0,1},{1,0},{2,3},{3,2},{4,5},{5,4},{6,7},{7,6},{8,9},{9,8},{10,11... | collective-permute-start | bytes 1179656 | tf_op jit(solution)/shard_map/ppermute | solution.py:628
  25.4 5.6 %collective-permute-start.8 = (bf16[384,512]{1,0:T(8,128)(2,1)S(1)}, bf16[384,512]{1,0:T(8,128)(2,1)S(1)}, u32[]{:S(2)}, u32[]{:S(2)}) collective-permute-start(bf16[384,512]{1,0:T(8,128)(2,1)S(1)} %collective-permute-done.7.b2.refs_17_), channel_id=1, source_target_pairs={{0,1},{1,0},{2,3},{3,2},{4,5},{5,4},{6,7},{7,6},{8,9},{9,8},{10,11... | collective-permute-start | bytes 1179656 | tf_op jit(solution)/shard_map/ppermute | solution.py:628
  25.5 8.6 %collective-permute-start.5 = (f32[12,512]{1,0:T(8,128)S(1)}, f32[12,512]{1,0:T(8,128)S(1)}, u32[]{:S(2)}, u32[]{:S(2)}) collective-permute-start(f32[12,512]{1,0:T(8,128)S(1)} %shard_map.277), channel_id=1, source_target_pairs={{0,16},{4,20},{8,24},{12,28},{1,17},{5,21},{9,25},{13,29},{2,18},{... | collective-permute-start | bytes 73736 | tf_op jit(solution)/shard_map/ppermute | solution.py:649
  30.7 3.7 %collective-permute-start.9 = (bf16[512,512]{1,0:T(8,128)(2,1)S(1)}, bf16[512,512]{1,0:T(8,128)(2,1)S(1)}, u32[]{:S(2)}, u32[]{:S(2)}) collective-permute-start(bf16[512,512]{1,0:T(8,128)(2,1)S(1)} %get-tuple-element.102.refs_19_), channel_id=1, source_target_pairs={{0,1},{1,0},{2,3},{3,2},{4,5},{5,4},{6,7},{7,6},{8,9},{9,8},{10,11... | collective-permute-start | bytes 1572872 | tf_op jit(solution)/shard_map/ppermute | solution.py:628
  31.0 5.0 %copy-start = (f32[512]{0:T(512)S(1)}, f32[512]{0:T(512)}, u32[]{:S(2)}) copy-start(f32[512]{0:T(512)} %param.18) | copy-start | bytes 6148
  31.0 5.0 %copy-start.1 = (f32[512]{0:T(512)S(1)}, f32[512]{0:T(512)}, u32[]{:S(2)}) copy-start(f32[512]{0:T(512)} %param.19) | copy-start | bytes 6148
  31.0 5.0 %copy-start.2 = (f32[512]{0:T(512)S(1)}, f32[512]{0:T(512)}, u32[]{:S(2)}) copy-start(f32[512]{0:T(512)} %param.20) | copy-start | bytes 6148
  34.1 2.0 %collective-permute-start.11 = (bf16[512,512]{1,0:T(8,128)(2,1)S(1)}, bf16[512,512]{1,0:T(8,128)(2,1)S(1)}, u32[]{:S(2)}, u32[]{:S(2)}) collective-permute-start(bf16[512,512]{1,0:T(8,128)(2,1)S(1)} %collective-permute-done.10.refs_21_), channel_id=1, source_target_pairs={{0,1},{1,0},{2,3},{3,2},{4,5},{5,4},{6,7},{7,6},{8,9},{9,8},{10,11... | collective-permute-start | bytes 1572872 | tf_op jit(solution)/shard_map/ppermute | solution.py:628
  48.9 5.2 %collective-permute-start.12 = (f32[12,512]{1,0:T(8,128)S(1)}, f32[12,512]{1,0:T(8,128)S(1)}, u32[]{:S(2)}, u32[]{:S(2)}) collective-permute-start(f32[12,512]{1,0:T(8,128)S(1)} %get-tuple-element.105.mine_ref), channel_id=1, source_target_pairs={{0,4},{4,0},{8,12},{12,8},{16,20},{20,16},{24,28},{28,24},{1,5},{5... | collective-permute-start | bytes 73736 | tf_op jit(solution)/shard_map/ppermute | solution.py:645
  54.0 2.5 %collective-permute-start.15 = (bf16[896,512]{1,0:T(8,128)(2,1)S(1)}, bf16[896,512]{1,0:T(8,128)(2,1)S(1)}, u32[]{:S(2)}, u32[]{:S(2)}) collective-permute-start(bf16[896,512]{1,0:T(8,128)(2,1)S(1)} %get-tuple-element.117), channel_id=1, source_target_pairs={{0,1},{1,0},{2,3},{3,2},{4,5},{5,4},{6,7},{7,6},{8,9},{9,8},{10,11... | collective-permute-start | bytes 2752520 | tf_op jit(solution)/shard_map/ppermute | solution.py:628
  57.3 13.1 %collective-permute-start.16 = (bf16[448,512]{1,0:T(8,128)(2,1)S(1)}, bf16[448,512]{1,0:T(8,128)(2,1)S(1)}, u32[]{:S(2)}, u32[]{:S(2)}) collective-permute-start(bf16[448,512]{1,0:T(8,128)(2,1)S(1)} %get-tuple-element.121), channel_id=1, source_target_pairs={{0,4},{4,0},{8,12},{12,8},{16,20},{20,16},{24,28},{28,24},{1,5},{5... | collective-permute-start | bytes 1376264 | tf_op jit(solution)/shard_map/ppermute | solution.py:645
  57.9 5.8 %collective-permute-start.13 = (f32[12,512]{1,0:T(8,128)S(1)}, f32[12,512]{1,0:T(8,128)S(1)}, u32[]{:S(2)}, u32[]{:S(2)}) collective-permute-start(f32[12,512]{1,0:T(8,128)S(1)} %shard_map.281.mine_ref), channel_id=1, source_target_pairs={{8,0},{12,4},{16,8},{20,12},{24,16},{28,20},{9,1},{13,5},{17,9},{2... | collective-permute-start | bytes 73736 | tf_op jit(solution)/shard_map/ppermute | solution.py:649
  59.2 6.0 %copy-start.3 = (s32[24]{0:T(128)S(1)}, s32[24]{0:T(128)}, u32[]{:S(2)}) copy-start(s32[24]{0:T(128)} %lens_ref.1) | copy-start | bytes 292
  63.7 6.7 %collective-permute-start.14 = (f32[12,512]{1,0:T(8,128)S(1)}, f32[12,512]{1,0:T(8,128)S(1)}, u32[]{:S(2)}, u32[]{:S(2)}) collective-permute-start(f32[12,512]{1,0:T(8,128)S(1)} %shard_map.283), channel_id=1, source_target_pairs={{16,0},{20,4},{24,8},{28,12},{17,1},{21,5},{25,9},{29,13},{18,2},{... | collective-permute-start | bytes 73736 | tf_op jit(solution)/shard_map/ppermute | solution.py:649
  71.0 9.9 %collective-permute-start.18 = (bf16[112,512]{1,0:T(8,128)(2,1)S(1)}, bf16[112,512]{1,0:T(8,128)(2,1)S(1)}, u32[]{:S(2)}, u32[]{:S(2)}) collective-permute-start(bf16[112,512]{1,0:T(8,128)(2,1)S(1)} %get-tuple-element.127), channel_id=1, source_target_pairs={{0,8},{4,12},{8,0},{12,4},{16,24},{20,28},{24,16},{28,20},{1,9},{5... | collective-permute-start | bytes 344072 | tf_op jit(solution)/shard_map/ppermute | solution.py:645
  72.7 10.6 %collective-permute-start.19 = (bf16[112,512]{1,0:T(8,128)(2,1)S(1)}, bf16[112,512]{1,0:T(8,128)(2,1)S(1)}, u32[]{:S(2)}, u32[]{:S(2)}) collective-permute-start(bf16[112,512]{1,0:T(8,128)(2,1)S(1)} %get-tuple-element.128), channel_id=1, source_target_pairs={{0,16},{4,20},{8,24},{12,28},{16,0},{20,4},{24,8},{28,12},{1,17},{... | collective-permute-start | bytes 344072 | tf_op jit(solution)/shard_map/ppermute | solution.py:645
  74.1 9.3 %collective-permute-start.20 = (bf16[112,512]{1,0:T(8,128)(2,1)S(1)}, bf16[112,512]{1,0:T(8,128)(2,1)S(1)}, u32[]{:S(2)}, u32[]{:S(2)}) collective-permute-start(bf16[112,512]{1,0:T(8,128)(2,1)S(1)} %get-tuple-element.129), channel_id=1, source_target_pairs={{0,24},{4,28},{8,16},{12,20},{16,8},{20,12},{24,0},{28,4},{1,25},{... | collective-permute-start | bytes 344072 | tf_op jit(solution)/shard_map/ppermute | solution.py:645
  80.9 2.5 %collective-permute-start.17 = (bf16[144,512]{1,0:T(8,128)(2,1)S(1)}, bf16[144,512]{1,0:T(8,128)(2,1)S(1)}, u32[]{:S(2)}, u32[]{:S(2)}) collective-permute-start(bf16[144,512]{1,0:T(8,128)(2,1)S(1)} %get-tuple-element.126), channel_id=1, source_target_pairs={{0,1},{1,0},{2,3},{3,2},{4,5},{5,4},{6,7},{7,6},{8,9},{9,8},{10,11... | collective-permute-start | bytes 442376 | tf_op jit(solution)/shard_map/ppermute | solution.py:628
  83.4 4.4 %collective-permute-start.21 = (bf16[1536,512]{1,0:T(8,128)(2,1)S(1)}, bf16[1536,512]{1,0:T(8,128)(2,1)S(1)}, u32[]{:S(2)}, u32[]{:S(2)}) collective-permute-start(bf16[1536,512]{1,0:T(8,128)(2,1)S(1)} %shard_map.284.own_ref), channel_id=1, source_target_pairs={{0,1},{1,0},{2,3},{3,2},{4,5},{5,4},{6,7},{7,6},{8,9},{9,8},{10,11... | collective-permute-start | bytes 4718600 | tf_op jit(solution)/shard_map/ppermute | solution.py:628
  83.5 20.1 %collective-permute-start.22 = (bf16[1536,512]{1,0:T(8,128)(2,1)S(1)}, bf16[1536,512]{1,0:T(8,128)(2,1)S(1)}, u32[]{:S(2)}, u32[]{:S(2)}) collective-permute-start(bf16[1536,512]{1,0:T(8,128)(2,1)S(1)} %get-tuple-element.133.own_ref), channel_id=1, source_target_pairs={{0,1},{1,0},{2,3},{3,2},{4,5},{5,4},{6,7},{7,6},{8,9},{9,8},{10,11... | collective-permute-start | bytes 4718600 | tf_op jit(solution)/shard_map/ppermute | solution.py:628
  84.0 7.2 %collective-permute-start.23 = (bf16[144,512]{1,0:T(8,128)(2,1)S(1)}, bf16[144,512]{1,0:T(8,128)(2,1)S(1)}, u32[]{:S(2)}, u32[]{:S(2)}) collective-permute-start(bf16[144,512]{1,0:T(8,128)(2,1)S(1)} %add_convert_fusion.2), channel_id=1, source_target_pairs={{0,4},{4,0},{8,12},{12,8},{16,20},{20,16},{24,28},{28,24},{1,5},{5... | collective-permute-start | bytes 442376 | tf_op jit(solution)/shard_map/ppermute | solution.py:645
  84.6 7.9 %collective-permute-start.28 = (bf16[112,512]{1,0:T(8,128)(2,1)S(1)}, bf16[112,512]{1,0:T(8,128)(2,1)S(1)}, u32[]{:S(2)}, u32[]{:S(2)}) collective-permute-start(bf16[112,512]{1,0:T(8,128)(2,1)S(1)} %add_convert_fusion.3.refs_0_), channel_id=1, source_target_pairs={{0,24},{4,28},{8,16},{12,20},{16,8},{20,12},{24,0},{28,4},{1,25},{... | collective-permute-start | bytes 344072 | tf_op jit(solution)/shard_map/ppermute | solution.py:645
  86.6 11.6 %collective-permute-start.27 = (bf16[112,512]{1,0:T(8,128)(2,1)S(1)}, bf16[112,512]{1,0:T(8,128)(2,1)S(1)}, u32[]{:S(2)}, u32[]{:S(2)}) collective-permute-start(bf16[112,512]{1,0:T(8,128)(2,1)S(1)} %add_convert_fusion.3.refs_0_), channel_id=1, source_target_pairs={{0,16},{4,20},{8,24},{12,28},{16,0},{20,4},{24,8},{28,12},{1,17},{... | collective-permute-start | bytes 344072 | tf_op jit(solution)/shard_map/ppermute | solution.py:645
  87.8 10.3 %collective-permute-start.26 = (bf16[112,512]{1,0:T(8,128)(2,1)S(1)}, bf16[112,512]{1,0:T(8,128)(2,1)S(1)}, u32[]{:S(2)}, u32[]{:S(2)}) collective-permute-start(bf16[112,512]{1,0:T(8,128)(2,1)S(1)} %add_convert_fusion.3.refs_0_), channel_id=1, source_target_pairs={{0,8},{4,12},{8,0},{12,4},{16,24},{20,28},{24,16},{28,20},{1,9},{5... | collective-permute-start | bytes 344072 | tf_op jit(solution)/shard_map/ppermute | solution.py:645
  91.2 8.5 %collective-permute-start.24 = (bf16[144,512]{1,0:T(8,128)(2,1)S(1)}, bf16[144,512]{1,0:T(8,128)(2,1)S(1)}, u32[]{:S(2)}, u32[]{:S(2)}) collective-permute-start(bf16[144,512]{1,0:T(8,128)(2,1)S(1)} %add_convert_fusion.1), channel_id=1, source_target_pairs={{0,8},{4,12},{8,0},{12,4},{16,24},{20,28},{24,16},{28,20},{1,9},{5... | collective-permute-start | bytes 442376 | tf_op jit(solution)/shard_map/ppermute | solution.py:645
  92.4 7.2 %collective-permute-start.25 = (bf16[112,512]{1,0:T(8,128)(2,1)S(1)}, bf16[112,512]{1,0:T(8,128)(2,1)S(1)}, u32[]{:S(2)}, u32[]{:S(2)}) collective-permute-start(bf16[112,512]{1,0:T(8,128)(2,1)S(1)} %add_convert_fusion.3.refs_0_), channel_id=1, source_target_pairs={{0,4},{4,0},{8,12},{12,8},{16,20},{20,16},{24,28},{28,24},{1,5},{5... | collective-permute-start | bytes 344072 | tf_op jit(solution)/shard_map/ppermute | solution.py:645
  98.1 9.4 %collective-permute-start.30 = (bf16[336,512]{1,0:T(8,128)(2,1)S(1)}, bf16[336,512]{1,0:T(8,128)(2,1)S(1)}, u32[]{:S(2)}, u32[]{:S(2)}) collective-permute-start(bf16[336,512]{1,0:T(8,128)(2,1)S(1)} %pad_maximum_fusion), channel_id=1, source_target_pairs={{0,4},{4,0},{8,12},{12,8},{16,20},{20,16},{24,28},{28,24},{1,5},{5... | collective-permute-start | bytes 1032200 | tf_op jit(solution)/shard_map/ppermute | solution.py:645
  99.7 9.7 %collective-permute-start.29 = (bf16[144,512]{1,0:T(8,128)(2,1)S(1)}, bf16[144,512]{1,0:T(8,128)(2,1)S(1)}, u32[]{:S(2)}, u32[]{:S(2)}) collective-permute-start(bf16[144,512]{1,0:T(8,128)(2,1)S(1)} %add_convert_fusion.mine_ref), channel_id=1, source_target_pairs={{0,16},{4,20},{8,24},{12,28},{16,0},{20,4},{24,8},{28,12},{1,17},{... | collective-permute-start | bytes 442376 | tf_op jit(solution)/shard_map/ppermute | solution.py:645

commit v7 on v6

--- a/solution.py
+++ b/solution.py
@@ -322,9 +322,10 @@
     far_refs, refs = refs[:levels], refs[levels:]
     beside_ref, powers_ref, local_all, normed_all, hg_all, cotm_all, a0, a1, a2, a3 = refs[:10]
     gain_ref, bias_ref, skip_ref, b0, b1, b2, b3, g0, g1, g2, g3 = refs[10:21]
-    state_all, back_all, backends_ref, ylow_all, hid_all, act_all, ul_all = refs[21:28]
-    c_all, ug_all, weigh, full, carry, sems = refs[28:]
+    state_all, back_all, backends_ref, ylow_all, hid_all, own_ref, sent_ref = refs[21:28]
+    c_all, ug_all, weigh, full, carry, act_ref, ul, acc_out, acc_down, acc_ug, sems = refs[28:]
     place, core, shard = where_ref[0], where_ref[1], where_ref[2]
+    side = shard // 2
     states = c_all.shape[0] // 2
     rows, width = normed_all.shape
     per_block = LARGE // length
@@ -347,6 +348,9 @@
     fill_powers(dr, di, False, 1, full)
     incoming(far_refs, beside_ref, place % 2, powers_ref, False, carry)
     fill_powers(dr, di, False, 0, weigh)
+    acc_out[...] = jnp.zeros(acc_out.shape, F32)
+    acc_down[...] = jnp.zeros(acc_down.shape, F32)
+    acc_ug[...] = jnp.zeros(acc_ug.shape, F32)
     for copy in copies:
         copy.wait()
     skip = skip_ref[...]
@@ -354,7 +358,7 @@
 
     def body(block, view):
         local_ref, state_ref, hid_ref, ylow_ref = view(local_all), view(state_all), view(hid_all), view(ylow_all)
-        hg_ref, act_ref, back_ref, ul = view(hg_all), view(act_all), view(back_all), view(ul_all)
+        hg_ref, back_ref = view(hg_all), view(back_all)
         for s in range(per_block):
             seq = block * per_block + s
             span = slice(s * length, (s + 1) * length)
@@ -382,31 +386,23 @@
         y_grad = dot_nt(ul[...], ug_all[...]) * slope
         ylow_ref[...] = y_grad.astype(BF16)
         back_ref[...] = dot_nt(ylow_ref[...], c_all[...])
+        acc_ug[...] += dot_tn(act, ul[:, pl.ds(pl.multiple_of(side * 4 * per_f, 4 * per_f), 4 * per_f)])
+        hid = hid_ref[:, pl.ds(pl.multiple_of(side * 2 * per_f, 2 * per_f), 2 * per_f)]
+        acc_down[...] += dot_tn(hid, view(cotm_all)[...])
+        for k in range(2):
+            cols = state_ref[:, pl.ds(pl.multiple_of(k * states + side * 2 * per_s, 2 * per_s), 2 * per_s)]
+            acc_out[k * 2 * per_s : (k + 1) * 2 * per_s, :] += dot_tn(cols, ylow_ref[...])
         weighted_ends(back_ref, weigh, length, block * per_block, backends_ref)
 
     each_block(rows, LARGE, body)
-
-
-def weight_kernel(where_ref, hid_ref, cotm_ref, act_ref, ul_ref, state_ref, ylow_ref, own_ref, sent_ref):
-    core, side = where_ref[1], where_ref[2] // 2
-    states = state_ref.shape[1] // 2
-    per_s = states // TENSOR
-    per_f = hid_ref.shape[1] // TENSOR
-    width = act_ref.shape[1]
-    cols = [
-        state_ref[:, pl.ds(pl.multiple_of(k * states + side * 2 * per_s, 2 * per_s), 2 * per_s)] for k in range(2)
-    ]
-    out_grad = dot_tn(jnp.concatenate(cols, axis=1), ylow_ref[...])
-    act, cotm = act_ref[...], cotm_ref[...]
-    for n, ref in ((1 - core, sent_ref), (core, own_ref)):
-        ul = ul_ref[:, pl.ds(pl.multiple_of((2 * side + n) * 2 * per_f, 2 * per_f), 2 * per_f)]
-        ref[2 * per_s + per_f : 2 * per_s + per_f + width, :] = dot_tn(act, ul).astype(ref.dtype)
-        hid = hid_ref[:, pl.ds(pl.multiple_of((2 * side + n) * per_f, per_f), per_f)]
-        ref[2 * per_s : 2 * per_s + per_f, :] = dot_tn(hid, cotm).astype(ref.dtype)
+    for n, ref in ((core, own_ref), (1 - core, sent_ref)):
         for k in range(2):
-            at = 2 * per_s * k
-            part = jnp.where(n == 0, out_grad[at : at + per_s, :], out_grad[at + per_s : at + 2 * per_s, :])
+            part = acc_out[pl.ds(pl.multiple_of(2 * per_s * k + n * per_s, per_s), per_s), :]
             ref[k * per_s : (k + 1) * per_s, :] = part.astype(ref.dtype)
+        part = acc_down[pl.ds(pl.multiple_of(n * per_f, per_f), per_f), :]
+        ref[2 * per_s : 2 * per_s + per_f, :] = part.astype(ref.dtype)
+        part = acc_ug[:, pl.ds(pl.multiple_of(n * 2 * per_f, 2 * per_f), 2 * per_f)]
+        ref[2 * per_s + per_f : 2 * per_s + per_f + width, :] = part.astype(ref.dtype)
 
 
 def down_kernel(where_ref, lens_ref, tok, hid_all, b0, b1, b2, b3, out_all, down_all, *, length, per_s):
@@ -778,7 +774,7 @@
     packs_g = gather_tensor(pack_g, hid_grad, *far_ends)
 
     pack_rows = -(-(2 * per_s + per_f + width) // (16 * groups)) * 16 * groups
-    state, back_drive, back_ends, y_low, hid, act, ul = call(
+    state, back_drive, back_ends, y_low, hid, own_b, sent_b = call(
         functools.partial(middle_kernel, length=length, levels=levels),
         [where],
         [
@@ -802,8 +798,8 @@
             ends_shape,
             ((rows, width), BF16),
             ((rows, units), BF16),
-            ((rows, width), BF16),
-            ((rows, 2 * units), BF16),
+            ((pack_rows, width), F32),
+            ((pack_rows, width), BF16),
         ],
         [
             pltpu.VMEM((lanes, width), BF16),
@@ -811,20 +807,24 @@
             pltpu.VMEM((2, length, states), F32),
             pltpu.VMEM((2, length, states), F32),
             pltpu.VMEM((own_seqs, lanes), F32),
+            pltpu.VMEM((LARGE, width), BF16),
+            pltpu.VMEM((LARGE, 2 * units), BF16),
+            pltpu.VMEM((states, width), F32),
+            pltpu.VMEM((2 * per_f, width), F32),
+            pltpu.VMEM((width, 4 * per_f), F32),
             dma((TENSOR, 3)),
         ],
-        16,
-    )
-    own_b, sent_b = call(
-        weight_kernel,
-        [where],
-        [hid, cot_m, act, ul, state, y_low],
-        [((pack_rows, width), F32), ((pack_rows, width), BF16)],
+        24,
+    )
+    half, part = pack_rows // 2, pack_rows // groups
+    keep_b, send_b = call(
+        fold_kernel,
+        [where],
+        [own_b, core_swap(sent_b)],
+        [((half, width), F32), ((half, width), BF16)],
         [],
-        10,
-    )
-
-    half, part = pack_rows // 2, pack_rows // groups
+        4,
+    )
     made = []
 
     def scan_work(pair_back):
@@ -840,17 +840,9 @@
         )
         return made[0]
 
-    far_back, beside_back, found_back = exchange(back_ends, True, own_b, scan_work)
+    far_back, beside_back, found_back = exchange(back_ends, True, send_b, scan_work)
     back = made[0]
-    keep_b, send_b = call(
-        fold_kernel,
-        [where],
-        [own_b, core_swap(after(sent_b, beside_back))],
-        [((half, width), F32), ((half, width), BF16)],
-        [],
-        4,
-    )
-    half_b = flip_dp(after(send_b, found_back[0]), 1, groups)
+    half_b = flip_dp(after(send_b, beside_back), 1, groups)
     out_own = call(
         functools.partial(down_kernel, length=length, per_s=per_s),
         [where, lengths],

time: 111 us -> 110 us (level)
  waiting for transfers between devices: 17.9 us -> 16.6 us
    pallas_call x21 -> x20, Pallas kernels: 52.4 us -> 52.1 us  [call(): pl.pallas_call(kernel, in_specs=[pl.BlockSpec(memory_space=pltpu.SMEM)] *...]
  transfers between devices with their start and end apart: 31 -> 31, of which waited for: 12 -> 14; matrix products, arithmetic and copies ran while one was open for 0% -> 0% of each run, Pallas kernels for 31% -> 29%
where the time goes in v7:
time: 110 us
  Pallas kernels  52.1 us (47%)
  starting transfers between devices  39.6 us (36%)
  waiting for transfers between devices  16.6 us (15%)
  between operations  1.13 us (1%)
    pallas_call x20, Pallas kernels, call(): pl.pallas_call(kernel, in_specs=[pl.BlockSpec(memory_space=pltpu.SMEM)] *...  52.1 us
    ppermute x14, starting transfers between devices, flip_dp(): return lax.ppermute(value, 'dp', [(i, i ^ bits) for i in range(groups)])  20.7 us
    ppermute x4, starting transfers between devices, shift_dp(): lax.ppermute(value, 'dp', [(i, i + by) for i in range(groups) if 0 <= i +...  11.5 us
    ppermute x14, waiting for transfers between devices, flip_dp(): return lax.ppermute(value, 'dp', [(i, i ^ bits) for i in range(groups)])  6.8 us
    ppermute x4, waiting for transfers between devices, shift_dp(): lax.ppermute(value, 'dp', [(i, i + by) for i in range(groups) if 0 <= i +...  6.38 us
    ppermute x3, starting transfers between devices, side_swap(): return lax.ppermute(value, 'tensor', [(t, t ^ 2) for t in range(TENSOR)])  5.12 us
    ppermute x10, waiting for transfers between devices, core_swap(): return lax.ppermute(value, 'tensor', [(t, t ^ 1) for t in range(TENSOR)])  3.44 us
    ppermute x10, starting transfers between devices, core_swap(): return lax.ppermute(value, 'tensor', [(t, t ^ 1) for t in range(TENSOR)])  2.23 us
  transfers between devices with their start and end apart: 31, of which 14 were waited for; matrix products, arithmetic and copies ran while one was open for 0% of the time, Pallas kernels for 29%

profile of v7, /device:TPU:0, one launch (start us, length us, event | category | flops | bytes accessed | tf_op | source)
XLA Modules:
  0.0 109.7 jit_solution(4545804333144201338)
XLA Ops:
  0.7 2.6 %shard_map.271 = (bf16[144,512]{1,0:T(8,128)(2,1)S(1)}, f32[3,1,64]{2,1,0:T(1,128)S(1)}, bf16[1536,512]{1,0:T(8,128)(2,1)S(1)}, bf16[1536,512]{1,0:T(8,128)(2,1)S(1)}) custom-call(s32[3]{0:T(128)S(1)} %pad_add_fusion.where_ref, bf16[64,512]{1,0:T(8,128)(2,1)} %bitcast.35, bf16[64,512]{1,0:T(8,128)(2,1)} %bitcast.36, f32[1,64]{1,0:T(1,128)} %bitcast.37, ...), custom_call_target="tpu_custom_call" | custom-call | tf_op jit(solution)/shard_map/pallas_call | solution.py:606
  3.3 3.0 %collective-permute-start.1 = (bf16[144,512]{1,0:T(8,128)(2,1)S(1)}, bf16[144,512]{1,0:T(8,128)(2,1)S(1)}, u32[]{:S(2)}, u32[]{:S(2)}) collective-permute-start(bf16[144,512]{1,0:T(8,128)(2,1)S(1)} %get-tuple-element.83.a0.refs_8_.refs_11_.a_ref), channel_id=1, source_target_pairs={{0,2},{1,3},{2,0},{3,1},{4,6},{5,7},{6,4},{7,5},{8,10},{9,11},{10,... | collective-permute-start | bytes 442376 | tf_op jit(solution)/shard_map/ppermute | solution.py:628
  6.4 1.2 %shard_map.272 = (bf16[384,512]{1,0:T(8,128)(2,1)S(1)}, bf16[512,512]{1,0:T(8,128)(2,1)S(1)}) custom-call(bf16[64,512]{1,0:T(8,128)(2,1)} %out_real, bf16[64,512]{1,0:T(8,128)(2,1)} %out_imag.1, bf16[512,256]{1,0:T(8,128)(2,1)} %up.1, bf16[512,256]{1,0:T(8,128)(2,1)} %gate.1, bf16[256,512]{1,0:T(8,128)(2,1)} %down.1), custom_call_target="tpu_custom_call" | custom-call | tf_op jit(solution)/shard_map/pallas_call | solution.py:606
  7.6 2.9 %shard_map.273 = (bf16[1536,512]{1,0:T(8,128)(2,1)S(1)}, f32[1536,512]{1,0:T(8,128)S(1)}, f32[1536,128]{1,0:T(8,128)S(1)}, bf16[1536,512]{1,0:T(8,128)(2,1)S(1)}) custom-call(s32[3]{0:T(128)S(1)} %pad_add_fusion.where_ref, bf16[1536,512]{1,0:T(8,128)(2,1)S(1)} %get-tuple-element.81.tok, bf16[1536,512]{1,0:T(8,128)(2,1)S(1)} %get-tuple-element.86.cot, ...), custom_call_target="tpu_custom_call" | custom-call | tf_op jit(solution)/shard_map/pallas_call | solution.py:606
  10.5 1.4 %collective-permute-start.7 = (bf16[384,512]{1,0:T(8,128)(2,1)S(1)}, bf16[384,512]{1,0:T(8,128)(2,1)S(1)}, u32[]{:S(2)}, u32[]{:S(2)}) collective-permute-start(bf16[384,512]{1,0:T(8,128)(2,1)S(1)} %get-tuple-element.97.b0.refs_15_), channel_id=1, source_target_pairs={{0,2},{1,3},{2,0},{3,1},{4,6},{5,7},{6,4},{7,5},{8,10},{9,11},{10,... | collective-permute-start | bytes 1179656 | tf_op jit(solution)/shard_map/ppermute | solution.py:628
  12.0 0.5 collective-permute-start.2
  12.5 0.6 collective-permute-start.10
  13.6 2.3 %shard_map.274 = (f32[1536,512]{1,0:T(8,128)S(1)}, f32[12,512]{1,0:T(8,128)S(1)}, f32[8,512]{1,0:T(8,128)S(1)}) custom-call(s32[3]{0:T(128)S(1)} %pad_add_fusion.where_ref, bf16[1536,512]{1,0:T(8,128)(2,1)S(1)} %get-tuple-element.87.low_all.refs_4_, bf16[144,512]{1,0:T(8,128)(2,1)S(1)} %get-tuple-element.83.a0.refs_8_.refs_11_.a_ref, ...), custom_call_target="tpu_custom_call" | custom-call | tf_op jit(solution)/shard_map/pallas_call | solution.py:606
  15.8 1.6 %collective-permute-start.3 = (f32[12,512]{1,0:T(8,128)S(1)}, f32[12,512]{1,0:T(8,128)S(1)}, u32[]{:S(2)}, u32[]{:S(2)}) collective-permute-start(f32[12,512]{1,0:T(8,128)S(1)} %get-tuple-element.89.mine_ref), channel_id=1, source_target_pairs={{0,4},{4,0},{8,12},{12,8},{16,20},{20,16},{24,28},{28,24},{1,5},{5... | collective-permute-start | bytes 73736 | tf_op jit(solution)/shard_map/ppermute | solution.py:641
  17.4 2.1 %shard_map.275.refs_4_ = f32[1536,512]{1,0:T(8,128)S(1)} custom-call(f32[1536,512]{1,0:T(8,128)S(1)} %get-tuple-element.90.drive_all, bf16[144,512]{1,0:T(8,128)(2,1)S(1)} %get-tuple-element.83.a0.refs_8_.refs_11_.a_ref, bf16[144,512]{1,0:T(8,128)(2,1)S(1)} %collective-permute-done.a1.refs_9_.refs_12_, ...), custom_call_target="tpu_custom_call" | custom-call | tf_op jit(solution)/shard_map/pallas_call | solution.py:606
  19.8 0.6 shard_map.276.mine_ref
  20.4 3.5 %collective-permute-start.4 = (f32[12,512]{1,0:T(8,128)S(1)}, f32[12,512]{1,0:T(8,128)S(1)}, u32[]{:S(2)}, u32[]{:S(2)}) collective-permute-start(f32[12,512]{1,0:T(8,128)S(1)} %shard_map.276.mine_ref), channel_id=1, source_target_pairs={{0,8},{4,12},{8,16},{12,20},{16,24},{20,28},{1,9},{5,13},{9,17},{1... | collective-permute-start | bytes 73736 | tf_op jit(solution)/shard_map/ppermute | solution.py:645
  24.0 1.5 %collective-permute-done.4.other_ref.refs_0_ = f32[12,512]{1,0:T(8,128)S(1)} collective-permute-done((f32[12,512]{1,0:T(8,128)S(1)}, f32[12,512]{1,0:T(8,128)S(1)}, u32[]{:S(2)}, u32[]{:S(2)}) %collective-permute-start.4) | collective-permute-done | bytes 24608 | tf_op jit(solution)/shard_map/ppermute | solution.py:645
  25.5 5.2 %collective-permute-start.5 = (f32[12,512]{1,0:T(8,128)S(1)}, f32[12,512]{1,0:T(8,128)S(1)}, u32[]{:S(2)}, u32[]{:S(2)}) collective-permute-start(f32[12,512]{1,0:T(8,128)S(1)} %shard_map.277), channel_id=1, source_target_pairs={{0,16},{4,20},{8,24},{12,28},{1,17},{5,21},{9,25},{13,29},{2,18},{... | collective-permute-start | bytes 73736 | tf_op jit(solution)/shard_map/ppermute | solution.py:645
  31.0 3.0 %shard_map.278.refs_6_ = bf16[1536,1024]{1,0:T(8,128)(2,1)S(1)} custom-call(s32[3]{0:T(128)S(1)} %pad_add_fusion.where_ref, bf16[1536,512]{1,0:T(8,128)(2,1)S(1)} %get-tuple-element.95.cotm_all.refs_7_, bf16[384,512]{1,0:T(8,128)(2,1)S(1)} %get-tuple-element.97.b0.refs_15_, bf16[384,512]{1,0:T(8,128)(2,1)S(1)} %collective-permute-done.6.b1.refs_16_, ...), custom_call_target="tpu_custom_call" | custom-call | tf_op jit(solution)/shard_map/pallas_call | solution.py:606
  34.4 1.6 %collective-permute-done.11.refs_22_ = bf16[512,512]{1,0:T(8,128)(2,1)S(1)} collective-permute-done((bf16[512,512]{1,0:T(8,128)(2,1)S(1)}, bf16[512,512]{1,0:T(8,128)(2,1)S(1)}, u32[]{:S(2)}, u32[]{:S(2)}) %collective-permute-start.11) | collective-permute-done | bytes 524320 | tf_op jit(solution)/shard_map/ppermute | solution.py:624
  36.1 16.0 %shard_map.279 = (bf16[1536,512]{1,0:T(8,128)(2,1)S(1)}, f32[1536,512]{1,0:T(8,128)S(1)}, f32[12,512]{1,0:T(8,128)S(1)}, bf16[1536,512]{1,0:T(8,128)(2,1)S(1)}, ...) custom-call(s32[3]{0:T(128)S(1)} %pad_add_fusion.where_ref, ...), custom_call_target="tpu_custom_call" | custom-call | tf_op jit(solution)/shard_map/pallas_call | solution.py:606
  52.4 1.5 %collective-permute-start.12 = (f32[12,512]{1,0:T(8,128)S(1)}, f32[12,512]{1,0:T(8,128)S(1)}, u32[]{:S(2)}, u32[]{:S(2)}) collective-permute-start(f32[12,512]{1,0:T(8,128)S(1)} %get-tuple-element.102.mine_ref), channel_id=1, source_target_pairs={{0,4},{4,0},{8,12},{12,8},{16,20},{20,16},{24,28},{28,24},{1,5},{5... | collective-permute-start | bytes 73736 | tf_op jit(solution)/shard_map/ppermute | solution.py:641
  53.9 0.7 collective-permute-done.13.other_ref
  54.6 0.7 shard_map.280
  55.3 1.0 collective-permute-done.12.other_ref.refs_2_
  56.3 1.5 %collective-permute-start.16 = (bf16[448,512]{1,0:T(8,128)(2,1)S(1)}, bf16[448,512]{1,0:T(8,128)(2,1)S(1)}, u32[]{:S(2)}, u32[]{:S(2)}) collective-permute-start(bf16[448,512]{1,0:T(8,128)(2,1)S(1)} %get-tuple-element.113), channel_id=1, source_target_pairs={{0,4},{4,0},{8,12},{12,8},{16,20},{20,16},{24,28},{28,24},{1,5},{5... | collective-permute-start | bytes 1376264 | tf_op jit(solution)/shard_map/ppermute | solution.py:641
  57.8 0.6 shard_map.281.mine_ref
  58.4 1.3 %collective-permute-start.14 = (f32[12,512]{1,0:T(8,128)S(1)}, f32[12,512]{1,0:T(8,128)S(1)}, u32[]{:S(2)}, u32[]{:S(2)}) collective-permute-start(f32[12,512]{1,0:T(8,128)S(1)} %shard_map.281.mine_ref), channel_id=1, source_target_pairs={{8,0},{12,4},{16,8},{20,12},{24,16},{28,20},{9,1},{13,5},{17,9},{2... | collective-permute-start | bytes 73736 | tf_op jit(solution)/shard_map/ppermute | solution.py:645
  59.7 2.1 %shard_map.282.refs_8_ = f32[1536,512]{1,0:T(8,128)S(1)} custom-call(f32[1536,512]{1,0:T(8,128)S(1)} %get-tuple-element.108.drive_all, bf16[144,512]{1,0:T(8,128)(2,1)S(1)} %get-tuple-element.83.a0.refs_8_.refs_11_.a_ref, bf16[144,512]{1,0:T(8,128)(2,1)S(1)} %collective-permute-done.a1.refs_9_.refs_12_, ...), custom_call_target="tpu_custom_call" | custom-call | tf_op jit(solution)/shard_map/pallas_call | solution.py:606
  61.8 2.4 %collective-permute-done.14.other_ref.refs_0_ = f32[12,512]{1,0:T(8,128)S(1)} collective-permute-done((f32[12,512]{1,0:T(8,128)S(1)}, f32[12,512]{1,0:T(8,128)S(1)}, u32[]{:S(2)}, u32[]{:S(2)}) %collective-permute-start.14) | collective-permute-done | bytes 24608 | tf_op jit(solution)/shard_map/ppermute | solution.py:645
  64.2 1.5 %collective-permute-start.15 = (f32[12,512]{1,0:T(8,128)S(1)}, f32[12,512]{1,0:T(8,128)S(1)}, u32[]{:S(2)}, u32[]{:S(2)}) collective-permute-start(f32[12,512]{1,0:T(8,128)S(1)} %shard_map.283), channel_id=1, source_target_pairs={{16,0},{20,4},{24,8},{28,12},{17,1},{21,5},{25,9},{29,13},{18,2},{... | collective-permute-start | bytes 73736 | tf_op jit(solution)/shard_map/ppermute | solution.py:645
  65.7 2.8 %shard_map.284.own_ref = bf16[1536,512]{1,0:T(8,128)(2,1)S(1)} custom-call(s32[3]{0:T(128)S(1)} %pad_add_fusion.where_ref, s32[24]{0:T(128)S(1)} %copy-done.3, bf16[1536,512]{1,0:T(8,128)(2,1)S(1)} %get-tuple-element.81.tok, bf16[1536,1024]{1,0:T(8,128)(2,1)S(1)} %get-tuple-element.110.hid_all, bf16[384,512]{1,0:T(8,128)(2,1)S(1)} %get-tuple-element.97.b0.refs_15_, ...), custom_call_target="tpu_custom_call" | custom-call | tf_op jit(solution)/shard_map/pallas_call | solution.py:606
  68.5 2.5 %collective-permute-done.15.refs_1_ = f32[12,512]{1,0:T(8,128)S(1)} collective-permute-done((f32[12,512]{1,0:T(8,128)S(1)}, f32[12,512]{1,0:T(8,128)S(1)}, u32[]{:S(2)}, u32[]{:S(2)}) %collective-permute-start.15) | collective-permute-done | bytes 24608 | tf_op jit(solution)/shard_map/ppermute | solution.py:645
  70.9 0.7 shard_map.285
  71.6 1.6 %collective-permute-start.18 = (bf16[112,512]{1,0:T(8,128)(2,1)S(1)}, bf16[112,512]{1,0:T(8,128)(2,1)S(1)}, u32[]{:S(2)}, u32[]{:S(2)}) collective-permute-start(bf16[112,512]{1,0:T(8,128)(2,1)S(1)} %get-tuple-element.121), channel_id=1, source_target_pairs={{0,8},{4,12},{8,0},{12,4},{16,24},{20,28},{24,16},{28,20},{1,9},{5... | collective-permute-start | bytes 344072 | tf_op jit(solution)/shard_map/ppermute | solution.py:641
  73.2 1.1 %collective-permute-start.19 = (bf16[112,512]{1,0:T(8,128)(2,1)S(1)}, bf16[112,512]{1,0:T(8,128)(2,1)S(1)}, u32[]{:S(2)}, u32[]{:S(2)}) collective-permute-start(bf16[112,512]{1,0:T(8,128)(2,1)S(1)} %get-tuple-element.122), channel_id=1, source_target_pairs={{0,16},{4,20},{8,24},{12,28},{16,0},{20,4},{24,8},{28,12},{1,17},{... | collective-permute-start | bytes 344072 | tf_op jit(solution)/shard_map/ppermute | solution.py:641
  74.3 1.7 %collective-permute-start.20 = (bf16[112,512]{1,0:T(8,128)(2,1)S(1)}, bf16[112,512]{1,0:T(8,128)(2,1)S(1)}, u32[]{:S(2)}, u32[]{:S(2)}) collective-permute-start(bf16[112,512]{1,0:T(8,128)(2,1)S(1)} %get-tuple-element.123), channel_id=1, source_target_pairs={{0,24},{4,28},{8,16},{12,20},{16,8},{20,12},{24,0},{28,4},{1,25},{... | collective-permute-start | bytes 344072 | tf_op jit(solution)/shard_map/ppermute | solution.py:641
  76.0 5.4 %shard_map.286 = (bf16[1536,512]{1,0:T(8,128)(2,1)S(1)}, bf16[144,512]{1,0:T(8,128)(2,1)S(1)}, bf16[144,512]{1,0:T(8,128)(2,1)S(1)}) custom-call(s32[3]{0:T(128)S(1)} %pad_add_fusion.where_ref, f32[12,512]{1,0:T(8,128)S(1)} %collective-permute-done.14.other_ref.refs_0_, f32[12,512]{1,0:T(8,128)S(1)} %collective-permute-done.15.refs_1_, ...), custom_call_target="tpu_custom_call" | custom-call | tf_op jit(solution)/shard_map/pallas_call | solution.py:606
  81.6 0.6 collective-permute-done.19
  82.2 0.7 collective-permute-done.17
  83.5 0.5 collective-permute-start.23
  84.0 2.1 %collective-permute-start.28 = (bf16[112,512]{1,0:T(8,128)(2,1)S(1)}, bf16[112,512]{1,0:T(8,128)(2,1)S(1)}, u32[]{:S(2)}, u32[]{:S(2)}) collective-permute-start(bf16[112,512]{1,0:T(8,128)(2,1)S(1)} %add_convert_fusion.3.refs_0_), channel_id=1, source_target_pairs={{0,24},{4,28},{8,16},{12,20},{16,8},{20,12},{24,0},{28,4},{1,25},{... | collective-permute-start | bytes 344072 | tf_op jit(solution)/shard_map/ppermute | solution.py:641
  86.6 1.8 %collective-permute-start.26 = (bf16[112,512]{1,0:T(8,128)(2,1)S(1)}, bf16[112,512]{1,0:T(8,128)(2,1)S(1)}, u32[]{:S(2)}, u32[]{:S(2)}) collective-permute-start(bf16[112,512]{1,0:T(8,128)(2,1)S(1)} %add_convert_fusion.3.refs_0_), channel_id=1, source_target_pairs={{0,8},{4,12},{8,0},{12,4},{16,24},{20,28},{24,16},{28,20},{1,9},{5... | collective-permute-start | bytes 344072 | tf_op jit(solution)/shard_map/ppermute | solution.py:641
  88.4 2.2 %shard_map.287 = bf16[3072,512]{1,0:T(8,128)(2,1)} custom-call(s32[3]{0:T(128)S(1)} %pad_add_fusion.where_ref, bf16[1536,512]{1,0:T(8,128)(2,1)S(1)} %shard_map.284.own_ref, bf16[1536,512]{1,0:T(8,128)(2,1)S(1)} %collective-permute-done.21.other_ref), custom_call_target="tpu_custom_call" | custom-call | tf_op jit(solution)/shard_map/pallas_call | solution.py:606
  91.0 0.9 collective-permute-done.28.refs_3_
  91.9 1.5 %collective-permute-start.25 = (bf16[112,512]{1,0:T(8,128)(2,1)S(1)}, bf16[112,512]{1,0:T(8,128)(2,1)S(1)}, u32[]{:S(2)}, u32[]{:S(2)}) collective-permute-start(bf16[112,512]{1,0:T(8,128)(2,1)S(1)} %add_convert_fusion.3.refs_0_), channel_id=1, source_target_pairs={{0,4},{4,0},{8,12},{12,8},{16,20},{20,16},{24,28},{28,24},{1,5},{5... | collective-permute-start | bytes 344072 | tf_op jit(solution)/shard_map/ppermute | solution.py:641
  93.4 3.4 %collective-permute-done.27.refs_2_ = bf16[112,512]{1,0:T(8,128)(2,1)S(1)} collective-permute-done((bf16[112,512]{1,0:T(8,128)(2,1)S(1)}, bf16[112,512]{1,0:T(8,128)(2,1)S(1)}, u32[]{:S(2)}, u32[]{:S(2)}) %collective-permute-start.27) | collective-permute-done | bytes 114720 | tf_op jit(solution)/shard_map/ppermute | solution.py:641
  96.9 1.6 %collective-permute-start.30 = (bf16[336,512]{1,0:T(8,128)(2,1)S(1)}, bf16[336,512]{1,0:T(8,128)(2,1)S(1)}, u32[]{:S(2)}, u32[]{:S(2)}) collective-permute-start(bf16[336,512]{1,0:T(8,128)(2,1)S(1)} %pad_maximum_fusion), channel_id=1, source_target_pairs={{0,4},{4,0},{8,12},{12,8},{16,20},{20,16},{24,28},{28,24},{1,5},{5... | collective-permute-start | bytes 1032200 | tf_op jit(solution)/shard_map/ppermute | solution.py:641
  99.0 3.5 %collective-permute-start.29 = (bf16[144,512]{1,0:T(8,128)(2,1)S(1)}, bf16[144,512]{1,0:T(8,128)(2,1)S(1)}, u32[]{:S(2)}, u32[]{:S(2)}) collective-permute-start(bf16[144,512]{1,0:T(8,128)(2,1)S(1)} %add_convert_fusion.mine_ref), channel_id=1, source_target_pairs={{0,16},{4,20},{8,24},{12,28},{16,0},{20,4},{24,8},{28,12},{1,17},{... | collective-permute-start | bytes 442376 | tf_op jit(solution)/shard_map/ppermute | solution.py:641
  102.5 3.6 %shard_map.288 = f32[3072,512]{1,0:T(8,128)} custom-call(s32[3]{0:T(128)S(1)} %pad_add_fusion.where_ref, bf16[1536,512]{1,0:T(8,128)(2,1)S(1)} %get-tuple-element.127.own_ref, bf16[1536,512]{1,0:T(8,128)(2,1)S(1)} %collective-permute-done.22.other_ref), custom_call_target="tpu_custom_call" | custom-call | tf_op jit(solution)/shard_map/pallas_call | solution.py:606
  106.1 1.9 %shard_map.289 = (f32[64,512]{1,0:T(8,128)}, f32[64,512]{1,0:T(8,128)}, f32[512,256]{1,0:T(8,128)}, f32[512,256]{1,0:T(8,128)}, f32[256,512]{1,0:T(8,128)}) custom-call(s32[3]{0:T(128)S(1)} %pad_add_fusion.where_ref, bf16[112,512]{1,0:T(8,128)(2,1)S(1)} %add_convert_fusion.3.refs_0_, bf16[112,512]{1,0:T(8,128)(2,1)S(1)} %collective-permute-done.26.refs_1_, ...), custom_call_target="tpu_custom_call" | custom-call | tf_op jit(solution)/shard_map/pallas_call | solution.py:606
  108.0 1.5 %shard_map.290 = (f32[1,512]{1,0:T(1,128)}, f32[1,512]{1,0:T(1,128)}, f32[1,512]{1,0:T(1,128)}, f32[64,512]{1,0:T(8,128)}, f32[64,512]{1,0:T(8,128)}, /*index=5*...) custom-call(s32[3]{0:T(128)S(1)} %pad_add_fusion.where_ref, bf16[144,512]{1,0:T(8,128)(2,1)S(1)} %add_convert_fusion.mine_ref, ...), custom_call_target="tpu_custom_call" | custom-call | tf_op jit(solution)/shard_map/pallas_call | solution.py:606
  (48 shorter events, 4.0 us)
Async XLA Ops:
  3.3 7.2 %collective-permute-start.1 = (bf16[144,512]{1,0:T(8,128)(2,1)S(1)}, bf16[144,512]{1,0:T(8,128)(2,1)S(1)}, u32[]{:S(2)}, u32[]{:S(2)}) collective-permute-start(bf16[144,512]{1,0:T(8,128)(2,1)S(1)} %get-tuple-element.83.a0.refs_8_.refs_11_.a_ref), channel_id=1, source_target_pairs={{0,2},{1,3},{2,0},{3,1},{4,6},{5,7},{6,4},{7,5},{8,10},{9,11},{10,... | collective-permute-start | bytes 442376 | tf_op jit(solution)/shard_map/ppermute | solution.py:628
  10.5 14.9 %collective-permute-start.7 = (bf16[384,512]{1,0:T(8,128)(2,1)S(1)}, bf16[384,512]{1,0:T(8,128)(2,1)S(1)}, u32[]{:S(2)}, u32[]{:S(2)}) collective-permute-start(bf16[384,512]{1,0:T(8,128)(2,1)S(1)} %get-tuple-element.97.b0.refs_15_), channel_id=1, source_target_pairs={{0,2},{1,3},{2,0},{3,1},{4,6},{5,7},{6,4},{7,5},{8,10},{9,11},{10,... | collective-permute-start | bytes 1179656 | tf_op jit(solution)/shard_map/ppermute | solution.py:628
  12.0 1.4 %collective-permute-start = (bf16[144,512]{1,0:T(8,128)(2,1)S(1)}, bf16[144,512]{1,0:T(8,128)(2,1)S(1)}, u32[]{:S(2)}, u32[]{:S(2)}) collective-permute-start(bf16[144,512]{1,0:T(8,128)(2,1)S(1)} %get-tuple-element.83.a0.refs_8_.refs_11_.a_ref), channel_id=1, source_target_pairs={{0,1},{1,0},{2,3},{3,2},{4,5},{5,4},{6,7},{7,6},{8,9},{9,8},{10,11... | collective-permute-start | bytes 442376 | tf_op jit(solution)/shard_map/ppermute | solution.py:624
  12.0 1.6 %collective-permute-start.2 = (bf16[144,512]{1,0:T(8,128)(2,1)S(1)}, bf16[144,512]{1,0:T(8,128)(2,1)S(1)}, u32[]{:S(2)}, u32[]{:S(2)}) collective-permute-start(bf16[144,512]{1,0:T(8,128)(2,1)S(1)} %collective-permute-done.1.a2.refs_10_.refs_13_), channel_id=1, source_target_pairs={{0,1},{1,0},{2,3},{3,2},{4,5},{5,4},{6,7},{7,6},{8,9},{9,8},{10,11... | collective-permute-start | bytes 442376 | tf_op jit(solution)/shard_map/ppermute | solution.py:624
  12.5 21.6 %collective-permute-start.10 = (bf16[512,512]{1,0:T(8,128)(2,1)S(1)}, bf16[512,512]{1,0:T(8,128)(2,1)S(1)}, u32[]{:S(2)}, u32[]{:S(2)}) collective-permute-start(bf16[512,512]{1,0:T(8,128)(2,1)S(1)} %get-tuple-element.99.refs_19_), channel_id=1, source_target_pairs={{0,2},{1,3},{2,0},{3,1},{4,6},{5,7},{6,4},{7,5},{8,10},{9,11},{10,... | collective-permute-start | bytes 1572872 | tf_op jit(solution)/shard_map/ppermute | solution.py:628
  15.8 4.0 %collective-permute-start.3 = (f32[12,512]{1,0:T(8,128)S(1)}, f32[12,512]{1,0:T(8,128)S(1)}, u32[]{:S(2)}, u32[]{:S(2)}) collective-permute-start(f32[12,512]{1,0:T(8,128)S(1)} %get-tuple-element.89.mine_ref), channel_id=1, source_target_pairs={{0,4},{4,0},{8,12},{12,8},{16,20},{20,16},{24,28},{28,24},{1,5},{5... | collective-permute-start | bytes 73736 | tf_op jit(solution)/shard_map/ppermute | solution.py:641
  20.4 5.1 %collective-permute-start.4 = (f32[12,512]{1,0:T(8,128)S(1)}, f32[12,512]{1,0:T(8,128)S(1)}, u32[]{:S(2)}, u32[]{:S(2)}) collective-permute-start(f32[12,512]{1,0:T(8,128)S(1)} %shard_map.276.mine_ref), channel_id=1, source_target_pairs={{0,8},{4,12},{8,16},{12,20},{16,24},{20,28},{1,9},{5,13},{9,17},{1... | collective-permute-start | bytes 73736 | tf_op jit(solution)/shard_map/ppermute | solution.py:645
  23.9 7.1 %collective-permute-start.6 = (bf16[384,512]{1,0:T(8,128)(2,1)S(1)}, bf16[384,512]{1,0:T(8,128)(2,1)S(1)}, u32[]{:S(2)}, u32[]{:S(2)}) collective-permute-start(bf16[384,512]{1,0:T(8,128)(2,1)S(1)} %get-tuple-element.97.b0.refs_15_), channel_id=1, source_target_pairs={{0,1},{1,0},{2,3},{3,2},{4,5},{5,4},{6,7},{7,6},{8,9},{9,8},{10,11... | collective-permute-start | bytes 1179656 | tf_op jit(solution)/shard_map/ppermute | solution.py:624
  25.5 5.6 %collective-permute-start.8 = (bf16[384,512]{1,0:T(8,128)(2,1)S(1)}, bf16[384,512]{1,0:T(8,128)(2,1)S(1)}, u32[]{:S(2)}, u32[]{:S(2)}) collective-permute-start(bf16[384,512]{1,0:T(8,128)(2,1)S(1)} %collective-permute-done.7.b2.refs_17_), channel_id=1, source_target_pairs={{0,1},{1,0},{2,3},{3,2},{4,5},{5,4},{6,7},{7,6},{8,9},{9,8},{10,11... | collective-permute-start | bytes 1179656 | tf_op jit(solution)/shard_map/ppermute | solution.py:624
  25.5 8.6 %collective-permute-start.5 = (f32[12,512]{1,0:T(8,128)S(1)}, f32[12,512]{1,0:T(8,128)S(1)}, u32[]{:S(2)}, u32[]{:S(2)}) collective-permute-start(f32[12,512]{1,0:T(8,128)S(1)} %shard_map.277), channel_id=1, source_target_pairs={{0,16},{4,20},{8,24},{12,28},{1,17},{5,21},{9,25},{13,29},{2,18},{... | collective-permute-start | bytes 73736 | tf_op jit(solution)/shard_map/ppermute | solution.py:645
  30.7 3.7 %collective-permute-start.9 = (bf16[512,512]{1,0:T(8,128)(2,1)S(1)}, bf16[512,512]{1,0:T(8,128)(2,1)S(1)}, u32[]{:S(2)}, u32[]{:S(2)}) collective-permute-start(bf16[512,512]{1,0:T(8,128)(2,1)S(1)} %get-tuple-element.99.refs_19_), channel_id=1, source_target_pairs={{0,1},{1,0},{2,3},{3,2},{4,5},{5,4},{6,7},{7,6},{8,9},{9,8},{10,11... | collective-permute-start | bytes 1572872 | tf_op jit(solution)/shard_map/ppermute | solution.py:624
  31.0 5.1 %copy-start = (f32[512]{0:T(512)S(1)}, f32[512]{0:T(512)}, u32[]{:S(2)}) copy-start(f32[512]{0:T(512)} %param.18) | copy-start | bytes 6148
  31.0 5.1 %copy-start.1 = (f32[512]{0:T(512)S(1)}, f32[512]{0:T(512)}, u32[]{:S(2)}) copy-start(f32[512]{0:T(512)} %param.19) | copy-start | bytes 6148
  31.0 5.1 %copy-start.2 = (f32[512]{0:T(512)S(1)}, f32[512]{0:T(512)}, u32[]{:S(2)}) copy-start(f32[512]{0:T(512)} %param.20) | copy-start | bytes 6148
  34.1 2.0 %collective-permute-start.11 = (bf16[512,512]{1,0:T(8,128)(2,1)S(1)}, bf16[512,512]{1,0:T(8,128)(2,1)S(1)}, u32[]{:S(2)}, u32[]{:S(2)}) collective-permute-start(bf16[512,512]{1,0:T(8,128)(2,1)S(1)} %collective-permute-done.10.refs_21_), channel_id=1, source_target_pairs={{0,1},{1,0},{2,3},{3,2},{4,5},{5,4},{6,7},{7,6},{8,9},{9,8},{10,11... | collective-permute-start | bytes 1572872 | tf_op jit(solution)/shard_map/ppermute | solution.py:624
  52.0 2.5 %collective-permute-start.13 = (bf16[896,512]{1,0:T(8,128)(2,1)S(1)}, bf16[896,512]{1,0:T(8,128)(2,1)S(1)}, u32[]{:S(2)}, u32[]{:S(2)}) collective-permute-start(bf16[896,512]{1,0:T(8,128)(2,1)S(1)} %get-tuple-element.104), channel_id=1, source_target_pairs={{0,1},{1,0},{2,3},{3,2},{4,5},{5,4},{6,7},{7,6},{8,9},{9,8},{10,11... | collective-permute-start | bytes 2752520 | tf_op jit(solution)/shard_map/ppermute | solution.py:624
  52.4 3.9 %collective-permute-start.12 = (f32[12,512]{1,0:T(8,128)S(1)}, f32[12,512]{1,0:T(8,128)S(1)}, u32[]{:S(2)}, u32[]{:S(2)}) collective-permute-start(f32[12,512]{1,0:T(8,128)S(1)} %get-tuple-element.102.mine_ref), channel_id=1, source_target_pairs={{0,4},{4,0},{8,12},{12,8},{16,20},{20,16},{24,28},{28,24},{1,5},{5... | collective-permute-start | bytes 73736 | tf_op jit(solution)/shard_map/ppermute | solution.py:641
  56.3 14.6 %collective-permute-start.16 = (bf16[448,512]{1,0:T(8,128)(2,1)S(1)}, bf16[448,512]{1,0:T(8,128)(2,1)S(1)}, u32[]{:S(2)}, u32[]{:S(2)}) collective-permute-start(bf16[448,512]{1,0:T(8,128)(2,1)S(1)} %get-tuple-element.113), channel_id=1, source_target_pairs={{0,4},{4,0},{8,12},{12,8},{16,20},{20,16},{24,28},{28,24},{1,5},{5... | collective-permute-start | bytes 1376264 | tf_op jit(solution)/shard_map/ppermute | solution.py:641
  58.4 5.8 %collective-permute-start.14 = (f32[12,512]{1,0:T(8,128)S(1)}, f32[12,512]{1,0:T(8,128)S(1)}, u32[]{:S(2)}, u32[]{:S(2)}) collective-permute-start(f32[12,512]{1,0:T(8,128)S(1)} %shard_map.281.mine_ref), channel_id=1, source_target_pairs={{8,0},{12,4},{16,8},{20,12},{24,16},{28,20},{9,1},{13,5},{17,9},{2... | collective-permute-start | bytes 73736 | tf_op jit(solution)/shard_map/ppermute | solution.py:645
  59.7 6.0 %copy-start.3 = (s32[24]{0:T(128)S(1)}, s32[24]{0:T(128)}, u32[]{:S(2)}) copy-start(s32[24]{0:T(128)} %lens_ref.1) | copy-start | bytes 292
  64.2 6.7 %collective-permute-start.15 = (f32[12,512]{1,0:T(8,128)S(1)}, f32[12,512]{1,0:T(8,128)S(1)}, u32[]{:S(2)}, u32[]{:S(2)}) collective-permute-start(f32[12,512]{1,0:T(8,128)S(1)} %shard_map.283), channel_id=1, source_target_pairs={{16,0},{20,4},{24,8},{28,12},{17,1},{21,5},{25,9},{29,13},{18,2},{... | collective-permute-start | bytes 73736 | tf_op jit(solution)/shard_map/ppermute | solution.py:645
  71.6 10.0 %collective-permute-start.18 = (bf16[112,512]{1,0:T(8,128)(2,1)S(1)}, bf16[112,512]{1,0:T(8,128)(2,1)S(1)}, u32[]{:S(2)}, u32[]{:S(2)}) collective-permute-start(bf16[112,512]{1,0:T(8,128)(2,1)S(1)} %get-tuple-element.121), channel_id=1, source_target_pairs={{0,8},{4,12},{8,0},{12,4},{16,24},{20,28},{24,16},{28,20},{1,9},{5... | collective-permute-start | bytes 344072 | tf_op jit(solution)/shard_map/ppermute | solution.py:641
  73.2 8.9 %collective-permute-start.19 = (bf16[112,512]{1,0:T(8,128)(2,1)S(1)}, bf16[112,512]{1,0:T(8,128)(2,1)S(1)}, u32[]{:S(2)}, u32[]{:S(2)}) collective-permute-start(bf16[112,512]{1,0:T(8,128)(2,1)S(1)} %get-tuple-element.122), channel_id=1, source_target_pairs={{0,16},{4,20},{8,24},{12,28},{16,0},{20,4},{24,8},{28,12},{1,17},{... | collective-permute-start | bytes 344072 | tf_op jit(solution)/shard_map/ppermute | solution.py:641
  74.3 7.8 %collective-permute-start.20 = (bf16[112,512]{1,0:T(8,128)(2,1)S(1)}, bf16[112,512]{1,0:T(8,128)(2,1)S(1)}, u32[]{:S(2)}, u32[]{:S(2)}) collective-permute-start(bf16[112,512]{1,0:T(8,128)(2,1)S(1)} %get-tuple-element.123), channel_id=1, source_target_pairs={{0,24},{4,28},{8,16},{12,20},{16,8},{20,12},{24,0},{28,4},{1,25},{... | collective-permute-start | bytes 344072 | tf_op jit(solution)/shard_map/ppermute | solution.py:641
  81.5 1.4 %collective-permute-start.17 = (bf16[144,512]{1,0:T(8,128)(2,1)S(1)}, bf16[144,512]{1,0:T(8,128)(2,1)S(1)}, u32[]{:S(2)}, u32[]{:S(2)}) collective-permute-start(bf16[144,512]{1,0:T(8,128)(2,1)S(1)} %get-tuple-element.120), channel_id=1, source_target_pairs={{0,1},{1,0},{2,3},{3,2},{4,5},{5,4},{6,7},{7,6},{8,9},{9,8},{10,11... | collective-permute-start | bytes 442376 | tf_op jit(solution)/shard_map/ppermute | solution.py:624
  82.9 3.7 %collective-permute-start.21 = (bf16[1536,512]{1,0:T(8,128)(2,1)S(1)}, bf16[1536,512]{1,0:T(8,128)(2,1)S(1)}, u32[]{:S(2)}, u32[]{:S(2)}) collective-permute-start(bf16[1536,512]{1,0:T(8,128)(2,1)S(1)} %shard_map.284.own_ref), channel_id=1, source_target_pairs={{0,1},{1,0},{2,3},{3,2},{4,5},{5,4},{6,7},{7,6},{8,9},{9,8},{10,11... | collective-permute-start | bytes 4718600 | tf_op jit(solution)/shard_map/ppermute | solution.py:624
  83.2 19.3 %collective-permute-start.22 = (bf16[1536,512]{1,0:T(8,128)(2,1)S(1)}, bf16[1536,512]{1,0:T(8,128)(2,1)S(1)}, u32[]{:S(2)}, u32[]{:S(2)}) collective-permute-start(bf16[1536,512]{1,0:T(8,128)(2,1)S(1)} %get-tuple-element.127.own_ref), channel_id=1, source_target_pairs={{0,1},{1,0},{2,3},{3,2},{4,5},{5,4},{6,7},{7,6},{8,9},{9,8},{10,11... | collective-permute-start | bytes 4718600 | tf_op jit(solution)/shard_map/ppermute | solution.py:624
  83.5 7.2 %collective-permute-start.23 = (bf16[144,512]{1,0:T(8,128)(2,1)S(1)}, bf16[144,512]{1,0:T(8,128)(2,1)S(1)}, u32[]{:S(2)}, u32[]{:S(2)}) collective-permute-start(bf16[144,512]{1,0:T(8,128)(2,1)S(1)} %add_convert_fusion.2), channel_id=1, source_target_pairs={{0,4},{4,0},{8,12},{12,8},{16,20},{20,16},{24,28},{28,24},{1,5},{5... | collective-permute-start | bytes 442376 | tf_op jit(solution)/shard_map/ppermute | solution.py:641
  84.0 7.9 %collective-permute-start.28 = (bf16[112,512]{1,0:T(8,128)(2,1)S(1)}, bf16[112,512]{1,0:T(8,128)(2,1)S(1)}, u32[]{:S(2)}, u32[]{:S(2)}) collective-permute-start(bf16[112,512]{1,0:T(8,128)(2,1)S(1)} %add_convert_fusion.3.refs_0_), channel_id=1, source_target_pairs={{0,24},{4,28},{8,16},{12,20},{16,8},{20,12},{24,0},{28,4},{1,25},{... | collective-permute-start | bytes 344072 | tf_op jit(solution)/shard_map/ppermute | solution.py:641
  86.2 10.7 %collective-permute-start.27 = (bf16[112,512]{1,0:T(8,128)(2,1)S(1)}, bf16[112,512]{1,0:T(8,128)(2,1)S(1)}, u32[]{:S(2)}, u32[]{:S(2)}) collective-permute-start(bf16[112,512]{1,0:T(8,128)(2,1)S(1)} %add_convert_fusion.3.refs_0_), channel_id=1, source_target_pairs={{0,16},{4,20},{8,24},{12,28},{16,0},{20,4},{24,8},{28,12},{1,17},{... | collective-permute-start | bytes 344072 | tf_op jit(solution)/shard_map/ppermute | solution.py:641
  86.6 10.3 %collective-permute-start.26 = (bf16[112,512]{1,0:T(8,128)(2,1)S(1)}, bf16[112,512]{1,0:T(8,128)(2,1)S(1)}, u32[]{:S(2)}, u32[]{:S(2)}) collective-permute-start(bf16[112,512]{1,0:T(8,128)(2,1)S(1)} %add_convert_fusion.3.refs_0_), channel_id=1, source_target_pairs={{0,8},{4,12},{8,0},{12,4},{16,24},{20,28},{24,16},{28,20},{1,9},{5... | collective-permute-start | bytes 344072 | tf_op jit(solution)/shard_map/ppermute | solution.py:641
  90.7 8.2 %collective-permute-start.24 = (bf16[144,512]{1,0:T(8,128)(2,1)S(1)}, bf16[144,512]{1,0:T(8,128)(2,1)S(1)}, u32[]{:S(2)}, u32[]{:S(2)}) collective-permute-start(bf16[144,512]{1,0:T(8,128)(2,1)S(1)} %add_convert_fusion.1), channel_id=1, source_target_pairs={{0,8},{4,12},{8,0},{12,4},{16,24},{20,28},{24,16},{28,20},{1,9},{5... | collective-permute-start | bytes 442376 | tf_op jit(solution)/shard_map/ppermute | solution.py:641
  91.9 6.5 %collective-permute-start.25 = (bf16[112,512]{1,0:T(8,128)(2,1)S(1)}, bf16[112,512]{1,0:T(8,128)(2,1)S(1)}, u32[]{:S(2)}, u32[]{:S(2)}) collective-permute-start(bf16[112,512]{1,0:T(8,128)(2,1)S(1)} %add_convert_fusion.3.refs_0_), channel_id=1, source_target_pairs={{0,4},{4,0},{8,12},{12,8},{16,20},{20,16},{24,28},{28,24},{1,5},{5... | collective-permute-start | bytes 344072 | tf_op jit(solution)/shard_map/ppermute | solution.py:641
  96.9 9.2 %collective-permute-start.30 = (bf16[336,512]{1,0:T(8,128)(2,1)S(1)}, bf16[336,512]{1,0:T(8,128)(2,1)S(1)}, u32[]{:S(2)}, u32[]{:S(2)}) collective-permute-start(bf16[336,512]{1,0:T(8,128)(2,1)S(1)} %pad_maximum_fusion), channel_id=1, source_target_pairs={{0,4},{4,0},{8,12},{12,8},{16,20},{20,16},{24,28},{28,24},{1,5},{5... | collective-permute-start | bytes 1032200 | tf_op jit(solution)/shard_map/ppermute | solution.py:641
  99.0 9.0 %collective-permute-start.29 = (bf16[144,512]{1,0:T(8,128)(2,1)S(1)}, bf16[144,512]{1,0:T(8,128)(2,1)S(1)}, u32[]{:S(2)}, u32[]{:S(2)}) collective-permute-start(bf16[144,512]{1,0:T(8,128)(2,1)S(1)} %add_convert_fusion.mine_ref), channel_id=1, source_target_pairs={{0,16},{4,20},{8,24},{12,28},{16,0},{20,4},{24,8},{28,12},{1,17},{... | collective-permute-start | bytes 442376 | tf_op jit(solution)/shard_map/ppermute | solution.py:641

commit v8 on v7

--- a/solution.py
+++ b/solution.py
@@ -541,17 +541,20 @@
 
 
 def unpack_kernel(where_ref, *refs, ways):
-    parts, (real_ref, imag_ref, up_ref, gate_ref, down_ref, total, sems) = refs[: ways + 2], refs[ways + 2 :]
+    parts, (real_ref, imag_ref, up_ref, gate_ref, down_ref, total, sems) = refs[: ways + 3], refs[ways + 3 :]
     place = where_ref[0]
     rows = parts[0].shape[0]
     for n in range(2 * ways):
         k = n % ways
         half = place % 2 if n < ways else 1 - place % 2
         at = (half * ways + ((place // 2) ^ k)) * rows
+        middle = ways // 2 + 1
         if n <= ways:
             part = parts[n][...]
+        elif k >= middle:
+            part = parts[ways + 1][(k - middle) * rows : (k - middle + 1) * rows, :]
         else:
-            part = parts[-1][(k - 1) * rows : k * rows, :]
+            part = parts[ways + 2][(k - 1) * rows : k * rows, :]
         total[pl.ds(pl.multiple_of(at, 16), rows), :] = part.astype(F32)
     per_s, per_f, width = real_ref.shape[0], down_ref.shape[0], up_ref.shape[0]
     first = 2 * per_s + per_f
@@ -897,7 +900,11 @@
         mine_b = mine_b + flip_dp(dealt[k], 2 * k, groups).astype(F32)
     mine_b = mine_b.astype(BF16)
     gathered = [mine_b] + [flip_dp(mine_b, 2 * k, groups) for k in range(1, ways)]
-    beside = [flip_dp(mine_b, 1, groups), flip_dp(jnp.concatenate(gathered[1:], axis=0), 1, groups)]
+    middle = ways // 2 + 1
+    beside = [
+        flip_dp(jnp.concatenate(pieces, axis=0), 1, groups)
+        for pieces in (gathered[:1], gathered[middle:], gathered[1:middle])
+    ]
 
     grads_a = own_a.astype(F32) + after(core_swap(sent_a), mine_b).astype(F32)
     low_a = grads_a.astype(BF16)
@@ -925,7 +932,7 @@
     unpacked = call(
         functools.partial(unpack_kernel, ways=ways),
         [where],
-        [*gathered, beside[0], after(beside[1], input_grad)],
+        [*gathered, *beside[:2], after(beside[2], input_grad)],
         [state_shape] * 2 + [((width, per_f), F32)] * 2 + [((per_f, width), F32)],
         [pltpu.VMEM((pack_rows, width), F32), dma((5,))],
         8,

time: 110 us -> 108 us (0.982)
  starting transfers between devices: 39.6 us -> 37.9 us
    ppermute x14 -> x15, starting transfers between devices: 20.7 us -> 19 us  [flip_dp(): return lax.ppermute(value, 'dp', [(i, i ^ bits) for i in range(groups)])]
    ppermute x14 -> x15, waiting for transfers between devices: 6.8 us -> 6.95 us  [flip_dp(): return lax.ppermute(value, 'dp', [(i, i ^ bits) for i in range(groups)])]
  transfers between devices with their start and end apart: 31 -> 32, of which waited for: 14 -> 15; matrix products, arithmetic and copies ran while one was open for 0% -> 0% of each run, Pallas kernels for 29% -> 29%
where the time goes in v8:
time: 108 us
  Pallas kernels  52.1 us (48%)
  starting transfers between devices  37.9 us (35%)
  waiting for transfers between devices  16.8 us (16%)
  between operations  1.12 us (1%)
    pallas_call x20, Pallas kernels, call(): pl.pallas_call(kernel, in_specs=[pl.BlockSpec(memory_space=pltpu.SMEM)] *...  52.1 us
    ppermute x15, starting transfers between devices, flip_dp(): return lax.ppermute(value, 'dp', [(i, i ^ bits) for i in range(groups)])  19 us
    ppermute x4, starting transfers between devices, shift_dp(): lax.ppermute(value, 'dp', [(i, i + by) for i in range(groups) if 0 <= i +...  11.5 us
    ppermute x15, waiting for transfers between devices, flip_dp(): return lax.ppermute(value, 'dp', [(i, i ^ bits) for i in range(groups)])  6.95 us
    ppermute x4, waiting for transfers between devices, shift_dp(): lax.ppermute(value, 'dp', [(i, i + by) for i in range(groups) if 0 <= i +...  6.38 us
    ppermute x3, starting transfers between devices, side_swap(): return lax.ppermute(value, 'tensor', [(t, t ^ 2) for t in range(TENSOR)])  5.12 us
    ppermute x10, waiting for transfers between devices, core_swap(): return lax.ppermute(value, 'tensor', [(t, t ^ 1) for t in range(TENSOR)])  3.46 us
    ppermute x10, starting transfers between devices, core_swap(): return lax.ppermute(value, 'tensor', [(t, t ^ 1) for t in range(TENSOR)])  2.22 us
  transfers between devices with their start and end apart: 32, of which 15 were waited for; matrix products, arithmetic and copies ran while one was open for 0% of the time, Pallas kernels for 29%

profile of v8, /device:TPU:0, one launch (start us, length us, event | category | flops | bytes accessed | tf_op | source)
XLA Modules:
  0.0 108.1 jit_solution(298925806910949638)
XLA Ops:
  0.7 2.6 %shard_map.271 = (bf16[144,512]{1,0:T(8,128)(2,1)S(1)}, f32[3,1,64]{2,1,0:T(1,128)S(1)}, bf16[1536,512]{1,0:T(8,128)(2,1)S(1)}, bf16[1536,512]{1,0:T(8,128)(2,1)S(1)}) custom-call(s32[3]{0:T(128)S(1)} %pad_add_fusion.where_ref, bf16[64,512]{1,0:T(8,128)(2,1)} %bitcast.35, bf16[64,512]{1,0:T(8,128)(2,1)} %bitcast.36, f32[1,64]{1,0:T(1,128)} %bitcast.37, ...), custom_call_target="tpu_custom_call" | custom-call | tf_op jit(solution)/shard_map/pallas_call | solution.py:609
  3.4 3.0 %collective-permute-start.1 = (bf16[144,512]{1,0:T(8,128)(2,1)S(1)}, bf16[144,512]{1,0:T(8,128)(2,1)S(1)}, u32[]{:S(2)}, u32[]{:S(2)}) collective-permute-start(bf16[144,512]{1,0:T(8,128)(2,1)S(1)} %get-tuple-element.83.a0.refs_8_.refs_11_.a_ref), channel_id=1, source_target_pairs={{0,2},{1,3},{2,0},{3,1},{4,6},{5,7},{6,4},{7,5},{8,10},{9,11},{10,... | collective-permute-start | bytes 442376 | tf_op jit(solution)/shard_map/ppermute | solution.py:631
  6.4 1.2 %shard_map.272 = (bf16[384,512]{1,0:T(8,128)(2,1)S(1)}, bf16[512,512]{1,0:T(8,128)(2,1)S(1)}) custom-call(bf16[64,512]{1,0:T(8,128)(2,1)} %out_real, bf16[64,512]{1,0:T(8,128)(2,1)} %out_imag.1, bf16[512,256]{1,0:T(8,128)(2,1)} %up.1, bf16[512,256]{1,0:T(8,128)(2,1)} %gate.1, bf16[256,512]{1,0:T(8,128)(2,1)} %down.1), custom_call_target="tpu_custom_call" | custom-call | tf_op jit(solution)/shard_map/pallas_call | solution.py:609
  7.6 2.9 %shard_map.273 = (bf16[1536,512]{1,0:T(8,128)(2,1)S(1)}, f32[1536,512]{1,0:T(8,128)S(1)}, f32[1536,128]{1,0:T(8,128)S(1)}, bf16[1536,512]{1,0:T(8,128)(2,1)S(1)}) custom-call(s32[3]{0:T(128)S(1)} %pad_add_fusion.where_ref, bf16[1536,512]{1,0:T(8,128)(2,1)S(1)} %get-tuple-element.81.tok, bf16[1536,512]{1,0:T(8,128)(2,1)S(1)} %get-tuple-element.86.cot, ...), custom_call_target="tpu_custom_call" | custom-call | tf_op jit(solution)/shard_map/pallas_call | solution.py:609
  10.5 1.4 %collective-permute-start.7 = (bf16[384,512]{1,0:T(8,128)(2,1)S(1)}, bf16[384,512]{1,0:T(8,128)(2,1)S(1)}, u32[]{:S(2)}, u32[]{:S(2)}) collective-permute-start(bf16[384,512]{1,0:T(8,128)(2,1)S(1)} %get-tuple-element.97.b0.refs_15_), channel_id=1, source_target_pairs={{0,2},{1,3},{2,0},{3,1},{4,6},{5,7},{6,4},{7,5},{8,10},{9,11},{10,... | collective-permute-start | bytes 1179656 | tf_op jit(solution)/shard_map/ppermute | solution.py:631
  12.5 0.6 collective-permute-start.10
  13.6 2.3 %shard_map.274 = (f32[1536,512]{1,0:T(8,128)S(1)}, f32[12,512]{1,0:T(8,128)S(1)}, f32[8,512]{1,0:T(8,128)S(1)}) custom-call(s32[3]{0:T(128)S(1)} %pad_add_fusion.where_ref, bf16[1536,512]{1,0:T(8,128)(2,1)S(1)} %get-tuple-element.87.low_all.refs_4_, bf16[144,512]{1,0:T(8,128)(2,1)S(1)} %get-tuple-element.83.a0.refs_8_.refs_11_.a_ref, ...), custom_call_target="tpu_custom_call" | custom-call | tf_op jit(solution)/shard_map/pallas_call | solution.py:609
  15.8 1.6 %collective-permute-start.3 = (f32[12,512]{1,0:T(8,128)S(1)}, f32[12,512]{1,0:T(8,128)S(1)}, u32[]{:S(2)}, u32[]{:S(2)}) collective-permute-start(f32[12,512]{1,0:T(8,128)S(1)} %get-tuple-element.89.mine_ref), channel_id=1, source_target_pairs={{0,4},{4,0},{8,12},{12,8},{16,20},{20,16},{24,28},{28,24},{1,5},{5... | collective-permute-start | bytes 73736 | tf_op jit(solution)/shard_map/ppermute | solution.py:644
  17.4 2.1 %shard_map.275.refs_4_ = f32[1536,512]{1,0:T(8,128)S(1)} custom-call(f32[1536,512]{1,0:T(8,128)S(1)} %get-tuple-element.90.drive_all, bf16[144,512]{1,0:T(8,128)(2,1)S(1)} %get-tuple-element.83.a0.refs_8_.refs_11_.a_ref, bf16[144,512]{1,0:T(8,128)(2,1)S(1)} %collective-permute-done.a1.refs_9_.refs_12_, ...), custom_call_target="tpu_custom_call" | custom-call | tf_op jit(solution)/shard_map/pallas_call | solution.py:609
  19.8 0.6 shard_map.276.mine_ref
  20.4 3.5 %collective-permute-start.4 = (f32[12,512]{1,0:T(8,128)S(1)}, f32[12,512]{1,0:T(8,128)S(1)}, u32[]{:S(2)}, u32[]{:S(2)}) collective-permute-start(f32[12,512]{1,0:T(8,128)S(1)} %shard_map.276.mine_ref), channel_id=1, source_target_pairs={{0,8},{4,12},{8,16},{12,20},{16,24},{20,28},{1,9},{5,13},{9,17},{1... | collective-permute-start | bytes 73736 | tf_op jit(solution)/shard_map/ppermute | solution.py:648
  24.0 1.5 %collective-permute-done.4.other_ref.refs_0_ = f32[12,512]{1,0:T(8,128)S(1)} collective-permute-done((f32[12,512]{1,0:T(8,128)S(1)}, f32[12,512]{1,0:T(8,128)S(1)}, u32[]{:S(2)}, u32[]{:S(2)}) %collective-permute-start.4) | collective-permute-done | bytes 24608 | tf_op jit(solution)/shard_map/ppermute | solution.py:648
  25.5 5.2 %collective-permute-start.5 = (f32[12,512]{1,0:T(8,128)S(1)}, f32[12,512]{1,0:T(8,128)S(1)}, u32[]{:S(2)}, u32[]{:S(2)}) collective-permute-start(f32[12,512]{1,0:T(8,128)S(1)} %shard_map.277), channel_id=1, source_target_pairs={{0,16},{4,20},{8,24},{12,28},{1,17},{5,21},{9,25},{13,29},{2,18},{... | collective-permute-start | bytes 73736 | tf_op jit(solution)/shard_map/ppermute | solution.py:648
  31.0 3.0 %shard_map.278.refs_6_ = bf16[1536,1024]{1,0:T(8,128)(2,1)S(1)} custom-call(s32[3]{0:T(128)S(1)} %pad_add_fusion.where_ref, bf16[1536,512]{1,0:T(8,128)(2,1)S(1)} %get-tuple-element.95.cotm_all.refs_7_, bf16[384,512]{1,0:T(8,128)(2,1)S(1)} %get-tuple-element.97.b0.refs_15_, bf16[384,512]{1,0:T(8,128)(2,1)S(1)} %collective-permute-done.6.b1.refs_16_, ...), custom_call_target="tpu_custom_call" | custom-call | tf_op jit(solution)/shard_map/pallas_call | solution.py:609
  34.4 1.6 %collective-permute-done.11.refs_22_ = bf16[512,512]{1,0:T(8,128)(2,1)S(1)} collective-permute-done((bf16[512,512]{1,0:T(8,128)(2,1)S(1)}, bf16[512,512]{1,0:T(8,128)(2,1)S(1)}, u32[]{:S(2)}, u32[]{:S(2)}) %collective-permute-start.11) | collective-permute-done | bytes 524320 | tf_op jit(solution)/shard_map/ppermute | solution.py:627
  36.1 16.0 %shard_map.279 = (bf16[1536,512]{1,0:T(8,128)(2,1)S(1)}, f32[1536,512]{1,0:T(8,128)S(1)}, f32[12,512]{1,0:T(8,128)S(1)}, bf16[1536,512]{1,0:T(8,128)(2,1)S(1)}, ...) custom-call(s32[3]{0:T(128)S(1)} %pad_add_fusion.where_ref, ...), custom_call_target="tpu_custom_call" | custom-call | tf_op jit(solution)/shard_map/pallas_call | solution.py:609
  52.4 1.5 %collective-permute-start.12 = (f32[12,512]{1,0:T(8,128)S(1)}, f32[12,512]{1,0:T(8,128)S(1)}, u32[]{:S(2)}, u32[]{:S(2)}) collective-permute-start(f32[12,512]{1,0:T(8,128)S(1)} %get-tuple-element.102.mine_ref), channel_id=1, source_target_pairs={{0,4},{4,0},{8,12},{12,8},{16,20},{20,16},{24,28},{28,24},{1,5},{5... | collective-permute-start | bytes 73736 | tf_op jit(solution)/shard_map/ppermute | solution.py:644
  53.9 0.7 collective-permute-done.13.other_ref
  54.6 0.7 shard_map.280
  55.3 1.0 collective-permute-done.12.other_ref.refs_2_
  56.3 1.5 %collective-permute-start.16 = (bf16[448,512]{1,0:T(8,128)(2,1)S(1)}, bf16[448,512]{1,0:T(8,128)(2,1)S(1)}, u32[]{:S(2)}, u32[]{:S(2)}) collective-permute-start(bf16[448,512]{1,0:T(8,128)(2,1)S(1)} %get-tuple-element.113), channel_id=1, source_target_pairs={{0,4},{4,0},{8,12},{12,8},{16,20},{20,16},{24,28},{28,24},{1,5},{5... | collective-permute-start | bytes 1376264 | tf_op jit(solution)/shard_map/ppermute | solution.py:644
  57.8 0.6 shard_map.281.mine_ref
  58.4 1.3 %collective-permute-start.14 = (f32[12,512]{1,0:T(8,128)S(1)}, f32[12,512]{1,0:T(8,128)S(1)}, u32[]{:S(2)}, u32[]{:S(2)}) collective-permute-start(f32[12,512]{1,0:T(8,128)S(1)} %shard_map.281.mine_ref), channel_id=1, source_target_pairs={{8,0},{12,4},{16,8},{20,12},{24,16},{28,20},{9,1},{13,5},{17,9},{2... | collective-permute-start | bytes 73736 | tf_op jit(solution)/shard_map/ppermute | solution.py:648
  59.7 2.1 %shard_map.282.refs_8_ = f32[1536,512]{1,0:T(8,128)S(1)} custom-call(f32[1536,512]{1,0:T(8,128)S(1)} %get-tuple-element.108.drive_all, bf16[144,512]{1,0:T(8,128)(2,1)S(1)} %get-tuple-element.83.a0.refs_8_.refs_11_.a_ref, bf16[144,512]{1,0:T(8,128)(2,1)S(1)} %collective-permute-done.a1.refs_9_.refs_12_, ...), custom_call_target="tpu_custom_call" | custom-call | tf_op jit(solution)/shard_map/pallas_call | solution.py:609
  61.8 2.4 %collective-permute-done.14.other_ref.refs_0_ = f32[12,512]{1,0:T(8,128)S(1)} collective-permute-done((f32[12,512]{1,0:T(8,128)S(1)}, f32[12,512]{1,0:T(8,128)S(1)}, u32[]{:S(2)}, u32[]{:S(2)}) %collective-permute-start.14) | collective-permute-done | bytes 24608 | tf_op jit(solution)/shard_map/ppermute | solution.py:648
  64.2 1.5 %collective-permute-start.15 = (f32[12,512]{1,0:T(8,128)S(1)}, f32[12,512]{1,0:T(8,128)S(1)}, u32[]{:S(2)}, u32[]{:S(2)}) collective-permute-start(f32[12,512]{1,0:T(8,128)S(1)} %shard_map.283), channel_id=1, source_target_pairs={{16,0},{20,4},{24,8},{28,12},{17,1},{21,5},{25,9},{29,13},{18,2},{... | collective-permute-start | bytes 73736 | tf_op jit(solution)/shard_map/ppermute | solution.py:648
  65.7 2.8 %shard_map.284.own_ref = bf16[1536,512]{1,0:T(8,128)(2,1)S(1)} custom-call(s32[3]{0:T(128)S(1)} %pad_add_fusion.where_ref, s32[24]{0:T(128)S(1)} %copy-done.3, bf16[1536,512]{1,0:T(8,128)(2,1)S(1)} %get-tuple-element.81.tok, bf16[1536,1024]{1,0:T(8,128)(2,1)S(1)} %get-tuple-element.110.hid_all, bf16[384,512]{1,0:T(8,128)(2,1)S(1)} %get-tuple-element.97.b0.refs_15_, ...), custom_call_target="tpu_custom_call" | custom-call | tf_op jit(solution)/shard_map/pallas_call | solution.py:609
  68.5 2.5 %collective-permute-done.15.refs_1_ = f32[12,512]{1,0:T(8,128)S(1)} collective-permute-done((f32[12,512]{1,0:T(8,128)S(1)}, f32[12,512]{1,0:T(8,128)S(1)}, u32[]{:S(2)}, u32[]{:S(2)}) %collective-permute-start.15) | collective-permute-done | bytes 24608 | tf_op jit(solution)/shard_map/ppermute | solution.py:648
  70.9 0.7 shard_map.285
  71.6 1.6 %collective-permute-start.18 = (bf16[112,512]{1,0:T(8,128)(2,1)S(1)}, bf16[112,512]{1,0:T(8,128)(2,1)S(1)}, u32[]{:S(2)}, u32[]{:S(2)}) collective-permute-start(bf16[112,512]{1,0:T(8,128)(2,1)S(1)} %get-tuple-element.121), channel_id=1, source_target_pairs={{0,8},{4,12},{8,0},{12,4},{16,24},{20,28},{24,16},{28,20},{1,9},{5... | collective-permute-start | bytes 344072 | tf_op jit(solution)/shard_map/ppermute | solution.py:644
  73.2 1.1 %collective-permute-start.19 = (bf16[112,512]{1,0:T(8,128)(2,1)S(1)}, bf16[112,512]{1,0:T(8,128)(2,1)S(1)}, u32[]{:S(2)}, u32[]{:S(2)}) collective-permute-start(bf16[112,512]{1,0:T(8,128)(2,1)S(1)} %get-tuple-element.122), channel_id=1, source_target_pairs={{0,16},{4,20},{8,24},{12,28},{16,0},{20,4},{24,8},{28,12},{1,17},{... | collective-permute-start | bytes 344072 | tf_op jit(solution)/shard_map/ppermute | solution.py:644
  74.3 1.7 %collective-permute-start.20 = (bf16[112,512]{1,0:T(8,128)(2,1)S(1)}, bf16[112,512]{1,0:T(8,128)(2,1)S(1)}, u32[]{:S(2)}, u32[]{:S(2)}) collective-permute-start(bf16[112,512]{1,0:T(8,128)(2,1)S(1)} %get-tuple-element.123), channel_id=1, source_target_pairs={{0,24},{4,28},{8,16},{12,20},{16,8},{20,12},{24,0},{28,4},{1,25},{... | collective-permute-start | bytes 344072 | tf_op jit(solution)/shard_map/ppermute | solution.py:644
  76.0 5.4 %shard_map.286 = (bf16[1536,512]{1,0:T(8,128)(2,1)S(1)}, bf16[144,512]{1,0:T(8,128)(2,1)S(1)}, bf16[144,512]{1,0:T(8,128)(2,1)S(1)}) custom-call(s32[3]{0:T(128)S(1)} %pad_add_fusion.where_ref, f32[12,512]{1,0:T(8,128)S(1)} %collective-permute-done.14.other_ref.refs_0_, f32[12,512]{1,0:T(8,128)S(1)} %collective-permute-done.15.refs_1_, ...), custom_call_target="tpu_custom_call" | custom-call | tf_op jit(solution)/shard_map/pallas_call | solution.py:609
  81.6 0.6 collective-permute-done.19
  82.2 0.7 collective-permute-done.17
  84.0 1.6 %collective-permute-start.27 = (bf16[112,512]{1,0:T(8,128)(2,1)S(1)}, bf16[112,512]{1,0:T(8,128)(2,1)S(1)}, u32[]{:S(2)}, u32[]{:S(2)}) collective-permute-start(bf16[112,512]{1,0:T(8,128)(2,1)S(1)} %add_convert_fusion.3.refs_0_), channel_id=1, source_target_pairs={{0,16},{4,20},{8,24},{12,28},{16,0},{20,4},{24,8},{28,12},{1,17},{... | collective-permute-start | bytes 344072 | tf_op jit(solution)/shard_map/ppermute | solution.py:644
  85.6 1.1 %collective-permute-start.26 = (bf16[112,512]{1,0:T(8,128)(2,1)S(1)}, bf16[112,512]{1,0:T(8,128)(2,1)S(1)}, u32[]{:S(2)}, u32[]{:S(2)}) collective-permute-start(bf16[112,512]{1,0:T(8,128)(2,1)S(1)} %add_convert_fusion.3.refs_0_), channel_id=1, source_target_pairs={{0,8},{4,12},{8,0},{12,4},{16,24},{20,28},{24,16},{28,20},{1,9},{5... | collective-permute-start | bytes 344072 | tf_op jit(solution)/shard_map/ppermute | solution.py:644
  86.7 2.2 %shard_map.287 = bf16[3072,512]{1,0:T(8,128)(2,1)} custom-call(s32[3]{0:T(128)S(1)} %pad_add_fusion.where_ref, bf16[1536,512]{1,0:T(8,128)(2,1)S(1)} %shard_map.284.own_ref, bf16[1536,512]{1,0:T(8,128)(2,1)S(1)} %collective-permute-done.21.other_ref), custom_call_target="tpu_custom_call" | custom-call | tf_op jit(solution)/shard_map/pallas_call | solution.py:609
  89.5 1.1 %collective-permute-start.24 = (bf16[144,512]{1,0:T(8,128)(2,1)S(1)}, bf16[144,512]{1,0:T(8,128)(2,1)S(1)}, u32[]{:S(2)}, u32[]{:S(2)}) collective-permute-start(bf16[144,512]{1,0:T(8,128)(2,1)S(1)} %add_convert_fusion.1), channel_id=1, source_target_pairs={{0,8},{4,12},{8,0},{12,4},{16,24},{20,28},{24,16},{28,20},{1,9},{5... | collective-permute-start | bytes 442376 | tf_op jit(solution)/shard_map/ppermute | solution.py:644
  90.6 1.9 %collective-permute-start.28 = (bf16[112,512]{1,0:T(8,128)(2,1)S(1)}, bf16[112,512]{1,0:T(8,128)(2,1)S(1)}, u32[]{:S(2)}, u32[]{:S(2)}) collective-permute-start(bf16[112,512]{1,0:T(8,128)(2,1)S(1)} %add_convert_fusion.3.refs_0_), channel_id=1, source_target_pairs={{0,24},{4,28},{8,16},{12,20},{16,8},{20,12},{24,0},{28,4},{1,25},{... | collective-permute-start | bytes 344072 | tf_op jit(solution)/shard_map/ppermute | solution.py:644
  92.5 1.4 %collective-permute-start.25 = (bf16[112,512]{1,0:T(8,128)(2,1)S(1)}, bf16[112,512]{1,0:T(8,128)(2,1)S(1)}, u32[]{:S(2)}, u32[]{:S(2)}) collective-permute-start(bf16[112,512]{1,0:T(8,128)(2,1)S(1)} %add_convert_fusion.3.refs_0_), channel_id=1, source_target_pairs={{0,4},{4,0},{8,12},{12,8},{16,20},{20,16},{24,28},{28,24},{1,5},{5... | collective-permute-start | bytes 344072 | tf_op jit(solution)/shard_map/ppermute | solution.py:644
  93.9 0.7 collective-permute-start.31
  94.6 3.9 %collective-permute-done.25.refs_4_ = bf16[112,512]{1,0:T(8,128)(2,1)S(1)} collective-permute-done((bf16[112,512]{1,0:T(8,128)(2,1)S(1)}, bf16[112,512]{1,0:T(8,128)(2,1)S(1)}, u32[]{:S(2)}, u32[]{:S(2)}) %collective-permute-start.25) | collective-permute-done | bytes 114720 | tf_op jit(solution)/shard_map/ppermute | solution.py:644
  98.6 0.6 collective-permute-start.29
  99.2 1.1 collective-permute-start.30
  100.3 3.6 %shard_map.288 = f32[3072,512]{1,0:T(8,128)} custom-call(s32[3]{0:T(128)S(1)} %pad_add_fusion.where_ref, bf16[1536,512]{1,0:T(8,128)(2,1)S(1)} %get-tuple-element.127.own_ref, bf16[1536,512]{1,0:T(8,128)(2,1)S(1)} %collective-permute-done.22.other_ref), custom_call_target="tpu_custom_call" | custom-call | tf_op jit(solution)/shard_map/pallas_call | solution.py:609
  104.4 1.9 %shard_map.289 = (f32[64,512]{1,0:T(8,128)}, f32[64,512]{1,0:T(8,128)}, f32[512,256]{1,0:T(8,128)}, f32[512,256]{1,0:T(8,128)}, f32[256,512]{1,0:T(8,128)}) custom-call(s32[3]{0:T(128)S(1)} %pad_add_fusion.where_ref, bf16[112,512]{1,0:T(8,128)(2,1)S(1)} %add_convert_fusion.3.refs_0_, bf16[112,512]{1,0:T(8,128)(2,1)S(1)} %collective-permute-done.26.refs_1_, ...), custom_call_target="tpu_custom_call" | custom-call | tf_op jit(solution)/shard_map/pallas_call | solution.py:609
  106.5 1.5 %shard_map.290 = (f32[1,512]{1,0:T(1,128)}, f32[1,512]{1,0:T(1,128)}, f32[1,512]{1,0:T(1,128)}, f32[64,512]{1,0:T(8,128)}, f32[64,512]{1,0:T(8,128)}, /*index=5*...) custom-call(s32[3]{0:T(128)S(1)} %pad_add_fusion.where_ref, bf16[144,512]{1,0:T(8,128)(2,1)S(1)} %add_convert_fusion.mine_ref, ...), custom_call_target="tpu_custom_call" | custom-call | tf_op jit(solution)/shard_map/pallas_call | solution.py:609
  (50 shorter events, 5.0 us)
Async XLA Ops:
  3.4 7.2 %collective-permute-start.1 = (bf16[144,512]{1,0:T(8,128)(2,1)S(1)}, bf16[144,512]{1,0:T(8,128)(2,1)S(1)}, u32[]{:S(2)}, u32[]{:S(2)}) collective-permute-start(bf16[144,512]{1,0:T(8,128)(2,1)S(1)} %get-tuple-element.83.a0.refs_8_.refs_11_.a_ref), channel_id=1, source_target_pairs={{0,2},{1,3},{2,0},{3,1},{4,6},{5,7},{6,4},{7,5},{8,10},{9,11},{10,... | collective-permute-start | bytes 442376 | tf_op jit(solution)/shard_map/ppermute | solution.py:631
  10.5 14.9 %collective-permute-start.7 = (bf16[384,512]{1,0:T(8,128)(2,1)S(1)}, bf16[384,512]{1,0:T(8,128)(2,1)S(1)}, u32[]{:S(2)}, u32[]{:S(2)}) collective-permute-start(bf16[384,512]{1,0:T(8,128)(2,1)S(1)} %get-tuple-element.97.b0.refs_15_), channel_id=1, source_target_pairs={{0,2},{1,3},{2,0},{3,1},{4,6},{5,7},{6,4},{7,5},{8,10},{9,11},{10,... | collective-permute-start | bytes 1179656 | tf_op jit(solution)/shard_map/ppermute | solution.py:631
  12.0 1.4 %collective-permute-start = (bf16[144,512]{1,0:T(8,128)(2,1)S(1)}, bf16[144,512]{1,0:T(8,128)(2,1)S(1)}, u32[]{:S(2)}, u32[]{:S(2)}) collective-permute-start(bf16[144,512]{1,0:T(8,128)(2,1)S(1)} %get-tuple-element.83.a0.refs_8_.refs_11_.a_ref), channel_id=1, source_target_pairs={{0,1},{1,0},{2,3},{3,2},{4,5},{5,4},{6,7},{7,6},{8,9},{9,8},{10,11... | collective-permute-start | bytes 442376 | tf_op jit(solution)/shard_map/ppermute | solution.py:627
  12.0 1.6 %collective-permute-start.2 = (bf16[144,512]{1,0:T(8,128)(2,1)S(1)}, bf16[144,512]{1,0:T(8,128)(2,1)S(1)}, u32[]{:S(2)}, u32[]{:S(2)}) collective-permute-start(bf16[144,512]{1,0:T(8,128)(2,1)S(1)} %collective-permute-done.1.a2.refs_10_.refs_13_), channel_id=1, source_target_pairs={{0,1},{1,0},{2,3},{3,2},{4,5},{5,4},{6,7},{7,6},{8,9},{9,8},{10,11... | collective-permute-start | bytes 442376 | tf_op jit(solution)/shard_map/ppermute | solution.py:627
  12.5 21.6 %collective-permute-start.10 = (bf16[512,512]{1,0:T(8,128)(2,1)S(1)}, bf16[512,512]{1,0:T(8,128)(2,1)S(1)}, u32[]{:S(2)}, u32[]{:S(2)}) collective-permute-start(bf16[512,512]{1,0:T(8,128)(2,1)S(1)} %get-tuple-element.99.refs_19_), channel_id=1, source_target_pairs={{0,2},{1,3},{2,0},{3,1},{4,6},{5,7},{6,4},{7,5},{8,10},{9,11},{10,... | collective-permute-start | bytes 1572872 | tf_op jit(solution)/shard_map/ppermute | solution.py:631
  15.8 4.0 %collective-permute-start.3 = (f32[12,512]{1,0:T(8,128)S(1)}, f32[12,512]{1,0:T(8,128)S(1)}, u32[]{:S(2)}, u32[]{:S(2)}) collective-permute-start(f32[12,512]{1,0:T(8,128)S(1)} %get-tuple-element.89.mine_ref), channel_id=1, source_target_pairs={{0,4},{4,0},{8,12},{12,8},{16,20},{20,16},{24,28},{28,24},{1,5},{5... | collective-permute-start | bytes 73736 | tf_op jit(solution)/shard_map/ppermute | solution.py:644
  20.4 5.1 %collective-permute-start.4 = (f32[12,512]{1,0:T(8,128)S(1)}, f32[12,512]{1,0:T(8,128)S(1)}, u32[]{:S(2)}, u32[]{:S(2)}) collective-permute-start(f32[12,512]{1,0:T(8,128)S(1)} %shard_map.276.mine_ref), channel_id=1, source_target_pairs={{0,8},{4,12},{8,16},{12,20},{16,24},{20,28},{1,9},{5,13},{9,17},{1... | collective-permute-start | bytes 73736 | tf_op jit(solution)/shard_map/ppermute | solution.py:648
  23.9 7.1 %collective-permute-start.6 = (bf16[384,512]{1,0:T(8,128)(2,1)S(1)}, bf16[384,512]{1,0:T(8,128)(2,1)S(1)}, u32[]{:S(2)}, u32[]{:S(2)}) collective-permute-start(bf16[384,512]{1,0:T(8,128)(2,1)S(1)} %get-tuple-element.97.b0.refs_15_), channel_id=1, source_target_pairs={{0,1},{1,0},{2,3},{3,2},{4,5},{5,4},{6,7},{7,6},{8,9},{9,8},{10,11... | collective-permute-start | bytes 1179656 | tf_op jit(solution)/shard_map/ppermute | solution.py:627
  25.5 5.6 %collective-permute-start.8 = (bf16[384,512]{1,0:T(8,128)(2,1)S(1)}, bf16[384,512]{1,0:T(8,128)(2,1)S(1)}, u32[]{:S(2)}, u32[]{:S(2)}) collective-permute-start(bf16[384,512]{1,0:T(8,128)(2,1)S(1)} %collective-permute-done.7.b2.refs_17_), channel_id=1, source_target_pairs={{0,1},{1,0},{2,3},{3,2},{4,5},{5,4},{6,7},{7,6},{8,9},{9,8},{10,11... | collective-permute-start | bytes 1179656 | tf_op jit(solution)/shard_map/ppermute | solution.py:627
  25.5 8.6 %collective-permute-start.5 = (f32[12,512]{1,0:T(8,128)S(1)}, f32[12,512]{1,0:T(8,128)S(1)}, u32[]{:S(2)}, u32[]{:S(2)}) collective-permute-start(f32[12,512]{1,0:T(8,128)S(1)} %shard_map.277), channel_id=1, source_target_pairs={{0,16},{4,20},{8,24},{12,28},{1,17},{5,21},{9,25},{13,29},{2,18},{... | collective-permute-start | bytes 73736 | tf_op jit(solution)/shard_map/ppermute | solution.py:648
  30.7 3.7 %collective-permute-start.9 = (bf16[512,512]{1,0:T(8,128)(2,1)S(1)}, bf16[512,512]{1,0:T(8,128)(2,1)S(1)}, u32[]{:S(2)}, u32[]{:S(2)}) collective-permute-start(bf16[512,512]{1,0:T(8,128)(2,1)S(1)} %get-tuple-element.99.refs_19_), channel_id=1, source_target_pairs={{0,1},{1,0},{2,3},{3,2},{4,5},{5,4},{6,7},{7,6},{8,9},{9,8},{10,11... | collective-permute-start | bytes 1572872 | tf_op jit(solution)/shard_map/ppermute | solution.py:627
  31.0 5.1 %copy-start = (f32[512]{0:T(512)S(1)}, f32[512]{0:T(512)}, u32[]{:S(2)}) copy-start(f32[512]{0:T(512)} %param.18) | copy-start | bytes 6148
  31.0 5.1 %copy-start.1 = (f32[512]{0:T(512)S(1)}, f32[512]{0:T(512)}, u32[]{:S(2)}) copy-start(f32[512]{0:T(512)} %param.19) | copy-start | bytes 6148
  31.0 5.1 %copy-start.2 = (f32[512]{0:T(512)S(1)}, f32[512]{0:T(512)}, u32[]{:S(2)}) copy-start(f32[512]{0:T(512)} %param.20) | copy-start | bytes 6148
  34.1 2.0 %collective-permute-start.11 = (bf16[512,512]{1,0:T(8,128)(2,1)S(1)}, bf16[512,512]{1,0:T(8,128)(2,1)S(1)}, u32[]{:S(2)}, u32[]{:S(2)}) collective-permute-start(bf16[512,512]{1,0:T(8,128)(2,1)S(1)} %collective-permute-done.10.refs_21_), channel_id=1, source_target_pairs={{0,1},{1,0},{2,3},{3,2},{4,5},{5,4},{6,7},{7,6},{8,9},{9,8},{10,11... | collective-permute-start | bytes 1572872 | tf_op jit(solution)/shard_map/ppermute | solution.py:627
  52.1 2.5 %collective-permute-start.13 = (bf16[896,512]{1,0:T(8,128)(2,1)S(1)}, bf16[896,512]{1,0:T(8,128)(2,1)S(1)}, u32[]{:S(2)}, u32[]{:S(2)}) collective-permute-start(bf16[896,512]{1,0:T(8,128)(2,1)S(1)} %get-tuple-element.104), channel_id=1, source_target_pairs={{0,1},{1,0},{2,3},{3,2},{4,5},{5,4},{6,7},{7,6},{8,9},{9,8},{10,11... | collective-permute-start | bytes 2752520 | tf_op jit(solution)/shard_map/ppermute | solution.py:627
  52.4 3.9 %collective-permute-start.12 = (f32[12,512]{1,0:T(8,128)S(1)}, f32[12,512]{1,0:T(8,128)S(1)}, u32[]{:S(2)}, u32[]{:S(2)}) collective-permute-start(f32[12,512]{1,0:T(8,128)S(1)} %get-tuple-element.102.mine_ref), channel_id=1, source_target_pairs={{0,4},{4,0},{8,12},{12,8},{16,20},{20,16},{24,28},{28,24},{1,5},{5... | collective-permute-start | bytes 73736 | tf_op jit(solution)/shard_map/ppermute | solution.py:644
  56.3 14.6 %collective-permute-start.16 = (bf16[448,512]{1,0:T(8,128)(2,1)S(1)}, bf16[448,512]{1,0:T(8,128)(2,1)S(1)}, u32[]{:S(2)}, u32[]{:S(2)}) collective-permute-start(bf16[448,512]{1,0:T(8,128)(2,1)S(1)} %get-tuple-element.113), channel_id=1, source_target_pairs={{0,4},{4,0},{8,12},{12,8},{16,20},{20,16},{24,28},{28,24},{1,5},{5... | collective-permute-start | bytes 1376264 | tf_op jit(solution)/shard_map/ppermute | solution.py:644
  58.4 5.8 %collective-permute-start.14 = (f32[12,512]{1,0:T(8,128)S(1)}, f32[12,512]{1,0:T(8,128)S(1)}, u32[]{:S(2)}, u32[]{:S(2)}) collective-permute-start(f32[12,512]{1,0:T(8,128)S(1)} %shard_map.281.mine_ref), channel_id=1, source_target_pairs={{8,0},{12,4},{16,8},{20,12},{24,16},{28,20},{9,1},{13,5},{17,9},{2... | collective-permute-start | bytes 73736 | tf_op jit(solution)/shard_map/ppermute | solution.py:648
  59.7 6.0 %copy-start.3 = (s32[24]{0:T(128)S(1)}, s32[24]{0:T(128)}, u32[]{:S(2)}) copy-start(s32[24]{0:T(128)} %lens_ref.1) | copy-start | bytes 292
  64.2 6.7 %collective-permute-start.15 = (f32[12,512]{1,0:T(8,128)S(1)}, f32[12,512]{1,0:T(8,128)S(1)}, u32[]{:S(2)}, u32[]{:S(2)}) collective-permute-start(f32[12,512]{1,0:T(8,128)S(1)} %shard_map.283), channel_id=1, source_target_pairs={{16,0},{20,4},{24,8},{28,12},{17,1},{21,5},{25,9},{29,13},{18,2},{... | collective-permute-start | bytes 73736 | tf_op jit(solution)/shard_map/ppermute | solution.py:648
  71.6 10.0 %collective-permute-start.18 = (bf16[112,512]{1,0:T(8,128)(2,1)S(1)}, bf16[112,512]{1,0:T(8,128)(2,1)S(1)}, u32[]{:S(2)}, u32[]{:S(2)}) collective-permute-start(bf16[112,512]{1,0:T(8,128)(2,1)S(1)} %get-tuple-element.121), channel_id=1, source_target_pairs={{0,8},{4,12},{8,0},{12,4},{16,24},{20,28},{24,16},{28,20},{1,9},{5... | collective-permute-start | bytes 344072 | tf_op jit(solution)/shard_map/ppermute | solution.py:644
  73.2 8.9 %collective-permute-start.19 = (bf16[112,512]{1,0:T(8,128)(2,1)S(1)}, bf16[112,512]{1,0:T(8,128)(2,1)S(1)}, u32[]{:S(2)}, u32[]{:S(2)}) collective-permute-start(bf16[112,512]{1,0:T(8,128)(2,1)S(1)} %get-tuple-element.122), channel_id=1, source_target_pairs={{0,16},{4,20},{8,24},{12,28},{16,0},{20,4},{24,8},{28,12},{1,17},{... | collective-permute-start | bytes 344072 | tf_op jit(solution)/shard_map/ppermute | solution.py:644
  74.3 7.8 %collective-permute-start.20 = (bf16[112,512]{1,0:T(8,128)(2,1)S(1)}, bf16[112,512]{1,0:T(8,128)(2,1)S(1)}, u32[]{:S(2)}, u32[]{:S(2)}) collective-permute-start(bf16[112,512]{1,0:T(8,128)(2,1)S(1)} %get-tuple-element.123), channel_id=1, source_target_pairs={{0,24},{4,28},{8,16},{12,20},{16,8},{20,12},{24,0},{28,4},{1,25},{... | collective-permute-start | bytes 344072 | tf_op jit(solution)/shard_map/ppermute | solution.py:644
  81.5 1.4 %collective-permute-start.17 = (bf16[144,512]{1,0:T(8,128)(2,1)S(1)}, bf16[144,512]{1,0:T(8,128)(2,1)S(1)}, u32[]{:S(2)}, u32[]{:S(2)}) collective-permute-start(bf16[144,512]{1,0:T(8,128)(2,1)S(1)} %get-tuple-element.120), channel_id=1, source_target_pairs={{0,1},{1,0},{2,3},{3,2},{4,5},{5,4},{6,7},{7,6},{8,9},{9,8},{10,11... | collective-permute-start | bytes 442376 | tf_op jit(solution)/shard_map/ppermute | solution.py:627
  82.9 3.8 %collective-permute-start.21 = (bf16[1536,512]{1,0:T(8,128)(2,1)S(1)}, bf16[1536,512]{1,0:T(8,128)(2,1)S(1)}, u32[]{:S(2)}, u32[]{:S(2)}) collective-permute-start(bf16[1536,512]{1,0:T(8,128)(2,1)S(1)} %shard_map.284.own_ref), channel_id=1, source_target_pairs={{0,1},{1,0},{2,3},{3,2},{4,5},{5,4},{6,7},{7,6},{8,9},{9,8},{10,11... | collective-permute-start | bytes 4718600 | tf_op jit(solution)/shard_map/ppermute | solution.py:627
  83.2 17.1 %collective-permute-start.22 = (bf16[1536,512]{1,0:T(8,128)(2,1)S(1)}, bf16[1536,512]{1,0:T(8,128)(2,1)S(1)}, u32[]{:S(2)}, u32[]{:S(2)}) collective-permute-start(bf16[1536,512]{1,0:T(8,128)(2,1)S(1)} %get-tuple-element.127.own_ref), channel_id=1, source_target_pairs={{0,1},{1,0},{2,3},{3,2},{4,5},{5,4},{6,7},{7,6},{8,9},{9,8},{10,11... | collective-permute-start | bytes 4718600 | tf_op jit(solution)/shard_map/ppermute | solution.py:627
  83.5 5.9 %collective-permute-start.23 = (bf16[144,512]{1,0:T(8,128)(2,1)S(1)}, bf16[144,512]{1,0:T(8,128)(2,1)S(1)}, u32[]{:S(2)}, u32[]{:S(2)}) collective-permute-start(bf16[144,512]{1,0:T(8,128)(2,1)S(1)} %add_convert_fusion.2), channel_id=1, source_target_pairs={{0,4},{4,0},{8,12},{12,8},{16,20},{20,16},{24,28},{28,24},{1,5},{5... | collective-permute-start | bytes 442376 | tf_op jit(solution)/shard_map/ppermute | solution.py:644
  84.0 8.5 %collective-permute-start.27 = (bf16[112,512]{1,0:T(8,128)(2,1)S(1)}, bf16[112,512]{1,0:T(8,128)(2,1)S(1)}, u32[]{:S(2)}, u32[]{:S(2)}) collective-permute-start(bf16[112,512]{1,0:T(8,128)(2,1)S(1)} %add_convert_fusion.3.refs_0_), channel_id=1, source_target_pairs={{0,16},{4,20},{8,24},{12,28},{16,0},{20,4},{24,8},{28,12},{1,17},{... | collective-permute-start | bytes 344072 | tf_op jit(solution)/shard_map/ppermute | solution.py:644
  85.6 8.3 %collective-permute-start.26 = (bf16[112,512]{1,0:T(8,128)(2,1)S(1)}, bf16[112,512]{1,0:T(8,128)(2,1)S(1)}, u32[]{:S(2)}, u32[]{:S(2)}) collective-permute-start(bf16[112,512]{1,0:T(8,128)(2,1)S(1)} %add_convert_fusion.3.refs_0_), channel_id=1, source_target_pairs={{0,8},{4,12},{8,0},{12,4},{16,24},{20,28},{24,16},{28,20},{1,9},{5... | collective-permute-start | bytes 344072 | tf_op jit(solution)/shard_map/ppermute | solution.py:644
  89.5 9.1 %collective-permute-start.24 = (bf16[144,512]{1,0:T(8,128)(2,1)S(1)}, bf16[144,512]{1,0:T(8,128)(2,1)S(1)}, u32[]{:S(2)}, u32[]{:S(2)}) collective-permute-start(bf16[144,512]{1,0:T(8,128)(2,1)S(1)} %add_convert_fusion.1), channel_id=1, source_target_pairs={{0,8},{4,12},{8,0},{12,4},{16,24},{20,28},{24,16},{28,20},{1,9},{5... | collective-permute-start | bytes 442376 | tf_op jit(solution)/shard_map/ppermute | solution.py:644
  90.6 8.0 %collective-permute-start.28 = (bf16[112,512]{1,0:T(8,128)(2,1)S(1)}, bf16[112,512]{1,0:T(8,128)(2,1)S(1)}, u32[]{:S(2)}, u32[]{:S(2)}) collective-permute-start(bf16[112,512]{1,0:T(8,128)(2,1)S(1)} %add_convert_fusion.3.refs_0_), channel_id=1, source_target_pairs={{0,24},{4,28},{8,16},{12,20},{16,8},{20,12},{24,0},{28,4},{1,25},{... | collective-permute-start | bytes 344072 | tf_op jit(solution)/shard_map/ppermute | solution.py:644
  92.5 6.0 %collective-permute-start.25 = (bf16[112,512]{1,0:T(8,128)(2,1)S(1)}, bf16[112,512]{1,0:T(8,128)(2,1)S(1)}, u32[]{:S(2)}, u32[]{:S(2)}) collective-permute-start(bf16[112,512]{1,0:T(8,128)(2,1)S(1)} %add_convert_fusion.3.refs_0_), channel_id=1, source_target_pairs={{0,4},{4,0},{8,12},{12,8},{16,20},{20,16},{24,28},{28,24},{1,5},{5... | collective-permute-start | bytes 344072 | tf_op jit(solution)/shard_map/ppermute | solution.py:644
  93.9 9.9 %collective-permute-start.31 = (bf16[224,512]{1,0:T(8,128)(2,1)S(1)}, bf16[224,512]{1,0:T(8,128)(2,1)S(1)}, u32[]{:S(2)}, u32[]{:S(2)}) collective-permute-start(bf16[224,512]{1,0:T(8,128)(2,1)S(1)} %pad_maximum_fusion), channel_id=1, source_target_pairs={{0,4},{4,0},{8,12},{12,8},{16,20},{20,16},{24,28},{28,24},{1,5},{5... | collective-permute-start | bytes 688136 | tf_op jit(solution)/shard_map/ppermute | solution.py:644
  98.6 7.9 %collective-permute-start.29 = (bf16[144,512]{1,0:T(8,128)(2,1)S(1)}, bf16[144,512]{1,0:T(8,128)(2,1)S(1)}, u32[]{:S(2)}, u32[]{:S(2)}) collective-permute-start(bf16[144,512]{1,0:T(8,128)(2,1)S(1)} %add_convert_fusion.mine_ref), channel_id=1, source_target_pairs={{0,16},{4,20},{8,24},{12,28},{16,0},{20,4},{24,8},{28,12},{1,17},{... | collective-permute-start | bytes 442376 | tf_op jit(solution)/shard_map/ppermute | solution.py:644
  99.2 5.1 %collective-permute-start.30 = (bf16[112,512]{1,0:T(8,128)(2,1)S(1)}, bf16[112,512]{1,0:T(8,128)(2,1)S(1)}, u32[]{:S(2)}, u32[]{:S(2)}) collective-permute-start(bf16[112,512]{1,0:T(8,128)(2,1)S(1)} %collective-permute-done.28.refs_3_), channel_id=1, source_target_pairs={{0,4},{4,0},{8,12},{12,8},{16,20},{20,16},{24,28},{28,24},{1,5},{5... | collective-permute-start | bytes 344072 | tf_op jit(solution)/shard_map/ppermute | solution.py:644

commit v9 on v8

--- a/solution.py
+++ b/solution.py
@@ -12,7 +12,7 @@
 TENSOR = 4
 TILE = 8
 BLOCK = 256
-LARGE = 512
+LARGE = 768
 PARAM_ROWS = 16
 F32 = jnp.float32
 BF16 = jnp.bfloat16
@@ -817,7 +817,7 @@
             pltpu.VMEM((width, 4 * per_f), F32),
             dma((TENSOR, 3)),
         ],
-        24,
+        30,
     )
     half, part = pack_rows // 2, pack_rows // groups
     keep_b, send_b = call(
@@ -892,7 +892,7 @@
             pltpu.VMEM((1, lanes), F32),
             pltpu.VMEM((TILE, width), F32),
         ],
-        12,
+        16,
     )
 
     mine_b = dealt[0]

time: 108 us -> 108 us (level)
  no operation moved by 1% of the time
where the time goes in v9:
time: 108 us
  Pallas kernels  51.8 us (48%)
  starting transfers between devices  37.2 us (34%)
  waiting for transfers between devices  17.6 us (16%)
  between operations  1.14 us (1%)
    pallas_call x20, Pallas kernels, call(): pl.pallas_call(kernel, in_specs=[pl.BlockSpec(memory_space=pltpu.SMEM)] *...  51.8 us
    ppermute x15, starting transfers between devices, flip_dp(): return lax.ppermute(value, 'dp', [(i, i ^ bits) for i in range(groups)])  18.4 us
    ppermute x4, starting transfers between devices, shift_dp(): lax.ppermute(value, 'dp', [(i, i + by) for i in range(groups) if 0 <= i +...  11.5 us
    ppermute x15, waiting for transfers between devices, flip_dp(): return lax.ppermute(value, 'dp', [(i, i ^ bits) for i in range(groups)])  7.3 us
    ppermute x4, waiting for transfers between devices, shift_dp(): lax.ppermute(value, 'dp', [(i, i + by) for i in range(groups) if 0 <= i +...  6.53 us
    ppermute x3, starting transfers between devices, side_swap(): return lax.ppermute(value, 'tensor', [(t, t ^ 2) for t in range(TENSOR)])  5.12 us
    ppermute x10, waiting for transfers between devices, core_swap(): return lax.ppermute(value, 'tensor', [(t, t ^ 1) for t in range(TENSOR)])  3.77 us
    ppermute x10, starting transfers between devices, core_swap(): return lax.ppermute(value, 'tensor', [(t, t ^ 1) for t in range(TENSOR)])  2.22 us
  transfers between devices with their start and end apart: 32, of which 15 were waited for; matrix products, arithmetic and copies ran while one was open for 0% of the time, Pallas kernels for 29%

profile of v9, /device:TPU:0, one launch (start us, length us, event | category | flops | bytes accessed | tf_op | source)
XLA Modules:
  0.0 108.0 jit_solution(1258220054003566137)
XLA Ops:
  0.7 2.6 %shard_map.271 = (bf16[144,512]{1,0:T(8,128)(2,1)S(1)}, f32[3,1,64]{2,1,0:T(1,128)S(1)}, bf16[1536,512]{1,0:T(8,128)(2,1)S(1)}, bf16[1536,512]{1,0:T(8,128)(2,1)S(1)}) custom-call(s32[3]{0:T(128)S(1)} %pad_add_fusion.where_ref, bf16[64,512]{1,0:T(8,128)(2,1)} %bitcast.35, bf16[64,512]{1,0:T(8,128)(2,1)} %bitcast.36, f32[1,64]{1,0:T(1,128)} %bitcast.37, ...), custom_call_target="tpu_custom_call" | custom-call | tf_op jit(solution)/shard_map/pallas_call | solution.py:609
  3.4 3.0 %collective-permute-start.1 = (bf16[144,512]{1,0:T(8,128)(2,1)S(1)}, bf16[144,512]{1,0:T(8,128)(2,1)S(1)}, u32[]{:S(2)}, u32[]{:S(2)}) collective-permute-start(bf16[144,512]{1,0:T(8,128)(2,1)S(1)} %get-tuple-element.83.a0.refs_8_.refs_11_.a_ref), channel_id=1, source_target_pairs={{0,2},{1,3},{2,0},{3,1},{4,6},{5,7},{6,4},{7,5},{8,10},{9,11},{10,... | collective-permute-start | bytes 442376 | tf_op jit(solution)/shard_map/ppermute | solution.py:631
  6.4 1.2 %shard_map.272 = (bf16[384,512]{1,0:T(8,128)(2,1)S(1)}, bf16[512,512]{1,0:T(8,128)(2,1)S(1)}) custom-call(bf16[64,512]{1,0:T(8,128)(2,1)} %out_real, bf16[64,512]{1,0:T(8,128)(2,1)} %out_imag.1, bf16[512,256]{1,0:T(8,128)(2,1)} %up.1, bf16[512,256]{1,0:T(8,128)(2,1)} %gate.1, bf16[256,512]{1,0:T(8,128)(2,1)} %down.1), custom_call_target="tpu_custom_call" | custom-call | tf_op jit(solution)/shard_map/pallas_call | solution.py:609
  7.6 2.9 %shard_map.273 = (bf16[1536,512]{1,0:T(8,128)(2,1)S(1)}, f32[1536,512]{1,0:T(8,128)S(1)}, f32[1536,128]{1,0:T(8,128)S(1)}, bf16[1536,512]{1,0:T(8,128)(2,1)S(1)}) custom-call(s32[3]{0:T(128)S(1)} %pad_add_fusion.where_ref, bf16[1536,512]{1,0:T(8,128)(2,1)S(1)} %get-tuple-element.81.tok, bf16[1536,512]{1,0:T(8,128)(2,1)S(1)} %get-tuple-element.86.cot, ...), custom_call_target="tpu_custom_call" | custom-call | tf_op jit(solution)/shard_map/pallas_call | solution.py:609
  10.5 1.4 %collective-permute-start.7 = (bf16[384,512]{1,0:T(8,128)(2,1)S(1)}, bf16[384,512]{1,0:T(8,128)(2,1)S(1)}, u32[]{:S(2)}, u32[]{:S(2)}) collective-permute-start(bf16[384,512]{1,0:T(8,128)(2,1)S(1)} %get-tuple-element.97.b0.refs_15_), channel_id=1, source_target_pairs={{0,2},{1,3},{2,0},{3,1},{4,6},{5,7},{6,4},{7,5},{8,10},{9,11},{10,... | collective-permute-start | bytes 1179656 | tf_op jit(solution)/shard_map/ppermute | solution.py:631
  12.5 0.7 collective-permute-start.10
  13.6 2.1 %shard_map.274 = (f32[1536,512]{1,0:T(8,128)S(1)}, f32[12,512]{1,0:T(8,128)S(1)}, f32[8,512]{1,0:T(8,128)S(1)}) custom-call(s32[3]{0:T(128)S(1)} %pad_add_fusion.where_ref, bf16[1536,512]{1,0:T(8,128)(2,1)S(1)} %get-tuple-element.87.low_all.refs_4_, bf16[144,512]{1,0:T(8,128)(2,1)S(1)} %get-tuple-element.83.a0.refs_8_.refs_11_.a_ref, ...), custom_call_target="tpu_custom_call" | custom-call | tf_op jit(solution)/shard_map/pallas_call | solution.py:609
  15.6 1.6 %collective-permute-start.3 = (f32[12,512]{1,0:T(8,128)S(1)}, f32[12,512]{1,0:T(8,128)S(1)}, u32[]{:S(2)}, u32[]{:S(2)}) collective-permute-start(f32[12,512]{1,0:T(8,128)S(1)} %get-tuple-element.89.mine_ref), channel_id=1, source_target_pairs={{0,4},{4,0},{8,12},{12,8},{16,20},{20,16},{24,28},{28,24},{1,5},{5... | collective-permute-start | bytes 73736 | tf_op jit(solution)/shard_map/ppermute | solution.py:644
  17.2 2.1 %shard_map.275.refs_4_ = f32[1536,512]{1,0:T(8,128)S(1)} custom-call(f32[1536,512]{1,0:T(8,128)S(1)} %get-tuple-element.90.drive_all, bf16[144,512]{1,0:T(8,128)(2,1)S(1)} %get-tuple-element.83.a0.refs_8_.refs_11_.a_ref, bf16[144,512]{1,0:T(8,128)(2,1)S(1)} %collective-permute-done.a1.refs_9_.refs_12_, ...), custom_call_target="tpu_custom_call" | custom-call | tf_op jit(solution)/shard_map/pallas_call | solution.py:609
  19.6 0.6 shard_map.276.mine_ref
  20.2 3.5 %collective-permute-start.4 = (f32[12,512]{1,0:T(8,128)S(1)}, f32[12,512]{1,0:T(8,128)S(1)}, u32[]{:S(2)}, u32[]{:S(2)}) collective-permute-start(f32[12,512]{1,0:T(8,128)S(1)} %shard_map.276.mine_ref), channel_id=1, source_target_pairs={{0,8},{4,12},{8,16},{12,20},{16,24},{20,28},{1,9},{5,13},{9,17},{1... | collective-permute-start | bytes 73736 | tf_op jit(solution)/shard_map/ppermute | solution.py:648
  23.8 1.5 %collective-permute-done.4.other_ref.refs_0_ = f32[12,512]{1,0:T(8,128)S(1)} collective-permute-done((f32[12,512]{1,0:T(8,128)S(1)}, f32[12,512]{1,0:T(8,128)S(1)}, u32[]{:S(2)}, u32[]{:S(2)}) %collective-permute-start.4) | collective-permute-done | bytes 24608 | tf_op jit(solution)/shard_map/ppermute | solution.py:648
  25.3 5.2 %collective-permute-start.5 = (f32[12,512]{1,0:T(8,128)S(1)}, f32[12,512]{1,0:T(8,128)S(1)}, u32[]{:S(2)}, u32[]{:S(2)}) collective-permute-start(f32[12,512]{1,0:T(8,128)S(1)} %shard_map.277), channel_id=1, source_target_pairs={{0,16},{4,20},{8,24},{12,28},{1,17},{5,21},{9,25},{13,29},{2,18},{... | collective-permute-start | bytes 73736 | tf_op jit(solution)/shard_map/ppermute | solution.py:648
  30.8 2.8 %shard_map.278.refs_6_ = bf16[1536,1024]{1,0:T(8,128)(2,1)S(1)} custom-call(s32[3]{0:T(128)S(1)} %pad_add_fusion.where_ref, bf16[1536,512]{1,0:T(8,128)(2,1)S(1)} %get-tuple-element.95.cotm_all.refs_7_, bf16[384,512]{1,0:T(8,128)(2,1)S(1)} %get-tuple-element.97.b0.refs_15_, bf16[384,512]{1,0:T(8,128)(2,1)S(1)} %collective-permute-done.6.b1.refs_16_, ...), custom_call_target="tpu_custom_call" | custom-call | tf_op jit(solution)/shard_map/pallas_call | solution.py:609
  34.0 1.6 %collective-permute-done.11.refs_22_ = bf16[512,512]{1,0:T(8,128)(2,1)S(1)} collective-permute-done((bf16[512,512]{1,0:T(8,128)(2,1)S(1)}, bf16[512,512]{1,0:T(8,128)(2,1)S(1)}, u32[]{:S(2)}, u32[]{:S(2)}) %collective-permute-start.11) | collective-permute-done | bytes 524320 | tf_op jit(solution)/shard_map/ppermute | solution.py:627
  35.7 15.9 %shard_map.279 = (bf16[1536,512]{1,0:T(8,128)(2,1)S(1)}, f32[1536,512]{1,0:T(8,128)S(1)}, f32[12,512]{1,0:T(8,128)S(1)}, bf16[1536,512]{1,0:T(8,128)(2,1)S(1)}, ...) custom-call(s32[3]{0:T(128)} %copy-done, ...), custom_call_target="tpu_custom_call" | custom-call | tf_op jit(solution)/shard_map/pallas_call | solution.py:609
  52.0 1.5 %collective-permute-start.12 = (f32[12,512]{1,0:T(8,128)S(1)}, f32[12,512]{1,0:T(8,128)S(1)}, u32[]{:S(2)}, u32[]{:S(2)}) collective-permute-start(f32[12,512]{1,0:T(8,128)S(1)} %get-tuple-element.102.mine_ref), channel_id=1, source_target_pairs={{0,4},{4,0},{8,12},{12,8},{16,20},{20,16},{24,28},{28,24},{1,5},{5... | collective-permute-start | bytes 73736 | tf_op jit(solution)/shard_map/ppermute | solution.py:644
  53.5 0.7 collective-permute-done.13.other_ref
  54.2 0.8 shard_map.280
  54.9 1.0 collective-permute-done.12.other_ref.refs_2_
  55.9 1.5 %collective-permute-start.16 = (bf16[448,512]{1,0:T(8,128)(2,1)S(1)}, bf16[448,512]{1,0:T(8,128)(2,1)S(1)}, u32[]{:S(2)}, u32[]{:S(2)}) collective-permute-start(bf16[448,512]{1,0:T(8,128)(2,1)S(1)} %get-tuple-element.113), channel_id=1, source_target_pairs={{0,4},{4,0},{8,12},{12,8},{16,20},{20,16},{24,28},{28,24},{1,5},{5... | collective-permute-start | bytes 1376264 | tf_op jit(solution)/shard_map/ppermute | solution.py:644
  57.4 0.6 shard_map.281.mine_ref
  57.9 1.5 %collective-permute-start.14 = (f32[12,512]{1,0:T(8,128)S(1)}, f32[12,512]{1,0:T(8,128)S(1)}, u32[]{:S(2)}, u32[]{:S(2)}) collective-permute-start(f32[12,512]{1,0:T(8,128)S(1)} %shard_map.281.mine_ref), channel_id=1, source_target_pairs={{8,0},{12,4},{16,8},{20,12},{24,16},{28,20},{9,1},{13,5},{17,9},{2... | collective-permute-start | bytes 73736 | tf_op jit(solution)/shard_map/ppermute | solution.py:648
  59.4 2.1 %shard_map.282.refs_8_ = f32[1536,512]{1,0:T(8,128)S(1)} custom-call(f32[1536,512]{1,0:T(8,128)S(1)} %get-tuple-element.108.drive_all, bf16[144,512]{1,0:T(8,128)(2,1)S(1)} %get-tuple-element.83.a0.refs_8_.refs_11_.a_ref, bf16[144,512]{1,0:T(8,128)(2,1)S(1)} %collective-permute-done.a1.refs_9_.refs_12_, ...), custom_call_target="tpu_custom_call" | custom-call | tf_op jit(solution)/shard_map/pallas_call | solution.py:609
  61.5 2.2 %collective-permute-done.14.other_ref.refs_0_ = f32[12,512]{1,0:T(8,128)S(1)} collective-permute-done((f32[12,512]{1,0:T(8,128)S(1)}, f32[12,512]{1,0:T(8,128)S(1)}, u32[]{:S(2)}, u32[]{:S(2)}) %collective-permute-start.14) | collective-permute-done | bytes 24608 | tf_op jit(solution)/shard_map/ppermute | solution.py:648
  63.8 1.3 %collective-permute-start.15 = (f32[12,512]{1,0:T(8,128)S(1)}, f32[12,512]{1,0:T(8,128)S(1)}, u32[]{:S(2)}, u32[]{:S(2)}) collective-permute-start(f32[12,512]{1,0:T(8,128)S(1)} %shard_map.283), channel_id=1, source_target_pairs={{16,0},{20,4},{24,8},{28,12},{17,1},{21,5},{25,9},{29,13},{18,2},{... | collective-permute-start | bytes 73736 | tf_op jit(solution)/shard_map/ppermute | solution.py:648
  65.1 2.6 %shard_map.284.own_ref = bf16[1536,512]{1,0:T(8,128)(2,1)S(1)} custom-call(s32[3]{0:T(128)S(1)} %copy-done.1, s32[24]{0:T(128)S(1)} %copy-done.5, bf16[1536,512]{1,0:T(8,128)(2,1)S(1)} %get-tuple-element.81.tok, bf16[1536,1024]{1,0:T(8,128)(2,1)S(1)} %get-tuple-element.110.hid_all, bf16[384,512]{1,0:T(8,128)(2,1)S(1)} %get-tuple-element.97.b0.refs_15_, ...), custom_call_target="tpu_custom_call" | custom-call | tf_op jit(solution)/shard_map/pallas_call | solution.py:609
  67.7 2.8 %collective-permute-done.15.refs_1_ = f32[12,512]{1,0:T(8,128)S(1)} collective-permute-done((f32[12,512]{1,0:T(8,128)S(1)}, f32[12,512]{1,0:T(8,128)S(1)}, u32[]{:S(2)}, u32[]{:S(2)}) %collective-permute-start.15) | collective-permute-done | bytes 24608 | tf_op jit(solution)/shard_map/ppermute | solution.py:648
  70.5 0.7 shard_map.285
  71.1 1.6 %collective-permute-start.18 = (bf16[112,512]{1,0:T(8,128)(2,1)S(1)}, bf16[112,512]{1,0:T(8,128)(2,1)S(1)}, u32[]{:S(2)}, u32[]{:S(2)}) collective-permute-start(bf16[112,512]{1,0:T(8,128)(2,1)S(1)} %get-tuple-element.121), channel_id=1, source_target_pairs={{0,8},{4,12},{8,0},{12,4},{16,24},{20,28},{24,16},{28,20},{1,9},{5... | collective-permute-start | bytes 344072 | tf_op jit(solution)/shard_map/ppermute | solution.py:644
  72.8 0.8 collective-permute-start.19
  73.5 2.1 %collective-permute-start.20 = (bf16[112,512]{1,0:T(8,128)(2,1)S(1)}, bf16[112,512]{1,0:T(8,128)(2,1)S(1)}, u32[]{:S(2)}, u32[]{:S(2)}) collective-permute-start(bf16[112,512]{1,0:T(8,128)(2,1)S(1)} %get-tuple-element.123), channel_id=1, source_target_pairs={{0,24},{4,28},{8,16},{12,20},{16,8},{20,12},{24,0},{28,4},{1,25},{... | collective-permute-start | bytes 344072 | tf_op jit(solution)/shard_map/ppermute | solution.py:644
  75.6 5.7 %shard_map.286 = (bf16[1536,512]{1,0:T(8,128)(2,1)S(1)}, bf16[144,512]{1,0:T(8,128)(2,1)S(1)}, bf16[144,512]{1,0:T(8,128)(2,1)S(1)}) custom-call(s32[3]{0:T(128)S(1)} %copy-done.1, f32[12,512]{1,0:T(8,128)S(1)} %collective-permute-done.14.other_ref.refs_0_, f32[12,512]{1,0:T(8,128)S(1)} %collective-permute-done.15.refs_1_, ...), custom_call_target="tpu_custom_call" | custom-call | tf_op jit(solution)/shard_map/pallas_call | solution.py:609
  81.8 1.0 collective-permute-done.17
  83.9 1.0 collective-permute-start.27
  84.9 1.4 %collective-permute-start.26 = (bf16[112,512]{1,0:T(8,128)(2,1)S(1)}, bf16[112,512]{1,0:T(8,128)(2,1)S(1)}, u32[]{:S(2)}, u32[]{:S(2)}) collective-permute-start(bf16[112,512]{1,0:T(8,128)(2,1)S(1)} %add_convert_fusion.3.refs_0_), channel_id=1, source_target_pairs={{0,8},{4,12},{8,0},{12,4},{16,24},{20,28},{24,16},{28,20},{1,9},{5... | collective-permute-start | bytes 344072 | tf_op jit(solution)/shard_map/ppermute | solution.py:644
  86.3 2.2 %shard_map.287 = bf16[3072,512]{1,0:T(8,128)(2,1)} custom-call(s32[3]{0:T(128)S(1)} %copy-done.1, bf16[1536,512]{1,0:T(8,128)(2,1)S(1)} %shard_map.284.own_ref, bf16[1536,512]{1,0:T(8,128)(2,1)S(1)} %collective-permute-done.21.other_ref), custom_call_target="tpu_custom_call" | custom-call | tf_op jit(solution)/shard_map/pallas_call | solution.py:609
  88.5 0.8 collective-permute-done.23
  89.3 0.8 collective-permute-start.24
  90.1 1.6 %collective-permute-start.28 = (bf16[112,512]{1,0:T(8,128)(2,1)S(1)}, bf16[112,512]{1,0:T(8,128)(2,1)S(1)}, u32[]{:S(2)}, u32[]{:S(2)}) collective-permute-start(bf16[112,512]{1,0:T(8,128)(2,1)S(1)} %add_convert_fusion.3.refs_0_), channel_id=1, source_target_pairs={{0,24},{4,28},{8,16},{12,20},{16,8},{20,12},{24,0},{28,4},{1,25},{... | collective-permute-start | bytes 344072 | tf_op jit(solution)/shard_map/ppermute | solution.py:644
  92.3 1.7 %collective-permute-start.25 = (bf16[112,512]{1,0:T(8,128)(2,1)S(1)}, bf16[112,512]{1,0:T(8,128)(2,1)S(1)}, u32[]{:S(2)}, u32[]{:S(2)}) collective-permute-start(bf16[112,512]{1,0:T(8,128)(2,1)S(1)} %add_convert_fusion.3.refs_0_), channel_id=1, source_target_pairs={{0,4},{4,0},{8,12},{12,8},{16,20},{20,16},{24,28},{28,24},{1,5},{5... | collective-permute-start | bytes 344072 | tf_op jit(solution)/shard_map/ppermute | solution.py:644
  94.4 3.8 %collective-permute-done.25.refs_4_ = bf16[112,512]{1,0:T(8,128)(2,1)S(1)} collective-permute-done((bf16[112,512]{1,0:T(8,128)(2,1)S(1)}, bf16[112,512]{1,0:T(8,128)(2,1)S(1)}, u32[]{:S(2)}, u32[]{:S(2)}) %collective-permute-start.25) | collective-permute-done | bytes 114720 | tf_op jit(solution)/shard_map/ppermute | solution.py:644
  98.2 0.9 collective-permute-start.29
  99.1 1.2 %collective-permute-start.30 = (bf16[112,512]{1,0:T(8,128)(2,1)S(1)}, bf16[112,512]{1,0:T(8,128)(2,1)S(1)}, u32[]{:S(2)}, u32[]{:S(2)}) collective-permute-start(bf16[112,512]{1,0:T(8,128)(2,1)S(1)} %collective-permute-done.28.refs_3_), channel_id=1, source_target_pairs={{0,4},{4,0},{8,12},{12,8},{16,20},{20,16},{24,28},{28,24},{1,5},{5... | collective-permute-start | bytes 344072 | tf_op jit(solution)/shard_map/ppermute | solution.py:644
  100.2 3.6 %shard_map.288 = f32[3072,512]{1,0:T(8,128)} custom-call(s32[3]{0:T(128)S(1)} %copy-done.1, bf16[1536,512]{1,0:T(8,128)(2,1)S(1)} %get-tuple-element.127.own_ref, bf16[1536,512]{1,0:T(8,128)(2,1)S(1)} %collective-permute-done.22.other_ref), custom_call_target="tpu_custom_call" | custom-call | tf_op jit(solution)/shard_map/pallas_call | solution.py:609
  103.8 0.6 collective-permute-done.30.refs_5_
  104.4 1.9 %shard_map.289 = (f32[64,512]{1,0:T(8,128)}, f32[64,512]{1,0:T(8,128)}, f32[512,256]{1,0:T(8,128)}, f32[512,256]{1,0:T(8,128)}, f32[256,512]{1,0:T(8,128)}) custom-call(s32[3]{0:T(128)S(1)} %copy-done.1, bf16[112,512]{1,0:T(8,128)(2,1)S(1)} %add_convert_fusion.3.refs_0_, bf16[112,512]{1,0:T(8,128)(2,1)S(1)} %collective-permute-done.26.refs_1_, ...), custom_call_target="tpu_custom_call" | custom-call | tf_op jit(solution)/shard_map/pallas_call | solution.py:609
  106.4 1.5 %shard_map.290 = (f32[1,512]{1,0:T(1,128)}, f32[1,512]{1,0:T(1,128)}, f32[1,512]{1,0:T(1,128)}, f32[64,512]{1,0:T(8,128)}, f32[64,512]{1,0:T(8,128)}, /*index=5*...) custom-call(s32[3]{0:T(128)S(1)} %copy-done.1, bf16[144,512]{1,0:T(8,128)(2,1)S(1)} %add_convert_fusion.mine_ref, ...), custom_call_target="tpu_custom_call" | custom-call | tf_op jit(solution)/shard_map/pallas_call | solution.py:609
  (54 shorter events, 5.1 us)
Async XLA Ops:
  0.7 30.1 %copy-start = (s32[3]{0:T(128)}, s32[3]{0:T(128)S(1)}, u32[]{:S(2)}) copy-start(s32[3]{0:T(128)S(1)} %pad_add_fusion.where_ref) | copy-start | bytes 40
  3.4 7.2 %collective-permute-start.1 = (bf16[144,512]{1,0:T(8,128)(2,1)S(1)}, bf16[144,512]{1,0:T(8,128)(2,1)S(1)}, u32[]{:S(2)}, u32[]{:S(2)}) collective-permute-start(bf16[144,512]{1,0:T(8,128)(2,1)S(1)} %get-tuple-element.83.a0.refs_8_.refs_11_.a_ref), channel_id=1, source_target_pairs={{0,2},{1,3},{2,0},{3,1},{4,6},{5,7},{6,4},{7,5},{8,10},{9,11},{10,... | collective-permute-start | bytes 442376 | tf_op jit(solution)/shard_map/ppermute | solution.py:631
  10.5 14.7 %collective-permute-start.7 = (bf16[384,512]{1,0:T(8,128)(2,1)S(1)}, bf16[384,512]{1,0:T(8,128)(2,1)S(1)}, u32[]{:S(2)}, u32[]{:S(2)}) collective-permute-start(bf16[384,512]{1,0:T(8,128)(2,1)S(1)} %get-tuple-element.97.b0.refs_15_), channel_id=1, source_target_pairs={{0,2},{1,3},{2,0},{3,1},{4,6},{5,7},{6,4},{7,5},{8,10},{9,11},{10,... | collective-permute-start | bytes 1179656 | tf_op jit(solution)/shard_map/ppermute | solution.py:631
  12.0 1.4 %collective-permute-start = (bf16[144,512]{1,0:T(8,128)(2,1)S(1)}, bf16[144,512]{1,0:T(8,128)(2,1)S(1)}, u32[]{:S(2)}, u32[]{:S(2)}) collective-permute-start(bf16[144,512]{1,0:T(8,128)(2,1)S(1)} %get-tuple-element.83.a0.refs_8_.refs_11_.a_ref), channel_id=1, source_target_pairs={{0,1},{1,0},{2,3},{3,2},{4,5},{5,4},{6,7},{7,6},{8,9},{9,8},{10,11... | collective-permute-start | bytes 442376 | tf_op jit(solution)/shard_map/ppermute | solution.py:627
  12.0 1.6 %collective-permute-start.2 = (bf16[144,512]{1,0:T(8,128)(2,1)S(1)}, bf16[144,512]{1,0:T(8,128)(2,1)S(1)}, u32[]{:S(2)}, u32[]{:S(2)}) collective-permute-start(bf16[144,512]{1,0:T(8,128)(2,1)S(1)} %collective-permute-done.1.a2.refs_10_.refs_13_), channel_id=1, source_target_pairs={{0,1},{1,0},{2,3},{3,2},{4,5},{5,4},{6,7},{7,6},{8,9},{9,8},{10,11... | collective-permute-start | bytes 442376 | tf_op jit(solution)/shard_map/ppermute | solution.py:627
  12.5 21.2 %collective-permute-start.10 = (bf16[512,512]{1,0:T(8,128)(2,1)S(1)}, bf16[512,512]{1,0:T(8,128)(2,1)S(1)}, u32[]{:S(2)}, u32[]{:S(2)}) collective-permute-start(bf16[512,512]{1,0:T(8,128)(2,1)S(1)} %get-tuple-element.99.refs_19_), channel_id=1, source_target_pairs={{0,2},{1,3},{2,0},{3,1},{4,6},{5,7},{6,4},{7,5},{8,10},{9,11},{10,... | collective-permute-start | bytes 1572872 | tf_op jit(solution)/shard_map/ppermute | solution.py:631
  15.6 4.0 %collective-permute-start.3 = (f32[12,512]{1,0:T(8,128)S(1)}, f32[12,512]{1,0:T(8,128)S(1)}, u32[]{:S(2)}, u32[]{:S(2)}) collective-permute-start(f32[12,512]{1,0:T(8,128)S(1)} %get-tuple-element.89.mine_ref), channel_id=1, source_target_pairs={{0,4},{4,0},{8,12},{12,8},{16,20},{20,16},{24,28},{28,24},{1,5},{5... | collective-permute-start | bytes 73736 | tf_op jit(solution)/shard_map/ppermute | solution.py:644
  20.2 5.1 %collective-permute-start.4 = (f32[12,512]{1,0:T(8,128)S(1)}, f32[12,512]{1,0:T(8,128)S(1)}, u32[]{:S(2)}, u32[]{:S(2)}) collective-permute-start(f32[12,512]{1,0:T(8,128)S(1)} %shard_map.276.mine_ref), channel_id=1, source_target_pairs={{0,8},{4,12},{8,16},{12,20},{16,24},{20,28},{1,9},{5,13},{9,17},{1... | collective-permute-start | bytes 73736 | tf_op jit(solution)/shard_map/ppermute | solution.py:648
  23.7 7.1 %collective-permute-start.6 = (bf16[384,512]{1,0:T(8,128)(2,1)S(1)}, bf16[384,512]{1,0:T(8,128)(2,1)S(1)}, u32[]{:S(2)}, u32[]{:S(2)}) collective-permute-start(bf16[384,512]{1,0:T(8,128)(2,1)S(1)} %get-tuple-element.97.b0.refs_15_), channel_id=1, source_target_pairs={{0,1},{1,0},{2,3},{3,2},{4,5},{5,4},{6,7},{7,6},{8,9},{9,8},{10,11... | collective-permute-start | bytes 1179656 | tf_op jit(solution)/shard_map/ppermute | solution.py:627
  25.3 5.6 %collective-permute-start.8 = (bf16[384,512]{1,0:T(8,128)(2,1)S(1)}, bf16[384,512]{1,0:T(8,128)(2,1)S(1)}, u32[]{:S(2)}, u32[]{:S(2)}) collective-permute-start(bf16[384,512]{1,0:T(8,128)(2,1)S(1)} %collective-permute-done.7.b2.refs_17_), channel_id=1, source_target_pairs={{0,1},{1,0},{2,3},{3,2},{4,5},{5,4},{6,7},{7,6},{8,9},{9,8},{10,11... | collective-permute-start | bytes 1179656 | tf_op jit(solution)/shard_map/ppermute | solution.py:627
  25.3 8.4 %collective-permute-start.5 = (f32[12,512]{1,0:T(8,128)S(1)}, f32[12,512]{1,0:T(8,128)S(1)}, u32[]{:S(2)}, u32[]{:S(2)}) collective-permute-start(f32[12,512]{1,0:T(8,128)S(1)} %shard_map.277), channel_id=1, source_target_pairs={{0,16},{4,20},{8,24},{12,28},{1,17},{5,21},{9,25},{13,29},{2,18},{... | collective-permute-start | bytes 73736 | tf_op jit(solution)/shard_map/ppermute | solution.py:648
  30.5 3.5 %collective-permute-start.9 = (bf16[512,512]{1,0:T(8,128)(2,1)S(1)}, bf16[512,512]{1,0:T(8,128)(2,1)S(1)}, u32[]{:S(2)}, u32[]{:S(2)}) collective-permute-start(bf16[512,512]{1,0:T(8,128)(2,1)S(1)} %get-tuple-element.99.refs_19_), channel_id=1, source_target_pairs={{0,1},{1,0},{2,3},{3,2},{4,5},{5,4},{6,7},{7,6},{8,9},{9,8},{10,11... | collective-permute-start | bytes 1572872 | tf_op jit(solution)/shard_map/ppermute | solution.py:627
  30.8 4.9 %copy-start.2 = (f32[512]{0:T(512)S(1)}, f32[512]{0:T(512)}, u32[]{:S(2)}) copy-start(f32[512]{0:T(512)} %param.18) | copy-start | bytes 6148
  30.8 4.9 %copy-start.3 = (f32[512]{0:T(512)S(1)}, f32[512]{0:T(512)}, u32[]{:S(2)}) copy-start(f32[512]{0:T(512)} %param.19) | copy-start | bytes 6148
  30.8 4.9 %copy-start.4 = (f32[512]{0:T(512)S(1)}, f32[512]{0:T(512)}, u32[]{:S(2)}) copy-start(f32[512]{0:T(512)} %param.20) | copy-start | bytes 6148
  33.7 2.0 %collective-permute-start.11 = (bf16[512,512]{1,0:T(8,128)(2,1)S(1)}, bf16[512,512]{1,0:T(8,128)(2,1)S(1)}, u32[]{:S(2)}, u32[]{:S(2)}) collective-permute-start(bf16[512,512]{1,0:T(8,128)(2,1)S(1)} %collective-permute-done.10.refs_21_), channel_id=1, source_target_pairs={{0,1},{1,0},{2,3},{3,2},{4,5},{5,4},{6,7},{7,6},{8,9},{9,8},{10,11... | collective-permute-start | bytes 1572872 | tf_op jit(solution)/shard_map/ppermute | solution.py:627
  35.7 18.5 %copy-start.1 = (s32[3]{0:T(128)S(1)}, s32[3]{0:T(128)}, u32[]{:S(2)}) copy-start(s32[3]{0:T(128)} %copy-done) | copy-start | bytes 40
  51.6 2.5 %collective-permute-start.13 = (bf16[896,512]{1,0:T(8,128)(2,1)S(1)}, bf16[896,512]{1,0:T(8,128)(2,1)S(1)}, u32[]{:S(2)}, u32[]{:S(2)}) collective-permute-start(bf16[896,512]{1,0:T(8,128)(2,1)S(1)} %get-tuple-element.104), channel_id=1, source_target_pairs={{0,1},{1,0},{2,3},{3,2},{4,5},{5,4},{6,7},{7,6},{8,9},{9,8},{10,11... | collective-permute-start | bytes 2752520 | tf_op jit(solution)/shard_map/ppermute | solution.py:627
  52.0 3.9 %collective-permute-start.12 = (f32[12,512]{1,0:T(8,128)S(1)}, f32[12,512]{1,0:T(8,128)S(1)}, u32[]{:S(2)}, u32[]{:S(2)}) collective-permute-start(f32[12,512]{1,0:T(8,128)S(1)} %get-tuple-element.102.mine_ref), channel_id=1, source_target_pairs={{0,4},{4,0},{8,12},{12,8},{16,20},{20,16},{24,28},{28,24},{1,5},{5... | collective-permute-start | bytes 73736 | tf_op jit(solution)/shard_map/ppermute | solution.py:644
  55.9 14.6 %collective-permute-start.16 = (bf16[448,512]{1,0:T(8,128)(2,1)S(1)}, bf16[448,512]{1,0:T(8,128)(2,1)S(1)}, u32[]{:S(2)}, u32[]{:S(2)}) collective-permute-start(bf16[448,512]{1,0:T(8,128)(2,1)S(1)} %get-tuple-element.113), channel_id=1, source_target_pairs={{0,4},{4,0},{8,12},{12,8},{16,20},{20,16},{24,28},{28,24},{1,5},{5... | collective-permute-start | bytes 1376264 | tf_op jit(solution)/shard_map/ppermute | solution.py:644
  57.9 5.8 %collective-permute-start.14 = (f32[12,512]{1,0:T(8,128)S(1)}, f32[12,512]{1,0:T(8,128)S(1)}, u32[]{:S(2)}, u32[]{:S(2)}) collective-permute-start(f32[12,512]{1,0:T(8,128)S(1)} %shard_map.281.mine_ref), channel_id=1, source_target_pairs={{8,0},{12,4},{16,8},{20,12},{24,16},{28,20},{9,1},{13,5},{17,9},{2... | collective-permute-start | bytes 73736 | tf_op jit(solution)/shard_map/ppermute | solution.py:648
  59.4 5.6 %copy-start.5 = (s32[24]{0:T(128)S(1)}, s32[24]{0:T(128)}, u32[]{:S(2)}) copy-start(s32[24]{0:T(128)} %lens_ref.1) | copy-start | bytes 292
  63.8 6.7 %collective-permute-start.15 = (f32[12,512]{1,0:T(8,128)S(1)}, f32[12,512]{1,0:T(8,128)S(1)}, u32[]{:S(2)}, u32[]{:S(2)}) collective-permute-start(f32[12,512]{1,0:T(8,128)S(1)} %shard_map.283), channel_id=1, source_target_pairs={{16,0},{20,4},{24,8},{28,12},{17,1},{21,5},{25,9},{29,13},{18,2},{... | collective-permute-start | bytes 73736 | tf_op jit(solution)/shard_map/ppermute | solution.py:648
  71.1 10.3 %collective-permute-start.18 = (bf16[112,512]{1,0:T(8,128)(2,1)S(1)}, bf16[112,512]{1,0:T(8,128)(2,1)S(1)}, u32[]{:S(2)}, u32[]{:S(2)}) collective-permute-start(bf16[112,512]{1,0:T(8,128)(2,1)S(1)} %get-tuple-element.121), channel_id=1, source_target_pairs={{0,8},{4,12},{8,0},{12,4},{16,24},{20,28},{24,16},{28,20},{1,9},{5... | collective-permute-start | bytes 344072 | tf_op jit(solution)/shard_map/ppermute | solution.py:644
  72.8 8.9 %collective-permute-start.19 = (bf16[112,512]{1,0:T(8,128)(2,1)S(1)}, bf16[112,512]{1,0:T(8,128)(2,1)S(1)}, u32[]{:S(2)}, u32[]{:S(2)}) collective-permute-start(bf16[112,512]{1,0:T(8,128)(2,1)S(1)} %get-tuple-element.122), channel_id=1, source_target_pairs={{0,16},{4,20},{8,24},{12,28},{16,0},{20,4},{24,8},{28,12},{1,17},{... | collective-permute-start | bytes 344072 | tf_op jit(solution)/shard_map/ppermute | solution.py:644
  73.5 8.2 %collective-permute-start.20 = (bf16[112,512]{1,0:T(8,128)(2,1)S(1)}, bf16[112,512]{1,0:T(8,128)(2,1)S(1)}, u32[]{:S(2)}, u32[]{:S(2)}) collective-permute-start(bf16[112,512]{1,0:T(8,128)(2,1)S(1)} %get-tuple-element.123), channel_id=1, source_target_pairs={{0,24},{4,28},{8,16},{12,20},{16,8},{20,12},{24,0},{28,4},{1,25},{... | collective-permute-start | bytes 344072 | tf_op jit(solution)/shard_map/ppermute | solution.py:644
  81.3 1.4 %collective-permute-start.17 = (bf16[144,512]{1,0:T(8,128)(2,1)S(1)}, bf16[144,512]{1,0:T(8,128)(2,1)S(1)}, u32[]{:S(2)}, u32[]{:S(2)}) collective-permute-start(bf16[144,512]{1,0:T(8,128)(2,1)S(1)} %get-tuple-element.120), channel_id=1, source_target_pairs={{0,1},{1,0},{2,3},{3,2},{4,5},{5,4},{6,7},{7,6},{8,9},{9,8},{10,11... | collective-permute-start | bytes 442376 | tf_op jit(solution)/shard_map/ppermute | solution.py:627
  82.8 3.5 %collective-permute-start.21 = (bf16[1536,512]{1,0:T(8,128)(2,1)S(1)}, bf16[1536,512]{1,0:T(8,128)(2,1)S(1)}, u32[]{:S(2)}, u32[]{:S(2)}) collective-permute-start(bf16[1536,512]{1,0:T(8,128)(2,1)S(1)} %shard_map.284.own_ref), channel_id=1, source_target_pairs={{0,1},{1,0},{2,3},{3,2},{4,5},{5,4},{6,7},{7,6},{8,9},{9,8},{10,11... | collective-permute-start | bytes 4718600 | tf_op jit(solution)/shard_map/ppermute | solution.py:627
  83.0 17.2 %collective-permute-start.22 = (bf16[1536,512]{1,0:T(8,128)(2,1)S(1)}, bf16[1536,512]{1,0:T(8,128)(2,1)S(1)}, u32[]{:S(2)}, u32[]{:S(2)}) collective-permute-start(bf16[1536,512]{1,0:T(8,128)(2,1)S(1)} %get-tuple-element.127.own_ref), channel_id=1, source_target_pairs={{0,1},{1,0},{2,3},{3,2},{4,5},{5,4},{6,7},{7,6},{8,9},{9,8},{10,11... | collective-permute-start | bytes 4718600 | tf_op jit(solution)/shard_map/ppermute | solution.py:627
  83.4 5.9 %collective-permute-start.23 = (bf16[144,512]{1,0:T(8,128)(2,1)S(1)}, bf16[144,512]{1,0:T(8,128)(2,1)S(1)}, u32[]{:S(2)}, u32[]{:S(2)}) collective-permute-start(bf16[144,512]{1,0:T(8,128)(2,1)S(1)} %add_convert_fusion.2), channel_id=1, source_target_pairs={{0,4},{4,0},{8,12},{12,8},{16,20},{20,16},{24,28},{28,24},{1,5},{5... | collective-permute-start | bytes 442376 | tf_op jit(solution)/shard_map/ppermute | solution.py:644
  83.9 8.4 %collective-permute-start.27 = (bf16[112,512]{1,0:T(8,128)(2,1)S(1)}, bf16[112,512]{1,0:T(8,128)(2,1)S(1)}, u32[]{:S(2)}, u32[]{:S(2)}) collective-permute-start(bf16[112,512]{1,0:T(8,128)(2,1)S(1)} %add_convert_fusion.3.refs_0_), channel_id=1, source_target_pairs={{0,16},{4,20},{8,24},{12,28},{16,0},{20,4},{24,8},{28,12},{1,17},{... | collective-permute-start | bytes 344072 | tf_op jit(solution)/shard_map/ppermute | solution.py:644
  84.9 9.1 %collective-permute-start.26 = (bf16[112,512]{1,0:T(8,128)(2,1)S(1)}, bf16[112,512]{1,0:T(8,128)(2,1)S(1)}, u32[]{:S(2)}, u32[]{:S(2)}) collective-permute-start(bf16[112,512]{1,0:T(8,128)(2,1)S(1)} %add_convert_fusion.3.refs_0_), channel_id=1, source_target_pairs={{0,8},{4,12},{8,0},{12,4},{16,24},{20,28},{24,16},{28,20},{1,9},{5... | collective-permute-start | bytes 344072 | tf_op jit(solution)/shard_map/ppermute | solution.py:644
  89.3 8.9 %collective-permute-start.24 = (bf16[144,512]{1,0:T(8,128)(2,1)S(1)}, bf16[144,512]{1,0:T(8,128)(2,1)S(1)}, u32[]{:S(2)}, u32[]{:S(2)}) collective-permute-start(bf16[144,512]{1,0:T(8,128)(2,1)S(1)} %add_convert_fusion.1), channel_id=1, source_target_pairs={{0,8},{4,12},{8,0},{12,4},{16,24},{20,28},{24,16},{28,20},{1,9},{5... | collective-permute-start | bytes 442376 | tf_op jit(solution)/shard_map/ppermute | solution.py:644
  90.1 8.1 %collective-permute-start.28 = (bf16[112,512]{1,0:T(8,128)(2,1)S(1)}, bf16[112,512]{1,0:T(8,128)(2,1)S(1)}, u32[]{:S(2)}, u32[]{:S(2)}) collective-permute-start(bf16[112,512]{1,0:T(8,128)(2,1)S(1)} %add_convert_fusion.3.refs_0_), channel_id=1, source_target_pairs={{0,24},{4,28},{8,16},{12,20},{16,8},{20,12},{24,0},{28,4},{1,25},{... | collective-permute-start | bytes 344072 | tf_op jit(solution)/shard_map/ppermute | solution.py:644
  92.3 5.9 %collective-permute-start.25 = (bf16[112,512]{1,0:T(8,128)(2,1)S(1)}, bf16[112,512]{1,0:T(8,128)(2,1)S(1)}, u32[]{:S(2)}, u32[]{:S(2)}) collective-permute-start(bf16[112,512]{1,0:T(8,128)(2,1)S(1)} %add_convert_fusion.3.refs_0_), channel_id=1, source_target_pairs={{0,4},{4,0},{8,12},{12,8},{16,20},{20,16},{24,28},{28,24},{1,5},{5... | collective-permute-start | bytes 344072 | tf_op jit(solution)/shard_map/ppermute | solution.py:644
  94.0 9.8 %collective-permute-start.31 = (bf16[224,512]{1,0:T(8,128)(2,1)S(1)}, bf16[224,512]{1,0:T(8,128)(2,1)S(1)}, u32[]{:S(2)}, u32[]{:S(2)}) collective-permute-start(bf16[224,512]{1,0:T(8,128)(2,1)S(1)} %pad_maximum_fusion), channel_id=1, source_target_pairs={{0,4},{4,0},{8,12},{12,8},{16,20},{20,16},{24,28},{28,24},{1,5},{5... | collective-permute-start | bytes 688136 | tf_op jit(solution)/shard_map/ppermute | solution.py:644
  98.2 8.1 %collective-permute-start.29 = (bf16[144,512]{1,0:T(8,128)(2,1)S(1)}, bf16[144,512]{1,0:T(8,128)(2,1)S(1)}, u32[]{:S(2)}, u32[]{:S(2)}) collective-permute-start(bf16[144,512]{1,0:T(8,128)(2,1)S(1)} %add_convert_fusion.mine_ref), channel_id=1, source_target_pairs={{0,16},{4,20},{8,24},{12,28},{16,0},{20,4},{24,8},{28,12},{1,17},{... | collective-permute-start | bytes 442376 | tf_op jit(solution)/shard_map/ppermute | solution.py:644
  99.1 5.3 %collective-permute-start.30 = (bf16[112,512]{1,0:T(8,128)(2,1)S(1)}, bf16[112,512]{1,0:T(8,128)(2,1)S(1)}, u32[]{:S(2)}, u32[]{:S(2)}) collective-permute-start(bf16[112,512]{1,0:T(8,128)(2,1)S(1)} %collective-permute-done.28.refs_3_), channel_id=1, source_target_pairs={{0,4},{4,0},{8,12},{12,8},{16,20},{20,16},{24,28},{28,24},{1,5},{5... | collective-permute-start | bytes 344072 | tf_op jit(solution)/shard_map/ppermute | solution.py:644
